TPU v7x, 512 devices: a whole 4x8x8 slice. The times are simulated.
512 devices in a mesh: dp: 32 (over z_hi, y), feat: 16 (over z_lo, x, core).
Axes of the slice: x: 4, y: 8, z: 8 (z_hi: 4, z_lo: 2; z = z_hi * 2 + z_lo), core: 2. Of those that a mesh axis runs over, the one named last changes fastest.
Arguments:
- first_view_outputs: bfloat16 [2048, 8192], P('dp', 'feat'), may hold values from -120 to 120
- second_view_outputs: bfloat16 [2048, 8192], P('feat', 'dp'), may hold values from -120 to 120
Outputs:
- first_view_gradient: bfloat16 [2048, 8192], P('dp', 'feat')
- second_view_gradient: bfloat16 [2048, 8192], P('feat', 'dp')
All inputs are finite; a program needn't handle non-finite values.
Results may differ from a plain program's by a relative error of at most 0.033.
Values may be sent and summed in bfloat16 or wider, within the bound.
No kernel may reach another device: no remote copies, remote signals or barrier semaphores. Data moves between devices by JAX's collectives and lax.ppermute only.
A program may use at most 64 MiB of HBM per device.

v0:
```python
import jax
import jax.numpy as jnp
from jax import lax
from jax.sharding import PartitionSpec as P

EPSILON = 1e-05
OFF_WEIGHT = 0.0051


def normalize_backward(
    normalized_gradient, standardized_values, inverse_scale, column_sums, total_count
):
    centering_term = column_sums[0] / total_count
    projection_term = column_sums[1] / total_count
    return (
        (normalized_gradient - centering_term - standardized_values * projection_term)
        * inverse_scale
    ).astype(jnp.bfloat16)


def shards(first_view_outputs, second_view_outputs):
    rows_a, width_a = first_view_outputs.shape
    rows_b, width_b = second_view_outputs.shape
    total_count = rows_a * lax.axis_size("dp")
    local_a = first_view_outputs.astype(jnp.float32)
    center_a = lax.psum(jnp.sum(local_a, axis=0), "dp") / total_count
    centered_first = local_a - center_a
    inverse_deviation_first = lax.rsqrt(
        lax.psum(jnp.sum(centered_first * centered_first, axis=0), "dp") / total_count + EPSILON
    )
    standardized_first = centered_first * inverse_deviation_first
    normalized_first = lax.all_gather(
        standardized_first.astype(jnp.bfloat16), "dp", axis=0, tiled=True
    )
    local_b = second_view_outputs.astype(jnp.float32)
    center_b = lax.psum(jnp.sum(local_b, axis=0), "feat") / total_count
    centered_second = local_b - center_b
    inverse_deviation_second = lax.rsqrt(
        lax.psum(jnp.sum(centered_second * centered_second, axis=0), "feat") / total_count + EPSILON
    )
    standardized_second = centered_second * inverse_deviation_second
    normalized_second = lax.all_gather(
        standardized_second.astype(jnp.bfloat16), "feat", axis=0, tiled=True
    )
    correlation = (
        lax.dot_general(
            normalized_first,
            normalized_second,
            (((0,), (0,)), ((), ())),
            preferred_element_type=jnp.float32,
        )
        / total_count
    )
    row_ids = lax.axis_index("feat") * width_a + lax.broadcasted_iota(
        jnp.int32, (width_a, width_b), 0
    )
    col_ids = lax.axis_index("dp") * width_b + lax.broadcasted_iota(
        jnp.int32, (width_a, width_b), 1
    )
    grad_tile = jnp.where(
        row_ids == col_ids, 2.0 * (correlation - 1.0), 2.0 * OFF_WEIGHT * correlation
    ).astype(jnp.bfloat16)
    normalized_gradient_first = lax.psum_scatter(
        lax.dot_general(
            normalized_second,
            grad_tile,
            (((1,), (1,)), ((), ())),
            preferred_element_type=jnp.float32,
        ).astype(jnp.bfloat16),
        "dp",
        scatter_dimension=0,
        tiled=True,
    ).astype(jnp.float32)
    column_sums_first = lax.psum(
        (
            jnp.sum(normalized_gradient_first, axis=0),
            jnp.sum(normalized_gradient_first * standardized_first, axis=0),
        ),
        "dp",
    )
    first_view_gradient = normalize_backward(
        normalized_gradient_first,
        standardized_first,
        inverse_deviation_first,
        column_sums_first,
        total_count,
    )
    normalized_gradient_second = lax.psum_scatter(
        jnp.dot(normalized_first, grad_tile, preferred_element_type=jnp.float32).astype(
            jnp.bfloat16
        ),
        "feat",
        scatter_dimension=0,
        tiled=True,
    ).astype(jnp.float32)
    column_sums_second = lax.psum(
        (
            jnp.sum(normalized_gradient_second, axis=0),
            jnp.sum(normalized_gradient_second * standardized_second, axis=0),
        ),
        "feat",
    )
    second_view_gradient = normalize_backward(
        normalized_gradient_second,
        standardized_second,
        inverse_deviation_second,
        column_sums_second,
        total_count,
    )
    return (first_view_gradient, second_view_gradient)


def solution(mesh):
    placed = (P("dp", "feat"), P("feat", "dp"))
    return jax.shard_map(
        shards,
        mesh=mesh,
        in_specs=placed,
        out_specs=(P("dp", "feat"), P("feat", "dp")),
        check_vma=False,
    )
```

profile of v0, /device:TPU:6, one launch (start us, length us, event | category | flops | bytes accessed | tf_op | source)
XLA Modules:
  0.0 703.5 jit_solution(12489234128783055013)
XLA Ops:
  7.2 0.0 all-gather.3.cloned.1.call-start
  7.2 0.9 convert_reduce_fusion.3
  8.1 24.6 %psum.56 = f32[256]{0:T(256)S(1)} all-reduce(f32[256]{0:T(256)S(1)} %convert_reduce_fusion.3), channel_id=1, replica_groups=mesh['dp'=32,'feat'=16] {'feat'}, use_global_device_ids=true, to_apply=%region_1.0 | all-reduce | flops 256 | bytes 2048 | tf_op jit(solution)/shard_map/psum | solution.py:36
  32.7 0.9 fusion.29
  33.5 28.4 %psum.57 = f32[256]{0:T(256)S(1)} all-reduce(f32[256]{0:T(256)S(1)} %fusion.29), channel_id=1, replica_groups=mesh['dp'=32,'feat'=16] {'feat'}, use_global_device_ids=true, to_apply=%region_3.0 | all-reduce | flops 256 | bytes 2048 | tf_op jit(solution)/shard_map/psum | solution.py:39
  62.0 1.5 fusion.17
  63.5 0.0 all-gather.3.cloned.1.call-update
  63.5 0.0 all-gather.5.cloned.1.call-start
  63.5 0.9 convert_reduce_fusion.2
  64.4 88.8 %psum.58 = f32[512]{0:T(512)S(1)} all-reduce(f32[512]{0:T(512)S(1)} %convert_reduce_fusion.2), channel_id=1, replica_groups=mesh['dp'=32,'feat'=16] {'dp'}, use_global_device_ids=true, to_apply=%region_5.0 | all-reduce | flops 512 | bytes 4096 | tf_op jit(solution)/shard_map/psum | solution.py:26
  153.2 0.9 fusion.25
  154.1 76.8 %psum.59 = f32[512]{0:T(512)S(1)} all-reduce(f32[512]{0:T(512)S(1)} %fusion.25), channel_id=1, replica_groups=mesh['dp'=32,'feat'=16] {'dp'}, use_global_device_ids=true, to_apply=%region_7.0 | all-reduce | flops 512 | bytes 4096 | tf_op jit(solution)/shard_map/psum | solution.py:29
  230.9 1.5 fusion.21
  232.4 0.0 all-gather.5.cloned.1.call-update
  232.4 0.0 reduce-scatter.5.cloned.1.call-start
  232.5 0.0 all-gather.3.cloned.1.call-done
  232.5 82.2 %all-gather.5.cloned.1.call-done = bf16[2048,512]{1,0:T(8,128)(2,1)} async-done(((bf16[64,512]{1,0:T(8,128)(2,1)}), bf16[2048,512]{1,0:T(8,128)(2,1)}) %all-gather.5.cloned.1.call-update) | async-done | bytes 2097168 | tf_op jit(solution)/shard_map/all_gather | solution.py:32
  314.7 0.0 copy-start.1
  314.7 2.7 fusion.40
  317.5 0.0 copy-done.1
  317.5 0.0 copy-start
  317.5 1.8 convolution_convert_fusion.1
  319.3 0.0 reduce-scatter.5.cloned.1.call-update
  319.3 0.0 copy-start.2
  319.4 0.0 reduce-scatter.3.cloned.1.call-start
  319.4 0.0 copy-done
  319.4 2.2 convolution_convert_fusion
  321.6 0.0 copy-start.3
  321.6 0.0 reduce-scatter.3.cloned.1.call-update
  321.6 56.0 %reduce-scatter.5.cloned.1.call-done = bf16[128,256]{1,0:T(8,128)(2,1)} async-done(((bf16[2048,256]{1,0:T(8,128)(2,1)}), bf16[128,256]{1,0:T(8,128)(2,1)}) %reduce-scatter.5.cloned.1.call-update) | async-done | bytes 65552 | tf_op jit(solution)/shard_map/reduce_scatter | solution.py:88
  377.6 0.0 copy-done.2
  377.6 0.9 convert_reduce_fusion
  378.5 27.0 %all-reduce.1 = (f32[256]{0:T(256)S(1)}, f32[256]{0:T(256)S(1)}) all-reduce(f32[256]{0:T(256)S(1)} %get-tuple-element.3, f32[256]{0:T(256)S(1)} %get-tuple-element.2), channel_id=1, replica_groups=mesh['dp'=32,'feat'=16] {'feat'}, use_global_device_ids=true, to_apply=%region_17.18 | all-reduce | flops 512 | bytes 4096 | tf_op jit(solution)/shard_map/psum | solution.py:96
  405.5 1.5 fusion.28
  407.0 207.5 %reduce-scatter.3.cloned.1.call-done = bf16[64,512]{1,0:T(8,128)(2,1)} async-done(((bf16[2048,512]{1,0:T(8,128)(2,1)}), bf16[64,512]{1,0:T(8,128)(2,1)}) %reduce-scatter.3.cloned.1.call-update) | async-done | bytes 65552 | tf_op jit(solution)/shard_map/reduce_scatter | solution.py:63
  614.4 0.0 copy-done.3
  614.4 0.9 convert_reduce_fusion.1
  615.3 80.1 %all-reduce = (f32[512]{0:T(512)S(1)}, f32[512]{0:T(512)S(1)}) all-reduce(f32[512]{0:T(512)S(1)} %get-tuple-element.5, f32[512]{0:T(512)S(1)} %get-tuple-element.4), channel_id=1, replica_groups=mesh['dp'=32,'feat'=16] {'dp'}, use_global_device_ids=true, to_apply=%region_12.13 | all-reduce | flops 1024 | bytes 8192 | tf_op jit(solution)/shard_map/psum | solution.py:74
  695.4 1.5 fusion.24
  (8 shorter events, 0.1 us)
Async XLA Ops:
  7.2 225.4 %all-gather.3.cloned.1.call-start = ((), (), s32[]{:S(2)}) async-start(), calls=%async_computation.2 | async-start | bytes 1114112 | tf_op jit(solution)/shard_map/all_gather | solution.py:42
  63.5 251.2 %all-gather.5.cloned.1.call-start = ((), (), s32[]{:S(2)}) async-start(), calls=%async_computation.3 | async-start | bytes 2162688 | tf_op jit(solution)/shard_map/all_gather | solution.py:32
  232.4 145.2 %reduce-scatter.5.cloned.1.call-start = ((), (), s32[]{:S(2)}) async-start(), calls=%async_computation.5 | async-start | bytes 1114112 | tf_op jit(solution)/shard_map/reduce_scatter | solution.py:88
  314.7 2.8 copy-start.1
  317.5 1.9 copy-start
  319.3 58.3 %copy-start.2 = (bf16[128,256]{1,0:T(8,128)(2,1)S(1)}, bf16[128,256]{1,0:T(8,128)(2,1)}, u32[]{:S(2)}) copy-start(bf16[128,256]{1,0:T(8,128)(2,1)} %param.3) | copy-start | bytes 196612
  319.4 295.1 %reduce-scatter.3.cloned.1.call-start = ((), (), s32[]{:S(2)}) async-start(), calls=%async_computation.4 | async-start | bytes 2162688 | tf_op jit(solution)/shard_map/reduce_scatter | solution.py:63
  321.6 292.9 %copy-start.3 = (bf16[64,512]{1,0:T(8,128)(2,1)S(1)}, bf16[64,512]{1,0:T(8,128)(2,1)}, u32[]{:S(2)}) copy-start(bf16[64,512]{1,0:T(8,128)(2,1)} %param.2) | copy-start | bytes 196612
Sparse Core Ops, SparseCore 0:
  63.6 43.5 all-gather.2
  232.6 82.1 all-gather.4
  319.5 58.0 reduce-scatter.4
  382.6 231.8 reduce-scatter.2
where the time goes:
time: 704 us; the launch traced here: 703 us
  waiting for transfers between devices  346 us (49%)
  blocking collectives  326 us (46%)
  between operations  13.8 us (2%)
  other arithmetic  11.3 us (2%)
    reduce_scatter x1, waiting for transfers between devices, shards(): lax.psum_scatter(lax.dot_general(normalized_second, grad_tile, (((1,), (1...  207 us
    psum x1, blocking collectives, shards(): center_a = lax.psum(jnp.sum(local_a, axis=0), 'dp') / total_count  88.8 us
    all_gather x1, waiting for transfers between devices, shards(): lax.all_gather(standardized_first.astype(jnp.bfloat16), 'dp', axis=0, til...  82.2 us
    psum x1, blocking collectives, shards(): lax.psum((jnp.sum(normalized_gradient_first, axis=0), jnp.sum(normalized_...  80.1 us
    psum x1, blocking collectives, shards(): lax.psum(jnp.sum(centered_first * centered_first, axis=0), 'dp')  76.8 us
    reduce_scatter x1, waiting for transfers between devices, shards(): lax.psum_scatter(jnp.dot(normalized_first, grad_tile, preferred_element_t...  56 us
    psum x1, blocking collectives, shards(): lax.psum(jnp.sum(centered_second * centered_second, axis=0), 'feat')  28.4 us
    psum x1, blocking collectives, shards(): lax.psum((jnp.sum(normalized_gradient_second, axis=0), jnp.sum(normalized...  27 us
  transfers between devices with their start and end apart: 4, of which 3 were waited for; matrix products, arithmetic and copies ran while one was open for 1% of the time, Pallas kernels for 0%

commit v1 on v0

v1 whole, which is shorter than its diff:
```python
import jax
import jax.numpy as jnp
from jax import lax
from jax.sharding import Mesh, PartitionSpec as P

EPSILON = 1e-05
OFF_WEIGHT = 0.0051

SAMPLES = ("zh", "yk", "yl")
FEATURES = ("zl", "x", "core")
NEAR = ("yl", "zl", "x")


def exchange(values, axes):
    return lax.all_to_all(values, axes, 0, 0, tiled=True)


def statistics(values):
    wide = values.astype(jnp.float32)
    center = jnp.mean(wide, axis=0)
    shifted = wide - center
    inverse_scale = lax.rsqrt(jnp.mean(shifted * shifted, axis=0) + EPSILON)
    return (shifted * inverse_scale).astype(jnp.bfloat16), inverse_scale


def shards(first_view_outputs, second_view_outputs):
    rows_a, width_a = first_view_outputs.shape
    rows_b, width_b = second_view_outputs.shape
    n_dp = lax.axis_size(SAMPLES)
    n_near = lax.axis_size(NEAR)
    half = width_a // 2
    total_count = rows_a * n_dp
    parity = lax.axis_index("yl")

    gathered = exchange(
        jnp.broadcast_to(second_view_outputs, (n_near, rows_b, width_b)), NEAR
    )
    gathered = exchange(jnp.broadcast_to(gathered, (2, n_near, rows_b, width_b)), "core")
    second = (
        gathered.reshape(2, 2, n_near // 2, rows_b, width_b)
        .transpose(2, 0, 3, 1, 4)
        .reshape(total_count, 2 * width_b)
    )
    norm_second, inverse_second = statistics(second)

    halves = first_view_outputs.reshape(rows_a, 2, half).transpose(1, 0, 2)
    first = exchange(
        jnp.broadcast_to(halves, (n_dp // 2, 2, rows_a, half)).reshape(n_dp, rows_a, half),
        SAMPLES,
    ).reshape(total_count, half)
    norm_first, inverse_first = statistics(first)

    correlation = (
        lax.dot_general(
            norm_first,
            norm_second,
            (((0,), (0,)), ((), ())),
            preferred_element_type=jnp.float32,
        )
        / total_count
    )
    shape = correlation.shape
    row_ids = (
        lax.axis_index(FEATURES) * width_a
        + parity * half
        + lax.broadcasted_iota(jnp.int32, shape, 0)
    )
    col_ids = lax.axis_index(("zh", "yk")) * (2 * width_b) + lax.broadcasted_iota(
        jnp.int32, shape, 1
    )
    grad_tile = jnp.where(
        row_ids == col_ids, 2.0 * (correlation - 1.0), 2.0 * OFF_WEIGHT * correlation
    ).astype(jnp.bfloat16)
    grad_wide = grad_tile.astype(jnp.float32)
    weighted = grad_wide * correlation
    projection_first = jnp.sum(weighted, axis=1)
    projection_second = jnp.sum(weighted, axis=0)
    mean_first = jnp.mean(norm_first.astype(jnp.float32), axis=0)
    mean_second = jnp.mean(norm_second.astype(jnp.float32), axis=0)
    centering_first = jnp.sum(grad_wide * mean_second[None, :], axis=1)
    centering_second = jnp.sum(grad_wide * mean_first[:, None], axis=0)

    partial_second = (
        (
            jnp.dot(norm_first, grad_tile, preferred_element_type=jnp.float32)
            - centering_second
            - norm_second.astype(jnp.float32) * projection_second
        )
        * inverse_second
    ).astype(jnp.bfloat16)
    partial_first = (
        (
            lax.dot_general(
                norm_second,
                grad_tile,
                (((1,), (1,)), ((), ())),
                preferred_element_type=jnp.float32,
            )
            - centering_first
            - norm_first.astype(jnp.float32) * projection_first
        )
        * inverse_first
    ).astype(jnp.bfloat16)

    pieces = partial_second.reshape(n_near // 2, 2, rows_b, 2, width_b).transpose(1, 3, 0, 2, 4)
    pieces = exchange(pieces, "core")
    pieces = (pieces[0].astype(jnp.float32) + pieces[1].astype(jnp.float32)).astype(jnp.bfloat16)
    pieces = exchange(pieces.reshape(n_near, rows_b, width_b), NEAR)
    second_view_gradient = jnp.sum(pieces.astype(jnp.float32), axis=0).astype(jnp.bfloat16)

    parts = exchange(partial_first.reshape(n_dp, rows_a, half), SAMPLES)
    first_view_gradient = (
        jnp.sum(parts.reshape(n_dp // 2, 2, rows_a, half).astype(jnp.float32), axis=0)
        .astype(jnp.bfloat16)
        .transpose(1, 0, 2)
        .reshape(rows_a, width_a)
    )
    return first_view_gradient, second_view_gradient


def solution(mesh):
    fine = Mesh(
        mesh.devices.reshape(4, 4, 2, 2, 4, 2), ("zh", "yk", "yl", "zl", "x", "core")
    )
    specs = (P(SAMPLES, FEATURES), P(FEATURES, SAMPLES))
    return jax.shard_map(
        shards, mesh=fine, in_specs=specs, out_specs=specs, check_vma=False
    )
```

time: 704 us -> 153 us (0.22)
  the two profiles are of different devices: /device:TPU:6 before, /device:TPU:8 now
where the time goes in v1:
time: 153 us; the launch traced here: 152 us
  waiting for transfers between devices  74.4 us (49%)
  starting transfers between devices  35.2 us (23%)
  local copies, waits for them, and re-layouts  17.7 us (12%)
  blocking collectives  10.8 us (7%)
  matrix products  7.53 us (5%)
  other arithmetic  5.75 us (4%)
    all_to_all x4, waiting for transfers between devices, exchange(): return lax.all_to_all(values, axes, 0, 0, tiled=True)  74.4 us
    all_to_all x4, starting transfers between devices, exchange(): return lax.all_to_all(values, axes, 0, 0, tiled=True)  35.2 us
    all_to_all x2, blocking collectives, exchange(): return lax.all_to_all(values, axes, 0, 0, tiled=True)  10.8 us
    unnamed x11, local copies, waits for them, and re-layouts  5.15 us
    dot_general x1, matrix products, shards(): lax.dot_general(norm_second, grad_tile, (((1,), (1,)), ((), ())), preferr...  4.09 us
    convert_element_type x1, local copies, waits for them, and re-layouts, statistics(): wide = values.astype(jnp.float32)  3.27 us
    reshape x2, local copies, waits for them, and re-layouts, shards(): partial_second.reshape(n_near // 2, 2, rows_b, 2, width_b)  3.11 us
  transfers between devices with their start and end apart: 4, of which 4 were waited for; matrix products, arithmetic and copies ran while one was open for 11% of the time, Pallas kernels for 0%

profile of v1, /device:TPU:8, one launch (start us, length us, event | category | flops | bytes accessed | tf_op | source)
XLA Modules:
  0.0 152.2 jit_solution(18363944915597752109)
XLA Ops:
  0.6 0.0 copy-start.2
  0.6 2.0 %broadcast_in_dim.6 = bf16[16,128,256]{2,1,0:T(8,128)(2,1)} broadcast(bf16[128,256]{1,0:T(8,128)(2,1)} %param.3), dimensions={1,2} | broadcast | bytes 1114112 | tf_op jit(solution)/shard_map/broadcast_in_dim | solution.py:36
  2.6 9.3 %all-to-all-start = ((bf16[16,128,256]{2,1,0:T(8,128)(2,1)}), bf16[16,128,256]{2,1,0:T(8,128)(2,1)S(1)}, u32[]{:S(2)}, u32[]{:S(2)}) async-start(bf16[16,128,256]{2,1,0:T(8,128)(2,1)} %broadcast_in_dim.6), calls=%async_computation | async-start | bytes 2097152 | tf_op jit(solution)/shard_map/all_to_all | solution.py:15
  11.9 0.0 copy-done.2
  12.0 13.8 %all-to-all-done = bf16[16,128,256]{2,1,0:T(8,128)(2,1)S(1)} async-done(((bf16[16,128,256]{2,1,0:T(8,128)(2,1)}), bf16[16,128,256]{2,1,0:T(8,128)(2,1)S(1)}, u32[]{:S(2)}, u32[]{:S(2)}) %all-to-all-start) | async-done | bytes 1048608 | tf_op jit(solution)/shard_map/all_to_all | solution.py:15
  25.8 0.2 broadcast_in_dim.7
  26.0 5.4 %all_to_all.30 = bf16[2,16,128,256]{3,2,1,0:T(8,128)(2,1)S(1)} all-to-all(bf16[2,16,128,256]{3,2,1,0:T(8,128)(2,1)S(1)} %broadcast_in_dim.7), channel_id=1, replica_groups=mesh['zh'=4,'yk'=4,'yl'=2,'zl'=2,'x'=4,'core'=2] {'core'}, dimensions={0} | all-to-all | bytes 4194304 | tf_op jit(solution)/shard_map/all_to_all | solution.py:15
  31.4 1.1 broadcast_in_dim.8
  32.5 15.2 %all-to-all-start.2 = ((bf16[32,64,256]{2,1,0:T(8,128)(2,1)}), bf16[32,64,256]{2,1,0:T(8,128)(2,1)S(1)}, u32[]{:S(2)}, u32[]{:S(2)}) async-start(bf16[32,64,256]{2,1,0:T(8,128)(2,1)} %bitcast.58), calls=%async_computation.2 | async-start | bytes 2097152 | tf_op jit(solution)/shard_map/all_to_all | solution.py:15
  47.8 0.3 fusion
  48.2 0.6 multiply_reduce_fusion
  48.7 0.7 convert_reduce_fusion
  49.4 2.2 %copy.18 = bf16[8,2,128,2,256]{4,3,2,1,0:T(2,128)(2,1)S(1)} copy(bf16[8,2,128,2,256]{4,2,0,3,1:T(8,128)(2,1)S(1)} %get-tuple-element.8) | data formatting | bytes 4194304 | tf_op jit(solution)/shard_map/convert_element_type | solution.py:23
  51.6 1.8 %copy.25 = bf16[256,8,2,256]{3,1,2,0:T(8,128)(2,1)} copy(bf16[256,8,2,256]{3,2,1,0:T(2,128)(2,1)S(1)} %bitcast.54) | data formatting | bytes 4194304
  53.5 0.5 convert_bitcast_fusion
  54.0 3.3 %copy.16 = f32[8,2,128,2,256]{4,3,2,1,0:T(2,128)S(1)} copy(f32[8,2,128,2,256]{4,2,0,3,1:T(8,128)S(1)} %convert_bitcast_fusion) | data formatting | bytes 8388608 | tf_op jit(solution)/shard_map/convert_element_type | solution.py:19
  57.3 2.4 %copy.22 = f32[256,8,2,256]{3,1,2,0:T(8,128)} copy(f32[256,8,2,256]{3,2,1,0:T(2,128)S(1)} %bitcast.53) | data formatting | bytes 8388608
  59.6 0.0 copy-start.1
  59.6 19.4 %all-to-all-done.2 = bf16[32,64,256]{2,1,0:T(8,128)(2,1)S(1)} async-done(((bf16[32,64,256]{2,1,0:T(8,128)(2,1)}), bf16[32,64,256]{2,1,0:T(8,128)(2,1)S(1)}, u32[]{:S(2)}, u32[]{:S(2)}) %all-to-all-start.2) | async-done | bytes 1048608 | tf_op jit(solution)/shard_map/all_to_all | solution.py:15
  79.0 0.3 convert_reduce_fusion.2
  79.3 0.3 multiply_reduce_fusion.1
  79.6 0.5 convert_reduce_fusion.1
  80.1 0.0 copy-done.1
  80.1 0.0 copy-start
  80.1 1.0 fusion.8
  81.1 0.3 fusion.5
  81.4 0.9 copy-done
  82.3 2.4 %multiply_convert_fusion = bf16[2048,512]{1,0:T(8,128)(2,1)} fusion(bf16[2048,256]{1,0:T(8,128)(2,1)S(1)} %fusion.5, bf16[256,512]{1,0:T(8,128)(2,1)S(1)} %get-tuple-element.6, f32[512]{0:T(512)S(1)} %get-tuple-element.2, f32[512]{0:T(512)S(1)} %get-tuple-element.4, f32[512]{0:T(512)S(1)} %bitcast.68, f32[2048,512]{1,0:T(8,128)S(1)} %bitcast.57, ...), kind=kOutput, calls=%fused_computation.1 | convolution fusion | flops 546308096 | bytes 7610368 | tf_op jit(solution)/shard_map/dot_general | solution.py:85
  84.7 2.7 %reshape.144 = bf16[8,2,128,2,256]{4,3,2,1,0:T(2,128)(2,1)S(1)} reshape(bf16[2048,512]{1,0:T(8,128)(2,1)} %multiply_convert_fusion) | data formatting | bytes 4194304 | tf_op jit(solution)/shard_map/reshape | solution.py:105
  87.5 0.4 copy.28
  87.9 5.4 %all_to_all.31 = bf16[2,2,8,128,256]{4,3,2,1,0:T(8,128)(2,1)S(1)} all-to-all(bf16[2,2,8,128,256]{4,3,2,1,0:T(8,128)(2,1)S(1)} %bitcast.55), channel_id=1, replica_groups=mesh['zh'=4,'yk'=4,'yl'=2,'zl'=2,'x'=4,'core'=2] {'core'}, dimensions={0} | all-to-all | bytes 4194304 | tf_op jit(solution)/shard_map/all_to_all | solution.py:15
  93.3 1.3 add_convert_fusion
  94.6 4.2 %all-to-all-start.5 = ((bf16[16,128,256]{2,1,0:T(8,128)(2,1)}), bf16[16,128,256]{2,1,0:T(8,128)(2,1)S(1)}, u32[]{:S(2)}, u32[]{:S(2)}) async-start(bf16[16,128,256]{2,1,0:T(8,128)(2,1)} %bitcast.11), calls=%async_computation.5 | async-start | bytes 2097152 | tf_op jit(solution)/shard_map/all_to_all | solution.py:15
  98.9 4.1 %fusion.3 = bf16[2048,256]{1,0:T(8,128)(2,1)} fusion(bf16[256,512]{1,0:T(8,128)(2,1)S(1)} %get-tuple-element.6, bf16[2048,256]{1,0:T(8,128)(2,1)S(1)} %fusion.5, f32[256]{0:T(256)S(1)} %get-tuple-element.3, f32[256]{0:T(256)S(1)} %add_rsqrt_fusion.1, f32[256]{0:T(256)S(1)} %get-tuple-element.5, f32[2048,512]{1,0:T(8,128)} %bitcast.56, f32[512]{0:T(512)S(1)} %bitcast.69, ...), kind=kOutput, calls=%fused_computation.10 | convolution fusion | flops 543162368 | bytes 6560768 | tf_op jit(solution)/shard_map/dot_general | solution.py:93
  103.0 11.6 %all-to-all-done.5 = bf16[16,128,256]{2,1,0:T(8,128)(2,1)S(1)} async-done(((bf16[16,128,256]{2,1,0:T(8,128)(2,1)}), bf16[16,128,256]{2,1,0:T(8,128)(2,1)S(1)}, u32[]{:S(2)}, u32[]{:S(2)}) %all-to-all-start.5) | async-done | bytes 1048608 | tf_op jit(solution)/shard_map/all_to_all | solution.py:15
  114.6 6.4 %all-to-all-start.3 = ((bf16[32,64,256]{2,1,0:T(8,128)(2,1)}), bf16[32,64,256]{2,1,0:T(8,128)(2,1)S(1)}, u32[]{:S(2)}, u32[]{:S(2)}) async-start(bf16[32,64,256]{2,1,0:T(8,128)(2,1)} %bitcast.61), calls=%async_computation.3 | async-start | bytes 2097152 | tf_op jit(solution)/shard_map/all_to_all | solution.py:15
  121.0 0.8 reduce_sum.125
  121.8 29.6 %all-to-all-done.3 = bf16[32,64,256]{2,1,0:T(8,128)(2,1)S(1)} async-done(((bf16[32,64,256]{2,1,0:T(8,128)(2,1)}), bf16[32,64,256]{2,1,0:T(8,128)(2,1)S(1)}, u32[]{:S(2)}, u32[]{:S(2)}) %all-to-all-start.3) | async-done | bytes 1048608 | tf_op jit(solution)/shard_map/all_to_all | solution.py:15
  151.4 0.1 reduce_sum.121
  151.5 0.6 copy.21
  (13 shorter events, 0.1 us)
Async XLA Ops:
  0.6 11.3 %copy-start.2 = (bf16[64,512]{1,0:T(8,128)(2,1)S(1)}, bf16[64,512]{1,0:T(8,128)(2,1)}, u32[]{:S(2)}) copy-start(bf16[64,512]{1,0:T(8,128)(2,1)} %param.2) | copy-start | bytes 196612
  2.6 23.2 %all-to-all-start = ((bf16[16,128,256]{2,1,0:T(8,128)(2,1)}), bf16[16,128,256]{2,1,0:T(8,128)(2,1)S(1)}, u32[]{:S(2)}, u32[]{:S(2)}) async-start(bf16[16,128,256]{2,1,0:T(8,128)(2,1)} %broadcast_in_dim.6), calls=%async_computation | async-start | bytes 2097152 | tf_op jit(solution)/shard_map/all_to_all | solution.py:15
  32.5 46.4 %all-to-all-start.2 = ((bf16[32,64,256]{2,1,0:T(8,128)(2,1)}), bf16[32,64,256]{2,1,0:T(8,128)(2,1)S(1)}, u32[]{:S(2)}, u32[]{:S(2)}) async-start(bf16[32,64,256]{2,1,0:T(8,128)(2,1)} %bitcast.58), calls=%async_computation.2 | async-start | bytes 2097152 | tf_op jit(solution)/shard_map/all_to_all | solution.py:15
  59.6 20.5 %copy-start.1 = (bf16[256,8,2,256]{3,1,2,0:T(8,128)(2,1)S(1)}, bf16[256,8,2,256]{3,1,2,0:T(8,128)(2,1)}, u32[]{:S(2)}) copy-start(bf16[256,8,2,256]{3,1,2,0:T(8,128)(2,1)} %copy.25) | copy-start | bytes 6291460
  80.1 2.2 %copy-start = (f32[256,8,2,256]{3,1,2,0:T(8,128)S(1)}, f32[256,8,2,256]{3,1,2,0:T(8,128)}, u32[]{:S(2)}) copy-start(f32[256,8,2,256]{3,1,2,0:T(8,128)} %copy.22) | copy-start | bytes 12582916
  94.6 20.0 %all-to-all-start.5 = ((bf16[16,128,256]{2,1,0:T(8,128)(2,1)}), bf16[16,128,256]{2,1,0:T(8,128)(2,1)S(1)}, u32[]{:S(2)}, u32[]{:S(2)}) async-start(bf16[16,128,256]{2,1,0:T(8,128)(2,1)} %bitcast.11), calls=%async_computation.5 | async-start | bytes 2097152 | tf_op jit(solution)/shard_map/all_to_all | solution.py:15
  114.6 36.8 %all-to-all-start.3 = ((bf16[32,64,256]{2,1,0:T(8,128)(2,1)}), bf16[32,64,256]{2,1,0:T(8,128)(2,1)S(1)}, u32[]{:S(2)}, u32[]{:S(2)}) async-start(bf16[32,64,256]{2,1,0:T(8,128)(2,1)} %bitcast.61), calls=%async_computation.3 | async-start | bytes 2097152 | tf_op jit(solution)/shard_map/all_to_all | solution.py:15

commit v2 on v1

--- a/solution.py
+++ b/solution.py
@@ -8,11 +8,22 @@
 
 SAMPLES = ("zh", "yk", "yl")
 FEATURES = ("zl", "x", "core")
-NEAR = ("yl", "zl", "x")
 
 
 def exchange(values, axes):
     return lax.all_to_all(values, axes, 0, 0, tiled=True)
+
+
+def swap(values, axis):
+    return lax.ppermute(values, axis, [(0, 1), (1, 0)])
+
+
+def shift(values, distance):
+    return lax.ppermute(values, "x", [(i, (i + distance) % 4) for i in range(4)])
+
+
+def narrow_sum(*terms):
+    return sum(term.astype(jnp.float32) for term in terms).astype(jnp.bfloat16)
 
 
 def statistics(values):
@@ -27,18 +38,23 @@
     rows_a, width_a = first_view_outputs.shape
     rows_b, width_b = second_view_outputs.shape
     n_dp = lax.axis_size(SAMPLES)
-    n_near = lax.axis_size(NEAR)
     half = width_a // 2
     total_count = rows_a * n_dp
     parity = lax.axis_index("yl")
 
-    gathered = exchange(
-        jnp.broadcast_to(second_view_outputs, (n_near, rows_b, width_b)), NEAR
-    )
-    gathered = exchange(jnp.broadcast_to(gathered, (2, n_near, rows_b, width_b)), "core")
+    grown = second_view_outputs
+    for axis in ("yl", "zl"):
+        other = swap(grown, axis)
+        first_here = lax.axis_index(axis) == 0
+        grown = jnp.stack(
+            [jnp.where(first_here, grown, other), jnp.where(first_here, other, grown)]
+        )
+    ahead = [grown] + [shift(grown, -k) for k in (1, 2, 3)]
+    grown = jnp.roll(jnp.stack(ahead), lax.axis_index("x"), axis=0)
+    gathered = exchange(jnp.broadcast_to(grown, (2,) + grown.shape), "core")
     second = (
-        gathered.reshape(2, 2, n_near // 2, rows_b, width_b)
-        .transpose(2, 0, 3, 1, 4)
+        gathered.reshape(2, 4, 2, 2, rows_b, width_b)
+        .transpose(2, 1, 0, 4, 3, 5)
         .reshape(total_count, 2 * width_b)
     )
     norm_second, inverse_second = statistics(second)
@@ -102,11 +118,17 @@
         * inverse_first
     ).astype(jnp.bfloat16)
 
-    pieces = partial_second.reshape(n_near // 2, 2, rows_b, 2, width_b).transpose(1, 3, 0, 2, 4)
+    pieces = partial_second.reshape(2, 4, 2, rows_b, 2, width_b).transpose(2, 1, 0, 4, 3, 5)
     pieces = exchange(pieces, "core")
-    pieces = (pieces[0].astype(jnp.float32) + pieces[1].astype(jnp.float32)).astype(jnp.bfloat16)
-    pieces = exchange(pieces.reshape(n_near, rows_b, width_b), NEAR)
-    second_view_gradient = jnp.sum(pieces.astype(jnp.float32), axis=0).astype(jnp.bfloat16)
+    pieces = narrow_sum(pieces[0], pieces[1])
+    here = lax.axis_index("x")
+    moved = [shift(lax.dynamic_index_in_dim(pieces, (here + k) % 4, 0, False), k) for k in (1, 2, 3)]
+    pieces = narrow_sum(lax.dynamic_index_in_dim(pieces, here, 0, False), *moved)
+    for axis in ("zl", "yl"):
+        here = lax.axis_index(axis)
+        moved = swap(lax.dynamic_index_in_dim(pieces, 1 - here, 0, False), axis)
+        pieces = narrow_sum(lax.dynamic_index_in_dim(pieces, here, 0, False), moved)
+    second_view_gradient = pieces
 
     parts = exchange(partial_first.reshape(n_dp, rows_a, half), SAMPLES)
     first_view_gradient = (

time: 153 us -> 157 us (1.026)
  the two profiles are of different devices: /device:TPU:8 before, /device:TPU:24 now
where the time goes in v2:
time: 157 us; the launch traced here: 156 us
  starting transfers between devices  56.3 us (36%)
  waiting for transfers between devices  51.4 us (33%)
  local copies, waits for them, and re-layouts  18.5 us (12%)
  other arithmetic  15.7 us (10%)
  matrix products  7.56 us (5%)
  blocking collectives  5.42 us (3%)
    all_to_all x3, starting transfers between devices, exchange(): return lax.all_to_all(values, axes, 0, 0, tiled=True)  26.8 us
    ppermute x6, waiting for transfers between devices, shift(): lax.ppermute(values, 'x', [(i, (i + distance) % 4) for i in range(4)])  20.5 us
    ppermute x4, waiting for transfers between devices, swap(): return lax.ppermute(values, axis, [(0, 1), (1, 0)])  19.2 us
    ppermute x6, starting transfers between devices, shift(): lax.ppermute(values, 'x', [(i, (i + distance) % 4) for i in range(4)])  18.2 us
    all_to_all x3, waiting for transfers between devices, exchange(): return lax.all_to_all(values, axes, 0, 0, tiled=True)  11.8 us
    ppermute x4, starting transfers between devices, swap(): return lax.ppermute(values, axis, [(0, 1), (1, 0)])  11.2 us
    all_to_all x1, blocking collectives, exchange(): return lax.all_to_all(values, axes, 0, 0, tiled=True)  5.42 us
    unnamed x14, local copies, waits for them, and re-layouts  5.24 us
  transfers between devices with their start and end apart: 13, of which 11 were waited for; matrix products, arithmetic and copies ran while one was open for 16% of the time, Pallas kernels for 0%

profile of v2, /device:TPU:24, one launch (start us, length us, event | category | flops | bytes accessed | tf_op | source)
XLA Modules:
  0.0 155.9 jit_solution(12844737517167700062)
XLA Ops:
  0.6 2.4 %collective-permute-start = (bf16[128,256]{1,0:T(8,128)(2,1)}, bf16[128,256]{1,0:T(8,128)(2,1)S(1)}, u32[]{:S(2)}, u32[]{:S(2)}) collective-permute-start(bf16[128,256]{1,0:T(8,128)(2,1)} %param.3), channel_id=1, source_target_pairs={{0,16},{16,0},{1,17},{17,1},{2,18},{18,2},{3,19},{19,3},{4,20},{20... | collective-permute-start | bytes 196616 | tf_op jit(solution)/shard_map/ppermute | solution.py:18
  3.0 4.0 %collective-permute-done = bf16[128,256]{1,0:T(8,128)(2,1)S(1)} collective-permute-done((bf16[128,256]{1,0:T(8,128)(2,1)}, bf16[128,256]{1,0:T(8,128)(2,1)S(1)}, u32[]{:S(2)}, u32[]{:S(2)}) %collective-permute-start) | collective-permute-done | bytes 65568 | tf_op jit(solution)/shard_map/ppermute | solution.py:18
  7.0 0.9 select_bitcast_fusion.3
  7.9 4.3 %collective-permute-start.1 = (bf16[2,128,256]{2,1,0:T(8,128)(2,1)S(1)}, bf16[2,128,256]{2,1,0:T(8,128)(2,1)S(1)}, u32[]{:S(2)}, u32[]{:S(2)}) collective-permute-start(bf16[2,128,256]{2,1,0:T(8,128)(2,1)S(1)} %pad_maximum_fusion.1), channel_id=1, source_target_pairs={{0,8},{8,0},{1,9},{9,1},{2,10},{10,2},{3,11},{11,3},{4,12},{12,4},... | collective-permute-start | bytes 393224 | tf_op jit(solution)/shard_map/ppermute | solution.py:18
  12.2 2.9 %collective-permute-done.1 = bf16[2,128,256]{2,1,0:T(8,128)(2,1)S(1)} collective-permute-done((bf16[2,128,256]{2,1,0:T(8,128)(2,1)S(1)}, bf16[2,128,256]{2,1,0:T(8,128)(2,1)S(1)}, u32[]{:S(2)}, u32[]{:S(2)}) %collective-permute-start.1) | collective-permute-done | bytes 131104 | tf_op jit(solution)/shard_map/ppermute | solution.py:18
  15.2 4.7 %collective-permute-start.2 = (bf16[2,2,128,256]{3,2,1,0:T(8,128)(2,1)S(1)}, bf16[2,2,128,256]{3,2,1,0:T(8,128)(2,1)S(1)}, u32[]{:S(2)}, u32[]{:S(2)}) collective-permute-start(bf16[2,2,128,256]{3,2,1,0:T(8,128)(2,1)S(1)} %pad_maximum_fusion), channel_id=1, source_target_pairs={{0,6},{2,0},{4,2},{6,4},{1,7},{3,1},{5,3},{7,5},{8,14},{10,8},{12,... | collective-permute-start | bytes 786440 | tf_op jit(solution)/shard_map/ppermute | solution.py:22
  19.9 0.9 reshape.146
  20.8 2.7 %collective-permute-start.3 = (bf16[2,2,128,256]{3,2,1,0:T(8,128)(2,1)S(1)}, bf16[2,2,128,256]{3,2,1,0:T(8,128)(2,1)S(1)}, u32[]{:S(2)}, u32[]{:S(2)}) collective-permute-start(bf16[2,2,128,256]{3,2,1,0:T(8,128)(2,1)S(1)} %pad_maximum_fusion), channel_id=1, source_target_pairs={{0,4},{2,6},{4,0},{6,2},{1,5},{3,7},{5,1},{7,3},{8,12},{10,14},{12... | collective-permute-start | bytes 786440 | tf_op jit(solution)/shard_map/ppermute | solution.py:22
  23.5 2.8 %collective-permute-start.4 = (bf16[2,2,128,256]{3,2,1,0:T(8,128)(2,1)S(1)}, bf16[2,2,128,256]{3,2,1,0:T(8,128)(2,1)S(1)}, u32[]{:S(2)}, u32[]{:S(2)}) collective-permute-start(bf16[2,2,128,256]{3,2,1,0:T(8,128)(2,1)S(1)} %pad_maximum_fusion), channel_id=1, source_target_pairs={{0,2},{2,4},{4,6},{6,0},{1,3},{3,5},{5,7},{7,1},{8,10},{10,12},{12... | collective-permute-start | bytes 786440 | tf_op jit(solution)/shard_map/ppermute | solution.py:22
  26.3 3.0 %collective-permute-done.2 = bf16[2,2,128,256]{3,2,1,0:T(8,128)(2,1)S(1)} collective-permute-done((bf16[2,2,128,256]{3,2,1,0:T(8,128)(2,1)S(1)}, bf16[2,2,128,256]{3,2,1,0:T(8,128)(2,1)S(1)}, u32[]{:S(2)}, u32[]{:S(2)}) %collective-permute-start.2) | collective-permute-done | bytes 262176 | tf_op jit(solution)/shard_map/ppermute | solution.py:22
  29.4 3.4 %collective-permute-done.3 = bf16[2,2,128,256]{3,2,1,0:T(8,128)(2,1)S(1)} collective-permute-done((bf16[2,2,128,256]{3,2,1,0:T(8,128)(2,1)S(1)}, bf16[2,2,128,256]{3,2,1,0:T(8,128)(2,1)S(1)}, u32[]{:S(2)}, u32[]{:S(2)}) %collective-permute-start.3) | collective-permute-done | bytes 262176 | tf_op jit(solution)/shard_map/ppermute | solution.py:22
  32.8 2.7 %collective-permute-done.4 = bf16[2,2,128,256]{3,2,1,0:T(8,128)(2,1)S(1)} collective-permute-done((bf16[2,2,128,256]{3,2,1,0:T(8,128)(2,1)S(1)}, bf16[2,2,128,256]{3,2,1,0:T(8,128)(2,1)S(1)}, u32[]{:S(2)}, u32[]{:S(2)}) %collective-permute-start.4) | collective-permute-done | bytes 262176 | tf_op jit(solution)/shard_map/ppermute | solution.py:22
  35.7 1.1 copy.11
  36.8 1.6 %broadcast_in_dim.4 = bf16[2,4,2,2,128,256]{5,3,4,1,2,0:T(2,128)(2,1)S(1)} broadcast(bf16[4,2,2,128,256]{4,2,3,0,1:T(2,128)(2,1)S(1)} %copy.11), dimensions={1,2,3,4,5} | broadcast | bytes 3145728 | tf_op jit(solution)/shard_map/broadcast_in_dim | solution.py:54
  38.5 5.4 %all_to_all.20 = bf16[2,4,2,2,128,256]{5,3,4,1,2,0:T(2,128)(2,1)S(1)} all-to-all(bf16[2,4,2,2,128,256]{5,3,4,1,2,0:T(2,128)(2,1)S(1)} %broadcast_in_dim.4), channel_id=1, replica_groups=mesh['zh'=4,'yk'=4,'yl'=2,'zl'=2,'x'=4,'core'=2] {'core'}, dimensions={0} | all-to-all | bytes 4194304 | tf_op jit(solution)/shard_map/all_to_all | solution.py:14
  43.9 1.1 broadcast_in_dim.5
  45.0 15.5 %all-to-all-start.1 = ((bf16[32,64,256]{2,1,0:T(8,128)(2,1)}), bf16[32,64,256]{2,1,0:T(8,128)(2,1)S(1)}, u32[]{:S(2)}, u32[]{:S(2)}) async-start(bf16[32,64,256]{2,1,0:T(8,128)(2,1)} %bitcast.90), calls=%async_computation.1 | async-start | bytes 2097152 | tf_op jit(solution)/shard_map/all_to_all | solution.py:14
  60.5 2.2 %fusion = f32[2,256]{1,0:T(2,128)S(1)} fusion(bf16[2,4,2,2,128,256]{5,3,4,1,2,0:T(2,128)(2,1)S(1)} %all_to_all.20), kind=kLoop, calls=%fused_computation.6 | loop fusion | flops 2096640 | bytes 2099200 | tf_op jit(solution)/shard_map/reduce_sum | solution.py:31
  62.7 2.8 %multiply_reduce_fusion = f32[2,256]{1,0:T(2,128)S(1)} fusion(bf16[2,4,2,2,128,256]{5,3,4,1,2,0:T(2,128)(2,1)S(1)} %all_to_all.20, f32[2,256]{1,0:T(2,128)S(1)} %get-tuple-element.19), kind=kLoop, calls=%fused_computation.5 | loop fusion | flops 4193792 | bytes 2101248 | tf_op jit(solution)/shard_map/reduce_sum | solution.py:33
  65.5 3.8 %convert_reduce_fusion = (f32[2,256]{1,0:T(2,128)S(1)}, bf16[2,4,2,128,2,256]{5,4,3,1,0,2:T(2,128)(2,1)S(1)}) fusion(f32[2,256]{1,0:T(2,128)S(1)} %get-tuple-element.21, f32[2,256]{1,0:T(2,128)S(1)} %get-tuple-element.19, bf16[2,4,2,2,128,256]{5,3,4,1,2,0:T(2,128)(2,1)S(1)} %all_to_all.20), kind=kLoop, calls=%fused_computation.2 | loop fusion | flops 6290944 | bytes 4200448 | tf_op jit(solution)/shard_map/reduce_sum | solution.py:95
  69.4 1.5 copy.14
  70.9 1.8 %copy.21 = bf16[256,8,2,256]{3,1,2,0:T(8,128)(2,1)} copy(bf16[256,8,2,256]{3,2,1,0:T(2,128)(2,1)S(1)} %bitcast.87) | data formatting | bytes 4194304
  72.8 2.0 %convert_bitcast_fusion = f32[2,4,2,128,2,256]{5,4,3,1,0,2:T(2,128)S(1)} fusion(bf16[2,4,2,2,128,256]{5,3,4,1,2,0:T(2,128)(2,1)S(1)} %all_to_all.20), kind=kLoop, calls=%fused_computation | loop fusion | flops 1048576 | bytes 6291456 | tf_op jit(solution)/shard_map/convert_element_type | solution.py:30
  74.7 1.9 %copy.12 = f32[2,4,2,128,2,256]{5,4,3,2,1,0:T(2,128)S(1)} copy(f32[2,4,2,128,2,256]{5,4,3,1,0,2:T(2,128)S(1)} %convert_bitcast_fusion) | data formatting | bytes 8388608 | tf_op jit(solution)/shard_map/convert_element_type | solution.py:30
  76.7 2.4 %copy.18 = f32[256,8,2,256]{3,1,2,0:T(8,128)} copy(f32[256,8,2,256]{3,2,1,0:T(2,128)S(1)} %bitcast.85) | data formatting | bytes 8388608
  79.0 11.8 %all-to-all-done.1 = bf16[32,64,256]{2,1,0:T(8,128)(2,1)S(1)} async-done(((bf16[32,64,256]{2,1,0:T(8,128)(2,1)}), bf16[32,64,256]{2,1,0:T(8,128)(2,1)S(1)}, u32[]{:S(2)}, u32[]{:S(2)}) %all-to-all-start.1) | async-done | bytes 1048608 | tf_op jit(solution)/shard_map/all_to_all | solution.py:14
  91.4 0.5 convert_reduce_fusion.1
  91.9 1.0 fusion.11
  93.2 0.9 copy-done
  94.1 2.4 %multiply_convert_fusion = bf16[2048,512]{1,0:T(8,128)(2,1)} fusion(bf16[2048,256]{1,0:T(8,128)(2,1)S(1)} %fusion.5, bf16[256,512]{1,0:T(8,128)(2,1)S(1)} %get-tuple-element.6, f32[512]{0:T(512)S(1)} %get-tuple-element.2, f32[512]{0:T(512)S(1)} %get-tuple-element.4, f32[512]{0:T(512)S(1)} %bitcast.97, f32[2048,512]{1,0:T(8,128)S(1)} %bitcast.89, ...), kind=kOutput, calls=%fused_computation.1 | convolution fusion | flops 546308096 | bytes 7610368 | tf_op jit(solution)/shard_map/dot_general | solution.py:101
  96.5 2.5 %reshape.151 = bf16[2,4,2,128,2,256]{5,4,3,2,1,0:T(2,128)(2,1)S(1)} reshape(bf16[2048,512]{1,0:T(8,128)(2,1)} %multiply_convert_fusion) | data formatting | bytes 4194304 | tf_op jit(solution)/shard_map/reshape | solution.py:121
  99.1 1.7 %copy.24 = bf16[2,4,2,128,2,256]{5,3,4,0,1,2:T(8,128)(2,1)} copy(bf16[2,4,2,128,2,256]{5,4,3,2,1,0:T(2,128)(2,1)S(1)} %reshape.151) | data formatting | bytes 4194304 | tf_op jit(solution)/shard_map/reshape | solution.py:121
  100.8 3.8 %all-to-all-start.3 = ((bf16[2,4,2,2,128,256]{5,4,3,2,1,0:T(8,128)(2,1)}), bf16[2,4,2,2,128,256]{5,4,3,2,1,0:T(8,128)(2,1)S(1)}, u32[]{:S(2)}, u32[]{:S(2)}) async-start(bf16[2,4,2,2,128,256]{5,4,3,2,1,0:T(8,128)(2,1)} %bitcast.86), calls=%async_computation.3 | async-start | bytes 4194304 | tf_op jit(solution)/shard_map/all_to_all | solution.py:14
  104.6 4.1 %fusion.3 = bf16[2048,256]{1,0:T(8,128)(2,1)} fusion(bf16[256,512]{1,0:T(8,128)(2,1)S(1)} %get-tuple-element.6, bf16[2048,256]{1,0:T(8,128)(2,1)S(1)} %fusion.5, f32[256]{0:T(256)S(1)} %get-tuple-element.3, f32[256]{0:T(256)S(1)} %add_rsqrt_fusion.1, f32[256]{0:T(256)S(1)} %get-tuple-element.5, f32[2048,512]{1,0:T(8,128)} %bitcast.88, f32[512]{0:T(512)S(1)} %bitcast.98, ...), kind=kOutput, calls=%fused_computation.10 | convolution fusion | flops 543162368 | bytes 6560768 | tf_op jit(solution)/shard_map/dot_general | solution.py:109
  108.7 7.6 %all-to-all-start.2 = ((bf16[32,64,256]{2,1,0:T(8,128)(2,1)}), bf16[32,64,256]{2,1,0:T(8,128)(2,1)}, u32[]{:S(2)}, u32[]{:S(2)}) async-start(bf16[32,64,256]{2,1,0:T(8,128)(2,1)} %bitcast.92), calls=%async_computation.2 | async-start | bytes 2097152 | tf_op jit(solution)/shard_map/all_to_all | solution.py:14
  116.8 2.5 %collective-permute-start.7 = (bf16[2,2,128,256]{3,2,1,0:T(8,128)(2,1)S(1)}, bf16[2,2,128,256]{3,2,1,0:T(8,128)(2,1)S(1)}, u32[]{:S(2)}, u32[]{:S(2)}) collective-permute-start(bf16[2,2,128,256]{3,2,1,0:T(8,128)(2,1)S(1)} %get-tuple-element.12), channel_id=1, source_target_pairs={{0,6},{2,0},{4,2},{6,4},{1,7},{3,1},{5,3},{7,5},{8,14},{10,8},{12,... | collective-permute-start | bytes 786440 | tf_op jit(solution)/shard_map/ppermute | solution.py:22
  119.3 2.7 %collective-permute-start.6 = (bf16[2,2,128,256]{3,2,1,0:T(8,128)(2,1)S(1)}, bf16[2,2,128,256]{3,2,1,0:T(8,128)(2,1)S(1)}, u32[]{:S(2)}, u32[]{:S(2)}) collective-permute-start(bf16[2,2,128,256]{3,2,1,0:T(8,128)(2,1)S(1)} %get-tuple-element.13), channel_id=1, source_target_pairs={{0,4},{2,6},{4,0},{6,2},{1,5},{3,7},{5,1},{7,3},{8,12},{10,14},{12... | collective-permute-start | bytes 786440 | tf_op jit(solution)/shard_map/ppermute | solution.py:22
  122.0 2.8 %collective-permute-start.5 = (bf16[2,2,128,256]{3,2,1,0:T(8,128)(2,1)S(1)}, bf16[2,2,128,256]{3,2,1,0:T(8,128)(2,1)S(1)}, u32[]{:S(2)}, u32[]{:S(2)}) collective-permute-start(bf16[2,2,128,256]{3,2,1,0:T(8,128)(2,1)S(1)} %get-tuple-element.11), channel_id=1, source_target_pairs={{0,2},{2,4},{4,6},{6,0},{1,3},{3,5},{5,7},{7,1},{8,10},{10,12},{12... | collective-permute-start | bytes 786440 | tf_op jit(solution)/shard_map/ppermute | solution.py:22
  124.8 3.0 %collective-permute-done.7 = bf16[2,2,128,256]{3,2,1,0:T(8,128)(2,1)S(1)} collective-permute-done((bf16[2,2,128,256]{3,2,1,0:T(8,128)(2,1)S(1)}, bf16[2,2,128,256]{3,2,1,0:T(8,128)(2,1)S(1)}, u32[]{:S(2)}, u32[]{:S(2)}) %collective-permute-start.7) | collective-permute-done | bytes 262176 | tf_op jit(solution)/shard_map/ppermute | solution.py:22
  127.8 4.1 %collective-permute-done.6 = bf16[2,2,128,256]{3,2,1,0:T(8,128)(2,1)S(1)} collective-permute-done((bf16[2,2,128,256]{3,2,1,0:T(8,128)(2,1)S(1)}, bf16[2,2,128,256]{3,2,1,0:T(8,128)(2,1)S(1)}, u32[]{:S(2)}, u32[]{:S(2)}) %collective-permute-start.6) | collective-permute-done | bytes 262176 | tf_op jit(solution)/shard_map/ppermute | solution.py:22
  131.9 4.2 %collective-permute-done.5 = bf16[2,2,128,256]{3,2,1,0:T(8,128)(2,1)S(1)} collective-permute-done((bf16[2,2,128,256]{3,2,1,0:T(8,128)(2,1)S(1)}, bf16[2,2,128,256]{3,2,1,0:T(8,128)(2,1)S(1)}, u32[]{:S(2)}, u32[]{:S(2)}) %collective-permute-start.5) | collective-permute-done | bytes 262176 | tf_op jit(solution)/shard_map/ppermute | solution.py:22
  136.3 2.7 %collective-permute-start.8 = (bf16[2,128,256]{2,1,0:T(8,128)(2,1)S(1)}, bf16[2,128,256]{2,1,0:T(8,128)(2,1)S(1)}, u32[]{:S(2)}, u32[]{:S(2)}) collective-permute-start(bf16[2,128,256]{2,1,0:T(8,128)(2,1)S(1)} %dynamic-slice_bitcast_fusion.3), channel_id=1, source_target_pairs={{0,8},{8,0},{1,9},{9,1},{2,10},{10,2},{3,11},{11,3},{4,12},{12,4},... | collective-permute-start | bytes 393224 | tf_op jit(solution)/shard_map/ppermute | solution.py:18
  139.0 8.1 %collective-permute-done.8 = bf16[2,128,256]{2,1,0:T(8,128)(2,1)S(1)} collective-permute-done((bf16[2,128,256]{2,1,0:T(8,128)(2,1)S(1)}, bf16[2,128,256]{2,1,0:T(8,128)(2,1)S(1)}, u32[]{:S(2)}, u32[]{:S(2)}) %collective-permute-start.8) | collective-permute-done | bytes 131104 | tf_op jit(solution)/shard_map/ppermute | solution.py:18
  147.1 1.9 %collective-permute-start.9 = (bf16[128,256]{1,0:T(8,128)(2,1)S(1)}, bf16[128,256]{1,0:T(8,128)(2,1)S(1)}, u32[]{:S(2)}, u32[]{:S(2)}) collective-permute-start(bf16[128,256]{1,0:T(8,128)(2,1)S(1)} %dynamic-slice_bitcast_fusion.4), channel_id=1, source_target_pairs={{0,16},{16,0},{1,17},{17,1},{2,18},{18,2},{3,19},{19,3},{4,20},{20... | collective-permute-start | bytes 196616 | tf_op jit(solution)/shard_map/ppermute | solution.py:18
  149.0 4.2 %collective-permute-done.9 = bf16[128,256]{1,0:T(8,128)(2,1)S(1)} collective-permute-done((bf16[128,256]{1,0:T(8,128)(2,1)S(1)}, bf16[128,256]{1,0:T(8,128)(2,1)S(1)}, u32[]{:S(2)}, u32[]{:S(2)}) %collective-permute-start.9) | collective-permute-done | bytes 65568 | tf_op jit(solution)/shard_map/ppermute | solution.py:18
  153.3 0.6 fusion.14
  153.9 1.4 reduce_sum.109
  155.3 0.6 copy.17
  (38 shorter events, 1.9 us)
Async XLA Ops:
  0.6 6.4 %collective-permute-start = (bf16[128,256]{1,0:T(8,128)(2,1)}, bf16[128,256]{1,0:T(8,128)(2,1)S(1)}, u32[]{:S(2)}, u32[]{:S(2)}) collective-permute-start(bf16[128,256]{1,0:T(8,128)(2,1)} %param.3), channel_id=1, source_target_pairs={{0,16},{16,0},{1,17},{17,1},{2,18},{18,2},{3,19},{19,3},{4,20},{20... | collective-permute-start | bytes 196616 | tf_op jit(solution)/shard_map/ppermute | solution.py:18
  7.9 7.2 %collective-permute-start.1 = (bf16[2,128,256]{2,1,0:T(8,128)(2,1)S(1)}, bf16[2,128,256]{2,1,0:T(8,128)(2,1)S(1)}, u32[]{:S(2)}, u32[]{:S(2)}) collective-permute-start(bf16[2,128,256]{2,1,0:T(8,128)(2,1)S(1)} %pad_maximum_fusion.1), channel_id=1, source_target_pairs={{0,8},{8,0},{1,9},{9,1},{2,10},{10,2},{3,11},{11,3},{4,12},{12,4},... | collective-permute-start | bytes 393224 | tf_op jit(solution)/shard_map/ppermute | solution.py:18
  15.2 14.2 %collective-permute-start.2 = (bf16[2,2,128,256]{3,2,1,0:T(8,128)(2,1)S(1)}, bf16[2,2,128,256]{3,2,1,0:T(8,128)(2,1)S(1)}, u32[]{:S(2)}, u32[]{:S(2)}) collective-permute-start(bf16[2,2,128,256]{3,2,1,0:T(8,128)(2,1)S(1)} %pad_maximum_fusion), channel_id=1, source_target_pairs={{0,6},{2,0},{4,2},{6,4},{1,7},{3,1},{5,3},{7,5},{8,14},{10,8},{12,... | collective-permute-start | bytes 786440 | tf_op jit(solution)/shard_map/ppermute | solution.py:22
  20.8 12.0 %collective-permute-start.3 = (bf16[2,2,128,256]{3,2,1,0:T(8,128)(2,1)S(1)}, bf16[2,2,128,256]{3,2,1,0:T(8,128)(2,1)S(1)}, u32[]{:S(2)}, u32[]{:S(2)}) collective-permute-start(bf16[2,2,128,256]{3,2,1,0:T(8,128)(2,1)S(1)} %pad_maximum_fusion), channel_id=1, source_target_pairs={{0,4},{2,6},{4,0},{6,2},{1,5},{3,7},{5,1},{7,3},{8,12},{10,14},{12... | collective-permute-start | bytes 786440 | tf_op jit(solution)/shard_map/ppermute | solution.py:22
  23.5 12.0 %collective-permute-start.4 = (bf16[2,2,128,256]{3,2,1,0:T(8,128)(2,1)S(1)}, bf16[2,2,128,256]{3,2,1,0:T(8,128)(2,1)S(1)}, u32[]{:S(2)}, u32[]{:S(2)}) collective-permute-start(bf16[2,2,128,256]{3,2,1,0:T(8,128)(2,1)S(1)} %pad_maximum_fusion), channel_id=1, source_target_pairs={{0,2},{2,4},{4,6},{6,0},{1,3},{3,5},{5,7},{7,1},{8,10},{10,12},{12... | collective-permute-start | bytes 786440 | tf_op jit(solution)/shard_map/ppermute | solution.py:22
  45.0 45.8 %all-to-all-start.1 = ((bf16[32,64,256]{2,1,0:T(8,128)(2,1)}), bf16[32,64,256]{2,1,0:T(8,128)(2,1)S(1)}, u32[]{:S(2)}, u32[]{:S(2)}) async-start(bf16[32,64,256]{2,1,0:T(8,128)(2,1)} %bitcast.90), calls=%async_computation.1 | async-start | bytes 2097152 | tf_op jit(solution)/shard_map/all_to_all | solution.py:14
  79.0 12.9 %copy-start.1 = (bf16[256,8,2,256]{3,1,2,0:T(8,128)(2,1)S(1)}, bf16[256,8,2,256]{3,1,2,0:T(8,128)(2,1)}, u32[]{:S(2)}) copy-start(bf16[256,8,2,256]{3,1,2,0:T(8,128)(2,1)} %copy.21) | copy-start | bytes 6291460
  91.9 2.2 %copy-start = (f32[256,8,2,256]{3,1,2,0:T(8,128)S(1)}, f32[256,8,2,256]{3,1,2,0:T(8,128)}, u32[]{:S(2)}) copy-start(f32[256,8,2,256]{3,1,2,0:T(8,128)} %copy.18) | copy-start | bytes 12582916
  100.8 7.9 %all-to-all-start.3 = ((bf16[2,4,2,2,128,256]{5,4,3,2,1,0:T(8,128)(2,1)}), bf16[2,4,2,2,128,256]{5,4,3,2,1,0:T(8,128)(2,1)S(1)}, u32[]{:S(2)}, u32[]{:S(2)}) async-start(bf16[2,4,2,2,128,256]{5,4,3,2,1,0:T(8,128)(2,1)} %bitcast.86), calls=%async_computation.3 | async-start | bytes 4194304 | tf_op jit(solution)/shard_map/all_to_all | solution.py:14
  108.7 45.2 %all-to-all-start.2 = ((bf16[32,64,256]{2,1,0:T(8,128)(2,1)}), bf16[32,64,256]{2,1,0:T(8,128)(2,1)}, u32[]{:S(2)}, u32[]{:S(2)}) async-start(bf16[32,64,256]{2,1,0:T(8,128)(2,1)} %bitcast.92), calls=%async_computation.2 | async-start | bytes 2097152 | tf_op jit(solution)/shard_map/all_to_all | solution.py:14
  116.8 11.1 %collective-permute-start.7 = (bf16[2,2,128,256]{3,2,1,0:T(8,128)(2,1)S(1)}, bf16[2,2,128,256]{3,2,1,0:T(8,128)(2,1)S(1)}, u32[]{:S(2)}, u32[]{:S(2)}) collective-permute-start(bf16[2,2,128,256]{3,2,1,0:T(8,128)(2,1)S(1)} %get-tuple-element.12), channel_id=1, source_target_pairs={{0,6},{2,0},{4,2},{6,4},{1,7},{3,1},{5,3},{7,5},{8,14},{10,8},{12,... | collective-permute-start | bytes 786440 | tf_op jit(solution)/shard_map/ppermute | solution.py:22
  119.3 12.6 %collective-permute-start.6 = (bf16[2,2,128,256]{3,2,1,0:T(8,128)(2,1)S(1)}, bf16[2,2,128,256]{3,2,1,0:T(8,128)(2,1)S(1)}, u32[]{:S(2)}, u32[]{:S(2)}) collective-permute-start(bf16[2,2,128,256]{3,2,1,0:T(8,128)(2,1)S(1)} %get-tuple-element.13), channel_id=1, source_target_pairs={{0,4},{2,6},{4,0},{6,2},{1,5},{3,7},{5,1},{7,3},{8,12},{10,14},{12... | collective-permute-start | bytes 786440 | tf_op jit(solution)/shard_map/ppermute | solution.py:22
  122.0 14.1 %collective-permute-start.5 = (bf16[2,2,128,256]{3,2,1,0:T(8,128)(2,1)S(1)}, bf16[2,2,128,256]{3,2,1,0:T(8,128)(2,1)S(1)}, u32[]{:S(2)}, u32[]{:S(2)}) collective-permute-start(bf16[2,2,128,256]{3,2,1,0:T(8,128)(2,1)S(1)} %get-tuple-element.11), channel_id=1, source_target_pairs={{0,2},{2,4},{4,6},{6,0},{1,3},{3,5},{5,7},{7,1},{8,10},{10,12},{12... | collective-permute-start | bytes 786440 | tf_op jit(solution)/shard_map/ppermute | solution.py:22
  136.3 10.7 %collective-permute-start.8 = (bf16[2,128,256]{2,1,0:T(8,128)(2,1)S(1)}, bf16[2,128,256]{2,1,0:T(8,128)(2,1)S(1)}, u32[]{:S(2)}, u32[]{:S(2)}) collective-permute-start(bf16[2,128,256]{2,1,0:T(8,128)(2,1)S(1)} %dynamic-slice_bitcast_fusion.3), channel_id=1, source_target_pairs={{0,8},{8,0},{1,9},{9,1},{2,10},{10,2},{3,11},{11,3},{4,12},{12,4},... | collective-permute-start | bytes 393224 | tf_op jit(solution)/shard_map/ppermute | solution.py:18
  147.1 6.2 %collective-permute-start.9 = (bf16[128,256]{1,0:T(8,128)(2,1)S(1)}, bf16[128,256]{1,0:T(8,128)(2,1)S(1)}, u32[]{:S(2)}, u32[]{:S(2)}) collective-permute-start(bf16[128,256]{1,0:T(8,128)(2,1)S(1)} %dynamic-slice_bitcast_fusion.4), channel_id=1, source_target_pairs={{0,16},{16,0},{1,17},{17,1},{2,18},{18,2},{3,19},{19,3},{4,20},{20... | collective-permute-start | bytes 196616 | tf_op jit(solution)/shard_map/ppermute | solution.py:18

commit v3 on v2

--- a/solution.py
+++ b/solution.py
@@ -42,6 +42,12 @@
     total_count = rows_a * n_dp
     parity = lax.axis_index("yl")
 
+    halves = first_view_outputs.reshape(rows_a, 2, half).transpose(1, 0, 2)
+    first = exchange(
+        jnp.broadcast_to(halves, (n_dp // 2, 2, rows_a, half)).reshape(n_dp, rows_a, half),
+        SAMPLES,
+    ).reshape(total_count, half)
+
     grown = second_view_outputs
     for axis in ("yl", "zl"):
         other = swap(grown, axis)
@@ -51,6 +57,7 @@
         )
     ahead = [grown] + [shift(grown, -k) for k in (1, 2, 3)]
     grown = jnp.roll(jnp.stack(ahead), lax.axis_index("x"), axis=0)
+    first, grown = lax.optimization_barrier((first, grown))
     gathered = exchange(jnp.broadcast_to(grown, (2,) + grown.shape), "core")
     second = (
         gathered.reshape(2, 4, 2, 2, rows_b, width_b)
@@ -59,11 +66,6 @@
     )
     norm_second, inverse_second = statistics(second)
 
-    halves = first_view_outputs.reshape(rows_a, 2, half).transpose(1, 0, 2)
-    first = exchange(
-        jnp.broadcast_to(halves, (n_dp // 2, 2, rows_a, half)).reshape(n_dp, rows_a, half),
-        SAMPLES,
-    ).reshape(total_count, half)
     norm_first, inverse_first = statistics(first)
 
     correlation = (

time: 157 us -> 142 us (0.904)
  the two profiles are of different devices: /device:TPU:24 before, /device:TPU:6 now
where the time goes in v3:
time: 142 us; the launch traced here: 141 us
  starting transfers between devices  57.5 us (40%)
  waiting for transfers between devices  42.9 us (30%)
  other arithmetic  14.7 us (10%)
  local copies, waits for them, and re-layouts  12.7 us (9%)
  matrix products  6.69 us (5%)
  blocking collectives  5.42 us (4%)
    all_to_all x3, starting transfers between devices, exchange(): return lax.all_to_all(values, axes, 0, 0, tiled=True)  26.2 us
    ppermute x6, waiting for transfers between devices, shift(): lax.ppermute(values, 'x', [(i, (i + distance) % 4) for i in range(4)])  18.6 us
    ppermute x6, starting transfers between devices, shift(): lax.ppermute(values, 'x', [(i, (i + distance) % 4) for i in range(4)])  18.4 us
    ppermute x4, waiting for transfers between devices, swap(): return lax.ppermute(values, axis, [(0, 1), (1, 0)])  14.2 us
    ppermute x4, starting transfers between devices, swap(): return lax.ppermute(values, axis, [(0, 1), (1, 0)])  12.9 us
    all_to_all x3, waiting for transfers between devices, exchange(): return lax.all_to_all(values, axes, 0, 0, tiled=True)  10.2 us
    all_to_all x1, blocking collectives, exchange(): return lax.all_to_all(values, axes, 0, 0, tiled=True)  5.42 us
    reshape x2, local copies, waits for them, and re-layouts, shards(): partial_second.reshape(2, 4, 2, rows_b, 2, width_b)  4.23 us
  transfers between devices with their start and end apart: 13, of which 9 were waited for; matrix products, arithmetic and copies ran while one was open for 5% of the time, Pallas kernels for 0%

profile of v3, /device:TPU:6, one launch (start us, length us, event | category | flops | bytes accessed | tf_op | source)
XLA Modules:
  0.0 141.0 jit_solution(15805405280079023338)
XLA Ops:
  0.6 3.5 %collective-permute-start = (bf16[128,256]{1,0:T(8,128)(2,1)}, bf16[128,256]{1,0:T(8,128)(2,1)S(1)}, u32[]{:S(2)}, u32[]{:S(2)}) collective-permute-start(bf16[128,256]{1,0:T(8,128)(2,1)} %param.3), channel_id=1, source_target_pairs={{0,16},{16,0},{1,17},{17,1},{2,18},{18,2},{3,19},{19,3},{4,20},{20... | collective-permute-start | bytes 196616 | tf_op jit(solution)/shard_map/ppermute | solution.py:18
  4.1 2.9 %collective-permute-done = bf16[128,256]{1,0:T(8,128)(2,1)S(1)} collective-permute-done((bf16[128,256]{1,0:T(8,128)(2,1)}, bf16[128,256]{1,0:T(8,128)(2,1)S(1)}, u32[]{:S(2)}, u32[]{:S(2)}) %collective-permute-start) | collective-permute-done | bytes 65568 | tf_op jit(solution)/shard_map/ppermute | solution.py:18
  7.0 0.9 select_bitcast_fusion.3
  7.9 4.3 %collective-permute-start.1 = (bf16[2,128,256]{2,1,0:T(8,128)(2,1)S(1)}, bf16[2,128,256]{2,1,0:T(8,128)(2,1)S(1)}, u32[]{:S(2)}, u32[]{:S(2)}) collective-permute-start(bf16[2,128,256]{2,1,0:T(8,128)(2,1)S(1)} %pad_maximum_fusion.1), channel_id=1, source_target_pairs={{0,8},{8,0},{1,9},{9,1},{2,10},{10,2},{3,11},{11,3},{4,12},{12,4},... | collective-permute-start | bytes 393224 | tf_op jit(solution)/shard_map/ppermute | solution.py:18
  12.2 0.9 reshape.109
  13.0 1.1 broadcast_in_dim.4
  14.2 15.1 %all-to-all-start = ((bf16[32,64,256]{2,1,0:T(8,128)(2,1)}), bf16[32,64,256]{2,1,0:T(8,128)(2,1)S(1)}, u32[]{:S(2)}, u32[]{:S(2)}) async-start(bf16[32,64,256]{2,1,0:T(8,128)(2,1)} %bitcast.1), calls=%async_computation | async-start | bytes 2097152 | tf_op jit(solution)/shard_map/all_to_all | solution.py:14
  29.3 2.7 %collective-permute-start.2 = (bf16[2,2,128,256]{3,2,1,0:T(8,128)(2,1)S(1)}, bf16[2,2,128,256]{3,2,1,0:T(8,128)(2,1)S(1)}, u32[]{:S(2)}, u32[]{:S(2)}) collective-permute-start(bf16[2,2,128,256]{3,2,1,0:T(8,128)(2,1)S(1)} %pad_maximum_fusion), channel_id=1, source_target_pairs={{0,6},{2,0},{4,2},{6,4},{1,7},{3,1},{5,3},{7,5},{8,14},{10,8},{12,... | collective-permute-start | bytes 786440 | tf_op jit(solution)/shard_map/ppermute | solution.py:22
  32.1 3.0 %collective-permute-start.3 = (bf16[2,2,128,256]{3,2,1,0:T(8,128)(2,1)S(1)}, bf16[2,2,128,256]{3,2,1,0:T(8,128)(2,1)S(1)}, u32[]{:S(2)}, u32[]{:S(2)}) collective-permute-start(bf16[2,2,128,256]{3,2,1,0:T(8,128)(2,1)S(1)} %pad_maximum_fusion), channel_id=1, source_target_pairs={{0,4},{2,6},{4,0},{6,2},{1,5},{3,7},{5,1},{7,3},{8,12},{10,14},{12... | collective-permute-start | bytes 786440 | tf_op jit(solution)/shard_map/ppermute | solution.py:22
  35.2 4.0 %collective-permute-start.4 = (bf16[2,2,128,256]{3,2,1,0:T(8,128)(2,1)S(1)}, bf16[2,2,128,256]{3,2,1,0:T(8,128)(2,1)S(1)}, u32[]{:S(2)}, u32[]{:S(2)}) collective-permute-start(bf16[2,2,128,256]{3,2,1,0:T(8,128)(2,1)S(1)} %pad_maximum_fusion), channel_id=1, source_target_pairs={{0,2},{2,4},{4,6},{6,0},{1,3},{3,5},{5,7},{7,1},{8,10},{10,12},{12... | collective-permute-start | bytes 786440 | tf_op jit(solution)/shard_map/ppermute | solution.py:22
  39.2 5.2 %collective-permute-done.2 = bf16[2,2,128,256]{3,2,1,0:T(8,128)(2,1)S(1)} collective-permute-done((bf16[2,2,128,256]{3,2,1,0:T(8,128)(2,1)S(1)}, bf16[2,2,128,256]{3,2,1,0:T(8,128)(2,1)S(1)}, u32[]{:S(2)}, u32[]{:S(2)}) %collective-permute-start.2) | collective-permute-done | bytes 262176 | tf_op jit(solution)/shard_map/ppermute | solution.py:22
  44.5 2.4 %collective-permute-done.4 = bf16[2,2,128,256]{3,2,1,0:T(8,128)(2,1)S(1)} collective-permute-done((bf16[2,2,128,256]{3,2,1,0:T(8,128)(2,1)S(1)}, bf16[2,2,128,256]{3,2,1,0:T(8,128)(2,1)S(1)}, u32[]{:S(2)}, u32[]{:S(2)}) %collective-permute-start.4) | collective-permute-done | bytes 262176 | tf_op jit(solution)/shard_map/ppermute | solution.py:22
  47.2 10.2 %all-to-all-done = bf16[32,64,256]{2,1,0:T(8,128)(2,1)S(1)} async-done(((bf16[32,64,256]{2,1,0:T(8,128)(2,1)}), bf16[32,64,256]{2,1,0:T(8,128)(2,1)S(1)}, u32[]{:S(2)}, u32[]{:S(2)}) %all-to-all-start) | async-done | bytes 1048608 | tf_op jit(solution)/shard_map/all_to_all | solution.py:14
  57.3 1.1 copy.12
  58.4 1.6 %broadcast_in_dim.5 = bf16[2,4,2,2,128,256]{5,3,4,1,2,0:T(2,128)(2,1)S(1)} broadcast(bf16[4,2,2,128,256]{4,2,3,0,1:T(2,128)(2,1)S(1)} %copy.12), dimensions={1,2,3,4,5} | broadcast | bytes 3145728 | tf_op jit(solution)/shard_map/broadcast_in_dim | solution.py:61
  60.0 5.4 %all_to_all.20 = bf16[2,4,2,2,128,256]{5,3,4,1,2,0:T(2,128)(2,1)S(1)} all-to-all(bf16[2,4,2,2,128,256]{5,3,4,1,2,0:T(2,128)(2,1)S(1)} %broadcast_in_dim.5), channel_id=1, replica_groups=mesh['zh'=4,'yk'=4,'yl'=2,'zl'=2,'x'=4,'core'=2] {'core'}, dimensions={0} | all-to-all | bytes 4194304 | tf_op jit(solution)/shard_map/all_to_all | solution.py:14
  65.5 2.2 %fusion = f32[2,256]{1,0:T(2,128)S(1)} fusion(bf16[2,4,2,2,128,256]{5,3,4,1,2,0:T(2,128)(2,1)S(1)} %all_to_all.20), kind=kLoop, calls=%fused_computation.6 | loop fusion | flops 2096640 | bytes 2099200 | tf_op jit(solution)/shard_map/reduce_sum | solution.py:31
  67.7 2.8 %multiply_reduce_fusion = f32[2,256]{1,0:T(2,128)S(1)} fusion(bf16[2,4,2,2,128,256]{5,3,4,1,2,0:T(2,128)(2,1)S(1)} %all_to_all.20, f32[2,256]{1,0:T(2,128)S(1)} %get-tuple-element.21), kind=kLoop, calls=%fused_computation.5 | loop fusion | flops 4193792 | bytes 2101248 | tf_op jit(solution)/shard_map/reduce_sum | solution.py:33
  70.5 2.8 %convert_reduce_fusion = f32[2,256]{1,0:T(2,128)S(1)} fusion(f32[2,256]{1,0:T(2,128)S(1)} %get-tuple-element.18, f32[2,256]{1,0:T(2,128)S(1)} %get-tuple-element.21, bf16[2,4,2,2,128,256]{5,3,4,1,2,0:T(2,128)(2,1)S(1)} %all_to_all.20), kind=kLoop, calls=%fused_computation.2 | loop fusion | flops 6290944 | bytes 2103296 | tf_op jit(solution)/shard_map/reduce_sum | solution.py:97
  73.3 0.3 convert_reduce_fusion.2
  73.6 0.3 fusion.6
  74.0 0.3 convert_reduce_fusion.1
  74.3 1.8 %convert_bitcast_fusion = f32[2,4,2,128,2,256]{5,4,3,1,0,2:T(2,128)S(1)} fusion(bf16[2,4,2,2,128,256]{5,3,4,1,2,0:T(2,128)(2,1)S(1)} %all_to_all.20), kind=kLoop, calls=%fused_computation | loop fusion | flops 1048576 | bytes 6291456 | tf_op jit(solution)/shard_map/convert_element_type | solution.py:30
  76.1 2.1 %copy.13 = f32[2,4,2,128,2,256]{5,4,3,2,1,0:T(2,128)S(1)} copy(f32[2,4,2,128,2,256]{5,4,3,1,0,2:T(2,128)S(1)} %convert_bitcast_fusion) | data formatting | bytes 8388608 | tf_op jit(solution)/shard_map/convert_element_type | solution.py:30
  78.2 0.4 copy.17
  78.7 0.6 multiply_convert_fusion.2
  79.3 1.0 fusion.13
  80.3 0.3 copy-done
  80.6 2.4 %multiply_convert_fusion = bf16[2048,512]{1,0:T(8,128)(2,1)} fusion(bf16[2048,512]{1,0:T(8,128)(2,1)S(1)} %multiply_convert_fusion.2, bf16[256,512]{1,0:T(8,128)(2,1)S(1)} %get-tuple-element.10, f32[512]{0:T(512)S(1)} %get-tuple-element.6, f32[512]{0:T(512)S(1)} %get-tuple-element.8, f32[512]{0:T(512)S(1)} %bitcast.90, bf16[2048,256]{1,0:T(8,128)(2,1)S(1)} %bitcast.82, ...), kind=kOutput, calls=%fused_computation.1 | convolution fusion | flops 545259520 | bytes 5513216 | tf_op jit(solution)/shard_map/dot_general | solution.py:103
  83.0 2.5 %reshape.115 = bf16[2,4,2,128,2,256]{5,4,3,2,1,0:T(2,128)(2,1)S(1)} reshape(bf16[2048,512]{1,0:T(8,128)(2,1)} %multiply_convert_fusion) | data formatting | bytes 4194304 | tf_op jit(solution)/shard_map/reshape | solution.py:123
  85.5 1.7 %copy.22 = bf16[2,4,2,128,2,256]{5,3,4,0,1,2:T(8,128)(2,1)} copy(bf16[2,4,2,128,2,256]{5,4,3,2,1,0:T(2,128)(2,1)S(1)} %reshape.115) | data formatting | bytes 4194304 | tf_op jit(solution)/shard_map/reshape | solution.py:123
  87.2 3.8 %all-to-all-start.3 = ((bf16[2,4,2,2,128,256]{5,4,3,2,1,0:T(8,128)(2,1)}), bf16[2,4,2,2,128,256]{5,4,3,2,1,0:T(8,128)(2,1)S(1)}, u32[]{:S(2)}, u32[]{:S(2)}) async-start(bf16[2,4,2,2,128,256]{5,4,3,2,1,0:T(8,128)(2,1)} %bitcast.84), calls=%async_computation.3 | async-start | bytes 4194304 | tf_op jit(solution)/shard_map/all_to_all | solution.py:14
  91.0 3.3 %fusion.3 = bf16[2048,256]{1,0:T(8,128)(2,1)} fusion(bf16[2048,512]{1,0:T(8,128)(2,1)} %copy-done, bf16[256,512]{1,0:T(8,128)(2,1)S(1)} %get-tuple-element.10, f32[256]{0:T(256)S(1)} %get-tuple-element.7, f32[256]{0:T(256)S(1)} %get-tuple-element.9, f32[256]{0:T(256)S(1)} %add_rsqrt_fusion.1, f32[256]{0:T(256)S(1)} %broadcast_multiply_fusion.2, ...), kind=kOutput, calls=%fused_computation.14 | convolution fusion | flops 542113792 | bytes 4460544 | tf_op jit(solution)/shard_map/dot_general | solution.py:111
  94.3 7.4 %all-to-all-start.2 = ((bf16[32,64,256]{2,1,0:T(8,128)(2,1)}), bf16[32,64,256]{2,1,0:T(8,128)(2,1)}, u32[]{:S(2)}, u32[]{:S(2)}) async-start(bf16[32,64,256]{2,1,0:T(8,128)(2,1)} %bitcast.85), calls=%async_computation.2 | async-start | bytes 2097152 | tf_op jit(solution)/shard_map/all_to_all | solution.py:14
  101.7 0.3 add_convert_fusion
  102.1 2.4 %collective-permute-start.5 = (bf16[2,2,128,256]{3,2,1,0:T(8,128)(2,1)S(1)}, bf16[2,2,128,256]{3,2,1,0:T(8,128)(2,1)S(1)}, u32[]{:S(2)}, u32[]{:S(2)}) collective-permute-start(bf16[2,2,128,256]{3,2,1,0:T(8,128)(2,1)S(1)} %get-tuple-element.11), channel_id=1, source_target_pairs={{0,2},{2,4},{4,6},{6,0},{1,3},{3,5},{5,7},{7,1},{8,10},{10,12},{12... | collective-permute-start | bytes 786440 | tf_op jit(solution)/shard_map/ppermute | solution.py:22
  104.5 4.3 %collective-permute-start.6 = (bf16[2,2,128,256]{3,2,1,0:T(8,128)(2,1)S(1)}, bf16[2,2,128,256]{3,2,1,0:T(8,128)(2,1)S(1)}, u32[]{:S(2)}, u32[]{:S(2)}) collective-permute-start(bf16[2,2,128,256]{3,2,1,0:T(8,128)(2,1)S(1)} %get-tuple-element.13), channel_id=1, source_target_pairs={{0,4},{2,6},{4,0},{6,2},{1,5},{3,7},{5,1},{7,3},{8,12},{10,14},{12... | collective-permute-start | bytes 786440 | tf_op jit(solution)/shard_map/ppermute | solution.py:22
  108.8 1.9 %collective-permute-start.7 = (bf16[2,2,128,256]{3,2,1,0:T(8,128)(2,1)S(1)}, bf16[2,2,128,256]{3,2,1,0:T(8,128)(2,1)S(1)}, u32[]{:S(2)}, u32[]{:S(2)}) collective-permute-start(bf16[2,2,128,256]{3,2,1,0:T(8,128)(2,1)S(1)} %get-tuple-element.12), channel_id=1, source_target_pairs={{0,6},{2,0},{4,2},{6,4},{1,7},{3,1},{5,3},{7,5},{8,14},{10,8},{12,... | collective-permute-start | bytes 786440 | tf_op jit(solution)/shard_map/ppermute | solution.py:22
  110.8 2.4 %collective-permute-done.5 = bf16[2,2,128,256]{3,2,1,0:T(8,128)(2,1)S(1)} collective-permute-done((bf16[2,2,128,256]{3,2,1,0:T(8,128)(2,1)S(1)}, bf16[2,2,128,256]{3,2,1,0:T(8,128)(2,1)S(1)}, u32[]{:S(2)}, u32[]{:S(2)}) %collective-permute-start.5) | collective-permute-done | bytes 262176 | tf_op jit(solution)/shard_map/ppermute | solution.py:22
  113.1 3.9 %collective-permute-done.6 = bf16[2,2,128,256]{3,2,1,0:T(8,128)(2,1)S(1)} collective-permute-done((bf16[2,2,128,256]{3,2,1,0:T(8,128)(2,1)S(1)}, bf16[2,2,128,256]{3,2,1,0:T(8,128)(2,1)S(1)}, u32[]{:S(2)}, u32[]{:S(2)}) %collective-permute-start.6) | collective-permute-done | bytes 262176 | tf_op jit(solution)/shard_map/ppermute | solution.py:22
  117.1 4.6 %collective-permute-done.7 = bf16[2,2,128,256]{3,2,1,0:T(8,128)(2,1)S(1)} collective-permute-done((bf16[2,2,128,256]{3,2,1,0:T(8,128)(2,1)S(1)}, bf16[2,2,128,256]{3,2,1,0:T(8,128)(2,1)S(1)}, u32[]{:S(2)}, u32[]{:S(2)}) %collective-permute-start.7) | collective-permute-done | bytes 262176 | tf_op jit(solution)/shard_map/ppermute | solution.py:22
  121.8 2.5 %collective-permute-start.8 = (bf16[2,128,256]{2,1,0:T(8,128)(2,1)S(1)}, bf16[2,128,256]{2,1,0:T(8,128)(2,1)S(1)}, u32[]{:S(2)}, u32[]{:S(2)}) collective-permute-start(bf16[2,128,256]{2,1,0:T(8,128)(2,1)S(1)} %dynamic-slice_bitcast_fusion.3), channel_id=1, source_target_pairs={{0,8},{8,0},{1,9},{9,1},{2,10},{10,2},{3,11},{11,3},{4,12},{12,4},... | collective-permute-start | bytes 393224 | tf_op jit(solution)/shard_map/ppermute | solution.py:18
  124.3 7.7 %collective-permute-done.8 = bf16[2,128,256]{2,1,0:T(8,128)(2,1)S(1)} collective-permute-done((bf16[2,128,256]{2,1,0:T(8,128)(2,1)S(1)}, bf16[2,128,256]{2,1,0:T(8,128)(2,1)S(1)}, u32[]{:S(2)}, u32[]{:S(2)}) %collective-permute-start.8) | collective-permute-done | bytes 131104 | tf_op jit(solution)/shard_map/ppermute | solution.py:18
  132.1 2.6 %collective-permute-start.9 = (bf16[128,256]{1,0:T(8,128)(2,1)S(1)}, bf16[128,256]{1,0:T(8,128)(2,1)S(1)}, u32[]{:S(2)}, u32[]{:S(2)}) collective-permute-start(bf16[128,256]{1,0:T(8,128)(2,1)S(1)} %dynamic-slice_bitcast_fusion.4), channel_id=1, source_target_pairs={{0,16},{16,0},{1,17},{17,1},{2,18},{18,2},{3,19},{19,3},{4,20},{20... | collective-permute-start | bytes 196616 | tf_op jit(solution)/shard_map/ppermute | solution.py:18
  134.7 3.6 %collective-permute-done.9 = bf16[128,256]{1,0:T(8,128)(2,1)S(1)} collective-permute-done((bf16[128,256]{1,0:T(8,128)(2,1)S(1)}, bf16[128,256]{1,0:T(8,128)(2,1)S(1)}, u32[]{:S(2)}, u32[]{:S(2)}) %collective-permute-start.9) | collective-permute-done | bytes 65568 | tf_op jit(solution)/shard_map/ppermute | solution.py:18
  138.3 0.6 fusion.19
  139.0 1.4 reduce_sum.109
  140.3 0.6 copy.16
  (34 shorter events, 0.7 us)
Async XLA Ops:
  0.6 6.4 %collective-permute-start = (bf16[128,256]{1,0:T(8,128)(2,1)}, bf16[128,256]{1,0:T(8,128)(2,1)S(1)}, u32[]{:S(2)}, u32[]{:S(2)}) collective-permute-start(bf16[128,256]{1,0:T(8,128)(2,1)} %param.3), channel_id=1, source_target_pairs={{0,16},{16,0},{1,17},{17,1},{2,18},{18,2},{3,19},{19,3},{4,20},{20... | collective-permute-start | bytes 196616 | tf_op jit(solution)/shard_map/ppermute | solution.py:18
  7.9 21.4 %collective-permute-start.1 = (bf16[2,128,256]{2,1,0:T(8,128)(2,1)S(1)}, bf16[2,128,256]{2,1,0:T(8,128)(2,1)S(1)}, u32[]{:S(2)}, u32[]{:S(2)}) collective-permute-start(bf16[2,128,256]{2,1,0:T(8,128)(2,1)S(1)} %pad_maximum_fusion.1), channel_id=1, source_target_pairs={{0,8},{8,0},{1,9},{9,1},{2,10},{10,2},{3,11},{11,3},{4,12},{12,4},... | collective-permute-start | bytes 393224 | tf_op jit(solution)/shard_map/ppermute | solution.py:18
  14.2 43.2 %all-to-all-start = ((bf16[32,64,256]{2,1,0:T(8,128)(2,1)}), bf16[32,64,256]{2,1,0:T(8,128)(2,1)S(1)}, u32[]{:S(2)}, u32[]{:S(2)}) async-start(bf16[32,64,256]{2,1,0:T(8,128)(2,1)} %bitcast.1), calls=%async_computation | async-start | bytes 2097152 | tf_op jit(solution)/shard_map/all_to_all | solution.py:14
  29.3 15.1 %collective-permute-start.2 = (bf16[2,2,128,256]{3,2,1,0:T(8,128)(2,1)S(1)}, bf16[2,2,128,256]{3,2,1,0:T(8,128)(2,1)S(1)}, u32[]{:S(2)}, u32[]{:S(2)}) collective-permute-start(bf16[2,2,128,256]{3,2,1,0:T(8,128)(2,1)S(1)} %pad_maximum_fusion), channel_id=1, source_target_pairs={{0,6},{2,0},{4,2},{6,4},{1,7},{3,1},{5,3},{7,5},{8,14},{10,8},{12,... | collective-permute-start | bytes 786440 | tf_op jit(solution)/shard_map/ppermute | solution.py:22
  32.1 12.3 %collective-permute-start.3 = (bf16[2,2,128,256]{3,2,1,0:T(8,128)(2,1)S(1)}, bf16[2,2,128,256]{3,2,1,0:T(8,128)(2,1)S(1)}, u32[]{:S(2)}, u32[]{:S(2)}) collective-permute-start(bf16[2,2,128,256]{3,2,1,0:T(8,128)(2,1)S(1)} %pad_maximum_fusion), channel_id=1, source_target_pairs={{0,4},{2,6},{4,0},{6,2},{1,5},{3,7},{5,1},{7,3},{8,12},{10,14},{12... | collective-permute-start | bytes 786440 | tf_op jit(solution)/shard_map/ppermute | solution.py:22
  35.2 11.8 %collective-permute-start.4 = (bf16[2,2,128,256]{3,2,1,0:T(8,128)(2,1)S(1)}, bf16[2,2,128,256]{3,2,1,0:T(8,128)(2,1)S(1)}, u32[]{:S(2)}, u32[]{:S(2)}) collective-permute-start(bf16[2,2,128,256]{3,2,1,0:T(8,128)(2,1)S(1)} %pad_maximum_fusion), channel_id=1, source_target_pairs={{0,2},{2,4},{4,6},{6,0},{1,3},{3,5},{5,7},{7,1},{8,10},{10,12},{12... | collective-permute-start | bytes 786440 | tf_op jit(solution)/shard_map/ppermute | solution.py:22
  79.3 1.4 copy-start
  87.2 7.1 %all-to-all-start.3 = ((bf16[2,4,2,2,128,256]{5,4,3,2,1,0:T(8,128)(2,1)}), bf16[2,4,2,2,128,256]{5,4,3,2,1,0:T(8,128)(2,1)S(1)}, u32[]{:S(2)}, u32[]{:S(2)}) async-start(bf16[2,4,2,2,128,256]{5,4,3,2,1,0:T(8,128)(2,1)} %bitcast.84), calls=%async_computation.3 | async-start | bytes 4194304 | tf_op jit(solution)/shard_map/all_to_all | solution.py:14
  94.3 44.7 %all-to-all-start.2 = ((bf16[32,64,256]{2,1,0:T(8,128)(2,1)}), bf16[32,64,256]{2,1,0:T(8,128)(2,1)}, u32[]{:S(2)}, u32[]{:S(2)}) async-start(bf16[32,64,256]{2,1,0:T(8,128)(2,1)} %bitcast.85), calls=%async_computation.2 | async-start | bytes 2097152 | tf_op jit(solution)/shard_map/all_to_all | solution.py:14
  102.1 11.0 %collective-permute-start.5 = (bf16[2,2,128,256]{3,2,1,0:T(8,128)(2,1)S(1)}, bf16[2,2,128,256]{3,2,1,0:T(8,128)(2,1)S(1)}, u32[]{:S(2)}, u32[]{:S(2)}) collective-permute-start(bf16[2,2,128,256]{3,2,1,0:T(8,128)(2,1)S(1)} %get-tuple-element.11), channel_id=1, source_target_pairs={{0,2},{2,4},{4,6},{6,0},{1,3},{3,5},{5,7},{7,1},{8,10},{10,12},{12... | collective-permute-start | bytes 786440 | tf_op jit(solution)/shard_map/ppermute | solution.py:22
  104.5 12.6 %collective-permute-start.6 = (bf16[2,2,128,256]{3,2,1,0:T(8,128)(2,1)S(1)}, bf16[2,2,128,256]{3,2,1,0:T(8,128)(2,1)S(1)}, u32[]{:S(2)}, u32[]{:S(2)}) collective-permute-start(bf16[2,2,128,256]{3,2,1,0:T(8,128)(2,1)S(1)} %get-tuple-element.13), channel_id=1, source_target_pairs={{0,4},{2,6},{4,0},{6,2},{1,5},{3,7},{5,1},{7,3},{8,12},{10,14},{12... | collective-permute-start | bytes 786440 | tf_op jit(solution)/shard_map/ppermute | solution.py:22
  108.8 12.8 %collective-permute-start.7 = (bf16[2,2,128,256]{3,2,1,0:T(8,128)(2,1)S(1)}, bf16[2,2,128,256]{3,2,1,0:T(8,128)(2,1)S(1)}, u32[]{:S(2)}, u32[]{:S(2)}) collective-permute-start(bf16[2,2,128,256]{3,2,1,0:T(8,128)(2,1)S(1)} %get-tuple-element.12), channel_id=1, source_target_pairs={{0,6},{2,0},{4,2},{6,4},{1,7},{3,1},{5,3},{7,5},{8,14},{10,8},{12,... | collective-permute-start | bytes 786440 | tf_op jit(solution)/shard_map/ppermute | solution.py:22
  121.8 10.3 %collective-permute-start.8 = (bf16[2,128,256]{2,1,0:T(8,128)(2,1)S(1)}, bf16[2,128,256]{2,1,0:T(8,128)(2,1)S(1)}, u32[]{:S(2)}, u32[]{:S(2)}) collective-permute-start(bf16[2,128,256]{2,1,0:T(8,128)(2,1)S(1)} %dynamic-slice_bitcast_fusion.3), channel_id=1, source_target_pairs={{0,8},{8,0},{1,9},{9,1},{2,10},{10,2},{3,11},{11,3},{4,12},{12,4},... | collective-permute-start | bytes 393224 | tf_op jit(solution)/shard_map/ppermute | solution.py:18
  132.1 6.2 %collective-permute-start.9 = (bf16[128,256]{1,0:T(8,128)(2,1)S(1)}, bf16[128,256]{1,0:T(8,128)(2,1)S(1)}, u32[]{:S(2)}, u32[]{:S(2)}) collective-permute-start(bf16[128,256]{1,0:T(8,128)(2,1)S(1)} %dynamic-slice_bitcast_fusion.4), channel_id=1, source_target_pairs={{0,16},{16,0},{1,17},{17,1},{2,18},{18,2},{3,19},{19,3},{4,20},{20... | collective-permute-start | bytes 196616 | tf_op jit(solution)/shard_map/ppermute | solution.py:18

commit v4 on v1

v4 whole, which is shorter than its diff:
```python
import functools

import jax
import jax.numpy as jnp
from jax import lax
from jax.experimental import pallas as pl
from jax.experimental.pallas import tpu as pltpu
from jax.sharding import Mesh, PartitionSpec as P

EPSILON = 1e-05
OFF_WEIGHT = 0.0051

SAMPLES = ("zh", "yk", "yl")
FEATURES = ("zl", "x", "core")
F32 = jnp.float32
BF16 = jnp.bfloat16
HIGHEST = lax.Precision.HIGHEST
VMEM_LIMIT = 28 * 1024 * 1024

BLOCK = 128
BLOCKS = 16


def exchange(values, axes):
    return lax.all_to_all(values, axes, 0, 0, tiled=True)


def near_swap(values, move):
    flip = 2 * (move % 2) + move // 2
    return lax.ppermute(values, ("yl", "zl"), [(i, i ^ flip) for i in range(4)])


def shift(values, distance):
    return lax.ppermute(values, "x", [(i, (i + distance) % 4) for i in range(4)])


def narrow_sum(*terms):
    return sum(term.astype(F32) for term in terms).astype(BF16)


def sample_row(place_ref, t):
    core = t // 8
    x = lax.rem(place_ref[0] + (t // 2) % 4, 4)
    zl = lax.rem(place_ref[1] + t % 2, 2)
    return pl.multiple_of(((zl * 4 + x) * 2 + core) * BLOCK, BLOCK)


def fold(values):
    return values.reshape(-1, 8, values.shape[-1]).sum(axis=0)


def tile_kernel(place_ref, first_ref, second_ref, moved_ref, na_ref, nb_ref, grad_ref, vectors_ref):
    count = BLOCK * BLOCKS
    width = first_ref.shape[1]

    def rows(t):
        return pl.ds(pl.multiple_of(t * BLOCK, BLOCK), BLOCK)

    def load(t):
        return (
            first_ref[rows(t), :].astype(F32),
            second_ref[t, 0].astype(F32),
            second_ref[t, 1].astype(F32),
        )

    zeros = (jnp.zeros((8, width), F32),) * 3

    def add_values(t, sums):
        return tuple(s + fold(v) for s, v in zip(sums, load(t)))

    sums = lax.fori_loop(0, BLOCKS, add_values, zeros)
    centers = [jnp.sum(s, axis=0, keepdims=True) / count for s in sums]

    def add_squares(t, sums):
        out = []
        for s, v, center in zip(sums, load(t), centers):
            shifted = v - center
            out.append(s + fold(shifted * shifted))
        return tuple(out)

    squares = lax.fori_loop(0, BLOCKS, add_squares, zeros)
    scales = [lax.rsqrt(jnp.sum(s, axis=0, keepdims=True) / count + EPSILON) for s in squares]

    def normalize(t, sums):
        a = first_ref[pl.ds(sample_row(place_ref, t), BLOCK), :].astype(F32)
        values = (a, second_ref[t, 0].astype(F32), second_ref[t, 1].astype(F32))
        out = []
        for i, (s, v, center, scale) in enumerate(zip(sums, values, centers, scales)):
            norm = ((v - center) * scale).astype(BF16)
            if i == 0:
                na_ref[rows(t), :] = norm
            else:
                nb_ref[rows(t), (i - 1) * width : i * width] = norm
            out.append(s + fold(norm.astype(F32)))
        return tuple(out)

    norm_sums = lax.fori_loop(0, BLOCKS, normalize, zeros)
    mean_first = norm_sums[0] / count
    mean_second = jnp.concatenate(norm_sums[1:], axis=1) / count

    correlation = (
        lax.dot_general(
            na_ref[...], nb_ref[...], (((0,), (0,)), ((), ())), preferred_element_type=F32
        )
        / count
    )
    row_ids = lax.broadcasted_iota(jnp.int32, correlation.shape, 0)
    col_ids = lax.broadcasted_iota(jnp.int32, correlation.shape, 1)
    grad = jnp.where(
        row_ids == col_ids + place_ref[2],
        2.0 * (correlation - 1.0),
        2.0 * OFF_WEIGHT * correlation,
    ).astype(BF16)
    grad_ref[...] = grad
    grad_wide = grad.astype(F32)
    weighted = grad_wide * correlation
    projection_second = jnp.sum(weighted, axis=0, keepdims=True)
    centering_second = jnp.sum(
        jnp.dot(mean_first, grad_wide, preferred_element_type=F32, precision=HIGHEST),
        axis=0,
        keepdims=True,
    )
    across = (((1,), (1,)), ((), ()))
    projection_first = lax.dot_general(
        jnp.ones((8, weighted.shape[1]), F32), weighted, across,
        preferred_element_type=F32, precision=HIGHEST,
    )
    centering_first = jnp.sum(
        lax.dot_general(
            mean_second, grad_wide, across, preferred_element_type=F32, precision=HIGHEST
        ),
        axis=0,
        keepdims=True,
    )
    vectors_ref[0:1, :] = centering_first
    vectors_ref[1:2, :] = projection_first[0:1]
    vectors_ref[2:3, :] = scales[0]
    scale_second = jnp.concatenate(scales[1:], axis=1)

    def back(t, carry):
        partial = jnp.dot(na_ref[rows(t), :], grad, preferred_element_type=F32)
        partial = (
            (partial - centering_second - nb_ref[rows(t), :].astype(F32) * projection_second)
            * scale_second
        ).astype(BF16)
        moved_ref[t, 0] = partial[:, :width]
        moved_ref[t, 1] = partial[:, width:]
        return carry

    lax.fori_loop(0, BLOCKS, back, 0)


def first_kernel(place_ref, na_ref, nb_ref, grad_ref, vectors_ref, out_ref):
    grad = grad_ref[...]
    centering, projection, scale = (vectors_ref[i : i + 1, :] for i in range(3))

    def back(t, carry):
        rows = pl.ds(pl.multiple_of(t * BLOCK, BLOCK), BLOCK)
        partial = lax.dot_general(
            nb_ref[rows, :], grad, (((1,), (1,)), ((), ())), preferred_element_type=F32
        )
        partial = (partial - centering - na_ref[rows, :].astype(F32) * projection) * scale
        out_ref[pl.ds(sample_row(place_ref, t), BLOCK), :] = partial.astype(BF16)
        return carry

    lax.fori_loop(0, BLOCKS, back, 0)


def call(kernel, outputs, flops, moved, *operands):
    spec = pl.BlockSpec(memory_space=pltpu.VMEM)
    return pl.pallas_call(
        kernel,
        out_shape=outputs,
        in_specs=[pl.BlockSpec(memory_space=pltpu.SMEM)] + [spec] * (len(operands) - 1),
        out_specs=jax.tree.map(lambda _: spec, outputs),
        compiler_params=pltpu.CompilerParams(vmem_limit_bytes=VMEM_LIMIT),
        cost_estimate=pl.CostEstimate(flops=flops, bytes_accessed=moved, transcendentals=0),
    )(*operands)


def shards(first_view_outputs, second_view_outputs):
    rows_a, width_a = first_view_outputs.shape
    rows_b, width_b = second_view_outputs.shape
    n_dp = lax.axis_size(SAMPLES)
    half = width_a // 2
    total_count = rows_a * n_dp
    shape = jax.ShapeDtypeStruct

    halves = jnp.stack([first_view_outputs[:, :half], first_view_outputs[:, half:]])
    first = exchange(
        jnp.broadcast_to(halves, (n_dp // 2, 2, rows_a, half)).reshape(n_dp, rows_a, half),
        SAMPLES,
    ).reshape(total_count, half)

    near = [second_view_outputs] + [near_swap(second_view_outputs, k) for k in (1, 2, 3)]
    near = jnp.stack(near)
    ahead = jnp.stack([near] + [shift(near, -k) for k in (1, 2, 3)])
    ahead = jnp.broadcast_to(ahead, (2,) + ahead.shape)
    first, ahead = lax.optimization_barrier((first, ahead))
    second = exchange(ahead, "core").reshape(BLOCKS, 2, rows_b, width_b)

    feat = lax.axis_index(FEATURES)
    pair = lax.axis_index(("zh", "yk"))
    place = jnp.stack(
        [
            lax.axis_index("x"),
            lax.axis_index("zl"),
            jnp.where(feat == pair, 0, 2 * width_a),
        ]
    ).astype(jnp.int32)
    flops = 2 * total_count * half * 2 * width_b
    moved, norm_first, norm_second, grad, vectors = call(
        tile_kernel,
        (
            shape((BLOCKS, 2, rows_b, width_b), BF16),
            shape((total_count, half), BF16),
            shape((total_count, 2 * width_b), BF16),
            shape((half, 2 * width_b), BF16),
            shape((8, half), F32),
        ),
        2 * flops, 8 << 20, place, first, second,
    )
    partial_first = call(
        first_kernel, shape((total_count, half), BF16), flops, 4 << 20,
        place, norm_first, norm_second, grad, vectors,
    )

    pieces = exchange(moved.reshape(2, 4, 4, rows_b, width_b), "core")
    pieces = narrow_sum(pieces[0], pieces[1])
    pieces = narrow_sum(pieces[0], *[shift(pieces[k], k) for k in (1, 2, 3)])
    second_view_gradient = narrow_sum(
        pieces[0], *[near_swap(pieces[k], k) for k in (1, 2, 3)]
    )

    parts = exchange(partial_first.reshape(n_dp, rows_a, half), SAMPLES)
    parts = jnp.sum(parts.reshape(n_dp // 2, 2, rows_a, half).astype(F32), axis=0).astype(BF16)
    first_view_gradient = jnp.concatenate([parts[0], parts[1]], axis=1)
    return first_view_gradient, second_view_gradient


def solution(mesh):
    fine = Mesh(
        mesh.devices.reshape(4, 4, 2, 2, 4, 2), ("zh", "yk", "yl", "zl", "x", "core")
    )
    specs = (P(SAMPLES, FEATURES), P(FEATURES, SAMPLES))
    return jax.shard_map(
        shards, mesh=fine, in_specs=specs, out_specs=specs, check_vma=False
    )
```

time: 153 us -> 139 us (0.908)
  the two profiles are of different devices: /device:TPU:8 before, /device:TPU:6 now
where the time goes in v4:
time: 139 us
  starting transfers between devices  70.4 us (51%)
  waiting for transfers between devices  39 us (28%)
  Pallas kernels  14.3 us (10%)
  blocking collectives  5.42 us (4%)
  local copies, waits for them, and re-layouts  4.78 us (3%)
  other arithmetic  3.71 us (3%)
    all_to_all x3, starting transfers between devices, exchange(): return lax.all_to_all(values, axes, 0, 0, tiled=True)  32.4 us
    ppermute x6, waiting for transfers between devices, near_swap(): return lax.ppermute(values, ('yl', 'zl'), [(i, i ^ flip) for i in range(4)])  22.4 us
    ppermute x6, starting transfers between devices, shift(): lax.ppermute(values, 'x', [(i, (i + distance) % 4) for i in range(4)])  19.6 us
    ppermute x6, starting transfers between devices, near_swap(): return lax.ppermute(values, ('yl', 'zl'), [(i, i ^ flip) for i in range(4)])  18.4 us
    ppermute x6, waiting for transfers between devices, shift(): lax.ppermute(values, 'x', [(i, (i + distance) % 4) for i in range(4)])  16.6 us
    pallas_call x2, Pallas kernels, call(): pl.pallas_call(kernel, out_shape=outputs, in_specs=[pl.BlockSpec(memory_s...  14.3 us
    all_to_all x1, blocking collectives, exchange(): return lax.all_to_all(values, axes, 0, 0, tiled=True)  5.42 us
  transfers between devices with their start and end apart: 15, of which 8 were waited for; matrix products, arithmetic and copies ran while one was open for 2% of the time, Pallas kernels for 4%

profile of v4, /device:TPU:6, one launch (start us, length us, event | category | flops | bytes accessed | tf_op | source)
XLA Modules:
  0.0 138.5 jit_solution(7287543565655762156)
XLA Ops:
  0.6 0.0 copy-start.3
  0.6 0.8 slice_bitcast_fusion.11
  1.5 1.1 broadcast_in_dim.6
  2.6 16.0 %all-to-all-start = ((bf16[32,64,256]{2,1,0:T(8,128)(2,1)}), bf16[32,64,256]{2,1,0:T(8,128)(2,1)S(1)}, u32[]{:S(2)}, u32[]{:S(2)}) async-start(bf16[32,64,256]{2,1,0:T(8,128)(2,1)} %bitcast.5), calls=%async_computation | async-start | bytes 2097152 | tf_op jit(solution)/shard_map/all_to_all | solution.py:25
  18.6 3.7 %collective-permute-start = (bf16[128,256]{1,0:T(8,128)(2,1)S(1)}, bf16[128,256]{1,0:T(8,128)(2,1)S(1)}, u32[]{:S(2)}, u32[]{:S(2)}) collective-permute-start(bf16[128,256]{1,0:T(8,128)(2,1)S(1)} %copy-done.3), channel_id=1, source_target_pairs={{0,16},{8,24},{16,0},{24,8},{1,17},{9,25},{17,1},{25,9},{2,18},{10... | collective-permute-start | bytes 196616 | tf_op jit(solution)/shard_map/ppermute | solution.py:30
  22.3 3.1 %collective-permute-start.2 = (bf16[128,256]{1,0:T(8,128)(2,1)S(1)}, bf16[128,256]{1,0:T(8,128)(2,1)S(1)}, u32[]{:S(2)}, u32[]{:S(2)}) collective-permute-start(bf16[128,256]{1,0:T(8,128)(2,1)S(1)} %copy-done.3), channel_id=1, source_target_pairs={{0,24},{8,16},{16,8},{24,0},{1,25},{9,17},{17,9},{25,1},{2,26},{10... | collective-permute-start | bytes 196616 | tf_op jit(solution)/shard_map/ppermute | solution.py:30
  25.3 2.5 %collective-permute-start.1 = (bf16[128,256]{1,0:T(8,128)(2,1)S(1)}, bf16[128,256]{1,0:T(8,128)(2,1)S(1)}, u32[]{:S(2)}, u32[]{:S(2)}) collective-permute-start(bf16[128,256]{1,0:T(8,128)(2,1)S(1)} %copy-done.3), channel_id=1, source_target_pairs={{0,8},{8,0},{16,24},{24,16},{1,9},{9,1},{17,25},{25,17},{2,10},{10... | collective-permute-start | bytes 196616 | tf_op jit(solution)/shard_map/ppermute | solution.py:30
  27.8 16.9 %collective-permute-done = bf16[128,256]{1,0:T(8,128)(2,1)S(1)} collective-permute-done((bf16[128,256]{1,0:T(8,128)(2,1)S(1)}, bf16[128,256]{1,0:T(8,128)(2,1)S(1)}, u32[]{:S(2)}, u32[]{:S(2)}) %collective-permute-start) | collective-permute-done | bytes 65568 | tf_op jit(solution)/shard_map/ppermute | solution.py:30
  44.7 2.8 %collective-permute-done.2 = bf16[128,256]{1,0:T(8,128)(2,1)S(1)} collective-permute-done((bf16[128,256]{1,0:T(8,128)(2,1)S(1)}, bf16[128,256]{1,0:T(8,128)(2,1)S(1)}, u32[]{:S(2)}, u32[]{:S(2)}) %collective-permute-start.2) | collective-permute-done | bytes 65568 | tf_op jit(solution)/shard_map/ppermute | solution.py:30
  47.5 0.0 collective-permute-done.1
  47.5 3.3 %collective-permute-start.4 = (bf16[4,128,256]{2,1,0:T(8,128)(2,1)S(1)}, bf16[4,128,256]{2,1,0:T(8,128)(2,1)S(1)}, u32[]{:S(2)}, u32[]{:S(2)}) collective-permute-start(bf16[4,128,256]{2,1,0:T(8,128)(2,1)S(1)} %get-tuple-element.23), channel_id=1, source_target_pairs={{0,4},{2,6},{4,0},{6,2},{1,5},{3,7},{5,1},{7,3},{8,12},{10,14},{12... | collective-permute-start | bytes 786440 | tf_op jit(solution)/shard_map/ppermute | solution.py:34
  50.9 1.9 %collective-permute-start.3 = (bf16[4,128,256]{2,1,0:T(8,128)(2,1)S(1)}, bf16[4,128,256]{2,1,0:T(8,128)(2,1)S(1)}, u32[]{:S(2)}, u32[]{:S(2)}) collective-permute-start(bf16[4,128,256]{2,1,0:T(8,128)(2,1)S(1)} %get-tuple-element.23), channel_id=1, source_target_pairs={{0,6},{2,0},{4,2},{6,4},{1,7},{3,1},{5,3},{7,5},{8,14},{10,8},{12,... | collective-permute-start | bytes 786440 | tf_op jit(solution)/shard_map/ppermute | solution.py:34
  52.8 5.1 %collective-permute-start.5 = (bf16[4,128,256]{2,1,0:T(8,128)(2,1)S(1)}, bf16[4,128,256]{2,1,0:T(8,128)(2,1)S(1)}, u32[]{:S(2)}, u32[]{:S(2)}) collective-permute-start(bf16[4,128,256]{2,1,0:T(8,128)(2,1)S(1)} %get-tuple-element.23), channel_id=1, source_target_pairs={{0,2},{2,4},{4,6},{6,0},{1,3},{3,5},{5,7},{7,1},{8,10},{10,12},{12... | collective-permute-start | bytes 786440 | tf_op jit(solution)/shard_map/ppermute | solution.py:34
  57.9 0.1 pad_add_fusion.place_ref
  58.0 1.9 %collective-permute-done.4 = bf16[4,128,256]{2,1,0:T(8,128)(2,1)S(1)} collective-permute-done((bf16[4,128,256]{2,1,0:T(8,128)(2,1)S(1)}, bf16[4,128,256]{2,1,0:T(8,128)(2,1)S(1)}, u32[]{:S(2)}, u32[]{:S(2)}) %collective-permute-start.4) | collective-permute-done | bytes 262176 | tf_op jit(solution)/shard_map/ppermute | solution.py:34
  60.0 3.1 %collective-permute-done.3 = bf16[4,128,256]{2,1,0:T(8,128)(2,1)S(1)} collective-permute-done((bf16[4,128,256]{2,1,0:T(8,128)(2,1)S(1)}, bf16[4,128,256]{2,1,0:T(8,128)(2,1)S(1)}, u32[]{:S(2)}, u32[]{:S(2)}) %collective-permute-start.3) | collective-permute-done | bytes 262176 | tf_op jit(solution)/shard_map/ppermute | solution.py:34
  63.0 0.0 collective-permute-done.5
  63.0 0.1 pad_maximum_fusion
  63.2 0.0 all-to-all-done
  63.2 0.2 broadcast_in_dim.7
  63.4 5.4 %all_to_all.20 = bf16[2,4,4,128,256]{4,3,2,1,0:T(8,128)(2,1)S(1)} all-to-all(bf16[2,4,4,128,256]{4,3,2,1,0:T(8,128)(2,1)S(1)} %broadcast_in_dim.7), channel_id=1, replica_groups=mesh['zh'=4,'yk'=4,'yl'=2,'zl'=2,'x'=4,'core'=2] {'core'}, dimensions={0} | all-to-all | bytes 4194304 | tf_op jit(solution)/shard_map/all_to_all | solution.py:25
  68.9 0.0 copy-done.1
  68.9 1.2 copy-done.2
  70.1 9.0 %shard_map.41 = (bf16[16,2,128,256]{3,2,1,0:T(8,128)(2,1)S(1)}, bf16[2048,256]{1,0:T(8,128)(2,1)S(1)}, bf16[2048,512]{1,0:T(8,128)(2,1)S(1)}, bf16[256,512]{1,0:T(8,128)(2,1)S(1)}, f32[8,256]{1,0:T(8,128)S(1)}) custom-call(s32[3]{0:T(128)S(1)} %pad_add_fusion.place_ref, bf16[2048,256]{1,0:T(8,128)(2,1)S(1)} %bitcast.50, bf16[16,2,128,256]{3,2,1,0:T(8,128)(2,1)S(1)} %bitcast.49), custom_call_target="tpu_custom_call" | custom-call | flops 1073741824 | bytes 8388608 | tf_op jit(solution)/shard_map/pallas_call | solution.py:171
  79.1 1.3 copy-done
  80.4 4.8 %all-to-all-start.3 = ((bf16[2,4,4,128,256]{4,3,2,1,0:T(8,128)(2,1)}), bf16[2,4,4,128,256]{4,3,2,1,0:T(8,128)(2,1)}, u32[]{:S(2)}, u32[]{:S(2)}) async-start(bf16[2,4,4,128,256]{4,3,2,1,0:T(8,128)(2,1)} %bitcast.48), calls=%async_computation.3 | async-start | bytes 4194304 | tf_op jit(solution)/shard_map/all_to_all | solution.py:25
  85.3 5.3 %shard_map.42 = bf16[2048,256]{1,0:T(8,128)(2,1)} custom-call(s32[3]{0:T(128)S(1)} %pad_add_fusion.place_ref, bf16[2048,256]{1,0:T(8,128)(2,1)S(1)} %get-tuple-element.11.na_ref, bf16[2048,512]{1,0:T(8,128)(2,1)S(1)} %get-tuple-element.12.nb_ref, bf16[256,512]{1,0:T(8,128)(2,1)S(1)} %get-tuple-element.13.grad_ref, f32[8,256]{1,0:T(8,128)S(1)} %get-tuple-element.14.vectors_ref), custom_call_target="tpu_custom_call" | custom-call | flops 536870912 | bytes 4194304 | tf_op jit(solution)/shard_map/pallas_call | solution.py:171
  90.6 0.0 all-to-all-done.3
  90.6 11.6 %all-to-all-start.2 = ((bf16[32,64,256]{2,1,0:T(8,128)(2,1)}), bf16[32,64,256]{2,1,0:T(8,128)(2,1)S(1)}, u32[]{:S(2)}, u32[]{:S(2)}) async-start(bf16[32,64,256]{2,1,0:T(8,128)(2,1)} %bitcast.16), calls=%async_computation.2 | async-start | bytes 2097152 | tf_op jit(solution)/shard_map/all_to_all | solution.py:25
  102.2 1.9 %add_convert_fusion = bf16[1,4,4,128,256]{4,3,2,1,0:T(8,128)(2,1)S(1)} fusion(bf16[2,4,4,128,256]{4,3,2,1,0:T(8,128)(2,1)} %all-to-all-done.3), kind=kLoop, calls=%fused_computation | loop fusion | flops 2097152 | bytes 3145728 | tf_op jit(solution)/shard_map/convert_element_type | solution.py:38
  104.1 0.1 slice_bitcast_fusion.2
  104.1 3.9 %collective-permute-start.6 = (bf16[4,128,256]{2,1,0:T(8,128)(2,1)S(1)}, bf16[4,128,256]{2,1,0:T(8,128)(2,1)S(1)}, u32[]{:S(2)}, u32[]{:S(2)}) collective-permute-start(bf16[4,128,256]{2,1,0:T(8,128)(2,1)S(1)} %get-tuple-element.16), channel_id=1, source_target_pairs={{0,2},{2,4},{4,6},{6,0},{1,3},{3,5},{5,7},{7,1},{8,10},{10,12},{12... | collective-permute-start | bytes 786440 | tf_op jit(solution)/shard_map/ppermute | solution.py:34
  108.0 1.9 %collective-permute-start.8 = (bf16[4,128,256]{2,1,0:T(8,128)(2,1)S(1)}, bf16[4,128,256]{2,1,0:T(8,128)(2,1)S(1)}, u32[]{:S(2)}, u32[]{:S(2)}) collective-permute-start(bf16[4,128,256]{2,1,0:T(8,128)(2,1)S(1)} %get-tuple-element.17), channel_id=1, source_target_pairs={{0,6},{2,0},{4,2},{6,4},{1,7},{3,1},{5,3},{7,5},{8,14},{10,8},{12,... | collective-permute-start | bytes 786440 | tf_op jit(solution)/shard_map/ppermute | solution.py:34
  110.0 3.4 %collective-permute-start.7 = (bf16[4,128,256]{2,1,0:T(8,128)(2,1)S(1)}, bf16[4,128,256]{2,1,0:T(8,128)(2,1)S(1)}, u32[]{:S(2)}, u32[]{:S(2)}) collective-permute-start(bf16[4,128,256]{2,1,0:T(8,128)(2,1)S(1)} %get-tuple-element.18), channel_id=1, source_target_pairs={{0,4},{2,6},{4,0},{6,2},{1,5},{3,7},{5,1},{7,3},{8,12},{10,14},{12... | collective-permute-start | bytes 786440 | tf_op jit(solution)/shard_map/ppermute | solution.py:34
  113.3 1.1 collective-permute-done.6
  114.4 10.5 %collective-permute-done.8 = bf16[4,128,256]{2,1,0:T(8,128)(2,1)S(1)} collective-permute-done((bf16[4,128,256]{2,1,0:T(8,128)(2,1)S(1)}, bf16[4,128,256]{2,1,0:T(8,128)(2,1)S(1)}, u32[]{:S(2)}, u32[]{:S(2)}) %collective-permute-start.8) | collective-permute-done | bytes 262176 | tf_op jit(solution)/shard_map/ppermute | solution.py:34
  124.9 0.0 collective-permute-done.7
  124.9 0.1 fusion.2
  125.1 3.4 %collective-permute-start.9 = (bf16[128,256]{1,0:T(8,128)(2,1)S(1)}, bf16[128,256]{1,0:T(8,128)(2,1)S(1)}, u32[]{:S(2)}, u32[]{:S(2)}) collective-permute-start(bf16[128,256]{1,0:T(8,128)(2,1)S(1)} %get-tuple-element.19), channel_id=1, source_target_pairs={{0,16},{8,24},{16,0},{24,8},{1,17},{9,25},{17,1},{25,9},{2,18},{10... | collective-permute-start | bytes 196616 | tf_op jit(solution)/shard_map/ppermute | solution.py:30
  128.5 2.4 %collective-permute-start.11 = (bf16[128,256]{1,0:T(8,128)(2,1)S(1)}, bf16[128,256]{1,0:T(8,128)(2,1)S(1)}, u32[]{:S(2)}, u32[]{:S(2)}) collective-permute-start(bf16[128,256]{1,0:T(8,128)(2,1)S(1)} %get-tuple-element.20), channel_id=1, source_target_pairs={{0,24},{8,16},{16,8},{24,0},{1,25},{9,17},{17,9},{25,1},{2,26},{10... | collective-permute-start | bytes 196616 | tf_op jit(solution)/shard_map/ppermute | solution.py:30
  130.9 3.4 %collective-permute-start.10 = (bf16[128,256]{1,0:T(8,128)(2,1)S(1)}, bf16[128,256]{1,0:T(8,128)(2,1)S(1)}, u32[]{:S(2)}, u32[]{:S(2)}) collective-permute-start(bf16[128,256]{1,0:T(8,128)(2,1)S(1)} %get-tuple-element.21), channel_id=1, source_target_pairs={{0,8},{8,0},{16,24},{24,16},{1,9},{9,1},{17,25},{25,17},{2,10},{10... | collective-permute-start | bytes 196616 | tf_op jit(solution)/shard_map/ppermute | solution.py:30
  134.3 0.0 collective-permute-done.9
  134.3 1.2 collective-permute-done.11
  135.6 1.5 %collective-permute-done.10 = bf16[128,256]{1,0:T(8,128)(2,1)S(1)} collective-permute-done((bf16[128,256]{1,0:T(8,128)(2,1)S(1)}, bf16[128,256]{1,0:T(8,128)(2,1)S(1)}, u32[]{:S(2)}, u32[]{:S(2)}) %collective-permute-start.10) | collective-permute-done | bytes 65568 | tf_op jit(solution)/shard_map/ppermute | solution.py:30
  137.1 0.7 fusion.5
  137.7 0.0 all-to-all-done.2
  137.7 0.1 reduce_sum.12
  137.9 0.6 pad_maximum_fusion.3
  (8 shorter events, 0.1 us)
Async XLA Ops:
  0.6 17.9 %copy-start.3 = (bf16[128,256]{1,0:T(8,128)(2,1)S(1)}, bf16[128,256]{1,0:T(8,128)(2,1)}, u32[]{:S(2)}) copy-start(bf16[128,256]{1,0:T(8,128)(2,1)} %param.3) | copy-start | bytes 196612
  2.6 60.6 %all-to-all-start = ((bf16[32,64,256]{2,1,0:T(8,128)(2,1)}), bf16[32,64,256]{2,1,0:T(8,128)(2,1)S(1)}, u32[]{:S(2)}, u32[]{:S(2)}) async-start(bf16[32,64,256]{2,1,0:T(8,128)(2,1)} %bitcast.5), calls=%async_computation | async-start | bytes 2097152 | tf_op jit(solution)/shard_map/all_to_all | solution.py:25
  18.6 26.1 %collective-permute-start = (bf16[128,256]{1,0:T(8,128)(2,1)S(1)}, bf16[128,256]{1,0:T(8,128)(2,1)S(1)}, u32[]{:S(2)}, u32[]{:S(2)}) collective-permute-start(bf16[128,256]{1,0:T(8,128)(2,1)S(1)} %copy-done.3), channel_id=1, source_target_pairs={{0,16},{8,24},{16,0},{24,8},{1,17},{9,25},{17,1},{25,9},{2,18},{10... | collective-permute-start | bytes 196616 | tf_op jit(solution)/shard_map/ppermute | solution.py:30
  22.3 25.2 %collective-permute-start.2 = (bf16[128,256]{1,0:T(8,128)(2,1)S(1)}, bf16[128,256]{1,0:T(8,128)(2,1)S(1)}, u32[]{:S(2)}, u32[]{:S(2)}) collective-permute-start(bf16[128,256]{1,0:T(8,128)(2,1)S(1)} %copy-done.3), channel_id=1, source_target_pairs={{0,24},{8,16},{16,8},{24,0},{1,25},{9,17},{17,9},{25,1},{2,26},{10... | collective-permute-start | bytes 196616 | tf_op jit(solution)/shard_map/ppermute | solution.py:30
  25.3 22.2 %collective-permute-start.1 = (bf16[128,256]{1,0:T(8,128)(2,1)S(1)}, bf16[128,256]{1,0:T(8,128)(2,1)S(1)}, u32[]{:S(2)}, u32[]{:S(2)}) collective-permute-start(bf16[128,256]{1,0:T(8,128)(2,1)S(1)} %copy-done.3), channel_id=1, source_target_pairs={{0,8},{8,0},{16,24},{24,16},{1,9},{9,1},{17,25},{25,17},{2,10},{10... | collective-permute-start | bytes 196616 | tf_op jit(solution)/shard_map/ppermute | solution.py:30
  47.5 12.4 %collective-permute-start.4 = (bf16[4,128,256]{2,1,0:T(8,128)(2,1)S(1)}, bf16[4,128,256]{2,1,0:T(8,128)(2,1)S(1)}, u32[]{:S(2)}, u32[]{:S(2)}) collective-permute-start(bf16[4,128,256]{2,1,0:T(8,128)(2,1)S(1)} %get-tuple-element.23), channel_id=1, source_target_pairs={{0,4},{2,6},{4,0},{6,2},{1,5},{3,7},{5,1},{7,3},{8,12},{10,14},{12... | collective-permute-start | bytes 786440 | tf_op jit(solution)/shard_map/ppermute | solution.py:34
  50.9 12.2 %collective-permute-start.3 = (bf16[4,128,256]{2,1,0:T(8,128)(2,1)S(1)}, bf16[4,128,256]{2,1,0:T(8,128)(2,1)S(1)}, u32[]{:S(2)}, u32[]{:S(2)}) collective-permute-start(bf16[4,128,256]{2,1,0:T(8,128)(2,1)S(1)} %get-tuple-element.23), channel_id=1, source_target_pairs={{0,6},{2,0},{4,2},{6,4},{1,7},{3,1},{5,3},{7,5},{8,14},{10,8},{12,... | collective-permute-start | bytes 786440 | tf_op jit(solution)/shard_map/ppermute | solution.py:34
  52.8 10.2 %collective-permute-start.5 = (bf16[4,128,256]{2,1,0:T(8,128)(2,1)S(1)}, bf16[4,128,256]{2,1,0:T(8,128)(2,1)S(1)}, u32[]{:S(2)}, u32[]{:S(2)}) collective-permute-start(bf16[4,128,256]{2,1,0:T(8,128)(2,1)S(1)} %get-tuple-element.23), channel_id=1, source_target_pairs={{0,2},{2,4},{4,6},{6,0},{1,3},{3,5},{5,7},{7,1},{8,10},{10,12},{12... | collective-permute-start | bytes 786440 | tf_op jit(solution)/shard_map/ppermute | solution.py:34
  63.2 5.7 %copy-start.1 = (bf16[32,64,256]{2,1,0:T(8,128)(2,1)}, bf16[32,64,256]{2,1,0:T(8,128)(2,1)S(1)}, u32[]{:S(2)}) copy-start(bf16[32,64,256]{2,1,0:T(8,128)(2,1)S(1)} %all-to-all-done) | copy-start | bytes 3145732
  68.9 1.2 copy-start.2
  79.1 1.3 copy-start
  80.4 10.2 %all-to-all-start.3 = ((bf16[2,4,4,128,256]{4,3,2,1,0:T(8,128)(2,1)}), bf16[2,4,4,128,256]{4,3,2,1,0:T(8,128)(2,1)}, u32[]{:S(2)}, u32[]{:S(2)}) async-start(bf16[2,4,4,128,256]{4,3,2,1,0:T(8,128)(2,1)} %bitcast.48), calls=%async_computation.3 | async-start | bytes 4194304 | tf_op jit(solution)/shard_map/all_to_all | solution.py:25
  90.6 47.1 %all-to-all-start.2 = ((bf16[32,64,256]{2,1,0:T(8,128)(2,1)}), bf16[32,64,256]{2,1,0:T(8,128)(2,1)S(1)}, u32[]{:S(2)}, u32[]{:S(2)}) async-start(bf16[32,64,256]{2,1,0:T(8,128)(2,1)} %bitcast.16), calls=%async_computation.2 | async-start | bytes 2097152 | tf_op jit(solution)/shard_map/all_to_all | solution.py:25
  104.1 10.3 %collective-permute-start.6 = (bf16[4,128,256]{2,1,0:T(8,128)(2,1)S(1)}, bf16[4,128,256]{2,1,0:T(8,128)(2,1)S(1)}, u32[]{:S(2)}, u32[]{:S(2)}) collective-permute-start(bf16[4,128,256]{2,1,0:T(8,128)(2,1)S(1)} %get-tuple-element.16), channel_id=1, source_target_pairs={{0,2},{2,4},{4,6},{6,0},{1,3},{3,5},{5,7},{7,1},{8,10},{10,12},{12... | collective-permute-start | bytes 786440 | tf_op jit(solution)/shard_map/ppermute | solution.py:34
  108.0 16.9 %collective-permute-start.8 = (bf16[4,128,256]{2,1,0:T(8,128)(2,1)S(1)}, bf16[4,128,256]{2,1,0:T(8,128)(2,1)S(1)}, u32[]{:S(2)}, u32[]{:S(2)}) collective-permute-start(bf16[4,128,256]{2,1,0:T(8,128)(2,1)S(1)} %get-tuple-element.17), channel_id=1, source_target_pairs={{0,6},{2,0},{4,2},{6,4},{1,7},{3,1},{5,3},{7,5},{8,14},{10,8},{12,... | collective-permute-start | bytes 786440 | tf_op jit(solution)/shard_map/ppermute | solution.py:34
  110.0 14.9 %collective-permute-start.7 = (bf16[4,128,256]{2,1,0:T(8,128)(2,1)S(1)}, bf16[4,128,256]{2,1,0:T(8,128)(2,1)S(1)}, u32[]{:S(2)}, u32[]{:S(2)}) collective-permute-start(bf16[4,128,256]{2,1,0:T(8,128)(2,1)S(1)} %get-tuple-element.18), channel_id=1, source_target_pairs={{0,4},{2,6},{4,0},{6,2},{1,5},{3,7},{5,1},{7,3},{8,12},{10,14},{12... | collective-permute-start | bytes 786440 | tf_op jit(solution)/shard_map/ppermute | solution.py:34
  125.1 9.2 %collective-permute-start.9 = (bf16[128,256]{1,0:T(8,128)(2,1)S(1)}, bf16[128,256]{1,0:T(8,128)(2,1)S(1)}, u32[]{:S(2)}, u32[]{:S(2)}) collective-permute-start(bf16[128,256]{1,0:T(8,128)(2,1)S(1)} %get-tuple-element.19), channel_id=1, source_target_pairs={{0,16},{8,24},{16,0},{24,8},{1,17},{9,25},{17,1},{25,9},{2,18},{10... | collective-permute-start | bytes 196616 | tf_op jit(solution)/shard_map/ppermute | solution.py:30
  128.5 7.1 %collective-permute-start.11 = (bf16[128,256]{1,0:T(8,128)(2,1)S(1)}, bf16[128,256]{1,0:T(8,128)(2,1)S(1)}, u32[]{:S(2)}, u32[]{:S(2)}) collective-permute-start(bf16[128,256]{1,0:T(8,128)(2,1)S(1)} %get-tuple-element.20), channel_id=1, source_target_pairs={{0,24},{8,16},{16,8},{24,0},{1,25},{9,17},{17,9},{25,1},{2,26},{10... | collective-permute-start | bytes 196616 | tf_op jit(solution)/shard_map/ppermute | solution.py:30
  130.9 6.2 %collective-permute-start.10 = (bf16[128,256]{1,0:T(8,128)(2,1)S(1)}, bf16[128,256]{1,0:T(8,128)(2,1)S(1)}, u32[]{:S(2)}, u32[]{:S(2)}) collective-permute-start(bf16[128,256]{1,0:T(8,128)(2,1)S(1)} %get-tuple-element.21), channel_id=1, source_target_pairs={{0,8},{8,0},{16,24},{24,16},{1,9},{9,1},{17,25},{25,17},{2,10},{10... | collective-permute-start | bytes 196616 | tf_op jit(solution)/shard_map/ppermute | solution.py:30

commit v5 on v4

--- a/solution.py
+++ b/solution.py
@@ -186,14 +186,14 @@
     total_count = rows_a * n_dp
     shape = jax.ShapeDtypeStruct
 
-    halves = jnp.stack([first_view_outputs[:, :half], first_view_outputs[:, half:]])
-    first = exchange(
-        jnp.broadcast_to(halves, (n_dp // 2, 2, rows_a, half)).reshape(n_dp, rows_a, half),
-        SAMPLES,
-    ).reshape(total_count, half)
-
     near = [second_view_outputs] + [near_swap(second_view_outputs, k) for k in (1, 2, 3)]
     near = jnp.stack(near)
+    halves = jnp.stack([first_view_outputs[:, :half], first_view_outputs[:, half:]])
+    spread = jnp.broadcast_to(halves, (n_dp // 2, 2, rows_a, half)).reshape(n_dp, rows_a, half)
+    near, spread = lax.optimization_barrier((near, spread))
+
+    first = exchange(spread, SAMPLES).reshape(total_count, half)
+
     ahead = jnp.stack([near] + [shift(near, -k) for k in (1, 2, 3)])
     ahead = jnp.broadcast_to(ahead, (2,) + ahead.shape)
     first, ahead = lax.optimization_barrier((first, ahead))

time: 139 us -> 130 us (0.935)
  starting transfers between devices: 70.4 us -> 63.9 us
  waiting for transfers between devices: 39 us -> 35.4 us
    ppermute x6, waiting for transfers between devices: 22.4 us -> 6.28 us  [near_swap(): return lax.ppermute(values, ('yl', 'zl'), [(i, i ^ flip) for i in range(4)])]
    all_to_all x3, waiting for transfers between devices: 0.01 us -> 9.97 us  [exchange(): return lax.all_to_all(values, axes, 0, 0, tiled=True)]
    all_to_all x3, starting transfers between devices: 32.4 us -> 27.2 us  [exchange(): return lax.all_to_all(values, axes, 0, 0, tiled=True)]
    ppermute x6, waiting for transfers between devices: 16.6 us -> 19.1 us  [shift(): lax.ppermute(values, 'x', [(i, (i + distance) % 4) for i in range(4)])]
    ppermute x6, starting transfers between devices: 19.6 us -> 17.8 us  [shift(): lax.ppermute(values, 'x', [(i, (i + distance) % 4) for i in range(4)])]
  transfers between devices with their start and end apart: 15 -> 15, of which waited for: 8 -> 10; matrix products, arithmetic and copies ran while one was open for 2% -> 3% of each run, Pallas kernels for 4% -> 4%
where the time goes in v5:
time: 130 us; the launch traced here: 129 us
  starting transfers between devices  63.9 us (49%)
  waiting for transfers between devices  35.4 us (27%)
  Pallas kernels  14.3 us (11%)
  blocking collectives  5.42 us (4%)
  local copies, waits for them, and re-layouts  4.72 us (4%)
  other arithmetic  4.53 us (3%)
    all_to_all x3, starting transfers between devices, exchange(): return lax.all_to_all(values, axes, 0, 0, tiled=True)  27.2 us
    ppermute x6, waiting for transfers between devices, shift(): lax.ppermute(values, 'x', [(i, (i + distance) % 4) for i in range(4)])  19.1 us
    ppermute x6, starting transfers between devices, near_swap(): return lax.ppermute(values, ('yl', 'zl'), [(i, i ^ flip) for i in range(4)])  18.9 us
    ppermute x6, starting transfers between devices, shift(): lax.ppermute(values, 'x', [(i, (i + distance) % 4) for i in range(4)])  17.8 us
    pallas_call x2, Pallas kernels, call(): pl.pallas_call(kernel, out_shape=outputs, in_specs=[pl.BlockSpec(memory_s...  14.3 us
    all_to_all x3, waiting for transfers between devices, exchange(): return lax.all_to_all(values, axes, 0, 0, tiled=True)  9.97 us
    ppermute x6, waiting for transfers between devices, near_swap(): return lax.ppermute(values, ('yl', 'zl'), [(i, i ^ flip) for i in range(4)])  6.28 us
    all_to_all x1, blocking collectives, exchange(): return lax.all_to_all(values, axes, 0, 0, tiled=True)  5.42 us
  transfers between devices with their start and end apart: 15, of which 10 were waited for; matrix products, arithmetic and copies ran while one was open for 3% of the time, Pallas kernels for 4%

profile of v5, /device:TPU:6, one launch (start us, length us, event | category | flops | bytes accessed | tf_op | source)
XLA Modules:
  0.0 129.1 jit_solution(13063870192474106511)
XLA Ops:
  0.6 3.5 %collective-permute-start = (bf16[128,256]{1,0:T(8,128)(2,1)}, bf16[128,256]{1,0:T(8,128)(2,1)S(1)}, u32[]{:S(2)}, u32[]{:S(2)}) collective-permute-start(bf16[128,256]{1,0:T(8,128)(2,1)} %param.3), channel_id=1, source_target_pairs={{0,16},{8,24},{16,0},{24,8},{1,17},{9,25},{17,1},{25,9},{2,18},{10... | collective-permute-start | bytes 196616 | tf_op jit(solution)/shard_map/ppermute | solution.py:30
  4.1 4.2 %collective-permute-start.2 = (bf16[128,256]{1,0:T(8,128)(2,1)}, bf16[128,256]{1,0:T(8,128)(2,1)S(1)}, u32[]{:S(2)}, u32[]{:S(2)}) collective-permute-start(bf16[128,256]{1,0:T(8,128)(2,1)} %param.3), channel_id=1, source_target_pairs={{0,24},{8,16},{16,8},{24,0},{1,25},{9,17},{17,9},{25,1},{2,26},{10... | collective-permute-start | bytes 196616 | tf_op jit(solution)/shard_map/ppermute | solution.py:30
  8.3 2.0 %collective-permute-start.1 = (bf16[128,256]{1,0:T(8,128)(2,1)}, bf16[128,256]{1,0:T(8,128)(2,1)S(1)}, u32[]{:S(2)}, u32[]{:S(2)}) collective-permute-start(bf16[128,256]{1,0:T(8,128)(2,1)} %param.3), channel_id=1, source_target_pairs={{0,8},{8,0},{16,24},{24,16},{1,9},{9,1},{17,25},{25,17},{2,10},{10... | collective-permute-start | bytes 196616 | tf_op jit(solution)/shard_map/ppermute | solution.py:30
  10.3 0.8 slice_bitcast_fusion.11
  11.1 0.0 collective-permute-done
  11.1 0.2 collective-permute-done.2
  11.4 3.3 %collective-permute-done.1 = bf16[128,256]{1,0:T(8,128)(2,1)S(1)} collective-permute-done((bf16[128,256]{1,0:T(8,128)(2,1)}, bf16[128,256]{1,0:T(8,128)(2,1)S(1)}, u32[]{:S(2)}, u32[]{:S(2)}) %collective-permute-start.1) | collective-permute-done | bytes 65568 | tf_op jit(solution)/shard_map/ppermute | solution.py:30
  14.7 0.9 pad_maximum_fusion.1
  15.5 1.1 broadcast_in_dim.6
  16.7 15.1 %all-to-all-start = ((bf16[32,64,256]{2,1,0:T(8,128)(2,1)}), bf16[32,64,256]{2,1,0:T(8,128)(2,1)S(1)}, u32[]{:S(2)}, u32[]{:S(2)}) async-start(bf16[32,64,256]{2,1,0:T(8,128)(2,1)} %bitcast.9), calls=%async_computation | async-start | bytes 2097152 | tf_op jit(solution)/shard_map/all_to_all | solution.py:25
  31.7 2.4 %collective-permute-start.5 = (bf16[4,128,256]{2,1,0:T(8,128)(2,1)S(1)}, bf16[4,128,256]{2,1,0:T(8,128)(2,1)S(1)}, u32[]{:S(2)}, u32[]{:S(2)}) collective-permute-start(bf16[4,128,256]{2,1,0:T(8,128)(2,1)S(1)} %pad_maximum_fusion.1), channel_id=1, source_target_pairs={{0,2},{2,4},{4,6},{6,0},{1,3},{3,5},{5,7},{7,1},{8,10},{10,12},{12... | collective-permute-start | bytes 786440 | tf_op jit(solution)/shard_map/ppermute | solution.py:34
  34.1 4.3 %collective-permute-start.4 = (bf16[4,128,256]{2,1,0:T(8,128)(2,1)S(1)}, bf16[4,128,256]{2,1,0:T(8,128)(2,1)S(1)}, u32[]{:S(2)}, u32[]{:S(2)}) collective-permute-start(bf16[4,128,256]{2,1,0:T(8,128)(2,1)S(1)} %pad_maximum_fusion.1), channel_id=1, source_target_pairs={{0,4},{2,6},{4,0},{6,2},{1,5},{3,7},{5,1},{7,3},{8,12},{10,14},{12... | collective-permute-start | bytes 786440 | tf_op jit(solution)/shard_map/ppermute | solution.py:34
  38.5 1.9 %collective-permute-start.3 = (bf16[4,128,256]{2,1,0:T(8,128)(2,1)S(1)}, bf16[4,128,256]{2,1,0:T(8,128)(2,1)S(1)}, u32[]{:S(2)}, u32[]{:S(2)}) collective-permute-start(bf16[4,128,256]{2,1,0:T(8,128)(2,1)S(1)} %pad_maximum_fusion.1), channel_id=1, source_target_pairs={{0,6},{2,0},{4,2},{6,4},{1,7},{3,1},{5,3},{7,5},{8,14},{10,8},{12,... | collective-permute-start | bytes 786440 | tf_op jit(solution)/shard_map/ppermute | solution.py:34
  40.4 0.1 pad_add_fusion.place_ref
  40.5 2.0 %collective-permute-done.5 = bf16[4,128,256]{2,1,0:T(8,128)(2,1)S(1)} collective-permute-done((bf16[4,128,256]{2,1,0:T(8,128)(2,1)S(1)}, bf16[4,128,256]{2,1,0:T(8,128)(2,1)S(1)}, u32[]{:S(2)}, u32[]{:S(2)}) %collective-permute-start.5) | collective-permute-done | bytes 262176 | tf_op jit(solution)/shard_map/ppermute | solution.py:34
  42.5 3.9 %collective-permute-done.4 = bf16[4,128,256]{2,1,0:T(8,128)(2,1)S(1)} collective-permute-done((bf16[4,128,256]{2,1,0:T(8,128)(2,1)S(1)}, bf16[4,128,256]{2,1,0:T(8,128)(2,1)S(1)}, u32[]{:S(2)}, u32[]{:S(2)}) %collective-permute-start.4) | collective-permute-done | bytes 262176 | tf_op jit(solution)/shard_map/ppermute | solution.py:34
  46.4 3.1 %collective-permute-done.3 = bf16[4,128,256]{2,1,0:T(8,128)(2,1)S(1)} collective-permute-done((bf16[4,128,256]{2,1,0:T(8,128)(2,1)S(1)}, bf16[4,128,256]{2,1,0:T(8,128)(2,1)S(1)}, u32[]{:S(2)}, u32[]{:S(2)}) %collective-permute-start.3) | collective-permute-done | bytes 262176 | tf_op jit(solution)/shard_map/ppermute | solution.py:34
  49.5 0.1 pad_maximum_fusion
  49.6 10.0 %all-to-all-done = bf16[32,64,256]{2,1,0:T(8,128)(2,1)S(1)} async-done(((bf16[32,64,256]{2,1,0:T(8,128)(2,1)}), bf16[32,64,256]{2,1,0:T(8,128)(2,1)S(1)}, u32[]{:S(2)}, u32[]{:S(2)}) %all-to-all-start) | async-done | bytes 1048608 | tf_op jit(solution)/shard_map/all_to_all | solution.py:25
  59.6 0.2 broadcast_in_dim.7
  59.9 5.4 %all_to_all.20 = bf16[2,4,4,128,256]{4,3,2,1,0:T(8,128)(2,1)S(1)} all-to-all(bf16[2,4,4,128,256]{4,3,2,1,0:T(8,128)(2,1)S(1)} %broadcast_in_dim.7), channel_id=1, replica_groups=mesh['zh'=4,'yk'=4,'yl'=2,'zl'=2,'x'=4,'core'=2] {'core'}, dimensions={0} | all-to-all | bytes 4194304 | tf_op jit(solution)/shard_map/all_to_all | solution.py:25
  65.3 1.2 copy-done.2
  66.5 9.0 %shard_map.41 = (bf16[16,2,128,256]{3,2,1,0:T(8,128)(2,1)S(1)}, bf16[2048,256]{1,0:T(8,128)(2,1)S(1)}, bf16[2048,512]{1,0:T(8,128)(2,1)S(1)}, bf16[256,512]{1,0:T(8,128)(2,1)S(1)}, f32[8,256]{1,0:T(8,128)S(1)}) custom-call(s32[3]{0:T(128)S(1)} %pad_add_fusion.place_ref, bf16[2048,256]{1,0:T(8,128)(2,1)S(1)} %bitcast.49, bf16[16,2,128,256]{3,2,1,0:T(8,128)(2,1)S(1)} %bitcast.48), custom_call_target="tpu_custom_call" | custom-call | flops 1073741824 | bytes 8388608 | tf_op jit(solution)/shard_map/pallas_call | solution.py:171
  75.5 0.0 copy-start
  75.6 1.3 copy-done
  76.8 4.8 %all-to-all-start.3 = ((bf16[2,4,4,128,256]{4,3,2,1,0:T(8,128)(2,1)}), bf16[2,4,4,128,256]{4,3,2,1,0:T(8,128)(2,1)}, u32[]{:S(2)}, u32[]{:S(2)}) async-start(bf16[2,4,4,128,256]{4,3,2,1,0:T(8,128)(2,1)} %bitcast.47), calls=%async_computation.3 | async-start | bytes 4194304 | tf_op jit(solution)/shard_map/all_to_all | solution.py:25
  81.7 5.3 %shard_map.42 = bf16[2048,256]{1,0:T(8,128)(2,1)} custom-call(s32[3]{0:T(128)S(1)} %pad_add_fusion.place_ref, bf16[2048,256]{1,0:T(8,128)(2,1)S(1)} %get-tuple-element.15.na_ref, bf16[2048,512]{1,0:T(8,128)(2,1)S(1)} %get-tuple-element.16.nb_ref, bf16[256,512]{1,0:T(8,128)(2,1)S(1)} %get-tuple-element.17.grad_ref, f32[8,256]{1,0:T(8,128)S(1)} %get-tuple-element.18.vectors_ref), custom_call_target="tpu_custom_call" | custom-call | flops 536870912 | bytes 4194304 | tf_op jit(solution)/shard_map/pallas_call | solution.py:171
  87.0 0.0 all-to-all-done.3
  87.0 7.3 %all-to-all-start.2 = ((bf16[32,64,256]{2,1,0:T(8,128)(2,1)}), bf16[32,64,256]{2,1,0:T(8,128)(2,1)S(1)}, u32[]{:S(2)}, u32[]{:S(2)}) async-start(bf16[32,64,256]{2,1,0:T(8,128)(2,1)} %bitcast.16), calls=%async_computation.2 | async-start | bytes 2097152 | tf_op jit(solution)/shard_map/all_to_all | solution.py:25
  94.2 1.9 %add_convert_fusion = bf16[1,4,4,128,256]{4,3,2,1,0:T(8,128)(2,1)S(1)} fusion(bf16[2,4,4,128,256]{4,3,2,1,0:T(8,128)(2,1)} %all-to-all-done.3), kind=kLoop, calls=%fused_computation | loop fusion | flops 2097152 | bytes 3145728 | tf_op jit(solution)/shard_map/convert_element_type | solution.py:38
  96.1 0.1 slice_bitcast_fusion.2
  96.2 2.4 %collective-permute-start.6 = (bf16[4,128,256]{2,1,0:T(8,128)(2,1)S(1)}, bf16[4,128,256]{2,1,0:T(8,128)(2,1)S(1)}, u32[]{:S(2)}, u32[]{:S(2)}) collective-permute-start(bf16[4,128,256]{2,1,0:T(8,128)(2,1)S(1)} %get-tuple-element.20), channel_id=1, source_target_pairs={{0,2},{2,4},{4,6},{6,0},{1,3},{3,5},{5,7},{7,1},{8,10},{10,12},{12... | collective-permute-start | bytes 786440 | tf_op jit(solution)/shard_map/ppermute | solution.py:34
  98.6 3.5 %collective-permute-start.8 = (bf16[4,128,256]{2,1,0:T(8,128)(2,1)S(1)}, bf16[4,128,256]{2,1,0:T(8,128)(2,1)S(1)}, u32[]{:S(2)}, u32[]{:S(2)}) collective-permute-start(bf16[4,128,256]{2,1,0:T(8,128)(2,1)S(1)} %get-tuple-element.21), channel_id=1, source_target_pairs={{0,6},{2,0},{4,2},{6,4},{1,7},{3,1},{5,3},{7,5},{8,14},{10,8},{12,... | collective-permute-start | bytes 786440 | tf_op jit(solution)/shard_map/ppermute | solution.py:34
  102.0 3.3 %collective-permute-start.7 = (bf16[4,128,256]{2,1,0:T(8,128)(2,1)S(1)}, bf16[4,128,256]{2,1,0:T(8,128)(2,1)S(1)}, u32[]{:S(2)}, u32[]{:S(2)}) collective-permute-start(bf16[4,128,256]{2,1,0:T(8,128)(2,1)S(1)} %get-tuple-element.22), channel_id=1, source_target_pairs={{0,4},{2,6},{4,0},{6,2},{1,5},{3,7},{5,1},{7,3},{8,12},{10,14},{12... | collective-permute-start | bytes 786440 | tf_op jit(solution)/shard_map/ppermute | solution.py:34
  105.3 1.1 collective-permute-done.6
  106.5 8.9 %collective-permute-done.8 = bf16[4,128,256]{2,1,0:T(8,128)(2,1)S(1)} collective-permute-done((bf16[4,128,256]{2,1,0:T(8,128)(2,1)S(1)}, bf16[4,128,256]{2,1,0:T(8,128)(2,1)S(1)}, u32[]{:S(2)}, u32[]{:S(2)}) %collective-permute-start.8) | collective-permute-done | bytes 262176 | tf_op jit(solution)/shard_map/ppermute | solution.py:34
  115.4 0.0 collective-permute-done.7
  115.4 0.1 fusion.2
  115.6 3.4 %collective-permute-start.9 = (bf16[128,256]{1,0:T(8,128)(2,1)S(1)}, bf16[128,256]{1,0:T(8,128)(2,1)S(1)}, u32[]{:S(2)}, u32[]{:S(2)}) collective-permute-start(bf16[128,256]{1,0:T(8,128)(2,1)S(1)} %get-tuple-element.23), channel_id=1, source_target_pairs={{0,16},{8,24},{16,0},{24,8},{1,17},{9,25},{17,1},{25,9},{2,18},{10... | collective-permute-start | bytes 196616 | tf_op jit(solution)/shard_map/ppermute | solution.py:30
  119.0 2.4 %collective-permute-start.11 = (bf16[128,256]{1,0:T(8,128)(2,1)S(1)}, bf16[128,256]{1,0:T(8,128)(2,1)S(1)}, u32[]{:S(2)}, u32[]{:S(2)}) collective-permute-start(bf16[128,256]{1,0:T(8,128)(2,1)S(1)} %get-tuple-element.24), channel_id=1, source_target_pairs={{0,24},{8,16},{16,8},{24,0},{1,25},{9,17},{17,9},{25,1},{2,26},{10... | collective-permute-start | bytes 196616 | tf_op jit(solution)/shard_map/ppermute | solution.py:30
  121.4 3.4 %collective-permute-start.10 = (bf16[128,256]{1,0:T(8,128)(2,1)S(1)}, bf16[128,256]{1,0:T(8,128)(2,1)S(1)}, u32[]{:S(2)}, u32[]{:S(2)}) collective-permute-start(bf16[128,256]{1,0:T(8,128)(2,1)S(1)} %get-tuple-element.25), channel_id=1, source_target_pairs={{0,8},{8,0},{16,24},{24,16},{1,9},{9,1},{17,25},{25,17},{2,10},{10... | collective-permute-start | bytes 196616 | tf_op jit(solution)/shard_map/ppermute | solution.py:30
  124.8 0.0 collective-permute-done.9
  124.8 1.2 collective-permute-done.11
  126.1 1.5 %collective-permute-done.10 = bf16[128,256]{1,0:T(8,128)(2,1)S(1)} collective-permute-done((bf16[128,256]{1,0:T(8,128)(2,1)S(1)}, bf16[128,256]{1,0:T(8,128)(2,1)S(1)}, u32[]{:S(2)}, u32[]{:S(2)}) %collective-permute-start.10) | collective-permute-done | bytes 65568 | tf_op jit(solution)/shard_map/ppermute | solution.py:30
  127.6 0.7 fusion.5
  128.3 0.0 all-to-all-done.2
  128.3 0.1 reduce_sum.12
  128.4 0.6 pad_maximum_fusion.3
  (6 shorter events, 0.0 us)
Async XLA Ops:
  0.6 10.5 %collective-permute-start = (bf16[128,256]{1,0:T(8,128)(2,1)}, bf16[128,256]{1,0:T(8,128)(2,1)S(1)}, u32[]{:S(2)}, u32[]{:S(2)}) collective-permute-start(bf16[128,256]{1,0:T(8,128)(2,1)} %param.3), channel_id=1, source_target_pairs={{0,16},{8,24},{16,0},{24,8},{1,17},{9,25},{17,1},{25,9},{2,18},{10... | collective-permute-start | bytes 196616 | tf_op jit(solution)/shard_map/ppermute | solution.py:30
  4.1 7.3 %collective-permute-start.2 = (bf16[128,256]{1,0:T(8,128)(2,1)}, bf16[128,256]{1,0:T(8,128)(2,1)S(1)}, u32[]{:S(2)}, u32[]{:S(2)}) collective-permute-start(bf16[128,256]{1,0:T(8,128)(2,1)} %param.3), channel_id=1, source_target_pairs={{0,24},{8,16},{16,8},{24,0},{1,25},{9,17},{17,9},{25,1},{2,26},{10... | collective-permute-start | bytes 196616 | tf_op jit(solution)/shard_map/ppermute | solution.py:30
  8.3 6.4 %collective-permute-start.1 = (bf16[128,256]{1,0:T(8,128)(2,1)}, bf16[128,256]{1,0:T(8,128)(2,1)S(1)}, u32[]{:S(2)}, u32[]{:S(2)}) collective-permute-start(bf16[128,256]{1,0:T(8,128)(2,1)} %param.3), channel_id=1, source_target_pairs={{0,8},{8,0},{16,24},{24,16},{1,9},{9,1},{17,25},{25,17},{2,10},{10... | collective-permute-start | bytes 196616 | tf_op jit(solution)/shard_map/ppermute | solution.py:30
  16.7 43.0 %all-to-all-start = ((bf16[32,64,256]{2,1,0:T(8,128)(2,1)}), bf16[32,64,256]{2,1,0:T(8,128)(2,1)S(1)}, u32[]{:S(2)}, u32[]{:S(2)}) async-start(bf16[32,64,256]{2,1,0:T(8,128)(2,1)} %bitcast.9), calls=%async_computation | async-start | bytes 2097152 | tf_op jit(solution)/shard_map/all_to_all | solution.py:25
  31.7 10.8 %collective-permute-start.5 = (bf16[4,128,256]{2,1,0:T(8,128)(2,1)S(1)}, bf16[4,128,256]{2,1,0:T(8,128)(2,1)S(1)}, u32[]{:S(2)}, u32[]{:S(2)}) collective-permute-start(bf16[4,128,256]{2,1,0:T(8,128)(2,1)S(1)} %pad_maximum_fusion.1), channel_id=1, source_target_pairs={{0,2},{2,4},{4,6},{6,0},{1,3},{3,5},{5,7},{7,1},{8,10},{10,12},{12... | collective-permute-start | bytes 786440 | tf_op jit(solution)/shard_map/ppermute | solution.py:34
  34.1 12.3 %collective-permute-start.4 = (bf16[4,128,256]{2,1,0:T(8,128)(2,1)S(1)}, bf16[4,128,256]{2,1,0:T(8,128)(2,1)S(1)}, u32[]{:S(2)}, u32[]{:S(2)}) collective-permute-start(bf16[4,128,256]{2,1,0:T(8,128)(2,1)S(1)} %pad_maximum_fusion.1), channel_id=1, source_target_pairs={{0,4},{2,6},{4,0},{6,2},{1,5},{3,7},{5,1},{7,3},{8,12},{10,14},{12... | collective-permute-start | bytes 786440 | tf_op jit(solution)/shard_map/ppermute | solution.py:34
  38.5 11.1 %collective-permute-start.3 = (bf16[4,128,256]{2,1,0:T(8,128)(2,1)S(1)}, bf16[4,128,256]{2,1,0:T(8,128)(2,1)S(1)}, u32[]{:S(2)}, u32[]{:S(2)}) collective-permute-start(bf16[4,128,256]{2,1,0:T(8,128)(2,1)S(1)} %pad_maximum_fusion.1), channel_id=1, source_target_pairs={{0,6},{2,0},{4,2},{6,4},{1,7},{3,1},{5,3},{7,5},{8,14},{10,8},{12,... | collective-permute-start | bytes 786440 | tf_op jit(solution)/shard_map/ppermute | solution.py:34
  59.6 5.7 %copy-start.1 = (bf16[32,64,256]{2,1,0:T(8,128)(2,1)}, bf16[32,64,256]{2,1,0:T(8,128)(2,1)S(1)}, u32[]{:S(2)}) copy-start(bf16[32,64,256]{2,1,0:T(8,128)(2,1)S(1)} %all-to-all-done) | copy-start | bytes 3145732
  65.3 1.2 copy-start.2
  75.5 1.3 %copy-start = (bf16[16,2,128,256]{3,2,1,0:T(8,128)(2,1)}, bf16[16,2,128,256]{3,2,1,0:T(8,128)(2,1)S(1)}, u32[]{:S(2)}) copy-start(bf16[16,2,128,256]{3,2,1,0:T(8,128)(2,1)S(1)} %get-tuple-element.19) | copy-start | bytes 6291460
  76.8 10.1 %all-to-all-start.3 = ((bf16[2,4,4,128,256]{4,3,2,1,0:T(8,128)(2,1)}), bf16[2,4,4,128,256]{4,3,2,1,0:T(8,128)(2,1)}, u32[]{:S(2)}, u32[]{:S(2)}) async-start(bf16[2,4,4,128,256]{4,3,2,1,0:T(8,128)(2,1)} %bitcast.47), calls=%async_computation.3 | async-start | bytes 4194304 | tf_op jit(solution)/shard_map/all_to_all | solution.py:25
  87.0 41.3 %all-to-all-start.2 = ((bf16[32,64,256]{2,1,0:T(8,128)(2,1)}), bf16[32,64,256]{2,1,0:T(8,128)(2,1)S(1)}, u32[]{:S(2)}, u32[]{:S(2)}) async-start(bf16[32,64,256]{2,1,0:T(8,128)(2,1)} %bitcast.16), calls=%async_computation.2 | async-start | bytes 2097152 | tf_op jit(solution)/shard_map/all_to_all | solution.py:25
  96.2 10.3 %collective-permute-start.6 = (bf16[4,128,256]{2,1,0:T(8,128)(2,1)S(1)}, bf16[4,128,256]{2,1,0:T(8,128)(2,1)S(1)}, u32[]{:S(2)}, u32[]{:S(2)}) collective-permute-start(bf16[4,128,256]{2,1,0:T(8,128)(2,1)S(1)} %get-tuple-element.20), channel_id=1, source_target_pairs={{0,2},{2,4},{4,6},{6,0},{1,3},{3,5},{5,7},{7,1},{8,10},{10,12},{12... | collective-permute-start | bytes 786440 | tf_op jit(solution)/shard_map/ppermute | solution.py:34
  98.6 16.9 %collective-permute-start.8 = (bf16[4,128,256]{2,1,0:T(8,128)(2,1)S(1)}, bf16[4,128,256]{2,1,0:T(8,128)(2,1)S(1)}, u32[]{:S(2)}, u32[]{:S(2)}) collective-permute-start(bf16[4,128,256]{2,1,0:T(8,128)(2,1)S(1)} %get-tuple-element.21), channel_id=1, source_target_pairs={{0,6},{2,0},{4,2},{6,4},{1,7},{3,1},{5,3},{7,5},{8,14},{10,8},{12,... | collective-permute-start | bytes 786440 | tf_op jit(solution)/shard_map/ppermute | solution.py:34
  102.0 13.4 %collective-permute-start.7 = (bf16[4,128,256]{2,1,0:T(8,128)(2,1)S(1)}, bf16[4,128,256]{2,1,0:T(8,128)(2,1)S(1)}, u32[]{:S(2)}, u32[]{:S(2)}) collective-permute-start(bf16[4,128,256]{2,1,0:T(8,128)(2,1)S(1)} %get-tuple-element.22), channel_id=1, source_target_pairs={{0,4},{2,6},{4,0},{6,2},{1,5},{3,7},{5,1},{7,3},{8,12},{10,14},{12... | collective-permute-start | bytes 786440 | tf_op jit(solution)/shard_map/ppermute | solution.py:34
  115.6 9.2 %collective-permute-start.9 = (bf16[128,256]{1,0:T(8,128)(2,1)S(1)}, bf16[128,256]{1,0:T(8,128)(2,1)S(1)}, u32[]{:S(2)}, u32[]{:S(2)}) collective-permute-start(bf16[128,256]{1,0:T(8,128)(2,1)S(1)} %get-tuple-element.23), channel_id=1, source_target_pairs={{0,16},{8,24},{16,0},{24,8},{1,17},{9,25},{17,1},{25,9},{2,18},{10... | collective-permute-start | bytes 196616 | tf_op jit(solution)/shard_map/ppermute | solution.py:30
  119.0 7.1 %collective-permute-start.11 = (bf16[128,256]{1,0:T(8,128)(2,1)S(1)}, bf16[128,256]{1,0:T(8,128)(2,1)S(1)}, u32[]{:S(2)}, u32[]{:S(2)}) collective-permute-start(bf16[128,256]{1,0:T(8,128)(2,1)S(1)} %get-tuple-element.24), channel_id=1, source_target_pairs={{0,24},{8,16},{16,8},{24,0},{1,25},{9,17},{17,9},{25,1},{2,26},{10... | collective-permute-start | bytes 196616 | tf_op jit(solution)/shard_map/ppermute | solution.py:30
  121.4 6.2 %collective-permute-start.10 = (bf16[128,256]{1,0:T(8,128)(2,1)S(1)}, bf16[128,256]{1,0:T(8,128)(2,1)S(1)}, u32[]{:S(2)}, u32[]{:S(2)}) collective-permute-start(bf16[128,256]{1,0:T(8,128)(2,1)S(1)} %get-tuple-element.25), channel_id=1, source_target_pairs={{0,8},{8,0},{16,24},{24,16},{1,9},{9,1},{17,25},{25,17},{2,10},{10... | collective-permute-start | bytes 196616 | tf_op jit(solution)/shard_map/ppermute | solution.py:30

commit v6 on v5

v6 whole, which is shorter than its diff:
```python
import functools

import jax
import jax.numpy as jnp
from jax import lax
from jax.experimental import pallas as pl
from jax.experimental.pallas import tpu as pltpu
from jax.sharding import Mesh, PartitionSpec as P

EPSILON = 1e-05
OFF_WEIGHT = 0.0051

SAMPLES = ("zh", "yk", "yl")
FEATURES = ("zl", "x", "core")
F32 = jnp.float32
BF16 = jnp.bfloat16
HIGHEST = lax.Precision.HIGHEST
VMEM_LIMIT = 28 * 1024 * 1024

BLOCK = 128
BLOCKS = 16
CHUNK = 4


def exchange(values, axes):
    return lax.all_to_all(values, axes, 0, 0, tiled=True)


def near_swap(values, move):
    flip = 2 * (move % 2) + move // 2
    return lax.ppermute(values, ("yl", "zl"), [(i, i ^ flip) for i in range(4)])


def shift(values, distance):
    return lax.ppermute(values, "x", [(i, (i + distance) % 4) for i in range(4)])


def narrow_sum(*terms):
    return sum(term.astype(F32) for term in terms).astype(BF16)


def sample_row(place_ref, t):
    core = t // 8
    x = lax.rem(place_ref[0] + (t // 2) % 4, 4)
    zl = lax.rem(place_ref[1] + t % 2, 2)
    return pl.multiple_of(((zl * 4 + x) * 2 + core) * BLOCK, BLOCK)


def fold(values):
    return values.reshape(-1, 8, values.shape[-1]).sum(axis=0)


def column_statistics(load, blocks, count):
    pivot = jnp.mean(load(0), axis=0, keepdims=True)
    sums = jnp.zeros((8, pivot.shape[1]), F32)
    squares = sums
    for t in range(blocks):
        shifted = load(t) - pivot
        sums += fold(shifted)
        squares += fold(shifted * shifted)
    offset = jnp.sum(sums, axis=0, keepdims=True) / count
    spread = jnp.sum(squares, axis=0, keepdims=True) / count - offset * offset
    return pivot + offset, lax.rsqrt(jnp.maximum(spread, 0.0) + EPSILON)


def tile_kernel(
    place_ref, first_hbm, second_ref, moved_hbm, na_ref, nb_ref, grad_ref, vectors_ref,
    first_ref, moved_ref, load_sem, store_sems,
):
    count = BLOCK * BLOCKS
    width = first_ref.shape[1]
    load_first = pltpu.make_async_copy(first_hbm, first_ref, load_sem)
    load_first.start()

    scales = []
    means = []
    for i in range(2):
        load = lambda t: second_ref[t, i].astype(F32)
        center, scale = column_statistics(load, BLOCKS, count)
        sums = jnp.zeros((8, width), F32)
        for t in range(BLOCKS):
            norm = ((load(t) - center) * scale).astype(BF16)
            nb_ref[t * BLOCK : (t + 1) * BLOCK, i * width : (i + 1) * width] = norm
            sums += fold(norm.astype(F32))
        scales.append(scale)
        means.append(sums / count)
    scale_second = jnp.concatenate(scales, axis=1)
    mean_second = jnp.concatenate(means, axis=1)

    load_first.wait()
    load = lambda t: first_ref[t * BLOCK : (t + 1) * BLOCK, :].astype(F32)
    center, scale_first = column_statistics(load, BLOCKS, count)
    sums = jnp.zeros((8, width), F32)
    for t in range(BLOCKS):
        values = first_ref[pl.ds(sample_row(place_ref, t), BLOCK), :].astype(F32)
        norm = ((values - center) * scale_first).astype(BF16)
        na_ref[t * BLOCK : (t + 1) * BLOCK, :] = norm
        sums += fold(norm.astype(F32))
    mean_first = sums / count

    correlation = (
        lax.dot_general(
            na_ref[...], nb_ref[...], (((0,), (0,)), ((), ())), preferred_element_type=F32
        )
        / count
    )
    row_ids = lax.broadcasted_iota(jnp.int32, correlation.shape, 0)
    col_ids = lax.broadcasted_iota(jnp.int32, correlation.shape, 1)
    grad = jnp.where(
        row_ids == col_ids + place_ref[2],
        2.0 * (correlation - 1.0),
        2.0 * OFF_WEIGHT * correlation,
    ).astype(BF16)
    grad_ref[...] = grad
    grad_wide = grad.astype(F32)
    weighted = grad_wide * correlation
    projection_second = jnp.sum(weighted, axis=0, keepdims=True)
    centering_second = jnp.sum(
        jnp.dot(mean_first, grad_wide, preferred_element_type=F32, precision=HIGHEST),
        axis=0,
        keepdims=True,
    )
    stores = []
    for start in range(0, BLOCKS, CHUNK):
        some = slice(start * BLOCK, (start + CHUNK) * BLOCK)
        partial = jnp.dot(na_ref[some, :], grad, preferred_element_type=F32)
        partial = (
            (partial - centering_second - nb_ref[some, :].astype(F32) * projection_second)
            * scale_second
        ).astype(BF16)
        for i in range(2):
            moved_ref[start : start + CHUNK, i] = partial[:, i * width : (i + 1) * width].reshape(
                CHUNK, BLOCK, width
            )
        part = pl.ds(start, CHUNK)
        store = pltpu.make_async_copy(
            moved_ref.at[part], moved_hbm.at[part], store_sems.at[start // CHUNK]
        )
        store.start()
        stores.append(store)

    across = (((1,), (1,)), ((), ()))
    projection_first = lax.dot_general(
        jnp.ones((8, weighted.shape[1]), F32), weighted, across,
        preferred_element_type=F32, precision=HIGHEST,
    )
    centering_first = jnp.sum(
        lax.dot_general(
            mean_second, grad_wide, across, preferred_element_type=F32, precision=HIGHEST
        ),
        axis=0,
        keepdims=True,
    )
    vectors_ref[0:1, :] = centering_first
    vectors_ref[1:2, :] = projection_first[0:1]
    vectors_ref[2:3, :] = scale_first
    vectors_ref[3:8, :] = jnp.zeros((5, width), F32)
    for store in stores:
        store.wait()


def first_kernel(place_ref, na_ref, nb_ref, grad_ref, vectors_ref, out_hbm, out_ref, store_sems):
    grad = grad_ref[...]
    centering, projection, scale = (vectors_ref[i : i + 1, :] for i in range(3))
    stores = []
    for start in range(0, BLOCKS, CHUNK):
        some = slice(start * BLOCK, (start + CHUNK) * BLOCK)
        partial = lax.dot_general(
            nb_ref[some, :], grad, (((1,), (1,)), ((), ())), preferred_element_type=F32
        )
        partial = (partial - centering - na_ref[some, :].astype(F32) * projection) * scale
        out_ref[some, :] = partial.astype(BF16)
        for t in range(start, start + CHUNK):
            store = pltpu.make_async_copy(
                out_ref.at[pl.ds(t * BLOCK, BLOCK)],
                out_hbm.at[pl.ds(sample_row(place_ref, t), BLOCK)],
                store_sems.at[t],
            )
            store.start()
            stores.append(store)
    for store in stores:
        store.wait()


def local_compute(place, first, second):
    count, width = first.shape
    shape = jax.ShapeDtypeStruct
    smem, vmem, hbm = (pl.BlockSpec(memory_space=m) for m in (pltpu.SMEM, pltpu.VMEM, pltpu.HBM))
    params = pltpu.CompilerParams(vmem_limit_bytes=VMEM_LIMIT)
    flops = 2 * count * width * 2 * width
    first = pltpu.with_memory_space_constraint(first, pltpu.HBM)
    moved, *kept = pl.pallas_call(
        tile_kernel,
        out_shape=(
            pltpu.HBM(second.shape, BF16),
            shape((count, width), BF16),
            shape((count, 2 * width), BF16),
            shape((width, 2 * width), BF16),
            shape((8, width), F32),
        ),
        in_specs=[smem, hbm, vmem],
        out_specs=(hbm, vmem, vmem, vmem, vmem),
        scratch_shapes=[
            pltpu.VMEM((count, width), BF16),
            pltpu.VMEM(second.shape, BF16),
            pltpu.SemaphoreType.DMA,
            pltpu.SemaphoreType.DMA((BLOCKS // CHUNK,)),
        ],
        compiler_params=params,
        cost_estimate=pl.CostEstimate(flops=2 * flops, bytes_accessed=8 << 20, transcendentals=0),
    )(place, first, second)
    partial_first = pl.pallas_call(
        first_kernel,
        out_shape=pltpu.HBM((count, width), BF16),
        in_specs=[smem, vmem, vmem, vmem, vmem],
        out_specs=hbm,
        scratch_shapes=[pltpu.VMEM((count, width), BF16), pltpu.SemaphoreType.DMA((BLOCKS,))],
        compiler_params=params,
        cost_estimate=pl.CostEstimate(flops=flops, bytes_accessed=4 << 20, transcendentals=0),
    )(place, *kept)
    return moved, partial_first


def shards(first_view_outputs, second_view_outputs):
    rows_a, width_a = first_view_outputs.shape
    rows_b, width_b = second_view_outputs.shape
    n_dp = lax.axis_size(SAMPLES)
    half = width_a // 2
    total_count = rows_a * n_dp

    near = [near_swap(second_view_outputs, k) for k in (1, 2, 3)]
    halves = jnp.stack([first_view_outputs[:, :half], first_view_outputs[:, half:]])
    spread = jnp.broadcast_to(halves, (n_dp // 2, 2, rows_a, half)).reshape(n_dp, rows_a, half)
    near, spread = lax.optimization_barrier((near, spread))
    near = jnp.stack([second_view_outputs] + near)

    first = exchange(spread, SAMPLES).reshape(total_count, half)

    ahead = jnp.stack([near] + [shift(near, -k) for k in (1, 2, 3)])
    ahead = jnp.broadcast_to(ahead, (2,) + ahead.shape)
    first, ahead = lax.optimization_barrier((first, ahead))
    second = exchange(ahead, "core").reshape(BLOCKS, 2, rows_b, width_b)

    feat = lax.axis_index(FEATURES)
    pair = lax.axis_index(("zh", "yk"))
    place = jnp.stack(
        [
            lax.axis_index("x"),
            lax.axis_index("zl"),
            jnp.where(feat == pair, 0, 2 * width_a),
        ]
    ).astype(jnp.int32)
    moved, partial_first = local_compute(place, first, second)

    pieces = exchange(moved.reshape(2, 4, 4, rows_b, width_b), "core")
    pieces = narrow_sum(pieces[0], pieces[1])
    pieces = narrow_sum(pieces[0], *[shift(pieces[k], k) for k in (1, 2, 3)])
    second_view_gradient = narrow_sum(
        pieces[0], *[near_swap(pieces[k], k) for k in (1, 2, 3)]
    )

    parts = exchange(partial_first.reshape(n_dp, rows_a, half), SAMPLES)
    parts = jnp.sum(parts.reshape(n_dp // 2, 2, rows_a, half).astype(F32), axis=0).astype(BF16)
    first_view_gradient = jnp.concatenate([parts[0], parts[1]], axis=1)
    return first_view_gradient, second_view_gradient


def solution(mesh):
    fine = Mesh(
        mesh.devices.reshape(4, 4, 2, 2, 4, 2), ("zh", "yk", "yl", "zl", "x", "core")
    )
    specs = (P(SAMPLES, FEATURES), P(FEATURES, SAMPLES))
    return jax.shard_map(
        shards, mesh=fine, in_specs=specs, out_specs=specs, check_vma=False
    )
```

time: 130 us -> 121 us (0.931)
  Pallas kernels: 14.3 us -> 8 us
  local copies, waits for them, and re-layouts: 4.72 us -> 2.21 us
    pallas_call x2, Pallas kernels: 14.3 us -> 8 us  [the longest x1 5.68 us: local_compute(): pl.pallas_call(tile_kernel, out_shape=(pltpu.HBM(second.shape, BF16), sha...]
    ppermute x6, waiting for transfers between devices: 19.1 us -> 14.3 us  [shift(): lax.ppermute(values, 'x', [(i, (i + distance) % 4) for i in range(4)])]
    all_to_all x3, waiting for transfers between devices: 9.97 us -> 13.2 us  [exchange(): return lax.all_to_all(values, axes, 0, 0, tiled=True)]
    unnamed x6 -> x4, local copies, waits for them, and re-layouts: 2.52 us -> 0.01 us
    ppermute x6, starting transfers between devices: 17.8 us -> 19.5 us  [shift(): lax.ppermute(values, 'x', [(i, (i + distance) % 4) for i in range(4)])]
  transfers between devices with their start and end apart: 15 -> 15, of which waited for: 10 -> 10; matrix products, arithmetic and copies ran while one was open for 3% -> 3% of each run, Pallas kernels for 4% -> 2%
where the time goes in v6:
time: 121 us; the launch traced here: 120 us
  starting transfers between devices  64.8 us (54%)
  waiting for transfers between devices  34.9 us (29%)
  Pallas kernels  8 us (7%)
  blocking collectives  5.42 us (4%)
  other arithmetic  3.71 us (3%)
  local copies, waits for them, and re-layouts  2.21 us (2%)
    all_to_all x3, starting transfers between devices, exchange(): return lax.all_to_all(values, axes, 0, 0, tiled=True)  26.2 us
    ppermute x6, starting transfers between devices, shift(): lax.ppermute(values, 'x', [(i, (i + distance) % 4) for i in range(4)])  19.5 us
    ppermute x6, starting transfers between devices, near_swap(): return lax.ppermute(values, ('yl', 'zl'), [(i, i ^ flip) for i in range(4)])  19 us
    ppermute x6, waiting for transfers between devices, shift(): lax.ppermute(values, 'x', [(i, (i + distance) % 4) for i in range(4)])  14.3 us
    all_to_all x3, waiting for transfers between devices, exchange(): return lax.all_to_all(values, axes, 0, 0, tiled=True)  13.2 us
    ppermute x6, waiting for transfers between devices, near_swap(): return lax.ppermute(values, ('yl', 'zl'), [(i, i ^ flip) for i in range(4)])  7.31 us
    pallas_call x1, Pallas kernels, local_compute(): pl.pallas_call(tile_kernel, out_shape=(pltpu.HBM(second.shape, BF16), sha...  5.68 us
    all_to_all x1, blocking collectives, exchange(): return lax.all_to_all(values, axes, 0, 0, tiled=True)  5.42 us
  transfers between devices with their start and end apart: 15, of which 10 were waited for; matrix products, arithmetic and copies ran while one was open for 3% of the time, Pallas kernels for 2%

profile of v6, /device:TPU:6, one launch (start us, length us, event | category | flops | bytes accessed | tf_op | source)
XLA Modules:
  0.0 119.8 jit_solution(1113980804864642093)
XLA Ops:
  0.6 0.0 copy-start.1
  0.6 4.4 %collective-permute-start.1 = (bf16[128,256]{1,0:T(8,128)(2,1)}, bf16[128,256]{1,0:T(8,128)(2,1)S(1)}, u32[]{:S(2)}, u32[]{:S(2)}) collective-permute-start(bf16[128,256]{1,0:T(8,128)(2,1)} %param.3), channel_id=1, source_target_pairs={{0,8},{8,0},{16,24},{24,16},{1,9},{9,1},{17,25},{25,17},{2,10},{10... | collective-permute-start | bytes 196616 | tf_op jit(solution)/shard_map/ppermute | solution.py:31
  5.1 3.5 %collective-permute-start = (bf16[128,256]{1,0:T(8,128)(2,1)}, bf16[128,256]{1,0:T(8,128)(2,1)S(1)}, u32[]{:S(2)}, u32[]{:S(2)}) collective-permute-start(bf16[128,256]{1,0:T(8,128)(2,1)} %param.3), channel_id=1, source_target_pairs={{0,16},{8,24},{16,0},{24,8},{1,17},{9,25},{17,1},{25,9},{2,18},{10... | collective-permute-start | bytes 196616 | tf_op jit(solution)/shard_map/ppermute | solution.py:31
  8.6 1.9 %collective-permute-start.2 = (bf16[128,256]{1,0:T(8,128)(2,1)}, bf16[128,256]{1,0:T(8,128)(2,1)S(1)}, u32[]{:S(2)}, u32[]{:S(2)}) collective-permute-start(bf16[128,256]{1,0:T(8,128)(2,1)} %param.3), channel_id=1, source_target_pairs={{0,24},{8,16},{16,8},{24,0},{1,25},{9,17},{17,9},{25,1},{2,26},{10... | collective-permute-start | bytes 196616 | tf_op jit(solution)/shard_map/ppermute | solution.py:31
  10.5 0.8 slice_bitcast_fusion.11
  11.3 0.0 collective-permute-done.1
  11.3 0.1 collective-permute-done
  11.4 4.4 %collective-permute-done.2 = bf16[128,256]{1,0:T(8,128)(2,1)S(1)} collective-permute-done((bf16[128,256]{1,0:T(8,128)(2,1)}, bf16[128,256]{1,0:T(8,128)(2,1)S(1)}, u32[]{:S(2)}, u32[]{:S(2)}) %collective-permute-start.2) | collective-permute-done | bytes 65568 | tf_op jit(solution)/shard_map/ppermute | solution.py:31
  15.8 1.1 broadcast_in_dim.6
  16.9 14.2 %all-to-all-start = ((bf16[32,64,256]{2,1,0:T(8,128)(2,1)}), bf16[32,64,256]{2,1,0:T(8,128)(2,1)S(1)}, u32[]{:S(2)}, u32[]{:S(2)}) async-start(bf16[32,64,256]{2,1,0:T(8,128)(2,1)} %bitcast.5), calls=%async_computation | async-start | bytes 2097152 | tf_op jit(solution)/shard_map/all_to_all | solution.py:26
  31.1 0.0 copy-done.1
  31.2 3.3 %collective-permute-start.4 = (bf16[4,128,256]{2,1,0:T(8,128)(2,1)S(1)}, bf16[4,128,256]{2,1,0:T(8,128)(2,1)S(1)}, u32[]{:S(2)}, u32[]{:S(2)}) collective-permute-start(bf16[4,128,256]{2,1,0:T(8,128)(2,1)S(1)} %get-tuple-element.31), channel_id=1, source_target_pairs={{0,4},{2,6},{4,0},{6,2},{1,5},{3,7},{5,1},{7,3},{8,12},{10,14},{12... | collective-permute-start | bytes 786440 | tf_op jit(solution)/shard_map/ppermute | solution.py:35
  34.5 1.9 %collective-permute-start.3 = (bf16[4,128,256]{2,1,0:T(8,128)(2,1)S(1)}, bf16[4,128,256]{2,1,0:T(8,128)(2,1)S(1)}, u32[]{:S(2)}, u32[]{:S(2)}) collective-permute-start(bf16[4,128,256]{2,1,0:T(8,128)(2,1)S(1)} %get-tuple-element.31), channel_id=1, source_target_pairs={{0,6},{2,0},{4,2},{6,4},{1,7},{3,1},{5,3},{7,5},{8,14},{10,8},{12,... | collective-permute-start | bytes 786440 | tf_op jit(solution)/shard_map/ppermute | solution.py:35
  36.4 5.1 %collective-permute-start.5 = (bf16[4,128,256]{2,1,0:T(8,128)(2,1)S(1)}, bf16[4,128,256]{2,1,0:T(8,128)(2,1)S(1)}, u32[]{:S(2)}, u32[]{:S(2)}) collective-permute-start(bf16[4,128,256]{2,1,0:T(8,128)(2,1)S(1)} %get-tuple-element.31), channel_id=1, source_target_pairs={{0,2},{2,4},{4,6},{6,0},{1,3},{3,5},{5,7},{7,1},{8,10},{10,12},{12... | collective-permute-start | bytes 786440 | tf_op jit(solution)/shard_map/ppermute | solution.py:35
  41.6 0.1 pad_add_fusion.place_ref
  41.6 2.1 %collective-permute-done.4 = bf16[4,128,256]{2,1,0:T(8,128)(2,1)S(1)} collective-permute-done((bf16[4,128,256]{2,1,0:T(8,128)(2,1)S(1)}, bf16[4,128,256]{2,1,0:T(8,128)(2,1)S(1)}, u32[]{:S(2)}, u32[]{:S(2)}) %collective-permute-start.4) | collective-permute-done | bytes 262176 | tf_op jit(solution)/shard_map/ppermute | solution.py:35
  43.7 2.5 %collective-permute-done.3 = bf16[4,128,256]{2,1,0:T(8,128)(2,1)S(1)} collective-permute-done((bf16[4,128,256]{2,1,0:T(8,128)(2,1)S(1)}, bf16[4,128,256]{2,1,0:T(8,128)(2,1)S(1)}, u32[]{:S(2)}, u32[]{:S(2)}) %collective-permute-start.3) | collective-permute-done | bytes 262176 | tf_op jit(solution)/shard_map/ppermute | solution.py:35
  46.2 0.0 collective-permute-done.5
  46.2 0.1 pad_maximum_fusion
  46.4 12.6 %all-to-all-done = bf16[32,64,256]{2,1,0:T(8,128)(2,1)S(1)} async-done(((bf16[32,64,256]{2,1,0:T(8,128)(2,1)}), bf16[32,64,256]{2,1,0:T(8,128)(2,1)S(1)}, u32[]{:S(2)}, u32[]{:S(2)}) %all-to-all-start) | async-done | bytes 1048608 | tf_op jit(solution)/shard_map/all_to_all | solution.py:26
  59.0 0.0 copy-start
  59.0 0.2 broadcast_in_dim.7
  59.2 5.4 %all_to_all.20 = bf16[2,4,4,128,256]{4,3,2,1,0:T(8,128)(2,1)S(1)} all-to-all(bf16[2,4,4,128,256]{4,3,2,1,0:T(8,128)(2,1)S(1)} %broadcast_in_dim.7), channel_id=1, replica_groups=mesh['zh'=4,'yk'=4,'yl'=2,'zl'=2,'x'=4,'core'=2] {'core'}, dimensions={0} | all-to-all | bytes 4194304 | tf_op jit(solution)/shard_map/all_to_all | solution.py:26
  64.6 0.0 copy-done
  64.6 5.7 %shard_map.41 = (bf16[16,2,128,256]{3,2,1,0:T(8,128)(2,1)}, bf16[2048,256]{1,0:T(8,128)(2,1)S(1)}, bf16[2048,512]{1,0:T(8,128)(2,1)S(1)}, bf16[256,512]{1,0:T(8,128)(2,1)S(1)}, f32[8,256]{1,0:T(8,128)S(1)}) custom-call(s32[3]{0:T(128)S(1)} %pad_add_fusion.place_ref, bf16[2048,256]{1,0:T(8,128)(2,1)} %bitcast.52, bf16[16,2,128,256]{3,2,1,0:T(8,128)(2,1)S(1)} %bitcast.48), custom_call_target="tpu_custom_call" | custom-call | flops 1073741824 | bytes 8388608 | tf_op jit(solution)/shard_map/pallas_call | solution.py:192
  70.3 4.8 %all-to-all-start.3 = ((bf16[2,4,4,128,256]{4,3,2,1,0:T(8,128)(2,1)}), bf16[2,4,4,128,256]{4,3,2,1,0:T(8,128)(2,1)}, u32[]{:S(2)}, u32[]{:S(2)}) async-start(bf16[2,4,4,128,256]{4,3,2,1,0:T(8,128)(2,1)} %bitcast.51), calls=%async_computation.3 | async-start | bytes 4194304 | tf_op jit(solution)/shard_map/all_to_all | solution.py:26
  75.1 2.3 %shard_map.42 = bf16[2048,256]{1,0:T(8,128)(2,1)} custom-call(s32[3]{0:T(128)S(1)} %pad_add_fusion.place_ref, bf16[2048,256]{1,0:T(8,128)(2,1)S(1)} %get-tuple-element.19.na_ref, bf16[2048,512]{1,0:T(8,128)(2,1)S(1)} %get-tuple-element.20.nb_ref, bf16[256,512]{1,0:T(8,128)(2,1)S(1)} %get-tuple-element.21.grad_ref, f32[8,256]{1,0:T(8,128)S(1)} %get-tuple-element.22.vectors_ref), custom_call_target="tpu_custom_call" | custom-call | flops 536870912 | bytes 4194304 | tf_op jit(solution)/shard_map/pallas_call | solution.py:212
  77.5 0.7 all-to-all-done.3
  78.1 7.2 %all-to-all-start.2 = ((bf16[32,64,256]{2,1,0:T(8,128)(2,1)}), bf16[32,64,256]{2,1,0:T(8,128)(2,1)S(1)}, u32[]{:S(2)}, u32[]{:S(2)}) async-start(bf16[32,64,256]{2,1,0:T(8,128)(2,1)} %bitcast.49), calls=%async_computation.2 | async-start | bytes 2097152 | tf_op jit(solution)/shard_map/all_to_all | solution.py:26
  85.4 1.9 %add_convert_fusion = bf16[1,4,4,128,256]{4,3,2,1,0:T(8,128)(2,1)S(1)} fusion(bf16[2,4,4,128,256]{4,3,2,1,0:T(8,128)(2,1)} %all-to-all-done.3), kind=kLoop, calls=%fused_computation | loop fusion | flops 2097152 | bytes 3145728 | tf_op jit(solution)/shard_map/convert_element_type | solution.py:39
  87.2 0.1 slice_bitcast_fusion.2
  87.3 2.4 %collective-permute-start.6 = (bf16[4,128,256]{2,1,0:T(8,128)(2,1)S(1)}, bf16[4,128,256]{2,1,0:T(8,128)(2,1)S(1)}, u32[]{:S(2)}, u32[]{:S(2)}) collective-permute-start(bf16[4,128,256]{2,1,0:T(8,128)(2,1)S(1)} %get-tuple-element.24), channel_id=1, source_target_pairs={{0,2},{2,4},{4,6},{6,0},{1,3},{3,5},{5,7},{7,1},{8,10},{10,12},{12... | collective-permute-start | bytes 786440 | tf_op jit(solution)/shard_map/ppermute | solution.py:35
  89.7 3.5 %collective-permute-start.8 = (bf16[4,128,256]{2,1,0:T(8,128)(2,1)S(1)}, bf16[4,128,256]{2,1,0:T(8,128)(2,1)S(1)}, u32[]{:S(2)}, u32[]{:S(2)}) collective-permute-start(bf16[4,128,256]{2,1,0:T(8,128)(2,1)S(1)} %get-tuple-element.25), channel_id=1, source_target_pairs={{0,6},{2,0},{4,2},{6,4},{1,7},{3,1},{5,3},{7,5},{8,14},{10,8},{12,... | collective-permute-start | bytes 786440 | tf_op jit(solution)/shard_map/ppermute | solution.py:35
  93.1 3.3 %collective-permute-start.7 = (bf16[4,128,256]{2,1,0:T(8,128)(2,1)S(1)}, bf16[4,128,256]{2,1,0:T(8,128)(2,1)S(1)}, u32[]{:S(2)}, u32[]{:S(2)}) collective-permute-start(bf16[4,128,256]{2,1,0:T(8,128)(2,1)S(1)} %get-tuple-element.26), channel_id=1, source_target_pairs={{0,4},{2,6},{4,0},{6,2},{1,5},{3,7},{5,1},{7,3},{8,12},{10,14},{12... | collective-permute-start | bytes 786440 | tf_op jit(solution)/shard_map/ppermute | solution.py:35
  96.5 0.8 collective-permute-done.6
  97.2 8.9 %collective-permute-done.8 = bf16[4,128,256]{2,1,0:T(8,128)(2,1)S(1)} collective-permute-done((bf16[4,128,256]{2,1,0:T(8,128)(2,1)S(1)}, bf16[4,128,256]{2,1,0:T(8,128)(2,1)S(1)}, u32[]{:S(2)}, u32[]{:S(2)}) %collective-permute-start.8) | collective-permute-done | bytes 262176 | tf_op jit(solution)/shard_map/ppermute | solution.py:35
  106.2 0.0 collective-permute-done.7
  106.2 0.1 fusion.2
  106.4 3.4 %collective-permute-start.9 = (bf16[128,256]{1,0:T(8,128)(2,1)S(1)}, bf16[128,256]{1,0:T(8,128)(2,1)S(1)}, u32[]{:S(2)}, u32[]{:S(2)}) collective-permute-start(bf16[128,256]{1,0:T(8,128)(2,1)S(1)} %get-tuple-element.27), channel_id=1, source_target_pairs={{0,16},{8,24},{16,0},{24,8},{1,17},{9,25},{17,1},{25,9},{2,18},{10... | collective-permute-start | bytes 196616 | tf_op jit(solution)/shard_map/ppermute | solution.py:31
  109.8 2.4 %collective-permute-start.11 = (bf16[128,256]{1,0:T(8,128)(2,1)S(1)}, bf16[128,256]{1,0:T(8,128)(2,1)S(1)}, u32[]{:S(2)}, u32[]{:S(2)}) collective-permute-start(bf16[128,256]{1,0:T(8,128)(2,1)S(1)} %get-tuple-element.28), channel_id=1, source_target_pairs={{0,24},{8,16},{16,8},{24,0},{1,25},{9,17},{17,9},{25,1},{2,26},{10... | collective-permute-start | bytes 196616 | tf_op jit(solution)/shard_map/ppermute | solution.py:31
  112.2 3.4 %collective-permute-start.10 = (bf16[128,256]{1,0:T(8,128)(2,1)S(1)}, bf16[128,256]{1,0:T(8,128)(2,1)S(1)}, u32[]{:S(2)}, u32[]{:S(2)}) collective-permute-start(bf16[128,256]{1,0:T(8,128)(2,1)S(1)} %get-tuple-element.29), channel_id=1, source_target_pairs={{0,8},{8,0},{16,24},{24,16},{1,9},{9,1},{17,25},{25,17},{2,10},{10... | collective-permute-start | bytes 196616 | tf_op jit(solution)/shard_map/ppermute | solution.py:31
  115.6 0.0 collective-permute-done.9
  115.6 1.2 %collective-permute-done.11 = bf16[128,256]{1,0:T(8,128)(2,1)S(1)} collective-permute-done((bf16[128,256]{1,0:T(8,128)(2,1)S(1)}, bf16[128,256]{1,0:T(8,128)(2,1)S(1)}, u32[]{:S(2)}, u32[]{:S(2)}) %collective-permute-start.11) | collective-permute-done | bytes 65568 | tf_op jit(solution)/shard_map/ppermute | solution.py:31
  116.8 1.5 %collective-permute-done.10 = bf16[128,256]{1,0:T(8,128)(2,1)S(1)} collective-permute-done((bf16[128,256]{1,0:T(8,128)(2,1)S(1)}, bf16[128,256]{1,0:T(8,128)(2,1)S(1)}, u32[]{:S(2)}, u32[]{:S(2)}) %collective-permute-start.10) | collective-permute-done | bytes 65568 | tf_op jit(solution)/shard_map/ppermute | solution.py:31
  118.4 0.7 fusion.5
  119.0 0.0 all-to-all-done.2
  119.0 0.1 reduce_sum.12
  119.2 0.6 pad_maximum_fusion.3
  (4 shorter events, 0.1 us)
Async XLA Ops:
  0.6 30.5 %copy-start.1 = (bf16[128,256]{1,0:T(8,128)(2,1)S(1)}, bf16[128,256]{1,0:T(8,128)(2,1)}, u32[]{:S(2)}) copy-start(bf16[128,256]{1,0:T(8,128)(2,1)} %param.3) | copy-start | bytes 196612
  0.6 10.6 %collective-permute-start.1 = (bf16[128,256]{1,0:T(8,128)(2,1)}, bf16[128,256]{1,0:T(8,128)(2,1)S(1)}, u32[]{:S(2)}, u32[]{:S(2)}) collective-permute-start(bf16[128,256]{1,0:T(8,128)(2,1)} %param.3), channel_id=1, source_target_pairs={{0,8},{8,0},{16,24},{24,16},{1,9},{9,1},{17,25},{25,17},{2,10},{10... | collective-permute-start | bytes 196616 | tf_op jit(solution)/shard_map/ppermute | solution.py:31
  5.1 6.4 %collective-permute-start = (bf16[128,256]{1,0:T(8,128)(2,1)}, bf16[128,256]{1,0:T(8,128)(2,1)S(1)}, u32[]{:S(2)}, u32[]{:S(2)}) collective-permute-start(bf16[128,256]{1,0:T(8,128)(2,1)} %param.3), channel_id=1, source_target_pairs={{0,16},{8,24},{16,0},{24,8},{1,17},{9,25},{17,1},{25,9},{2,18},{10... | collective-permute-start | bytes 196616 | tf_op jit(solution)/shard_map/ppermute | solution.py:31
  8.6 7.3 %collective-permute-start.2 = (bf16[128,256]{1,0:T(8,128)(2,1)}, bf16[128,256]{1,0:T(8,128)(2,1)S(1)}, u32[]{:S(2)}, u32[]{:S(2)}) collective-permute-start(bf16[128,256]{1,0:T(8,128)(2,1)} %param.3), channel_id=1, source_target_pairs={{0,24},{8,16},{16,8},{24,0},{1,25},{9,17},{17,9},{25,1},{2,26},{10... | collective-permute-start | bytes 196616 | tf_op jit(solution)/shard_map/ppermute | solution.py:31
  16.9 42.0 %all-to-all-start = ((bf16[32,64,256]{2,1,0:T(8,128)(2,1)}), bf16[32,64,256]{2,1,0:T(8,128)(2,1)S(1)}, u32[]{:S(2)}, u32[]{:S(2)}) async-start(bf16[32,64,256]{2,1,0:T(8,128)(2,1)} %bitcast.5), calls=%async_computation | async-start | bytes 2097152 | tf_op jit(solution)/shard_map/all_to_all | solution.py:26
  31.2 12.5 %collective-permute-start.4 = (bf16[4,128,256]{2,1,0:T(8,128)(2,1)S(1)}, bf16[4,128,256]{2,1,0:T(8,128)(2,1)S(1)}, u32[]{:S(2)}, u32[]{:S(2)}) collective-permute-start(bf16[4,128,256]{2,1,0:T(8,128)(2,1)S(1)} %get-tuple-element.31), channel_id=1, source_target_pairs={{0,4},{2,6},{4,0},{6,2},{1,5},{3,7},{5,1},{7,3},{8,12},{10,14},{12... | collective-permute-start | bytes 786440 | tf_op jit(solution)/shard_map/ppermute | solution.py:35
  34.5 11.8 %collective-permute-start.3 = (bf16[4,128,256]{2,1,0:T(8,128)(2,1)S(1)}, bf16[4,128,256]{2,1,0:T(8,128)(2,1)S(1)}, u32[]{:S(2)}, u32[]{:S(2)}) collective-permute-start(bf16[4,128,256]{2,1,0:T(8,128)(2,1)S(1)} %get-tuple-element.31), channel_id=1, source_target_pairs={{0,6},{2,0},{4,2},{6,4},{1,7},{3,1},{5,3},{7,5},{8,14},{10,8},{12,... | collective-permute-start | bytes 786440 | tf_op jit(solution)/shard_map/ppermute | solution.py:35
  36.4 9.8 %collective-permute-start.5 = (bf16[4,128,256]{2,1,0:T(8,128)(2,1)S(1)}, bf16[4,128,256]{2,1,0:T(8,128)(2,1)S(1)}, u32[]{:S(2)}, u32[]{:S(2)}) collective-permute-start(bf16[4,128,256]{2,1,0:T(8,128)(2,1)S(1)} %get-tuple-element.31), channel_id=1, source_target_pairs={{0,2},{2,4},{4,6},{6,0},{1,3},{3,5},{5,7},{7,1},{8,10},{10,12},{12... | collective-permute-start | bytes 786440 | tf_op jit(solution)/shard_map/ppermute | solution.py:35
  59.0 5.7 %copy-start = (bf16[32,64,256]{2,1,0:T(8,128)(2,1)}, bf16[32,64,256]{2,1,0:T(8,128)(2,1)S(1)}, u32[]{:S(2)}) copy-start(bf16[32,64,256]{2,1,0:T(8,128)(2,1)S(1)} %all-to-all-done) | copy-start | bytes 3145732
  70.3 7.8 %all-to-all-start.3 = ((bf16[2,4,4,128,256]{4,3,2,1,0:T(8,128)(2,1)}), bf16[2,4,4,128,256]{4,3,2,1,0:T(8,128)(2,1)}, u32[]{:S(2)}, u32[]{:S(2)}) async-start(bf16[2,4,4,128,256]{4,3,2,1,0:T(8,128)(2,1)} %bitcast.51), calls=%async_computation.3 | async-start | bytes 4194304 | tf_op jit(solution)/shard_map/all_to_all | solution.py:26
  78.1 40.9 %all-to-all-start.2 = ((bf16[32,64,256]{2,1,0:T(8,128)(2,1)}), bf16[32,64,256]{2,1,0:T(8,128)(2,1)S(1)}, u32[]{:S(2)}, u32[]{:S(2)}) async-start(bf16[32,64,256]{2,1,0:T(8,128)(2,1)} %bitcast.49), calls=%async_computation.2 | async-start | bytes 2097152 | tf_op jit(solution)/shard_map/all_to_all | solution.py:26
  87.3 10.0 %collective-permute-start.6 = (bf16[4,128,256]{2,1,0:T(8,128)(2,1)S(1)}, bf16[4,128,256]{2,1,0:T(8,128)(2,1)S(1)}, u32[]{:S(2)}, u32[]{:S(2)}) collective-permute-start(bf16[4,128,256]{2,1,0:T(8,128)(2,1)S(1)} %get-tuple-element.24), channel_id=1, source_target_pairs={{0,2},{2,4},{4,6},{6,0},{1,3},{3,5},{5,7},{7,1},{8,10},{10,12},{12... | collective-permute-start | bytes 786440 | tf_op jit(solution)/shard_map/ppermute | solution.py:35
  89.7 16.5 %collective-permute-start.8 = (bf16[4,128,256]{2,1,0:T(8,128)(2,1)S(1)}, bf16[4,128,256]{2,1,0:T(8,128)(2,1)S(1)}, u32[]{:S(2)}, u32[]{:S(2)}) collective-permute-start(bf16[4,128,256]{2,1,0:T(8,128)(2,1)S(1)} %get-tuple-element.25), channel_id=1, source_target_pairs={{0,6},{2,0},{4,2},{6,4},{1,7},{3,1},{5,3},{7,5},{8,14},{10,8},{12,... | collective-permute-start | bytes 786440 | tf_op jit(solution)/shard_map/ppermute | solution.py:35
  93.1 13.0 %collective-permute-start.7 = (bf16[4,128,256]{2,1,0:T(8,128)(2,1)S(1)}, bf16[4,128,256]{2,1,0:T(8,128)(2,1)S(1)}, u32[]{:S(2)}, u32[]{:S(2)}) collective-permute-start(bf16[4,128,256]{2,1,0:T(8,128)(2,1)S(1)} %get-tuple-element.26), channel_id=1, source_target_pairs={{0,4},{2,6},{4,0},{6,2},{1,5},{3,7},{5,1},{7,3},{8,12},{10,14},{12... | collective-permute-start | bytes 786440 | tf_op jit(solution)/shard_map/ppermute | solution.py:35
  106.4 9.2 %collective-permute-start.9 = (bf16[128,256]{1,0:T(8,128)(2,1)S(1)}, bf16[128,256]{1,0:T(8,128)(2,1)S(1)}, u32[]{:S(2)}, u32[]{:S(2)}) collective-permute-start(bf16[128,256]{1,0:T(8,128)(2,1)S(1)} %get-tuple-element.27), channel_id=1, source_target_pairs={{0,16},{8,24},{16,0},{24,8},{1,17},{9,25},{17,1},{25,9},{2,18},{10... | collective-permute-start | bytes 196616 | tf_op jit(solution)/shard_map/ppermute | solution.py:31
  109.8 7.1 %collective-permute-start.11 = (bf16[128,256]{1,0:T(8,128)(2,1)S(1)}, bf16[128,256]{1,0:T(8,128)(2,1)S(1)}, u32[]{:S(2)}, u32[]{:S(2)}) collective-permute-start(bf16[128,256]{1,0:T(8,128)(2,1)S(1)} %get-tuple-element.28), channel_id=1, source_target_pairs={{0,24},{8,16},{16,8},{24,0},{1,25},{9,17},{17,9},{25,1},{2,26},{10... | collective-permute-start | bytes 196616 | tf_op jit(solution)/shard_map/ppermute | solution.py:31
  112.2 6.2 %collective-permute-start.10 = (bf16[128,256]{1,0:T(8,128)(2,1)S(1)}, bf16[128,256]{1,0:T(8,128)(2,1)S(1)}, u32[]{:S(2)}, u32[]{:S(2)}) collective-permute-start(bf16[128,256]{1,0:T(8,128)(2,1)S(1)} %get-tuple-element.29), channel_id=1, source_target_pairs={{0,8},{8,0},{16,24},{24,16},{1,9},{9,1},{17,25},{25,17},{2,10},{10... | collective-permute-start | bytes 196616 | tf_op jit(solution)/shard_map/ppermute | solution.py:31

commit v7 on v6

--- a/solution.py
+++ b/solution.py
@@ -75,7 +75,7 @@
     scales = []
     means = []
     for i in range(2):
-        load = lambda t: second_ref[t, i].astype(F32)
+        load = lambda t: second_ref[t // 8, t % 2, i, (t // 2) % 4].astype(F32)
         center, scale = column_statistics(load, BLOCKS, count)
         sums = jnp.zeros((8, width), F32)
         for t in range(BLOCKS):
@@ -184,6 +184,7 @@
 
 def local_compute(place, first, second):
     count, width = first.shape
+    pieces = (BLOCKS, 2, BLOCK, width)
     shape = jax.ShapeDtypeStruct
     smem, vmem, hbm = (pl.BlockSpec(memory_space=m) for m in (pltpu.SMEM, pltpu.VMEM, pltpu.HBM))
     params = pltpu.CompilerParams(vmem_limit_bytes=VMEM_LIMIT)
@@ -192,7 +193,7 @@
     moved, *kept = pl.pallas_call(
         tile_kernel,
         out_shape=(
-            pltpu.HBM(second.shape, BF16),
+            pltpu.HBM(pieces, BF16),
             shape((count, width), BF16),
             shape((count, 2 * width), BF16),
             shape((width, 2 * width), BF16),
@@ -202,7 +203,7 @@
         out_specs=(hbm, vmem, vmem, vmem, vmem),
         scratch_shapes=[
             pltpu.VMEM((count, width), BF16),
-            pltpu.VMEM(second.shape, BF16),
+            pltpu.VMEM(pieces, BF16),
             pltpu.SemaphoreType.DMA,
             pltpu.SemaphoreType.DMA((BLOCKS // CHUNK,)),
         ],
@@ -228,18 +229,15 @@
     half = width_a // 2
     total_count = rows_a * n_dp
 
-    near = [near_swap(second_view_outputs, k) for k in (1, 2, 3)]
     halves = jnp.stack([first_view_outputs[:, :half], first_view_outputs[:, half:]])
     spread = jnp.broadcast_to(halves, (n_dp // 2, 2, rows_a, half)).reshape(n_dp, rows_a, half)
-    near, spread = lax.optimization_barrier((near, spread))
-    near = jnp.stack([second_view_outputs] + near)
-
     first = exchange(spread, SAMPLES).reshape(total_count, half)
 
-    ahead = jnp.stack([near] + [shift(near, -k) for k in (1, 2, 3)])
-    ahead = jnp.broadcast_to(ahead, (2,) + ahead.shape)
-    first, ahead = lax.optimization_barrier((first, ahead))
-    second = exchange(ahead, "core").reshape(BLOCKS, 2, rows_b, width_b)
+    ahead = jnp.stack([second_view_outputs] + [shift(second_view_outputs, -k) for k in (1, 2, 3)])
+    near = jnp.stack([ahead] + [near_swap(ahead, k) for k in (1, 2, 3)])
+    near = jnp.broadcast_to(near, (2,) + near.shape)
+    first, near = lax.optimization_barrier((first, near))
+    second = exchange(near, "core").reshape(2, 2, 2, 4, rows_b, width_b)
 
     feat = lax.axis_index(FEATURES)
     pair = lax.axis_index(("zh", "yk"))

time: 121 us -> 121 us (level)
  starting transfers between devices: 64.8 us -> 67.6 us
  waiting for transfers between devices: 34.9 us -> 32.3 us
    all_to_all x3, waiting for transfers between devices: 13.2 us -> 0.67 us  [exchange(): return lax.all_to_all(values, axes, 0, 0, tiled=True)]
    ppermute x6, waiting for transfers between devices: 7.31 us -> 16.4 us  [near_swap(): return lax.ppermute(values, ('yl', 'zl'), [(i, i ^ flip) for i in range(4)])]
    all_to_all x3, starting transfers between devices: 26.2 us -> 30.9 us  [exchange(): return lax.all_to_all(values, axes, 0, 0, tiled=True)]
  transfers between devices with their start and end apart: 15 -> 15, of which waited for: 10 -> 7; matrix products, arithmetic and copies ran while one was open for 3% -> 2% of each run, Pallas kernels for 2% -> 2%
where the time goes in v7:
time: 121 us; the launch traced here: 120 us
  starting transfers between devices  67.6 us (56%)
  waiting for transfers between devices  32.3 us (27%)
  Pallas kernels  7.99 us (7%)
  blocking collectives  5.42 us (4%)
  other arithmetic  3.7 us (3%)
  local copies, waits for them, and re-layouts  2.25 us (2%)
    all_to_all x3, starting transfers between devices, exchange(): return lax.all_to_all(values, axes, 0, 0, tiled=True)  30.9 us
    ppermute x6, starting transfers between devices, near_swap(): return lax.ppermute(values, ('yl', 'zl'), [(i, i ^ flip) for i in range(4)])  18.4 us
    ppermute x6, starting transfers between devices, shift(): lax.ppermute(values, 'x', [(i, (i + distance) % 4) for i in range(4)])  18.3 us
    ppermute x6, waiting for transfers between devices, near_swap(): return lax.ppermute(values, ('yl', 'zl'), [(i, i ^ flip) for i in range(4)])  16.4 us
    ppermute x6, waiting for transfers between devices, shift(): lax.ppermute(values, 'x', [(i, (i + distance) % 4) for i in range(4)])  15.3 us
    pallas_call x1, Pallas kernels, local_compute(): pl.pallas_call(tile_kernel, out_shape=(pltpu.HBM(pieces, BF16), shape((co...  5.69 us
    all_to_all x1, blocking collectives, exchange(): return lax.all_to_all(values, axes, 0, 0, tiled=True)  5.42 us
    convert_element_type x3, other arithmetic, narrow_sum(): return sum((term.astype(F32) for term in terms)).astype(BF16)  2.66 us
  transfers between devices with their start and end apart: 15, of which 7 were waited for; matrix products, arithmetic and copies ran while one was open for 2% of the time, Pallas kernels for 2%

profile of v7, /device:TPU:6, one launch (start us, length us, event | category | flops | bytes accessed | tf_op | source)
XLA Modules:
  0.0 120.1 jit_solution(15542223609356613201)
XLA Ops:
  0.6 0.0 copy-start.1
  0.6 0.8 slice_bitcast_fusion.11
  1.5 1.1 broadcast_in_dim.6
  2.6 16.0 %all-to-all-start = ((bf16[32,64,256]{2,1,0:T(8,128)(2,1)}), bf16[32,64,256]{2,1,0:T(8,128)(2,1)S(1)}, u32[]{:S(2)}, u32[]{:S(2)}) async-start(bf16[32,64,256]{2,1,0:T(8,128)(2,1)} %bitcast.5), calls=%async_computation | async-start | bytes 2097152 | tf_op jit(solution)/shard_map/all_to_all | solution.py:26
  18.5 0.0 copy-done.1
  18.6 2.7 %collective-permute-start = (bf16[128,256]{1,0:T(8,128)(2,1)S(1)}, bf16[128,256]{1,0:T(8,128)(2,1)S(1)}, u32[]{:S(2)}, u32[]{:S(2)}) collective-permute-start(bf16[128,256]{1,0:T(8,128)(2,1)S(1)} %copy-done.1), channel_id=1, source_target_pairs={{0,6},{2,0},{4,2},{6,4},{1,7},{3,1},{5,3},{7,5},{8,14},{10,8},{12,... | collective-permute-start | bytes 196616 | tf_op jit(solution)/shard_map/ppermute | solution.py:35
  21.3 4.3 %collective-permute-start.2 = (bf16[128,256]{1,0:T(8,128)(2,1)S(1)}, bf16[128,256]{1,0:T(8,128)(2,1)S(1)}, u32[]{:S(2)}, u32[]{:S(2)}) collective-permute-start(bf16[128,256]{1,0:T(8,128)(2,1)S(1)} %copy-done.1), channel_id=1, source_target_pairs={{0,2},{2,4},{4,6},{6,0},{1,3},{3,5},{5,7},{7,1},{8,10},{10,12},{12... | collective-permute-start | bytes 196616 | tf_op jit(solution)/shard_map/ppermute | solution.py:35
  25.6 2.1 %collective-permute-start.1 = (bf16[128,256]{1,0:T(8,128)(2,1)S(1)}, bf16[128,256]{1,0:T(8,128)(2,1)S(1)}, u32[]{:S(2)}, u32[]{:S(2)}) collective-permute-start(bf16[128,256]{1,0:T(8,128)(2,1)S(1)} %copy-done.1), channel_id=1, source_target_pairs={{0,4},{2,6},{4,0},{6,2},{1,5},{3,7},{5,1},{7,3},{8,12},{10,14},{12... | collective-permute-start | bytes 196616 | tf_op jit(solution)/shard_map/ppermute | solution.py:35
  27.7 0.0 collective-permute-done
  27.7 0.0 collective-permute-done.2
  27.8 5.5 %collective-permute-done.1 = bf16[128,256]{1,0:T(8,128)(2,1)S(1)} collective-permute-done((bf16[128,256]{1,0:T(8,128)(2,1)S(1)}, bf16[128,256]{1,0:T(8,128)(2,1)S(1)}, u32[]{:S(2)}, u32[]{:S(2)}) %collective-permute-start.1) | collective-permute-done | bytes 65568 | tf_op jit(solution)/shard_map/ppermute | solution.py:35
  33.3 3.4 %collective-permute-start.4 = (bf16[4,128,256]{2,1,0:T(8,128)(2,1)S(1)}, bf16[4,128,256]{2,1,0:T(8,128)(2,1)S(1)}, u32[]{:S(2)}, u32[]{:S(2)}) collective-permute-start(bf16[4,128,256]{2,1,0:T(8,128)(2,1)S(1)} %get-tuple-element.23), channel_id=1, source_target_pairs={{0,8},{8,0},{16,24},{24,16},{1,9},{9,1},{17,25},{25,17},{2,10},{10... | collective-permute-start | bytes 786440 | tf_op jit(solution)/shard_map/ppermute | solution.py:31
  36.7 3.7 %collective-permute-start.3 = (bf16[4,128,256]{2,1,0:T(8,128)(2,1)S(1)}, bf16[4,128,256]{2,1,0:T(8,128)(2,1)S(1)}, u32[]{:S(2)}, u32[]{:S(2)}) collective-permute-start(bf16[4,128,256]{2,1,0:T(8,128)(2,1)S(1)} %get-tuple-element.23), channel_id=1, source_target_pairs={{0,16},{8,24},{16,0},{24,8},{1,17},{9,25},{17,1},{25,9},{2,18},{10... | collective-permute-start | bytes 786440 | tf_op jit(solution)/shard_map/ppermute | solution.py:31
  40.4 2.1 %collective-permute-start.5 = (bf16[4,128,256]{2,1,0:T(8,128)(2,1)S(1)}, bf16[4,128,256]{2,1,0:T(8,128)(2,1)S(1)}, u32[]{:S(2)}, u32[]{:S(2)}) collective-permute-start(bf16[4,128,256]{2,1,0:T(8,128)(2,1)S(1)} %get-tuple-element.23), channel_id=1, source_target_pairs={{0,24},{8,16},{16,8},{24,0},{1,25},{9,17},{17,9},{25,1},{2,26},{10... | collective-permute-start | bytes 786440 | tf_op jit(solution)/shard_map/ppermute | solution.py:31
  42.6 0.1 pad_add_fusion.place_ref
  42.7 14.1 %collective-permute-done.4 = bf16[4,128,256]{2,1,0:T(8,128)(2,1)S(1)} collective-permute-done((bf16[4,128,256]{2,1,0:T(8,128)(2,1)S(1)}, bf16[4,128,256]{2,1,0:T(8,128)(2,1)S(1)}, u32[]{:S(2)}, u32[]{:S(2)}) %collective-permute-start.4) | collective-permute-done | bytes 262176 | tf_op jit(solution)/shard_map/ppermute | solution.py:31
  56.7 0.0 collective-permute-done.3
  56.7 0.0 collective-permute-done.5
  56.8 0.1 pad_maximum_fusion
  56.9 0.0 all-to-all-done
  56.9 0.0 copy-start
  56.9 0.2 broadcast_in_dim.7
  57.2 5.4 %all_to_all.20 = bf16[2,4,4,128,256]{4,3,2,1,0:T(8,128)(2,1)S(1)} all-to-all(bf16[2,4,4,128,256]{4,3,2,1,0:T(8,128)(2,1)S(1)} %broadcast_in_dim.7), channel_id=1, replica_groups=mesh['zh'=4,'yk'=4,'yl'=2,'zl'=2,'x'=4,'core'=2] {'core'}, dimensions={0} | all-to-all | bytes 4194304 | tf_op jit(solution)/shard_map/all_to_all | solution.py:26
  62.6 0.0 copy-done
  62.6 5.7 %shard_map.41 = (bf16[16,2,128,256]{3,2,1,0:T(8,128)(2,1)}, bf16[2048,256]{1,0:T(8,128)(2,1)S(1)}, bf16[2048,512]{1,0:T(8,128)(2,1)S(1)}, bf16[256,512]{1,0:T(8,128)(2,1)S(1)}, f32[8,256]{1,0:T(8,128)S(1)}) custom-call(s32[3]{0:T(128)S(1)} %pad_add_fusion.place_ref, bf16[2048,256]{1,0:T(8,128)(2,1)} %bitcast.52, bf16[2,2,2,4,128,256]{5,4,3,2,1,0:T(8,128)(2,1)S(1)} %bitcast.48), custom_call_target="tpu_custom_call" | custom-call | flops 1073741824 | bytes 8388608 | tf_op jit(solution)/shard_map/pallas_call | solution.py:193
  68.3 4.8 %all-to-all-start.3 = ((bf16[2,4,4,128,256]{4,3,2,1,0:T(8,128)(2,1)}), bf16[2,4,4,128,256]{4,3,2,1,0:T(8,128)(2,1)}, u32[]{:S(2)}, u32[]{:S(2)}) async-start(bf16[2,4,4,128,256]{4,3,2,1,0:T(8,128)(2,1)} %bitcast.51), calls=%async_computation.3 | async-start | bytes 4194304 | tf_op jit(solution)/shard_map/all_to_all | solution.py:26
  73.1 2.3 %shard_map.42 = bf16[2048,256]{1,0:T(8,128)(2,1)} custom-call(s32[3]{0:T(128)S(1)} %pad_add_fusion.place_ref, bf16[2048,256]{1,0:T(8,128)(2,1)S(1)} %get-tuple-element.11.na_ref, bf16[2048,512]{1,0:T(8,128)(2,1)S(1)} %get-tuple-element.12.nb_ref, bf16[256,512]{1,0:T(8,128)(2,1)S(1)} %get-tuple-element.13.grad_ref, f32[8,256]{1,0:T(8,128)S(1)} %get-tuple-element.14.vectors_ref), custom_call_target="tpu_custom_call" | custom-call | flops 536870912 | bytes 4194304 | tf_op jit(solution)/shard_map/pallas_call | solution.py:213
  75.4 0.7 all-to-all-done.3
  76.1 10.1 %all-to-all-start.2 = ((bf16[32,64,256]{2,1,0:T(8,128)(2,1)}), bf16[32,64,256]{2,1,0:T(8,128)(2,1)S(1)}, u32[]{:S(2)}, u32[]{:S(2)}) async-start(bf16[32,64,256]{2,1,0:T(8,128)(2,1)} %bitcast.49), calls=%async_computation.2 | async-start | bytes 2097152 | tf_op jit(solution)/shard_map/all_to_all | solution.py:26
  86.2 1.9 %add_convert_fusion = bf16[1,4,4,128,256]{4,3,2,1,0:T(8,128)(2,1)S(1)} fusion(bf16[2,4,4,128,256]{4,3,2,1,0:T(8,128)(2,1)} %all-to-all-done.3), kind=kLoop, calls=%fused_computation | loop fusion | flops 2097152 | bytes 3145728 | tf_op jit(solution)/shard_map/convert_element_type | solution.py:39
  88.0 0.1 slice_bitcast_fusion.2
  88.1 2.4 %collective-permute-start.6 = (bf16[4,128,256]{2,1,0:T(8,128)(2,1)S(1)}, bf16[4,128,256]{2,1,0:T(8,128)(2,1)S(1)}, u32[]{:S(2)}, u32[]{:S(2)}) collective-permute-start(bf16[4,128,256]{2,1,0:T(8,128)(2,1)S(1)} %get-tuple-element.16), channel_id=1, source_target_pairs={{0,2},{2,4},{4,6},{6,0},{1,3},{3,5},{5,7},{7,1},{8,10},{10,12},{12... | collective-permute-start | bytes 786440 | tf_op jit(solution)/shard_map/ppermute | solution.py:35
  90.5 3.5 %collective-permute-start.8 = (bf16[4,128,256]{2,1,0:T(8,128)(2,1)S(1)}, bf16[4,128,256]{2,1,0:T(8,128)(2,1)S(1)}, u32[]{:S(2)}, u32[]{:S(2)}) collective-permute-start(bf16[4,128,256]{2,1,0:T(8,128)(2,1)S(1)} %get-tuple-element.17), channel_id=1, source_target_pairs={{0,6},{2,0},{4,2},{6,4},{1,7},{3,1},{5,3},{7,5},{8,14},{10,8},{12,... | collective-permute-start | bytes 786440 | tf_op jit(solution)/shard_map/ppermute | solution.py:35
  93.9 3.3 %collective-permute-start.7 = (bf16[4,128,256]{2,1,0:T(8,128)(2,1)S(1)}, bf16[4,128,256]{2,1,0:T(8,128)(2,1)S(1)}, u32[]{:S(2)}, u32[]{:S(2)}) collective-permute-start(bf16[4,128,256]{2,1,0:T(8,128)(2,1)S(1)} %get-tuple-element.18), channel_id=1, source_target_pairs={{0,4},{2,6},{4,0},{6,2},{1,5},{3,7},{5,1},{7,3},{8,12},{10,14},{12... | collective-permute-start | bytes 786440 | tf_op jit(solution)/shard_map/ppermute | solution.py:35
  97.3 0.8 collective-permute-done.6
  98.0 8.9 %collective-permute-done.8 = bf16[4,128,256]{2,1,0:T(8,128)(2,1)S(1)} collective-permute-done((bf16[4,128,256]{2,1,0:T(8,128)(2,1)S(1)}, bf16[4,128,256]{2,1,0:T(8,128)(2,1)S(1)}, u32[]{:S(2)}, u32[]{:S(2)}) %collective-permute-start.8) | collective-permute-done | bytes 262176 | tf_op jit(solution)/shard_map/ppermute | solution.py:35
  107.0 0.0 collective-permute-done.7
  107.0 0.1 fusion.2
  107.2 3.4 %collective-permute-start.9 = (bf16[128,256]{1,0:T(8,128)(2,1)S(1)}, bf16[128,256]{1,0:T(8,128)(2,1)S(1)}, u32[]{:S(2)}, u32[]{:S(2)}) collective-permute-start(bf16[128,256]{1,0:T(8,128)(2,1)S(1)} %get-tuple-element.19), channel_id=1, source_target_pairs={{0,16},{8,24},{16,0},{24,8},{1,17},{9,25},{17,1},{25,9},{2,18},{10... | collective-permute-start | bytes 196616 | tf_op jit(solution)/shard_map/ppermute | solution.py:31
  110.6 1.9 %collective-permute-start.11 = (bf16[128,256]{1,0:T(8,128)(2,1)S(1)}, bf16[128,256]{1,0:T(8,128)(2,1)S(1)}, u32[]{:S(2)}, u32[]{:S(2)}) collective-permute-start(bf16[128,256]{1,0:T(8,128)(2,1)S(1)} %get-tuple-element.20), channel_id=1, source_target_pairs={{0,24},{8,16},{16,8},{24,0},{1,25},{9,17},{17,9},{25,1},{2,26},{10... | collective-permute-start | bytes 196616 | tf_op jit(solution)/shard_map/ppermute | solution.py:31
  112.5 3.9 %collective-permute-start.10 = (bf16[128,256]{1,0:T(8,128)(2,1)S(1)}, bf16[128,256]{1,0:T(8,128)(2,1)S(1)}, u32[]{:S(2)}, u32[]{:S(2)}) collective-permute-start(bf16[128,256]{1,0:T(8,128)(2,1)S(1)} %get-tuple-element.21), channel_id=1, source_target_pairs={{0,8},{8,0},{16,24},{24,16},{1,9},{9,1},{17,25},{25,17},{2,10},{10... | collective-permute-start | bytes 196616 | tf_op jit(solution)/shard_map/ppermute | solution.py:31
  116.4 0.0 collective-permute-done.9
  116.4 1.2 %collective-permute-done.11 = bf16[128,256]{1,0:T(8,128)(2,1)S(1)} collective-permute-done((bf16[128,256]{1,0:T(8,128)(2,1)S(1)}, bf16[128,256]{1,0:T(8,128)(2,1)S(1)}, u32[]{:S(2)}, u32[]{:S(2)}) %collective-permute-start.11) | collective-permute-done | bytes 65568 | tf_op jit(solution)/shard_map/ppermute | solution.py:31
  117.6 1.0 collective-permute-done.10
  118.7 0.7 fusion.5
  119.3 0.0 all-to-all-done.2
  119.3 0.1 reduce_sum.12
  119.5 0.6 pad_maximum_fusion.3
  (4 shorter events, 0.1 us)
Async XLA Ops:
  0.6 17.9 %copy-start.1 = (bf16[128,256]{1,0:T(8,128)(2,1)S(1)}, bf16[128,256]{1,0:T(8,128)(2,1)}, u32[]{:S(2)}) copy-start(bf16[128,256]{1,0:T(8,128)(2,1)} %param.3) | copy-start | bytes 196612
  2.6 54.3 %all-to-all-start = ((bf16[32,64,256]{2,1,0:T(8,128)(2,1)}), bf16[32,64,256]{2,1,0:T(8,128)(2,1)S(1)}, u32[]{:S(2)}, u32[]{:S(2)}) async-start(bf16[32,64,256]{2,1,0:T(8,128)(2,1)} %bitcast.5), calls=%async_computation | async-start | bytes 2097152 | tf_op jit(solution)/shard_map/all_to_all | solution.py:26
  18.6 9.2 %collective-permute-start = (bf16[128,256]{1,0:T(8,128)(2,1)S(1)}, bf16[128,256]{1,0:T(8,128)(2,1)S(1)}, u32[]{:S(2)}, u32[]{:S(2)}) collective-permute-start(bf16[128,256]{1,0:T(8,128)(2,1)S(1)} %copy-done.1), channel_id=1, source_target_pairs={{0,6},{2,0},{4,2},{6,4},{1,7},{3,1},{5,3},{7,5},{8,14},{10,8},{12,... | collective-permute-start | bytes 196616 | tf_op jit(solution)/shard_map/ppermute | solution.py:35
  21.3 6.4 %collective-permute-start.2 = (bf16[128,256]{1,0:T(8,128)(2,1)S(1)}, bf16[128,256]{1,0:T(8,128)(2,1)S(1)}, u32[]{:S(2)}, u32[]{:S(2)}) collective-permute-start(bf16[128,256]{1,0:T(8,128)(2,1)S(1)} %copy-done.1), channel_id=1, source_target_pairs={{0,2},{2,4},{4,6},{6,0},{1,3},{3,5},{5,7},{7,1},{8,10},{10,12},{12... | collective-permute-start | bytes 196616 | tf_op jit(solution)/shard_map/ppermute | solution.py:35
  25.6 7.7 %collective-permute-start.1 = (bf16[128,256]{1,0:T(8,128)(2,1)S(1)}, bf16[128,256]{1,0:T(8,128)(2,1)S(1)}, u32[]{:S(2)}, u32[]{:S(2)}) collective-permute-start(bf16[128,256]{1,0:T(8,128)(2,1)S(1)} %copy-done.1), channel_id=1, source_target_pairs={{0,4},{2,6},{4,0},{6,2},{1,5},{3,7},{5,1},{7,3},{8,12},{10,14},{12... | collective-permute-start | bytes 196616 | tf_op jit(solution)/shard_map/ppermute | solution.py:35
  33.3 23.4 %collective-permute-start.4 = (bf16[4,128,256]{2,1,0:T(8,128)(2,1)S(1)}, bf16[4,128,256]{2,1,0:T(8,128)(2,1)S(1)}, u32[]{:S(2)}, u32[]{:S(2)}) collective-permute-start(bf16[4,128,256]{2,1,0:T(8,128)(2,1)S(1)} %get-tuple-element.23), channel_id=1, source_target_pairs={{0,8},{8,0},{16,24},{24,16},{1,9},{9,1},{17,25},{25,17},{2,10},{10... | collective-permute-start | bytes 786440 | tf_op jit(solution)/shard_map/ppermute | solution.py:31
  36.7 20.0 %collective-permute-start.3 = (bf16[4,128,256]{2,1,0:T(8,128)(2,1)S(1)}, bf16[4,128,256]{2,1,0:T(8,128)(2,1)S(1)}, u32[]{:S(2)}, u32[]{:S(2)}) collective-permute-start(bf16[4,128,256]{2,1,0:T(8,128)(2,1)S(1)} %get-tuple-element.23), channel_id=1, source_target_pairs={{0,16},{8,24},{16,0},{24,8},{1,17},{9,25},{17,1},{25,9},{2,18},{10... | collective-permute-start | bytes 786440 | tf_op jit(solution)/shard_map/ppermute | solution.py:31
  40.4 16.3 %collective-permute-start.5 = (bf16[4,128,256]{2,1,0:T(8,128)(2,1)S(1)}, bf16[4,128,256]{2,1,0:T(8,128)(2,1)S(1)}, u32[]{:S(2)}, u32[]{:S(2)}) collective-permute-start(bf16[4,128,256]{2,1,0:T(8,128)(2,1)S(1)} %get-tuple-element.23), channel_id=1, source_target_pairs={{0,24},{8,16},{16,8},{24,0},{1,25},{9,17},{17,9},{25,1},{2,26},{10... | collective-permute-start | bytes 786440 | tf_op jit(solution)/shard_map/ppermute | solution.py:31
  56.9 5.7 %copy-start = (bf16[32,64,256]{2,1,0:T(8,128)(2,1)}, bf16[32,64,256]{2,1,0:T(8,128)(2,1)S(1)}, u32[]{:S(2)}) copy-start(bf16[32,64,256]{2,1,0:T(8,128)(2,1)S(1)} %all-to-all-done) | copy-start | bytes 3145732
  68.3 7.8 %all-to-all-start.3 = ((bf16[2,4,4,128,256]{4,3,2,1,0:T(8,128)(2,1)}), bf16[2,4,4,128,256]{4,3,2,1,0:T(8,128)(2,1)}, u32[]{:S(2)}, u32[]{:S(2)}) async-start(bf16[2,4,4,128,256]{4,3,2,1,0:T(8,128)(2,1)} %bitcast.51), calls=%async_computation.3 | async-start | bytes 4194304 | tf_op jit(solution)/shard_map/all_to_all | solution.py:26
  76.1 43.3 %all-to-all-start.2 = ((bf16[32,64,256]{2,1,0:T(8,128)(2,1)}), bf16[32,64,256]{2,1,0:T(8,128)(2,1)S(1)}, u32[]{:S(2)}, u32[]{:S(2)}) async-start(bf16[32,64,256]{2,1,0:T(8,128)(2,1)} %bitcast.49), calls=%async_computation.2 | async-start | bytes 2097152 | tf_op jit(solution)/shard_map/all_to_all | solution.py:26
  88.1 10.0 %collective-permute-start.6 = (bf16[4,128,256]{2,1,0:T(8,128)(2,1)S(1)}, bf16[4,128,256]{2,1,0:T(8,128)(2,1)S(1)}, u32[]{:S(2)}, u32[]{:S(2)}) collective-permute-start(bf16[4,128,256]{2,1,0:T(8,128)(2,1)S(1)} %get-tuple-element.16), channel_id=1, source_target_pairs={{0,2},{2,4},{4,6},{6,0},{1,3},{3,5},{5,7},{7,1},{8,10},{10,12},{12... | collective-permute-start | bytes 786440 | tf_op jit(solution)/shard_map/ppermute | solution.py:35
  90.5 16.5 %collective-permute-start.8 = (bf16[4,128,256]{2,1,0:T(8,128)(2,1)S(1)}, bf16[4,128,256]{2,1,0:T(8,128)(2,1)S(1)}, u32[]{:S(2)}, u32[]{:S(2)}) collective-permute-start(bf16[4,128,256]{2,1,0:T(8,128)(2,1)S(1)} %get-tuple-element.17), channel_id=1, source_target_pairs={{0,6},{2,0},{4,2},{6,4},{1,7},{3,1},{5,3},{7,5},{8,14},{10,8},{12,... | collective-permute-start | bytes 786440 | tf_op jit(solution)/shard_map/ppermute | solution.py:35
  93.9 13.0 %collective-permute-start.7 = (bf16[4,128,256]{2,1,0:T(8,128)(2,1)S(1)}, bf16[4,128,256]{2,1,0:T(8,128)(2,1)S(1)}, u32[]{:S(2)}, u32[]{:S(2)}) collective-permute-start(bf16[4,128,256]{2,1,0:T(8,128)(2,1)S(1)} %get-tuple-element.18), channel_id=1, source_target_pairs={{0,4},{2,6},{4,0},{6,2},{1,5},{3,7},{5,1},{7,3},{8,12},{10,14},{12... | collective-permute-start | bytes 786440 | tf_op jit(solution)/shard_map/ppermute | solution.py:35
  107.2 9.2 %collective-permute-start.9 = (bf16[128,256]{1,0:T(8,128)(2,1)S(1)}, bf16[128,256]{1,0:T(8,128)(2,1)S(1)}, u32[]{:S(2)}, u32[]{:S(2)}) collective-permute-start(bf16[128,256]{1,0:T(8,128)(2,1)S(1)} %get-tuple-element.19), channel_id=1, source_target_pairs={{0,16},{8,24},{16,0},{24,8},{1,17},{9,25},{17,1},{25,9},{2,18},{10... | collective-permute-start | bytes 196616 | tf_op jit(solution)/shard_map/ppermute | solution.py:31
  110.6 7.1 %collective-permute-start.11 = (bf16[128,256]{1,0:T(8,128)(2,1)S(1)}, bf16[128,256]{1,0:T(8,128)(2,1)S(1)}, u32[]{:S(2)}, u32[]{:S(2)}) collective-permute-start(bf16[128,256]{1,0:T(8,128)(2,1)S(1)} %get-tuple-element.20), channel_id=1, source_target_pairs={{0,24},{8,16},{16,8},{24,0},{1,25},{9,17},{17,9},{25,1},{2,26},{10... | collective-permute-start | bytes 196616 | tf_op jit(solution)/shard_map/ppermute | solution.py:31
  112.5 6.2 %collective-permute-start.10 = (bf16[128,256]{1,0:T(8,128)(2,1)S(1)}, bf16[128,256]{1,0:T(8,128)(2,1)S(1)}, u32[]{:S(2)}, u32[]{:S(2)}) collective-permute-start(bf16[128,256]{1,0:T(8,128)(2,1)S(1)} %get-tuple-element.21), channel_id=1, source_target_pairs={{0,8},{8,0},{16,24},{24,16},{1,9},{9,1},{17,25},{25,17},{2,10},{10... | collective-permute-start | bytes 196616 | tf_op jit(solution)/shard_map/ppermute | solution.py:31

commit v8 on v6

--- a/solution.py
+++ b/solution.py
@@ -12,6 +12,7 @@
 
 SAMPLES = ("zh", "yk", "yl")
 FEATURES = ("zl", "x", "core")
+NEAR = ("yl", "zl")
 F32 = jnp.float32
 BF16 = jnp.bfloat16
 HIGHEST = lax.Precision.HIGHEST
@@ -28,7 +29,7 @@
 
 def near_swap(values, move):
     flip = 2 * (move % 2) + move // 2
-    return lax.ppermute(values, ("yl", "zl"), [(i, i ^ flip) for i in range(4)])
+    return lax.ppermute(values, NEAR, [(i, i ^ flip) for i in range(4)])
 
 
 def shift(values, distance):
@@ -64,8 +65,8 @@
 
 
 def tile_kernel(
-    place_ref, first_hbm, second_ref, moved_hbm, na_ref, nb_ref, grad_ref, vectors_ref,
-    first_ref, moved_ref, load_sem, store_sems,
+    place_ref, first_hbm, second_ref, moved_hbm, out_hbm,
+    first_ref, na_ref, nb_ref, moved_ref, out_ref, load_sem, moved_sems, out_sems,
 ):
     count = BLOCK * BLOCKS
     width = first_ref.shape[1]
@@ -75,7 +76,10 @@
     scales = []
     means = []
     for i in range(2):
-        load = lambda t: second_ref[t, i].astype(F32)
+        y = lax.rem(place_ref[3] + i, 2)
+        load = lambda t: second_ref[
+            t // 8, (t // 2) % 4, y, lax.rem(place_ref[1] + t % 2, 2)
+        ].astype(F32)
         center, scale = column_statistics(load, BLOCKS, count)
         sums = jnp.zeros((8, width), F32)
         for t in range(BLOCKS):
@@ -111,7 +115,6 @@
         2.0 * (correlation - 1.0),
         2.0 * OFF_WEIGHT * correlation,
     ).astype(BF16)
-    grad_ref[...] = grad
     grad_wide = grad.astype(F32)
     weighted = grad_wide * correlation
     projection_second = jnp.sum(weighted, axis=0, keepdims=True)
@@ -134,7 +137,7 @@
             )
         part = pl.ds(start, CHUNK)
         store = pltpu.make_async_copy(
-            moved_ref.at[part], moved_hbm.at[part], store_sems.at[start // CHUNK]
+            moved_ref.at[part], moved_hbm.at[part], moved_sems.at[start // CHUNK]
         )
         store.start()
         stores.append(store)
@@ -151,30 +154,18 @@
         axis=0,
         keepdims=True,
     )
-    vectors_ref[0:1, :] = centering_first
-    vectors_ref[1:2, :] = projection_first[0:1]
-    vectors_ref[2:3, :] = scale_first
-    vectors_ref[3:8, :] = jnp.zeros((5, width), F32)
-    for store in stores:
-        store.wait()
-
-
-def first_kernel(place_ref, na_ref, nb_ref, grad_ref, vectors_ref, out_hbm, out_ref, store_sems):
-    grad = grad_ref[...]
-    centering, projection, scale = (vectors_ref[i : i + 1, :] for i in range(3))
-    stores = []
     for start in range(0, BLOCKS, CHUNK):
         some = slice(start * BLOCK, (start + CHUNK) * BLOCK)
-        partial = lax.dot_general(
-            nb_ref[some, :], grad, (((1,), (1,)), ((), ())), preferred_element_type=F32
-        )
-        partial = (partial - centering - na_ref[some, :].astype(F32) * projection) * scale
+        partial = lax.dot_general(nb_ref[some, :], grad, across, preferred_element_type=F32)
+        partial = (
+            partial - centering_first - na_ref[some, :].astype(F32) * projection_first[0:1]
+        ) * scale_first
         out_ref[some, :] = partial.astype(BF16)
         for t in range(start, start + CHUNK):
             store = pltpu.make_async_copy(
                 out_ref.at[pl.ds(t * BLOCK, BLOCK)],
                 out_hbm.at[pl.ds(sample_row(place_ref, t), BLOCK)],
-                store_sems.at[t],
+                out_sems.at[t],
             )
             store.start()
             stores.append(store)
@@ -184,41 +175,29 @@
 
 def local_compute(place, first, second):
     count, width = first.shape
-    shape = jax.ShapeDtypeStruct
+    pieces = (BLOCKS, 2, BLOCK, width)
     smem, vmem, hbm = (pl.BlockSpec(memory_space=m) for m in (pltpu.SMEM, pltpu.VMEM, pltpu.HBM))
-    params = pltpu.CompilerParams(vmem_limit_bytes=VMEM_LIMIT)
-    flops = 2 * count * width * 2 * width
     first = pltpu.with_memory_space_constraint(first, pltpu.HBM)
-    moved, *kept = pl.pallas_call(
+    return pl.pallas_call(
         tile_kernel,
-        out_shape=(
-            pltpu.HBM(second.shape, BF16),
-            shape((count, width), BF16),
-            shape((count, 2 * width), BF16),
-            shape((width, 2 * width), BF16),
-            shape((8, width), F32),
-        ),
+        out_shape=(pltpu.HBM(pieces, BF16), pltpu.HBM((count, width), BF16)),
         in_specs=[smem, hbm, vmem],
-        out_specs=(hbm, vmem, vmem, vmem, vmem),
+        out_specs=(hbm, hbm),
         scratch_shapes=[
             pltpu.VMEM((count, width), BF16),
-            pltpu.VMEM(second.shape, BF16),
+            pltpu.VMEM((count, width), BF16),
+            pltpu.VMEM((count, 2 * width), BF16),
+            pltpu.VMEM(pieces, BF16),
+            pltpu.VMEM((count, width), BF16),
             pltpu.SemaphoreType.DMA,
             pltpu.SemaphoreType.DMA((BLOCKS // CHUNK,)),
+            pltpu.SemaphoreType.DMA((BLOCKS,)),
         ],
-        compiler_params=params,
-        cost_estimate=pl.CostEstimate(flops=2 * flops, bytes_accessed=8 << 20, transcendentals=0),
+        compiler_params=pltpu.CompilerParams(vmem_limit_bytes=VMEM_LIMIT),
+        cost_estimate=pl.CostEstimate(
+            flops=12 * count * width * width, bytes_accessed=6 << 20, transcendentals=0
+        ),
     )(place, first, second)
-    partial_first = pl.pallas_call(
-        first_kernel,
-        out_shape=pltpu.HBM((count, width), BF16),
-        in_specs=[smem, vmem, vmem, vmem, vmem],
-        out_specs=hbm,
-        scratch_shapes=[pltpu.VMEM((count, width), BF16), pltpu.SemaphoreType.DMA((BLOCKS,))],
-        compiler_params=params,
-        cost_estimate=pl.CostEstimate(flops=flops, bytes_accessed=4 << 20, transcendentals=0),
-    )(place, *kept)
-    return moved, partial_first
 
 
 def shards(first_view_outputs, second_view_outputs):
@@ -228,18 +207,17 @@
     half = width_a // 2
     total_count = rows_a * n_dp
 
-    near = [near_swap(second_view_outputs, k) for k in (1, 2, 3)]
+    near = exchange(jnp.broadcast_to(second_view_outputs, (4, rows_b, width_b)), NEAR)
     halves = jnp.stack([first_view_outputs[:, :half], first_view_outputs[:, half:]])
     spread = jnp.broadcast_to(halves, (n_dp // 2, 2, rows_a, half)).reshape(n_dp, rows_a, half)
     near, spread = lax.optimization_barrier((near, spread))
-    near = jnp.stack([second_view_outputs] + near)
 
     first = exchange(spread, SAMPLES).reshape(total_count, half)
 
     ahead = jnp.stack([near] + [shift(near, -k) for k in (1, 2, 3)])
     ahead = jnp.broadcast_to(ahead, (2,) + ahead.shape)
     first, ahead = lax.optimization_barrier((first, ahead))
-    second = exchange(ahead, "core").reshape(BLOCKS, 2, rows_b, width_b)
+    second = exchange(ahead, "core").reshape(2, 4, 2, 2, rows_b, width_b)
 
     feat = lax.axis_index(FEATURES)
     pair = lax.axis_index(("zh", "yk"))
@@ -248,6 +226,7 @@
             lax.axis_index("x"),
             lax.axis_index("zl"),
             jnp.where(feat == pair, 0, 2 * width_a),
+            lax.axis_index("yl"),
         ]
     ).astype(jnp.int32)
     moved, partial_first = local_compute(place, first, second)

time: 121 us -> 119 us (0.983)
  starting transfers between devices: 64.8 us -> 53.7 us
  blocking collectives: 5.42 us -> 12 us
  waiting for transfers between devices: 34.9 us -> 38 us
  other arithmetic: 3.71 us -> 2.12 us
  local copies, waits for them, and re-layouts: 2.21 us -> 3.76 us
    ppermute x6 -> x3, starting transfers between devices: 19 us -> 9.21 us  [near_swap(): return lax.ppermute(values, NEAR, [(i, i ^ flip) for i in range(4)])]
    all_to_all x1 -> x2, blocking collectives: 5.42 us -> 12 us  [exchange(): return lax.all_to_all(values, axes, 0, 0, tiled=True)]
    ppermute x6, waiting for transfers between devices: 14.3 us -> 19.5 us  [shift(): lax.ppermute(values, 'x', [(i, (i + distance) % 4) for i in range(4)])]
    ppermute x6 -> x3, waiting for transfers between devices: 7.31 us -> 3.28 us  [near_swap(): return lax.ppermute(values, NEAR, [(i, i ^ flip) for i in range(4)])]
    all_to_all x3, waiting for transfers between devices: 13.2 us -> 15.2 us  [exchange(): return lax.all_to_all(values, axes, 0, 0, tiled=True)]
    ppermute x6, starting transfers between devices: 19.5 us -> 17.8 us  [shift(): lax.ppermute(values, 'x', [(i, (i + distance) % 4) for i in range(4)])]
    broadcast_in_dim x0 -> x1, local copies, waits for them, and re-layouts: none -> 1.56 us  [shards(): jnp.broadcast_to(second_view_outputs, (4, rows_b, width_b))]
    convert_element_type x3, other arithmetic: 2.66 us -> 1.12 us  [narrow_sum(): return sum((term.astype(F32) for term in terms)).astype(BF16)]
  transfers between devices with their start and end apart: 15 -> 12, of which waited for: 10 -> 9; matrix products, arithmetic and copies ran while one was open for 3% -> 2% of each run, Pallas kernels for 2% -> 0%
where the time goes in v8:
time: 119 us; the launch traced here: 118 us
  starting transfers between devices  53.7 us (45%)
  waiting for transfers between devices  38 us (32%)
  blocking collectives  12 us (10%)
  Pallas kernels  7.12 us (6%)
  local copies, waits for them, and re-layouts  3.76 us (3%)
  other arithmetic  2.12 us (2%)
    all_to_all x3, starting transfers between devices, exchange(): return lax.all_to_all(values, axes, 0, 0, tiled=True)  26.7 us
    ppermute x6, waiting for transfers between devices, shift(): lax.ppermute(values, 'x', [(i, (i + distance) % 4) for i in range(4)])  19.5 us
    ppermute x6, starting transfers between devices, shift(): lax.ppermute(values, 'x', [(i, (i + distance) % 4) for i in range(4)])  17.8 us
    all_to_all x3, waiting for transfers between devices, exchange(): return lax.all_to_all(values, axes, 0, 0, tiled=True)  15.2 us
    all_to_all x2, blocking collectives, exchange(): return lax.all_to_all(values, axes, 0, 0, tiled=True)  12 us
    ppermute x3, starting transfers between devices, near_swap(): return lax.ppermute(values, NEAR, [(i, i ^ flip) for i in range(4)])  9.21 us
    pallas_call x1, Pallas kernels, local_compute(): pl.pallas_call(tile_kernel, out_shape=(pltpu.HBM(pieces, BF16), pltpu.HBM...  7.12 us
    ppermute x3, waiting for transfers between devices, near_swap(): return lax.ppermute(values, NEAR, [(i, i ^ flip) for i in range(4)])  3.28 us
  transfers between devices with their start and end apart: 12, of which 9 were waited for; matrix products, arithmetic and copies ran while one was open for 2% of the time, Pallas kernels for 0%

profile of v8, /device:TPU:6, one launch (start us, length us, event | category | flops | bytes accessed | tf_op | source)
XLA Modules:
  0.0 117.5 jit_solution(10334143275992909526)
XLA Ops:
  0.6 1.6 %broadcast_in_dim.9 = bf16[4,128,256]{2,1,0:T(8,128)(2,1)} broadcast(bf16[128,256]{1,0:T(8,128)(2,1)} %param.3), dimensions={1,2} | broadcast | bytes 327680 | tf_op jit(solution)/shard_map/broadcast_in_dim | solution.py:210
  2.2 4.7 %all-to-all-start = ((bf16[4,128,256]{2,1,0:T(8,128)(2,1)}), bf16[4,128,256]{2,1,0:T(8,128)(2,1)S(1)}, u32[]{:S(2)}, u32[]{:S(2)}) async-start(bf16[4,128,256]{2,1,0:T(8,128)(2,1)} %broadcast_in_dim.9), calls=%async_computation | async-start | bytes 524288 | tf_op jit(solution)/shard_map/all_to_all | solution.py:27
  6.8 0.8 slice_bitcast_fusion.11
  7.6 4.6 %all-to-all-done = bf16[4,128,256]{2,1,0:T(8,128)(2,1)S(1)} async-done(((bf16[4,128,256]{2,1,0:T(8,128)(2,1)}), bf16[4,128,256]{2,1,0:T(8,128)(2,1)S(1)}, u32[]{:S(2)}, u32[]{:S(2)}) %all-to-all-start) | async-done | bytes 262176 | tf_op jit(solution)/shard_map/all_to_all | solution.py:27
  12.2 1.1 broadcast_in_dim.10
  13.3 15.0 %all-to-all-start.1 = ((bf16[32,64,256]{2,1,0:T(8,128)(2,1)}), bf16[32,64,256]{2,1,0:T(8,128)(2,1)S(1)}, u32[]{:S(2)}, u32[]{:S(2)}) async-start(bf16[32,64,256]{2,1,0:T(8,128)(2,1)} %bitcast.6), calls=%async_computation.1 | async-start | bytes 2097152 | tf_op jit(solution)/shard_map/all_to_all | solution.py:27
  28.3 2.4 %collective-permute-start.2 = (bf16[4,128,256]{2,1,0:T(8,128)(2,1)S(1)}, bf16[4,128,256]{2,1,0:T(8,128)(2,1)S(1)}, u32[]{:S(2)}, u32[]{:S(2)}) collective-permute-start(bf16[4,128,256]{2,1,0:T(8,128)(2,1)S(1)} %all-to-all-done), channel_id=1, source_target_pairs={{0,2},{2,4},{4,6},{6,0},{1,3},{3,5},{5,7},{7,1},{8,10},{10,12},{12... | collective-permute-start | bytes 786440 | tf_op jit(solution)/shard_map/ppermute | solution.py:36
  30.7 4.3 %collective-permute-start.1 = (bf16[4,128,256]{2,1,0:T(8,128)(2,1)S(1)}, bf16[4,128,256]{2,1,0:T(8,128)(2,1)S(1)}, u32[]{:S(2)}, u32[]{:S(2)}) collective-permute-start(bf16[4,128,256]{2,1,0:T(8,128)(2,1)S(1)} %all-to-all-done), channel_id=1, source_target_pairs={{0,4},{2,6},{4,0},{6,2},{1,5},{3,7},{5,1},{7,3},{8,12},{10,14},{12... | collective-permute-start | bytes 786440 | tf_op jit(solution)/shard_map/ppermute | solution.py:36
  35.0 1.9 %collective-permute-start = (bf16[4,128,256]{2,1,0:T(8,128)(2,1)S(1)}, bf16[4,128,256]{2,1,0:T(8,128)(2,1)S(1)}, u32[]{:S(2)}, u32[]{:S(2)}) collective-permute-start(bf16[4,128,256]{2,1,0:T(8,128)(2,1)S(1)} %all-to-all-done), channel_id=1, source_target_pairs={{0,6},{2,0},{4,2},{6,4},{1,7},{3,1},{5,3},{7,5},{8,14},{10,8},{12,... | collective-permute-start | bytes 786440 | tf_op jit(solution)/shard_map/ppermute | solution.py:36
  37.0 0.1 pad_add_fusion.place_ref
  37.0 2.4 %collective-permute-done.2 = bf16[4,128,256]{2,1,0:T(8,128)(2,1)S(1)} collective-permute-done((bf16[4,128,256]{2,1,0:T(8,128)(2,1)S(1)}, bf16[4,128,256]{2,1,0:T(8,128)(2,1)S(1)}, u32[]{:S(2)}, u32[]{:S(2)}) %collective-permute-start.2) | collective-permute-done | bytes 262176 | tf_op jit(solution)/shard_map/ppermute | solution.py:36
  39.4 3.5 %collective-permute-done.1 = bf16[4,128,256]{2,1,0:T(8,128)(2,1)S(1)} collective-permute-done((bf16[4,128,256]{2,1,0:T(8,128)(2,1)S(1)}, bf16[4,128,256]{2,1,0:T(8,128)(2,1)S(1)}, u32[]{:S(2)}, u32[]{:S(2)}) %collective-permute-start.1) | collective-permute-done | bytes 262176 | tf_op jit(solution)/shard_map/ppermute | solution.py:36
  42.9 3.9 %collective-permute-done = bf16[4,128,256]{2,1,0:T(8,128)(2,1)S(1)} collective-permute-done((bf16[4,128,256]{2,1,0:T(8,128)(2,1)S(1)}, bf16[4,128,256]{2,1,0:T(8,128)(2,1)S(1)}, u32[]{:S(2)}, u32[]{:S(2)}) %collective-permute-start) | collective-permute-done | bytes 262176 | tf_op jit(solution)/shard_map/ppermute | solution.py:36
  46.8 0.1 pad_maximum_fusion
  46.9 10.7 %all-to-all-done.1 = bf16[32,64,256]{2,1,0:T(8,128)(2,1)S(1)} async-done(((bf16[32,64,256]{2,1,0:T(8,128)(2,1)}), bf16[32,64,256]{2,1,0:T(8,128)(2,1)S(1)}, u32[]{:S(2)}, u32[]{:S(2)}) %all-to-all-start.1) | async-done | bytes 1048608 | tf_op jit(solution)/shard_map/all_to_all | solution.py:27
  57.6 0.0 copy-start
  57.6 0.2 broadcast_in_dim.11
  57.8 5.4 %all_to_all.25 = bf16[2,4,4,128,256]{4,3,2,1,0:T(8,128)(2,1)S(1)} all-to-all(bf16[2,4,4,128,256]{4,3,2,1,0:T(8,128)(2,1)S(1)} %broadcast_in_dim.11), channel_id=1, replica_groups=mesh['zh'=4,'yk'=4,'yl'=2,'zl'=2,'x'=4,'core'=2] {'core'}, dimensions={0} | all-to-all | bytes 4194304 | tf_op jit(solution)/shard_map/all_to_all | solution.py:27
  63.3 0.0 copy-done
  63.3 7.1 %shard_map.41 = (bf16[16,2,128,256]{3,2,1,0:T(8,128)(2,1)}, bf16[2048,256]{1,0:T(8,128)(2,1)}) custom-call(s32[4]{0:T(128)S(1)} %pad_add_fusion.place_ref, bf16[2048,256]{1,0:T(8,128)(2,1)} %bitcast.47, bf16[2,4,2,2,128,256]{5,4,3,2,1,0:T(8,128)(2,1)S(1)} %bitcast.44), custom_call_target="tpu_custom_call" | custom-call | flops 1610612736 | bytes 6291456 | tf_op jit(solution)/shard_map/pallas_call | solution.py:181
  70.4 6.6 %all_to_all.26 = bf16[2,4,4,128,256]{4,3,2,1,0:T(8,128)(2,1)S(1)} all-to-all(bf16[2,4,4,128,256]{4,3,2,1,0:T(8,128)(2,1)} %bitcast.46), channel_id=1, replica_groups=mesh['zh'=4,'yk'=4,'yl'=2,'zl'=2,'x'=4,'core'=2] {'core'}, dimensions={0} | all-to-all | bytes 4194304 | tf_op jit(solution)/shard_map/all_to_all | solution.py:27
  77.0 7.1 %all-to-all-start.3 = ((bf16[32,64,256]{2,1,0:T(8,128)(2,1)}), bf16[32,64,256]{2,1,0:T(8,128)(2,1)S(1)}, u32[]{:S(2)}, u32[]{:S(2)}) async-start(bf16[32,64,256]{2,1,0:T(8,128)(2,1)} %bitcast.48), calls=%async_computation.3 | async-start | bytes 2097152 | tf_op jit(solution)/shard_map/all_to_all | solution.py:27
  84.1 0.3 add_convert_fusion
  84.4 0.1 slice_bitcast_fusion.2
  84.5 2.4 %collective-permute-start.3 = (bf16[4,128,256]{2,1,0:T(8,128)(2,1)S(1)}, bf16[4,128,256]{2,1,0:T(8,128)(2,1)S(1)}, u32[]{:S(2)}, u32[]{:S(2)}) collective-permute-start(bf16[4,128,256]{2,1,0:T(8,128)(2,1)S(1)} %get-tuple-element.14), channel_id=1, source_target_pairs={{0,2},{2,4},{4,6},{6,0},{1,3},{3,5},{5,7},{7,1},{8,10},{10,12},{12... | collective-permute-start | bytes 786440 | tf_op jit(solution)/shard_map/ppermute | solution.py:36
  86.9 3.5 %collective-permute-start.5 = (bf16[4,128,256]{2,1,0:T(8,128)(2,1)S(1)}, bf16[4,128,256]{2,1,0:T(8,128)(2,1)S(1)}, u32[]{:S(2)}, u32[]{:S(2)}) collective-permute-start(bf16[4,128,256]{2,1,0:T(8,128)(2,1)S(1)} %get-tuple-element.15), channel_id=1, source_target_pairs={{0,6},{2,0},{4,2},{6,4},{1,7},{3,1},{5,3},{7,5},{8,14},{10,8},{12,... | collective-permute-start | bytes 786440 | tf_op jit(solution)/shard_map/ppermute | solution.py:36
  90.3 3.3 %collective-permute-start.4 = (bf16[4,128,256]{2,1,0:T(8,128)(2,1)S(1)}, bf16[4,128,256]{2,1,0:T(8,128)(2,1)S(1)}, u32[]{:S(2)}, u32[]{:S(2)}) collective-permute-start(bf16[4,128,256]{2,1,0:T(8,128)(2,1)S(1)} %get-tuple-element.16), channel_id=1, source_target_pairs={{0,4},{2,6},{4,0},{6,2},{1,5},{3,7},{5,1},{7,3},{8,12},{10,14},{12... | collective-permute-start | bytes 786440 | tf_op jit(solution)/shard_map/ppermute | solution.py:36
  93.6 0.8 collective-permute-done.3
  94.4 8.9 %collective-permute-done.5 = bf16[4,128,256]{2,1,0:T(8,128)(2,1)S(1)} collective-permute-done((bf16[4,128,256]{2,1,0:T(8,128)(2,1)S(1)}, bf16[4,128,256]{2,1,0:T(8,128)(2,1)S(1)}, u32[]{:S(2)}, u32[]{:S(2)}) %collective-permute-start.5) | collective-permute-done | bytes 262176 | tf_op jit(solution)/shard_map/ppermute | solution.py:36
  103.4 0.0 collective-permute-done.4
  103.4 0.1 fusion.2
  103.5 3.4 %collective-permute-start.6 = (bf16[128,256]{1,0:T(8,128)(2,1)S(1)}, bf16[128,256]{1,0:T(8,128)(2,1)S(1)}, u32[]{:S(2)}, u32[]{:S(2)}) collective-permute-start(bf16[128,256]{1,0:T(8,128)(2,1)S(1)} %get-tuple-element.17), channel_id=1, source_target_pairs={{0,16},{8,24},{16,0},{24,8},{1,17},{9,25},{17,1},{25,9},{2,18},{10... | collective-permute-start | bytes 196616 | tf_op jit(solution)/shard_map/ppermute | solution.py:32
  107.0 2.9 %collective-permute-start.8 = (bf16[128,256]{1,0:T(8,128)(2,1)S(1)}, bf16[128,256]{1,0:T(8,128)(2,1)S(1)}, u32[]{:S(2)}, u32[]{:S(2)}) collective-permute-start(bf16[128,256]{1,0:T(8,128)(2,1)S(1)} %get-tuple-element.18), channel_id=1, source_target_pairs={{0,24},{8,16},{16,8},{24,0},{1,25},{9,17},{17,9},{25,1},{2,26},{10... | collective-permute-start | bytes 196616 | tf_op jit(solution)/shard_map/ppermute | solution.py:32
  109.9 2.9 %collective-permute-start.7 = (bf16[128,256]{1,0:T(8,128)(2,1)S(1)}, bf16[128,256]{1,0:T(8,128)(2,1)S(1)}, u32[]{:S(2)}, u32[]{:S(2)}) collective-permute-start(bf16[128,256]{1,0:T(8,128)(2,1)S(1)} %get-tuple-element.19), channel_id=1, source_target_pairs={{0,8},{8,0},{16,24},{24,16},{1,9},{9,1},{17,25},{25,17},{2,10},{10... | collective-permute-start | bytes 196616 | tf_op jit(solution)/shard_map/ppermute | solution.py:32
  112.8 0.0 collective-permute-done.6
  112.8 1.2 %collective-permute-done.8 = bf16[128,256]{1,0:T(8,128)(2,1)S(1)} collective-permute-done((bf16[128,256]{1,0:T(8,128)(2,1)S(1)}, bf16[128,256]{1,0:T(8,128)(2,1)S(1)}, u32[]{:S(2)}, u32[]{:S(2)}) %collective-permute-start.8) | collective-permute-done | bytes 65568 | tf_op jit(solution)/shard_map/ppermute | solution.py:32
  114.0 2.0 %collective-permute-done.7 = bf16[128,256]{1,0:T(8,128)(2,1)S(1)} collective-permute-done((bf16[128,256]{1,0:T(8,128)(2,1)S(1)}, bf16[128,256]{1,0:T(8,128)(2,1)S(1)}, u32[]{:S(2)}, u32[]{:S(2)}) %collective-permute-start.7) | collective-permute-done | bytes 65568 | tf_op jit(solution)/shard_map/ppermute | solution.py:32
  116.1 0.7 fusion.5
  116.7 0.0 all-to-all-done.3
  116.7 0.1 reduce_sum.12
  116.9 0.6 pad_maximum_fusion.2
  (3 shorter events, 0.0 us)
Async XLA Ops:
  2.2 10.0 %all-to-all-start = ((bf16[4,128,256]{2,1,0:T(8,128)(2,1)}), bf16[4,128,256]{2,1,0:T(8,128)(2,1)S(1)}, u32[]{:S(2)}, u32[]{:S(2)}) async-start(bf16[4,128,256]{2,1,0:T(8,128)(2,1)} %broadcast_in_dim.9), calls=%async_computation | async-start | bytes 524288 | tf_op jit(solution)/shard_map/all_to_all | solution.py:27
  13.3 44.3 %all-to-all-start.1 = ((bf16[32,64,256]{2,1,0:T(8,128)(2,1)}), bf16[32,64,256]{2,1,0:T(8,128)(2,1)S(1)}, u32[]{:S(2)}, u32[]{:S(2)}) async-start(bf16[32,64,256]{2,1,0:T(8,128)(2,1)} %bitcast.6), calls=%async_computation.1 | async-start | bytes 2097152 | tf_op jit(solution)/shard_map/all_to_all | solution.py:27
  28.3 11.1 %collective-permute-start.2 = (bf16[4,128,256]{2,1,0:T(8,128)(2,1)S(1)}, bf16[4,128,256]{2,1,0:T(8,128)(2,1)S(1)}, u32[]{:S(2)}, u32[]{:S(2)}) collective-permute-start(bf16[4,128,256]{2,1,0:T(8,128)(2,1)S(1)} %all-to-all-done), channel_id=1, source_target_pairs={{0,2},{2,4},{4,6},{6,0},{1,3},{3,5},{5,7},{7,1},{8,10},{10,12},{12... | collective-permute-start | bytes 786440 | tf_op jit(solution)/shard_map/ppermute | solution.py:36
  30.7 12.3 %collective-permute-start.1 = (bf16[4,128,256]{2,1,0:T(8,128)(2,1)S(1)}, bf16[4,128,256]{2,1,0:T(8,128)(2,1)S(1)}, u32[]{:S(2)}, u32[]{:S(2)}) collective-permute-start(bf16[4,128,256]{2,1,0:T(8,128)(2,1)S(1)} %all-to-all-done), channel_id=1, source_target_pairs={{0,4},{2,6},{4,0},{6,2},{1,5},{3,7},{5,1},{7,3},{8,12},{10,14},{12... | collective-permute-start | bytes 786440 | tf_op jit(solution)/shard_map/ppermute | solution.py:36
  35.0 11.8 %collective-permute-start = (bf16[4,128,256]{2,1,0:T(8,128)(2,1)S(1)}, bf16[4,128,256]{2,1,0:T(8,128)(2,1)S(1)}, u32[]{:S(2)}, u32[]{:S(2)}) collective-permute-start(bf16[4,128,256]{2,1,0:T(8,128)(2,1)S(1)} %all-to-all-done), channel_id=1, source_target_pairs={{0,6},{2,0},{4,2},{6,4},{1,7},{3,1},{5,3},{7,5},{8,14},{10,8},{12,... | collective-permute-start | bytes 786440 | tf_op jit(solution)/shard_map/ppermute | solution.py:36
  57.6 5.7 %copy-start = (bf16[32,64,256]{2,1,0:T(8,128)(2,1)}, bf16[32,64,256]{2,1,0:T(8,128)(2,1)S(1)}, u32[]{:S(2)}) copy-start(bf16[32,64,256]{2,1,0:T(8,128)(2,1)S(1)} %all-to-all-done.1) | copy-start | bytes 3145732
  77.0 39.7 %all-to-all-start.3 = ((bf16[32,64,256]{2,1,0:T(8,128)(2,1)}), bf16[32,64,256]{2,1,0:T(8,128)(2,1)S(1)}, u32[]{:S(2)}, u32[]{:S(2)}) async-start(bf16[32,64,256]{2,1,0:T(8,128)(2,1)} %bitcast.48), calls=%async_computation.3 | async-start | bytes 2097152 | tf_op jit(solution)/shard_map/all_to_all | solution.py:27
  84.5 10.0 %collective-permute-start.3 = (bf16[4,128,256]{2,1,0:T(8,128)(2,1)S(1)}, bf16[4,128,256]{2,1,0:T(8,128)(2,1)S(1)}, u32[]{:S(2)}, u32[]{:S(2)}) collective-permute-start(bf16[4,128,256]{2,1,0:T(8,128)(2,1)S(1)} %get-tuple-element.14), channel_id=1, source_target_pairs={{0,2},{2,4},{4,6},{6,0},{1,3},{3,5},{5,7},{7,1},{8,10},{10,12},{12... | collective-permute-start | bytes 786440 | tf_op jit(solution)/shard_map/ppermute | solution.py:36
  86.9 16.5 %collective-permute-start.5 = (bf16[4,128,256]{2,1,0:T(8,128)(2,1)S(1)}, bf16[4,128,256]{2,1,0:T(8,128)(2,1)S(1)}, u32[]{:S(2)}, u32[]{:S(2)}) collective-permute-start(bf16[4,128,256]{2,1,0:T(8,128)(2,1)S(1)} %get-tuple-element.15), channel_id=1, source_target_pairs={{0,6},{2,0},{4,2},{6,4},{1,7},{3,1},{5,3},{7,5},{8,14},{10,8},{12,... | collective-permute-start | bytes 786440 | tf_op jit(solution)/shard_map/ppermute | solution.py:36
  90.3 13.0 %collective-permute-start.4 = (bf16[4,128,256]{2,1,0:T(8,128)(2,1)S(1)}, bf16[4,128,256]{2,1,0:T(8,128)(2,1)S(1)}, u32[]{:S(2)}, u32[]{:S(2)}) collective-permute-start(bf16[4,128,256]{2,1,0:T(8,128)(2,1)S(1)} %get-tuple-element.16), channel_id=1, source_target_pairs={{0,4},{2,6},{4,0},{6,2},{1,5},{3,7},{5,1},{7,3},{8,12},{10,14},{12... | collective-permute-start | bytes 786440 | tf_op jit(solution)/shard_map/ppermute | solution.py:36
  103.5 9.2 %collective-permute-start.6 = (bf16[128,256]{1,0:T(8,128)(2,1)S(1)}, bf16[128,256]{1,0:T(8,128)(2,1)S(1)}, u32[]{:S(2)}, u32[]{:S(2)}) collective-permute-start(bf16[128,256]{1,0:T(8,128)(2,1)S(1)} %get-tuple-element.17), channel_id=1, source_target_pairs={{0,16},{8,24},{16,0},{24,8},{1,17},{9,25},{17,1},{25,9},{2,18},{10... | collective-permute-start | bytes 196616 | tf_op jit(solution)/shard_map/ppermute | solution.py:32
  107.0 7.1 %collective-permute-start.8 = (bf16[128,256]{1,0:T(8,128)(2,1)S(1)}, bf16[128,256]{1,0:T(8,128)(2,1)S(1)}, u32[]{:S(2)}, u32[]{:S(2)}) collective-permute-start(bf16[128,256]{1,0:T(8,128)(2,1)S(1)} %get-tuple-element.18), channel_id=1, source_target_pairs={{0,24},{8,16},{16,8},{24,0},{1,25},{9,17},{17,9},{25,1},{2,26},{10... | collective-permute-start | bytes 196616 | tf_op jit(solution)/shard_map/ppermute | solution.py:32
  109.9 6.2 %collective-permute-start.7 = (bf16[128,256]{1,0:T(8,128)(2,1)S(1)}, bf16[128,256]{1,0:T(8,128)(2,1)S(1)}, u32[]{:S(2)}, u32[]{:S(2)}) collective-permute-start(bf16[128,256]{1,0:T(8,128)(2,1)S(1)} %get-tuple-element.19), channel_id=1, source_target_pairs={{0,8},{8,0},{16,24},{24,16},{1,9},{9,1},{17,25},{25,17},{2,10},{10... | collective-permute-start | bytes 196616 | tf_op jit(solution)/shard_map/ppermute | solution.py:32

commit v9 on v8

--- a/solution.py
+++ b/solution.py
@@ -65,8 +65,8 @@
 
 
 def tile_kernel(
-    place_ref, first_hbm, second_ref, moved_hbm, out_hbm,
-    first_ref, na_ref, nb_ref, moved_ref, out_ref, load_sem, moved_sems, out_sems,
+    place_ref, first_hbm, second_ref, moved_ref, out_hbm,
+    first_ref, na_ref, nb_ref, out_ref, load_sem, out_sems,
 ):
     count = BLOCK * BLOCKS
     width = first_ref.shape[1]
@@ -123,7 +123,6 @@
         axis=0,
         keepdims=True,
     )
-    stores = []
     for start in range(0, BLOCKS, CHUNK):
         some = slice(start * BLOCK, (start + CHUNK) * BLOCK)
         partial = jnp.dot(na_ref[some, :], grad, preferred_element_type=F32)
@@ -135,12 +134,6 @@
             moved_ref[start : start + CHUNK, i] = partial[:, i * width : (i + 1) * width].reshape(
                 CHUNK, BLOCK, width
             )
-        part = pl.ds(start, CHUNK)
-        store = pltpu.make_async_copy(
-            moved_ref.at[part], moved_hbm.at[part], moved_sems.at[start // CHUNK]
-        )
-        store.start()
-        stores.append(store)
 
     across = (((1,), (1,)), ((), ()))
     projection_first = lax.dot_general(
@@ -154,6 +147,7 @@
         axis=0,
         keepdims=True,
     )
+    stores = []
     for start in range(0, BLOCKS, CHUNK):
         some = slice(start * BLOCK, (start + CHUNK) * BLOCK)
         partial = lax.dot_general(nb_ref[some, :], grad, across, preferred_element_type=F32)
@@ -173,6 +167,33 @@
         store.wait()
 
 
+def spread_kernel(values_ref, out_hbm, halves_ref, sems):
+    width = halves_ref.shape[2]
+    for i in range(2):
+        halves_ref[i] = values_ref[:, i * width : (i + 1) * width]
+    copies = [
+        pltpu.make_async_copy(halves_ref, out_hbm.at[pl.ds(2 * i, 2)], sems.at[i])
+        for i in range(out_hbm.shape[0] // 2)
+    ]
+    for copy in copies:
+        copy.start()
+    for copy in copies:
+        copy.wait()
+
+
+def spread_halves(values, copies):
+    rows, width = values.shape
+    shape = (rows, width // 2)
+    return pl.pallas_call(
+        spread_kernel,
+        out_shape=pltpu.HBM((copies,) + shape, BF16),
+        in_specs=[pl.BlockSpec(memory_space=pltpu.VMEM)],
+        out_specs=pl.BlockSpec(memory_space=pltpu.HBM),
+        scratch_shapes=[pltpu.VMEM((2,) + shape, BF16), pltpu.SemaphoreType.DMA((copies // 2,))],
+        cost_estimate=pl.CostEstimate(flops=0, bytes_accessed=2 << 20, transcendentals=0),
+    )(values)
+
+
 def local_compute(place, first, second):
     count, width = first.shape
     pieces = (BLOCKS, 2, BLOCK, width)
@@ -180,17 +201,15 @@
     first = pltpu.with_memory_space_constraint(first, pltpu.HBM)
     return pl.pallas_call(
         tile_kernel,
-        out_shape=(pltpu.HBM(pieces, BF16), pltpu.HBM((count, width), BF16)),
+        out_shape=(jax.ShapeDtypeStruct(pieces, BF16), pltpu.HBM((count, width), BF16)),
         in_specs=[smem, hbm, vmem],
-        out_specs=(hbm, hbm),
+        out_specs=(vmem, hbm),
         scratch_shapes=[
             pltpu.VMEM((count, width), BF16),
             pltpu.VMEM((count, width), BF16),
             pltpu.VMEM((count, 2 * width), BF16),
-            pltpu.VMEM(pieces, BF16),
             pltpu.VMEM((count, width), BF16),
             pltpu.SemaphoreType.DMA,
-            pltpu.SemaphoreType.DMA((BLOCKS // CHUNK,)),
             pltpu.SemaphoreType.DMA((BLOCKS,)),
         ],
         compiler_params=pltpu.CompilerParams(vmem_limit_bytes=VMEM_LIMIT),
@@ -208,8 +227,7 @@
     total_count = rows_a * n_dp
 
     near = exchange(jnp.broadcast_to(second_view_outputs, (4, rows_b, width_b)), NEAR)
-    halves = jnp.stack([first_view_outputs[:, :half], first_view_outputs[:, half:]])
-    spread = jnp.broadcast_to(halves, (n_dp // 2, 2, rows_a, half)).reshape(n_dp, rows_a, half)
+    spread = spread_halves(first_view_outputs, n_dp)
     near, spread = lax.optimization_barrier((near, spread))
 
     first = exchange(spread, SAMPLES).reshape(total_count, half)

time: 119 us -> 116 us (0.975)
  local copies, waits for them, and re-layouts: 3.76 us -> 1.89 us
  Pallas kernels: 7.12 us -> 8.98 us
  waiting for transfers between devices: 38 us -> 36.8 us
  blocking collectives: 12 us -> 10.8 us
    pallas_call x1 -> x2, Pallas kernels: 7.12 us -> 8.98 us  [the longest x1 7.01 us: local_compute(): pl.pallas_call(tile_kernel, out_shape=(jax.ShapeDtypeStruct(pieces, BF16)...]
    all_to_all x2, blocking collectives: 12 us -> 10.8 us  [exchange(): return lax.all_to_all(values, axes, 0, 0, tiled=True)]
  transfers between devices with their start and end apart: 12 -> 12, of which waited for: 9 -> 9; matrix products, arithmetic and copies ran while one was open for 2% -> 1% of each run, Pallas kernels for 0% -> 2%
where the time goes in v9:
time: 116 us; the launch traced here: 115 us
  starting transfers between devices  53.7 us (46%)
  waiting for transfers between devices  36.8 us (32%)
  blocking collectives  10.8 us (9%)
  Pallas kernels  8.98 us (8%)
  other arithmetic  2.11 us (2%)
  local copies, waits for them, and re-layouts  1.89 us (2%)
    all_to_all x3, starting transfers between devices, exchange(): return lax.all_to_all(values, axes, 0, 0, tiled=True)  26.7 us
    ppermute x6, waiting for transfers between devices, shift(): lax.ppermute(values, 'x', [(i, (i + distance) % 4) for i in range(4)])  19.5 us
    ppermute x6, starting transfers between devices, shift(): lax.ppermute(values, 'x', [(i, (i + distance) % 4) for i in range(4)])  17.8 us
    all_to_all x3, waiting for transfers between devices, exchange(): return lax.all_to_all(values, axes, 0, 0, tiled=True)  14.1 us
    all_to_all x2, blocking collectives, exchange(): return lax.all_to_all(values, axes, 0, 0, tiled=True)  10.8 us
    ppermute x3, starting transfers between devices, near_swap(): return lax.ppermute(values, NEAR, [(i, i ^ flip) for i in range(4)])  9.21 us
    pallas_call x1, Pallas kernels, local_compute(): pl.pallas_call(tile_kernel, out_shape=(jax.ShapeDtypeStruct(pieces, BF16)...  7.01 us
    ppermute x3, waiting for transfers between devices, near_swap(): return lax.ppermute(values, NEAR, [(i, i ^ flip) for i in range(4)])  3.29 us
  transfers between devices with their start and end apart: 12, of which 9 were waited for; matrix products, arithmetic and copies ran while one was open for 1% of the time, Pallas kernels for 2%

profile of v9, /device:TPU:6, one launch (start us, length us, event | category | flops | bytes accessed | tf_op | source)
XLA Modules:
  0.0 115.1 jit_solution(13717974894801334038)
XLA Ops:
  0.6 1.6 %broadcast_in_dim.6 = bf16[4,128,256]{2,1,0:T(8,128)(2,1)} broadcast(bf16[128,256]{1,0:T(8,128)(2,1)} %param.3), dimensions={1,2} | broadcast | bytes 327680 | tf_op jit(solution)/shard_map/broadcast_in_dim | solution.py:229
  2.2 4.7 %all-to-all-start = ((bf16[4,128,256]{2,1,0:T(8,128)(2,1)}), bf16[4,128,256]{2,1,0:T(8,128)(2,1)S(1)}, u32[]{:S(2)}, u32[]{:S(2)}) async-start(bf16[4,128,256]{2,1,0:T(8,128)(2,1)} %broadcast_in_dim.6), calls=%async_computation | async-start | bytes 524288 | tf_op jit(solution)/shard_map/all_to_all | solution.py:27
  6.9 2.0 %shard_map.41 = bf16[32,64,256]{2,1,0:T(8,128)(2,1)} custom-call(bf16[64,512]{1,0:T(8,128)(2,1)} %values_ref.1), custom_call_target="tpu_custom_call" | custom-call | bytes 2097152 | tf_op jit(solution)/shard_map/pallas_call | solution.py:187
  8.8 3.4 %all-to-all-done = bf16[4,128,256]{2,1,0:T(8,128)(2,1)S(1)} async-done(((bf16[4,128,256]{2,1,0:T(8,128)(2,1)}), bf16[4,128,256]{2,1,0:T(8,128)(2,1)S(1)}, u32[]{:S(2)}, u32[]{:S(2)}) %all-to-all-start) | async-done | bytes 262176 | tf_op jit(solution)/shard_map/all_to_all | solution.py:27
  12.2 15.0 %all-to-all-start.1 = ((bf16[32,64,256]{2,1,0:T(8,128)(2,1)}), bf16[32,64,256]{2,1,0:T(8,128)(2,1)S(1)}, u32[]{:S(2)}, u32[]{:S(2)}) async-start(bf16[32,64,256]{2,1,0:T(8,128)(2,1)} %shard_map.41), calls=%async_computation.1 | async-start | bytes 2097152 | tf_op jit(solution)/shard_map/all_to_all | solution.py:27
  27.2 2.4 %collective-permute-start.2 = (bf16[4,128,256]{2,1,0:T(8,128)(2,1)S(1)}, bf16[4,128,256]{2,1,0:T(8,128)(2,1)S(1)}, u32[]{:S(2)}, u32[]{:S(2)}) collective-permute-start(bf16[4,128,256]{2,1,0:T(8,128)(2,1)S(1)} %all-to-all-done), channel_id=1, source_target_pairs={{0,2},{2,4},{4,6},{6,0},{1,3},{3,5},{5,7},{7,1},{8,10},{10,12},{12... | collective-permute-start | bytes 786440 | tf_op jit(solution)/shard_map/ppermute | solution.py:36
  29.6 4.3 %collective-permute-start.1 = (bf16[4,128,256]{2,1,0:T(8,128)(2,1)S(1)}, bf16[4,128,256]{2,1,0:T(8,128)(2,1)S(1)}, u32[]{:S(2)}, u32[]{:S(2)}) collective-permute-start(bf16[4,128,256]{2,1,0:T(8,128)(2,1)S(1)} %all-to-all-done), channel_id=1, source_target_pairs={{0,4},{2,6},{4,0},{6,2},{1,5},{3,7},{5,1},{7,3},{8,12},{10,14},{12... | collective-permute-start | bytes 786440 | tf_op jit(solution)/shard_map/ppermute | solution.py:36
  33.9 1.9 %collective-permute-start = (bf16[4,128,256]{2,1,0:T(8,128)(2,1)S(1)}, bf16[4,128,256]{2,1,0:T(8,128)(2,1)S(1)}, u32[]{:S(2)}, u32[]{:S(2)}) collective-permute-start(bf16[4,128,256]{2,1,0:T(8,128)(2,1)S(1)} %all-to-all-done), channel_id=1, source_target_pairs={{0,6},{2,0},{4,2},{6,4},{1,7},{3,1},{5,3},{7,5},{8,14},{10,8},{12,... | collective-permute-start | bytes 786440 | tf_op jit(solution)/shard_map/ppermute | solution.py:36
  35.9 0.1 pad_add_fusion.place_ref
  35.9 2.4 %collective-permute-done.2 = bf16[4,128,256]{2,1,0:T(8,128)(2,1)S(1)} collective-permute-done((bf16[4,128,256]{2,1,0:T(8,128)(2,1)S(1)}, bf16[4,128,256]{2,1,0:T(8,128)(2,1)S(1)}, u32[]{:S(2)}, u32[]{:S(2)}) %collective-permute-start.2) | collective-permute-done | bytes 262176 | tf_op jit(solution)/shard_map/ppermute | solution.py:36
  38.3 3.5 %collective-permute-done.1 = bf16[4,128,256]{2,1,0:T(8,128)(2,1)S(1)} collective-permute-done((bf16[4,128,256]{2,1,0:T(8,128)(2,1)S(1)}, bf16[4,128,256]{2,1,0:T(8,128)(2,1)S(1)}, u32[]{:S(2)}, u32[]{:S(2)}) %collective-permute-start.1) | collective-permute-done | bytes 262176 | tf_op jit(solution)/shard_map/ppermute | solution.py:36
  41.9 3.9 %collective-permute-done = bf16[4,128,256]{2,1,0:T(8,128)(2,1)S(1)} collective-permute-done((bf16[4,128,256]{2,1,0:T(8,128)(2,1)S(1)}, bf16[4,128,256]{2,1,0:T(8,128)(2,1)S(1)}, u32[]{:S(2)}, u32[]{:S(2)}) %collective-permute-start) | collective-permute-done | bytes 262176 | tf_op jit(solution)/shard_map/ppermute | solution.py:36
  45.7 0.1 pad_maximum_fusion
  45.8 10.7 %all-to-all-done.1 = bf16[32,64,256]{2,1,0:T(8,128)(2,1)S(1)} async-done(((bf16[32,64,256]{2,1,0:T(8,128)(2,1)}), bf16[32,64,256]{2,1,0:T(8,128)(2,1)S(1)}, u32[]{:S(2)}, u32[]{:S(2)}) %all-to-all-start.1) | async-done | bytes 1048608 | tf_op jit(solution)/shard_map/all_to_all | solution.py:27
  56.5 0.0 copy-start
  56.5 0.2 broadcast_in_dim.7
  56.8 5.4 %all_to_all.25 = bf16[2,4,4,128,256]{4,3,2,1,0:T(8,128)(2,1)S(1)} all-to-all(bf16[2,4,4,128,256]{4,3,2,1,0:T(8,128)(2,1)S(1)} %broadcast_in_dim.7), channel_id=1, replica_groups=mesh['zh'=4,'yk'=4,'yl'=2,'zl'=2,'x'=4,'core'=2] {'core'}, dimensions={0} | all-to-all | bytes 4194304 | tf_op jit(solution)/shard_map/all_to_all | solution.py:27
  62.2 0.0 copy-done
  62.2 7.0 %shard_map.42 = (bf16[16,2,128,256]{3,2,1,0:T(8,128)(2,1)S(1)}, bf16[2048,256]{1,0:T(8,128)(2,1)}) custom-call(s32[4]{0:T(128)S(1)} %pad_add_fusion.place_ref, bf16[2048,256]{1,0:T(8,128)(2,1)} %bitcast.42, bf16[2,4,2,2,128,256]{5,4,3,2,1,0:T(8,128)(2,1)S(1)} %bitcast.39), custom_call_target="tpu_custom_call" | custom-call | flops 1610612736 | bytes 6291456 | tf_op jit(solution)/shard_map/pallas_call | solution.py:202
  69.2 5.4 %all_to_all.26 = bf16[2,4,4,128,256]{4,3,2,1,0:T(8,128)(2,1)S(1)} all-to-all(bf16[2,4,4,128,256]{4,3,2,1,0:T(8,128)(2,1)S(1)} %bitcast.40), channel_id=1, replica_groups=mesh['zh'=4,'yk'=4,'yl'=2,'zl'=2,'x'=4,'core'=2] {'core'}, dimensions={0} | all-to-all | bytes 4194304 | tf_op jit(solution)/shard_map/all_to_all | solution.py:27
  74.6 7.1 %all-to-all-start.3 = ((bf16[32,64,256]{2,1,0:T(8,128)(2,1)}), bf16[32,64,256]{2,1,0:T(8,128)(2,1)S(1)}, u32[]{:S(2)}, u32[]{:S(2)}) async-start(bf16[32,64,256]{2,1,0:T(8,128)(2,1)} %bitcast.43), calls=%async_computation.3 | async-start | bytes 2097152 | tf_op jit(solution)/shard_map/all_to_all | solution.py:27
  81.7 0.3 add_convert_fusion
  82.0 0.1 slice_bitcast_fusion.2
  82.1 2.4 %collective-permute-start.3 = (bf16[4,128,256]{2,1,0:T(8,128)(2,1)S(1)}, bf16[4,128,256]{2,1,0:T(8,128)(2,1)S(1)}, u32[]{:S(2)}, u32[]{:S(2)}) collective-permute-start(bf16[4,128,256]{2,1,0:T(8,128)(2,1)S(1)} %get-tuple-element.14), channel_id=1, source_target_pairs={{0,2},{2,4},{4,6},{6,0},{1,3},{3,5},{5,7},{7,1},{8,10},{10,12},{12... | collective-permute-start | bytes 786440 | tf_op jit(solution)/shard_map/ppermute | solution.py:36
  84.4 3.5 %collective-permute-start.5 = (bf16[4,128,256]{2,1,0:T(8,128)(2,1)S(1)}, bf16[4,128,256]{2,1,0:T(8,128)(2,1)S(1)}, u32[]{:S(2)}, u32[]{:S(2)}) collective-permute-start(bf16[4,128,256]{2,1,0:T(8,128)(2,1)S(1)} %get-tuple-element.15), channel_id=1, source_target_pairs={{0,6},{2,0},{4,2},{6,4},{1,7},{3,1},{5,3},{7,5},{8,14},{10,8},{12,... | collective-permute-start | bytes 786440 | tf_op jit(solution)/shard_map/ppermute | solution.py:36
  87.9 3.3 %collective-permute-start.4 = (bf16[4,128,256]{2,1,0:T(8,128)(2,1)S(1)}, bf16[4,128,256]{2,1,0:T(8,128)(2,1)S(1)}, u32[]{:S(2)}, u32[]{:S(2)}) collective-permute-start(bf16[4,128,256]{2,1,0:T(8,128)(2,1)S(1)} %get-tuple-element.16), channel_id=1, source_target_pairs={{0,4},{2,6},{4,0},{6,2},{1,5},{3,7},{5,1},{7,3},{8,12},{10,14},{12... | collective-permute-start | bytes 786440 | tf_op jit(solution)/shard_map/ppermute | solution.py:36
  91.2 0.8 collective-permute-done.3
  92.0 8.9 %collective-permute-done.5 = bf16[4,128,256]{2,1,0:T(8,128)(2,1)S(1)} collective-permute-done((bf16[4,128,256]{2,1,0:T(8,128)(2,1)S(1)}, bf16[4,128,256]{2,1,0:T(8,128)(2,1)S(1)}, u32[]{:S(2)}, u32[]{:S(2)}) %collective-permute-start.5) | collective-permute-done | bytes 262176 | tf_op jit(solution)/shard_map/ppermute | solution.py:36
  101.0 0.0 collective-permute-done.4
  101.0 0.1 fusion.2
  101.1 3.4 %collective-permute-start.6 = (bf16[128,256]{1,0:T(8,128)(2,1)S(1)}, bf16[128,256]{1,0:T(8,128)(2,1)S(1)}, u32[]{:S(2)}, u32[]{:S(2)}) collective-permute-start(bf16[128,256]{1,0:T(8,128)(2,1)S(1)} %get-tuple-element.17), channel_id=1, source_target_pairs={{0,16},{8,24},{16,0},{24,8},{1,17},{9,25},{17,1},{25,9},{2,18},{10... | collective-permute-start | bytes 196616 | tf_op jit(solution)/shard_map/ppermute | solution.py:32
  104.5 2.9 %collective-permute-start.8 = (bf16[128,256]{1,0:T(8,128)(2,1)S(1)}, bf16[128,256]{1,0:T(8,128)(2,1)S(1)}, u32[]{:S(2)}, u32[]{:S(2)}) collective-permute-start(bf16[128,256]{1,0:T(8,128)(2,1)S(1)} %get-tuple-element.18), channel_id=1, source_target_pairs={{0,24},{8,16},{16,8},{24,0},{1,25},{9,17},{17,9},{25,1},{2,26},{10... | collective-permute-start | bytes 196616 | tf_op jit(solution)/shard_map/ppermute | solution.py:32
  107.5 2.9 %collective-permute-start.7 = (bf16[128,256]{1,0:T(8,128)(2,1)S(1)}, bf16[128,256]{1,0:T(8,128)(2,1)S(1)}, u32[]{:S(2)}, u32[]{:S(2)}) collective-permute-start(bf16[128,256]{1,0:T(8,128)(2,1)S(1)} %get-tuple-element.19), channel_id=1, source_target_pairs={{0,8},{8,0},{16,24},{24,16},{1,9},{9,1},{17,25},{25,17},{2,10},{10... | collective-permute-start | bytes 196616 | tf_op jit(solution)/shard_map/ppermute | solution.py:32
  110.4 0.0 collective-permute-done.6
  110.4 1.2 %collective-permute-done.8 = bf16[128,256]{1,0:T(8,128)(2,1)S(1)} collective-permute-done((bf16[128,256]{1,0:T(8,128)(2,1)S(1)}, bf16[128,256]{1,0:T(8,128)(2,1)S(1)}, u32[]{:S(2)}, u32[]{:S(2)}) %collective-permute-start.8) | collective-permute-done | bytes 65568 | tf_op jit(solution)/shard_map/ppermute | solution.py:32
  111.6 2.0 %collective-permute-done.7 = bf16[128,256]{1,0:T(8,128)(2,1)S(1)} collective-permute-done((bf16[128,256]{1,0:T(8,128)(2,1)S(1)}, bf16[128,256]{1,0:T(8,128)(2,1)S(1)}, u32[]{:S(2)}, u32[]{:S(2)}) %collective-permute-start.7) | collective-permute-done | bytes 65568 | tf_op jit(solution)/shard_map/ppermute | solution.py:32
  113.7 0.7 fusion.5
  114.3 0.0 all-to-all-done.3
  114.3 0.1 reduce_sum.12
  114.5 0.6 pad_maximum_fusion.1
  (2 shorter events, 0.0 us)
Async XLA Ops:
  2.2 10.0 %all-to-all-start = ((bf16[4,128,256]{2,1,0:T(8,128)(2,1)}), bf16[4,128,256]{2,1,0:T(8,128)(2,1)S(1)}, u32[]{:S(2)}, u32[]{:S(2)}) async-start(bf16[4,128,256]{2,1,0:T(8,128)(2,1)} %broadcast_in_dim.6), calls=%async_computation | async-start | bytes 524288 | tf_op jit(solution)/shard_map/all_to_all | solution.py:27
  12.2 44.3 %all-to-all-start.1 = ((bf16[32,64,256]{2,1,0:T(8,128)(2,1)}), bf16[32,64,256]{2,1,0:T(8,128)(2,1)S(1)}, u32[]{:S(2)}, u32[]{:S(2)}) async-start(bf16[32,64,256]{2,1,0:T(8,128)(2,1)} %shard_map.41), calls=%async_computation.1 | async-start | bytes 2097152 | tf_op jit(solution)/shard_map/all_to_all | solution.py:27
  27.2 11.1 %collective-permute-start.2 = (bf16[4,128,256]{2,1,0:T(8,128)(2,1)S(1)}, bf16[4,128,256]{2,1,0:T(8,128)(2,1)S(1)}, u32[]{:S(2)}, u32[]{:S(2)}) collective-permute-start(bf16[4,128,256]{2,1,0:T(8,128)(2,1)S(1)} %all-to-all-done), channel_id=1, source_target_pairs={{0,2},{2,4},{4,6},{6,0},{1,3},{3,5},{5,7},{7,1},{8,10},{10,12},{12... | collective-permute-start | bytes 786440 | tf_op jit(solution)/shard_map/ppermute | solution.py:36
  29.6 12.3 %collective-permute-start.1 = (bf16[4,128,256]{2,1,0:T(8,128)(2,1)S(1)}, bf16[4,128,256]{2,1,0:T(8,128)(2,1)S(1)}, u32[]{:S(2)}, u32[]{:S(2)}) collective-permute-start(bf16[4,128,256]{2,1,0:T(8,128)(2,1)S(1)} %all-to-all-done), channel_id=1, source_target_pairs={{0,4},{2,6},{4,0},{6,2},{1,5},{3,7},{5,1},{7,3},{8,12},{10,14},{12... | collective-permute-start | bytes 786440 | tf_op jit(solution)/shard_map/ppermute | solution.py:36
  33.9 11.8 %collective-permute-start = (bf16[4,128,256]{2,1,0:T(8,128)(2,1)S(1)}, bf16[4,128,256]{2,1,0:T(8,128)(2,1)S(1)}, u32[]{:S(2)}, u32[]{:S(2)}) collective-permute-start(bf16[4,128,256]{2,1,0:T(8,128)(2,1)S(1)} %all-to-all-done), channel_id=1, source_target_pairs={{0,6},{2,0},{4,2},{6,4},{1,7},{3,1},{5,3},{7,5},{8,14},{10,8},{12,... | collective-permute-start | bytes 786440 | tf_op jit(solution)/shard_map/ppermute | solution.py:36
  56.5 5.7 %copy-start = (bf16[32,64,256]{2,1,0:T(8,128)(2,1)}, bf16[32,64,256]{2,1,0:T(8,128)(2,1)S(1)}, u32[]{:S(2)}) copy-start(bf16[32,64,256]{2,1,0:T(8,128)(2,1)S(1)} %all-to-all-done.1) | copy-start | bytes 3145732
  74.6 39.7 %all-to-all-start.3 = ((bf16[32,64,256]{2,1,0:T(8,128)(2,1)}), bf16[32,64,256]{2,1,0:T(8,128)(2,1)S(1)}, u32[]{:S(2)}, u32[]{:S(2)}) async-start(bf16[32,64,256]{2,1,0:T(8,128)(2,1)} %bitcast.43), calls=%async_computation.3 | async-start | bytes 2097152 | tf_op jit(solution)/shard_map/all_to_all | solution.py:27
  82.1 10.0 %collective-permute-start.3 = (bf16[4,128,256]{2,1,0:T(8,128)(2,1)S(1)}, bf16[4,128,256]{2,1,0:T(8,128)(2,1)S(1)}, u32[]{:S(2)}, u32[]{:S(2)}) collective-permute-start(bf16[4,128,256]{2,1,0:T(8,128)(2,1)S(1)} %get-tuple-element.14), channel_id=1, source_target_pairs={{0,2},{2,4},{4,6},{6,0},{1,3},{3,5},{5,7},{7,1},{8,10},{10,12},{12... | collective-permute-start | bytes 786440 | tf_op jit(solution)/shard_map/ppermute | solution.py:36
  84.4 16.5 %collective-permute-start.5 = (bf16[4,128,256]{2,1,0:T(8,128)(2,1)S(1)}, bf16[4,128,256]{2,1,0:T(8,128)(2,1)S(1)}, u32[]{:S(2)}, u32[]{:S(2)}) collective-permute-start(bf16[4,128,256]{2,1,0:T(8,128)(2,1)S(1)} %get-tuple-element.15), channel_id=1, source_target_pairs={{0,6},{2,0},{4,2},{6,4},{1,7},{3,1},{5,3},{7,5},{8,14},{10,8},{12,... | collective-permute-start | bytes 786440 | tf_op jit(solution)/shard_map/ppermute | solution.py:36
  87.9 13.0 %collective-permute-start.4 = (bf16[4,128,256]{2,1,0:T(8,128)(2,1)S(1)}, bf16[4,128,256]{2,1,0:T(8,128)(2,1)S(1)}, u32[]{:S(2)}, u32[]{:S(2)}) collective-permute-start(bf16[4,128,256]{2,1,0:T(8,128)(2,1)S(1)} %get-tuple-element.16), channel_id=1, source_target_pairs={{0,4},{2,6},{4,0},{6,2},{1,5},{3,7},{5,1},{7,3},{8,12},{10,14},{12... | collective-permute-start | bytes 786440 | tf_op jit(solution)/shard_map/ppermute | solution.py:36
  101.1 9.2 %collective-permute-start.6 = (bf16[128,256]{1,0:T(8,128)(2,1)S(1)}, bf16[128,256]{1,0:T(8,128)(2,1)S(1)}, u32[]{:S(2)}, u32[]{:S(2)}) collective-permute-start(bf16[128,256]{1,0:T(8,128)(2,1)S(1)} %get-tuple-element.17), channel_id=1, source_target_pairs={{0,16},{8,24},{16,0},{24,8},{1,17},{9,25},{17,1},{25,9},{2,18},{10... | collective-permute-start | bytes 196616 | tf_op jit(solution)/shard_map/ppermute | solution.py:32
  104.5 7.1 %collective-permute-start.8 = (bf16[128,256]{1,0:T(8,128)(2,1)S(1)}, bf16[128,256]{1,0:T(8,128)(2,1)S(1)}, u32[]{:S(2)}, u32[]{:S(2)}) collective-permute-start(bf16[128,256]{1,0:T(8,128)(2,1)S(1)} %get-tuple-element.18), channel_id=1, source_target_pairs={{0,24},{8,16},{16,8},{24,0},{1,25},{9,17},{17,9},{25,1},{2,26},{10... | collective-permute-start | bytes 196616 | tf_op jit(solution)/shard_map/ppermute | solution.py:32
  107.5 6.2 %collective-permute-start.7 = (bf16[128,256]{1,0:T(8,128)(2,1)S(1)}, bf16[128,256]{1,0:T(8,128)(2,1)S(1)}, u32[]{:S(2)}, u32[]{:S(2)}) collective-permute-start(bf16[128,256]{1,0:T(8,128)(2,1)S(1)} %get-tuple-element.19), channel_id=1, source_target_pairs={{0,8},{8,0},{16,24},{24,16},{1,9},{9,1},{17,25},{25,17},{2,10},{10... | collective-permute-start | bytes 196616 | tf_op jit(solution)/shard_map/ppermute | solution.py:32

commit v10 on v9

--- a/solution.py
+++ b/solution.py
@@ -15,7 +15,6 @@
 NEAR = ("yl", "zl")
 F32 = jnp.float32
 BF16 = jnp.bfloat16
-HIGHEST = lax.Precision.HIGHEST
 VMEM_LIMIT = 28 * 1024 * 1024
 
 BLOCK = 128
@@ -49,6 +48,15 @@
 
 def fold(values):
     return values.reshape(-1, 8, values.shape[-1]).sum(axis=0)
+
+
+def split_rows(sums):
+    row = jnp.sum(sums, axis=0, keepdims=True)
+    rows = []
+    for _ in range(3):
+        rows.append(row.astype(BF16))
+        row = row - rows[-1].astype(F32)
+    return jnp.concatenate(rows + [jnp.zeros((13, row.shape[1]), BF16)], axis=0)
 
 
 def column_statistics(load, blocks, count):
@@ -119,9 +127,7 @@
     weighted = grad_wide * correlation
     projection_second = jnp.sum(weighted, axis=0, keepdims=True)
     centering_second = jnp.sum(
-        jnp.dot(mean_first, grad_wide, preferred_element_type=F32, precision=HIGHEST),
-        axis=0,
-        keepdims=True,
+        jnp.dot(split_rows(mean_first), grad, preferred_element_type=F32), axis=0, keepdims=True
     )
     for start in range(0, BLOCKS, CHUNK):
         some = slice(start * BLOCK, (start + CHUNK) * BLOCK)
@@ -136,14 +142,11 @@
             )
 
     across = (((1,), (1,)), ((), ()))
-    projection_first = lax.dot_general(
-        jnp.ones((8, weighted.shape[1]), F32), weighted, across,
-        preferred_element_type=F32, precision=HIGHEST,
-    )
+    lanes = 128
+    folded = sum(weighted[:, i : i + lanes] for i in range(0, 2 * width, lanes))
+    projection_first = jnp.sum(folded.T, axis=0, keepdims=True)
     centering_first = jnp.sum(
-        lax.dot_general(
-            mean_second, grad_wide, across, preferred_element_type=F32, precision=HIGHEST
-        ),
+        lax.dot_general(split_rows(mean_second), grad, across, preferred_element_type=F32),
         axis=0,
         keepdims=True,
     )
@@ -152,7 +155,7 @@
         some = slice(start * BLOCK, (start + CHUNK) * BLOCK)
         partial = lax.dot_general(nb_ref[some, :], grad, across, preferred_element_type=F32)
         partial = (
-            partial - centering_first - na_ref[some, :].astype(F32) * projection_first[0:1]
+            partial - centering_first - na_ref[some, :].astype(F32) * projection_first
         ) * scale_first
         out_ref[some, :] = partial.astype(BF16)
         for t in range(start, start + CHUNK):
@@ -252,14 +255,13 @@
     pieces = exchange(moved.reshape(2, 4, 4, rows_b, width_b), "core")
     pieces = narrow_sum(pieces[0], pieces[1])
     pieces = narrow_sum(pieces[0], *[shift(pieces[k], k) for k in (1, 2, 3)])
-    second_view_gradient = narrow_sum(
-        pieces[0], *[near_swap(pieces[k], k) for k in (1, 2, 3)]
-    )
+    pieces = [pieces[0]] + [near_swap(pieces[k], k) for k in (1, 2, 3)]
 
     parts = exchange(partial_first.reshape(n_dp, rows_a, half), SAMPLES)
     parts = jnp.sum(parts.reshape(n_dp // 2, 2, rows_a, half).astype(F32), axis=0).astype(BF16)
     first_view_gradient = jnp.concatenate([parts[0], parts[1]], axis=1)
-    return first_view_gradient, second_view_gradient
+    first_view_gradient, *pieces = lax.optimization_barrier([first_view_gradient] + pieces)
+    return first_view_gradient, narrow_sum(*pieces)
 
 
 def solution(mesh):

time: 116 us -> 115 us (level)
    ppermute x3, waiting for transfers between devices: 3.29 us -> 1.47 us  [near_swap(): return lax.ppermute(values, NEAR, [(i, i ^ flip) for i in range(4)])]
    all_to_all x3, waiting for transfers between devices: 14.1 us -> 15.5 us  [exchange(): return lax.all_to_all(values, axes, 0, 0, tiled=True)]
where the time goes in v10:
time: 115 us; the launch traced here: 114 us
  starting transfers between devices  53.7 us (47%)
  waiting for transfers between devices  36.5 us (32%)
  blocking collectives  10.8 us (9%)
  Pallas kernels  7.89 us (7%)
  other arithmetic  2.11 us (2%)
  local copies, waits for them, and re-layouts  1.89 us (2%)
    all_to_all x3, starting transfers between devices, exchange(): return lax.all_to_all(values, axes, 0, 0, tiled=True)  26.7 us
    ppermute x6, waiting for transfers between devices, shift(): lax.ppermute(values, 'x', [(i, (i + distance) % 4) for i in range(4)])  19.5 us
    ppermute x6, starting transfers between devices, shift(): lax.ppermute(values, 'x', [(i, (i + distance) % 4) for i in range(4)])  17.8 us
    all_to_all x3, waiting for transfers between devices, exchange(): return lax.all_to_all(values, axes, 0, 0, tiled=True)  15.5 us
    all_to_all x2, blocking collectives, exchange(): return lax.all_to_all(values, axes, 0, 0, tiled=True)  10.8 us
    ppermute x3, starting transfers between devices, near_swap(): return lax.ppermute(values, NEAR, [(i, i ^ flip) for i in range(4)])  9.21 us
    pallas_call x1, Pallas kernels, local_compute(): pl.pallas_call(tile_kernel, out_shape=(jax.ShapeDtypeStruct(pieces, BF16)...  5.92 us
  transfers between devices with their start and end apart: 12, of which 9 were waited for; matrix products, arithmetic and copies ran while one was open for 1% of the time, Pallas kernels for 2%

profile of v10, /device:TPU:6, one launch (start us, length us, event | category | flops | bytes accessed | tf_op | source)
XLA Modules:
  0.0 113.7 jit_solution(15193828470161120686)
XLA Ops:
  0.6 1.6 %broadcast_in_dim.6 = bf16[4,128,256]{2,1,0:T(8,128)(2,1)} broadcast(bf16[128,256]{1,0:T(8,128)(2,1)} %param.3), dimensions={1,2} | broadcast | bytes 327680 | tf_op jit(solution)/shard_map/broadcast_in_dim | solution.py:232
  2.2 4.7 %all-to-all-start = ((bf16[4,128,256]{2,1,0:T(8,128)(2,1)}), bf16[4,128,256]{2,1,0:T(8,128)(2,1)S(1)}, u32[]{:S(2)}, u32[]{:S(2)}) async-start(bf16[4,128,256]{2,1,0:T(8,128)(2,1)} %broadcast_in_dim.6), calls=%async_computation | async-start | bytes 524288 | tf_op jit(solution)/shard_map/all_to_all | solution.py:26
  6.9 2.0 %shard_map.41 = bf16[32,64,256]{2,1,0:T(8,128)(2,1)} custom-call(bf16[64,512]{1,0:T(8,128)(2,1)} %values_ref.1), custom_call_target="tpu_custom_call" | custom-call | bytes 2097152 | tf_op jit(solution)/shard_map/pallas_call | solution.py:190
  8.8 3.4 %all-to-all-done = bf16[4,128,256]{2,1,0:T(8,128)(2,1)S(1)} async-done(((bf16[4,128,256]{2,1,0:T(8,128)(2,1)}), bf16[4,128,256]{2,1,0:T(8,128)(2,1)S(1)}, u32[]{:S(2)}, u32[]{:S(2)}) %all-to-all-start) | async-done | bytes 262176 | tf_op jit(solution)/shard_map/all_to_all | solution.py:26
  12.2 15.0 %all-to-all-start.1 = ((bf16[32,64,256]{2,1,0:T(8,128)(2,1)}), bf16[32,64,256]{2,1,0:T(8,128)(2,1)S(1)}, u32[]{:S(2)}, u32[]{:S(2)}) async-start(bf16[32,64,256]{2,1,0:T(8,128)(2,1)} %shard_map.41), calls=%async_computation.1 | async-start | bytes 2097152 | tf_op jit(solution)/shard_map/all_to_all | solution.py:26
  27.2 2.4 %collective-permute-start.2 = (bf16[4,128,256]{2,1,0:T(8,128)(2,1)S(1)}, bf16[4,128,256]{2,1,0:T(8,128)(2,1)S(1)}, u32[]{:S(2)}, u32[]{:S(2)}) collective-permute-start(bf16[4,128,256]{2,1,0:T(8,128)(2,1)S(1)} %all-to-all-done), channel_id=1, source_target_pairs={{0,2},{2,4},{4,6},{6,0},{1,3},{3,5},{5,7},{7,1},{8,10},{10,12},{12... | collective-permute-start | bytes 786440 | tf_op jit(solution)/shard_map/ppermute | solution.py:35
  29.6 4.3 %collective-permute-start.1 = (bf16[4,128,256]{2,1,0:T(8,128)(2,1)S(1)}, bf16[4,128,256]{2,1,0:T(8,128)(2,1)S(1)}, u32[]{:S(2)}, u32[]{:S(2)}) collective-permute-start(bf16[4,128,256]{2,1,0:T(8,128)(2,1)S(1)} %all-to-all-done), channel_id=1, source_target_pairs={{0,4},{2,6},{4,0},{6,2},{1,5},{3,7},{5,1},{7,3},{8,12},{10,14},{12... | collective-permute-start | bytes 786440 | tf_op jit(solution)/shard_map/ppermute | solution.py:35
  33.9 1.9 %collective-permute-start = (bf16[4,128,256]{2,1,0:T(8,128)(2,1)S(1)}, bf16[4,128,256]{2,1,0:T(8,128)(2,1)S(1)}, u32[]{:S(2)}, u32[]{:S(2)}) collective-permute-start(bf16[4,128,256]{2,1,0:T(8,128)(2,1)S(1)} %all-to-all-done), channel_id=1, source_target_pairs={{0,6},{2,0},{4,2},{6,4},{1,7},{3,1},{5,3},{7,5},{8,14},{10,8},{12,... | collective-permute-start | bytes 786440 | tf_op jit(solution)/shard_map/ppermute | solution.py:35
  35.9 0.1 pad_add_fusion.place_ref
  35.9 2.4 %collective-permute-done.2 = bf16[4,128,256]{2,1,0:T(8,128)(2,1)S(1)} collective-permute-done((bf16[4,128,256]{2,1,0:T(8,128)(2,1)S(1)}, bf16[4,128,256]{2,1,0:T(8,128)(2,1)S(1)}, u32[]{:S(2)}, u32[]{:S(2)}) %collective-permute-start.2) | collective-permute-done | bytes 262176 | tf_op jit(solution)/shard_map/ppermute | solution.py:35
  38.3 3.5 %collective-permute-done.1 = bf16[4,128,256]{2,1,0:T(8,128)(2,1)S(1)} collective-permute-done((bf16[4,128,256]{2,1,0:T(8,128)(2,1)S(1)}, bf16[4,128,256]{2,1,0:T(8,128)(2,1)S(1)}, u32[]{:S(2)}, u32[]{:S(2)}) %collective-permute-start.1) | collective-permute-done | bytes 262176 | tf_op jit(solution)/shard_map/ppermute | solution.py:35
  41.9 3.9 %collective-permute-done = bf16[4,128,256]{2,1,0:T(8,128)(2,1)S(1)} collective-permute-done((bf16[4,128,256]{2,1,0:T(8,128)(2,1)S(1)}, bf16[4,128,256]{2,1,0:T(8,128)(2,1)S(1)}, u32[]{:S(2)}, u32[]{:S(2)}) %collective-permute-start) | collective-permute-done | bytes 262176 | tf_op jit(solution)/shard_map/ppermute | solution.py:35
  45.7 0.1 pad_maximum_fusion
  45.8 10.7 %all-to-all-done.1 = bf16[32,64,256]{2,1,0:T(8,128)(2,1)S(1)} async-done(((bf16[32,64,256]{2,1,0:T(8,128)(2,1)}), bf16[32,64,256]{2,1,0:T(8,128)(2,1)S(1)}, u32[]{:S(2)}, u32[]{:S(2)}) %all-to-all-start.1) | async-done | bytes 1048608 | tf_op jit(solution)/shard_map/all_to_all | solution.py:26
  56.5 0.0 copy-start
  56.5 0.2 broadcast_in_dim.7
  56.8 5.4 %all_to_all.25 = bf16[2,4,4,128,256]{4,3,2,1,0:T(8,128)(2,1)S(1)} all-to-all(bf16[2,4,4,128,256]{4,3,2,1,0:T(8,128)(2,1)S(1)} %broadcast_in_dim.7), channel_id=1, replica_groups=mesh['zh'=4,'yk'=4,'yl'=2,'zl'=2,'x'=4,'core'=2] {'core'}, dimensions={0} | all-to-all | bytes 4194304 | tf_op jit(solution)/shard_map/all_to_all | solution.py:26
  62.2 0.0 copy-done
  62.2 5.9 %shard_map.42 = (bf16[16,2,128,256]{3,2,1,0:T(8,128)(2,1)S(1)}, bf16[2048,256]{1,0:T(8,128)(2,1)}) custom-call(s32[4]{0:T(128)S(1)} %pad_add_fusion.place_ref, bf16[2048,256]{1,0:T(8,128)(2,1)} %bitcast.39, bf16[2,4,2,2,128,256]{5,4,3,2,1,0:T(8,128)(2,1)S(1)} %bitcast.36), custom_call_target="tpu_custom_call" | custom-call | flops 1610612736 | bytes 6291456 | tf_op jit(solution)/shard_map/pallas_call | solution.py:205
  68.1 5.4 %all_to_all.26 = bf16[2,4,4,128,256]{4,3,2,1,0:T(8,128)(2,1)S(1)} all-to-all(bf16[2,4,4,128,256]{4,3,2,1,0:T(8,128)(2,1)S(1)} %bitcast.37), channel_id=1, replica_groups=mesh['zh'=4,'yk'=4,'yl'=2,'zl'=2,'x'=4,'core'=2] {'core'}, dimensions={0} | all-to-all | bytes 4194304 | tf_op jit(solution)/shard_map/all_to_all | solution.py:26
  73.5 7.0 %all-to-all-start.3 = ((bf16[32,64,256]{2,1,0:T(8,128)(2,1)}), bf16[32,64,256]{2,1,0:T(8,128)(2,1)S(1)}, u32[]{:S(2)}, u32[]{:S(2)}) async-start(bf16[32,64,256]{2,1,0:T(8,128)(2,1)} %bitcast.40), calls=%async_computation.3 | async-start | bytes 2097152 | tf_op jit(solution)/shard_map/all_to_all | solution.py:26
  80.6 0.3 add_convert_fusion
  80.9 0.1 slice_bitcast_fusion.2
  81.0 2.4 %collective-permute-start.3 = (bf16[4,128,256]{2,1,0:T(8,128)(2,1)S(1)}, bf16[4,128,256]{2,1,0:T(8,128)(2,1)S(1)}, u32[]{:S(2)}, u32[]{:S(2)}) collective-permute-start(bf16[4,128,256]{2,1,0:T(8,128)(2,1)S(1)} %get-tuple-element.24), channel_id=1, source_target_pairs={{0,2},{2,4},{4,6},{6,0},{1,3},{3,5},{5,7},{7,1},{8,10},{10,12},{12... | collective-permute-start | bytes 786440 | tf_op jit(solution)/shard_map/ppermute | solution.py:35
  83.4 3.5 %collective-permute-start.5 = (bf16[4,128,256]{2,1,0:T(8,128)(2,1)S(1)}, bf16[4,128,256]{2,1,0:T(8,128)(2,1)S(1)}, u32[]{:S(2)}, u32[]{:S(2)}) collective-permute-start(bf16[4,128,256]{2,1,0:T(8,128)(2,1)S(1)} %get-tuple-element.25), channel_id=1, source_target_pairs={{0,6},{2,0},{4,2},{6,4},{1,7},{3,1},{5,3},{7,5},{8,14},{10,8},{12,... | collective-permute-start | bytes 786440 | tf_op jit(solution)/shard_map/ppermute | solution.py:35
  86.8 3.3 %collective-permute-start.4 = (bf16[4,128,256]{2,1,0:T(8,128)(2,1)S(1)}, bf16[4,128,256]{2,1,0:T(8,128)(2,1)S(1)}, u32[]{:S(2)}, u32[]{:S(2)}) collective-permute-start(bf16[4,128,256]{2,1,0:T(8,128)(2,1)S(1)} %get-tuple-element.26), channel_id=1, source_target_pairs={{0,4},{2,6},{4,0},{6,2},{1,5},{3,7},{5,1},{7,3},{8,12},{10,14},{12... | collective-permute-start | bytes 786440 | tf_op jit(solution)/shard_map/ppermute | solution.py:35
  90.1 0.8 collective-permute-done.3
  90.9 8.9 %collective-permute-done.5 = bf16[4,128,256]{2,1,0:T(8,128)(2,1)S(1)} collective-permute-done((bf16[4,128,256]{2,1,0:T(8,128)(2,1)S(1)}, bf16[4,128,256]{2,1,0:T(8,128)(2,1)S(1)}, u32[]{:S(2)}, u32[]{:S(2)}) %collective-permute-start.5) | collective-permute-done | bytes 262176 | tf_op jit(solution)/shard_map/ppermute | solution.py:35
  99.9 0.0 collective-permute-done.4
  99.9 0.1 fusion.2
  100.0 3.9 %collective-permute-start.8 = (bf16[128,256]{1,0:T(8,128)(2,1)S(1)}, bf16[128,256]{1,0:T(8,128)(2,1)S(1)}, u32[]{:S(2)}, u32[]{:S(2)}) collective-permute-start(bf16[128,256]{1,0:T(8,128)(2,1)S(1)} %get-tuple-element.27), channel_id=1, source_target_pairs={{0,24},{8,16},{16,8},{24,0},{1,25},{9,17},{17,9},{25,1},{2,26},{10... | collective-permute-start | bytes 196616 | tf_op jit(solution)/shard_map/ppermute | solution.py:31
  104.0 2.9 %collective-permute-start.7 = (bf16[128,256]{1,0:T(8,128)(2,1)S(1)}, bf16[128,256]{1,0:T(8,128)(2,1)S(1)}, u32[]{:S(2)}, u32[]{:S(2)}) collective-permute-start(bf16[128,256]{1,0:T(8,128)(2,1)S(1)} %get-tuple-element.28), channel_id=1, source_target_pairs={{0,8},{8,0},{16,24},{24,16},{1,9},{9,1},{17,25},{25,17},{2,10},{10... | collective-permute-start | bytes 196616 | tf_op jit(solution)/shard_map/ppermute | solution.py:31
  106.8 2.4 %collective-permute-start.6 = (bf16[128,256]{1,0:T(8,128)(2,1)S(1)}, bf16[128,256]{1,0:T(8,128)(2,1)S(1)}, u32[]{:S(2)}, u32[]{:S(2)}) collective-permute-start(bf16[128,256]{1,0:T(8,128)(2,1)S(1)} %get-tuple-element.29), channel_id=1, source_target_pairs={{0,16},{8,24},{16,0},{24,8},{1,17},{9,25},{17,1},{25,9},{2,18},{10... | collective-permute-start | bytes 196616 | tf_op jit(solution)/shard_map/ppermute | solution.py:31
  109.3 1.5 %all-to-all-done.3 = bf16[32,64,256]{2,1,0:T(8,128)(2,1)S(1)} async-done(((bf16[32,64,256]{2,1,0:T(8,128)(2,1)}), bf16[32,64,256]{2,1,0:T(8,128)(2,1)S(1)}, u32[]{:S(2)}, u32[]{:S(2)}) %all-to-all-start.3) | async-done | bytes 1048608 | tf_op jit(solution)/shard_map/all_to_all | solution.py:26
  110.7 0.1 reduce_sum.12
  110.9 0.6 pad_maximum_fusion.1
  111.5 0.0 collective-permute-done.8
  111.5 0.0 collective-permute-done.7
  111.5 1.5 %collective-permute-done.6 = bf16[128,256]{1,0:T(8,128)(2,1)S(1)} collective-permute-done((bf16[128,256]{1,0:T(8,128)(2,1)S(1)}, bf16[128,256]{1,0:T(8,128)(2,1)S(1)}, u32[]{:S(2)}, u32[]{:S(2)}) %collective-permute-start.6) | collective-permute-done | bytes 65568 | tf_op jit(solution)/shard_map/ppermute | solution.py:31
  113.0 0.7 add_convert_fusion.1
  (2 shorter events, 0.0 us)
Async XLA Ops:
  2.2 10.0 %all-to-all-start = ((bf16[4,128,256]{2,1,0:T(8,128)(2,1)}), bf16[4,128,256]{2,1,0:T(8,128)(2,1)S(1)}, u32[]{:S(2)}, u32[]{:S(2)}) async-start(bf16[4,128,256]{2,1,0:T(8,128)(2,1)} %broadcast_in_dim.6), calls=%async_computation | async-start | bytes 524288 | tf_op jit(solution)/shard_map/all_to_all | solution.py:26
  12.2 44.3 %all-to-all-start.1 = ((bf16[32,64,256]{2,1,0:T(8,128)(2,1)}), bf16[32,64,256]{2,1,0:T(8,128)(2,1)S(1)}, u32[]{:S(2)}, u32[]{:S(2)}) async-start(bf16[32,64,256]{2,1,0:T(8,128)(2,1)} %shard_map.41), calls=%async_computation.1 | async-start | bytes 2097152 | tf_op jit(solution)/shard_map/all_to_all | solution.py:26
  27.2 11.1 %collective-permute-start.2 = (bf16[4,128,256]{2,1,0:T(8,128)(2,1)S(1)}, bf16[4,128,256]{2,1,0:T(8,128)(2,1)S(1)}, u32[]{:S(2)}, u32[]{:S(2)}) collective-permute-start(bf16[4,128,256]{2,1,0:T(8,128)(2,1)S(1)} %all-to-all-done), channel_id=1, source_target_pairs={{0,2},{2,4},{4,6},{6,0},{1,3},{3,5},{5,7},{7,1},{8,10},{10,12},{12... | collective-permute-start | bytes 786440 | tf_op jit(solution)/shard_map/ppermute | solution.py:35
  29.6 12.3 %collective-permute-start.1 = (bf16[4,128,256]{2,1,0:T(8,128)(2,1)S(1)}, bf16[4,128,256]{2,1,0:T(8,128)(2,1)S(1)}, u32[]{:S(2)}, u32[]{:S(2)}) collective-permute-start(bf16[4,128,256]{2,1,0:T(8,128)(2,1)S(1)} %all-to-all-done), channel_id=1, source_target_pairs={{0,4},{2,6},{4,0},{6,2},{1,5},{3,7},{5,1},{7,3},{8,12},{10,14},{12... | collective-permute-start | bytes 786440 | tf_op jit(solution)/shard_map/ppermute | solution.py:35
  33.9 11.8 %collective-permute-start = (bf16[4,128,256]{2,1,0:T(8,128)(2,1)S(1)}, bf16[4,128,256]{2,1,0:T(8,128)(2,1)S(1)}, u32[]{:S(2)}, u32[]{:S(2)}) collective-permute-start(bf16[4,128,256]{2,1,0:T(8,128)(2,1)S(1)} %all-to-all-done), channel_id=1, source_target_pairs={{0,6},{2,0},{4,2},{6,4},{1,7},{3,1},{5,3},{7,5},{8,14},{10,8},{12,... | collective-permute-start | bytes 786440 | tf_op jit(solution)/shard_map/ppermute | solution.py:35
  56.5 5.7 %copy-start = (bf16[32,64,256]{2,1,0:T(8,128)(2,1)}, bf16[32,64,256]{2,1,0:T(8,128)(2,1)S(1)}, u32[]{:S(2)}) copy-start(bf16[32,64,256]{2,1,0:T(8,128)(2,1)S(1)} %all-to-all-done.1) | copy-start | bytes 3145732
  73.5 37.2 %all-to-all-start.3 = ((bf16[32,64,256]{2,1,0:T(8,128)(2,1)}), bf16[32,64,256]{2,1,0:T(8,128)(2,1)S(1)}, u32[]{:S(2)}, u32[]{:S(2)}) async-start(bf16[32,64,256]{2,1,0:T(8,128)(2,1)} %bitcast.40), calls=%async_computation.3 | async-start | bytes 2097152 | tf_op jit(solution)/shard_map/all_to_all | solution.py:26
  81.0 10.0 %collective-permute-start.3 = (bf16[4,128,256]{2,1,0:T(8,128)(2,1)S(1)}, bf16[4,128,256]{2,1,0:T(8,128)(2,1)S(1)}, u32[]{:S(2)}, u32[]{:S(2)}) collective-permute-start(bf16[4,128,256]{2,1,0:T(8,128)(2,1)S(1)} %get-tuple-element.24), channel_id=1, source_target_pairs={{0,2},{2,4},{4,6},{6,0},{1,3},{3,5},{5,7},{7,1},{8,10},{10,12},{12... | collective-permute-start | bytes 786440 | tf_op jit(solution)/shard_map/ppermute | solution.py:35
  83.4 16.5 %collective-permute-start.5 = (bf16[4,128,256]{2,1,0:T(8,128)(2,1)S(1)}, bf16[4,128,256]{2,1,0:T(8,128)(2,1)S(1)}, u32[]{:S(2)}, u32[]{:S(2)}) collective-permute-start(bf16[4,128,256]{2,1,0:T(8,128)(2,1)S(1)} %get-tuple-element.25), channel_id=1, source_target_pairs={{0,6},{2,0},{4,2},{6,4},{1,7},{3,1},{5,3},{7,5},{8,14},{10,8},{12,... | collective-permute-start | bytes 786440 | tf_op jit(solution)/shard_map/ppermute | solution.py:35
  86.8 13.1 %collective-permute-start.4 = (bf16[4,128,256]{2,1,0:T(8,128)(2,1)S(1)}, bf16[4,128,256]{2,1,0:T(8,128)(2,1)S(1)}, u32[]{:S(2)}, u32[]{:S(2)}) collective-permute-start(bf16[4,128,256]{2,1,0:T(8,128)(2,1)S(1)} %get-tuple-element.26), channel_id=1, source_target_pairs={{0,4},{2,6},{4,0},{6,2},{1,5},{3,7},{5,1},{7,3},{8,12},{10,14},{12... | collective-permute-start | bytes 786440 | tf_op jit(solution)/shard_map/ppermute | solution.py:35
  100.0 11.5 %collective-permute-start.8 = (bf16[128,256]{1,0:T(8,128)(2,1)S(1)}, bf16[128,256]{1,0:T(8,128)(2,1)S(1)}, u32[]{:S(2)}, u32[]{:S(2)}) collective-permute-start(bf16[128,256]{1,0:T(8,128)(2,1)S(1)} %get-tuple-element.27), channel_id=1, source_target_pairs={{0,24},{8,16},{16,8},{24,0},{1,25},{9,17},{17,9},{25,1},{2,26},{10... | collective-permute-start | bytes 196616 | tf_op jit(solution)/shard_map/ppermute | solution.py:31
  104.0 7.6 %collective-permute-start.7 = (bf16[128,256]{1,0:T(8,128)(2,1)S(1)}, bf16[128,256]{1,0:T(8,128)(2,1)S(1)}, u32[]{:S(2)}, u32[]{:S(2)}) collective-permute-start(bf16[128,256]{1,0:T(8,128)(2,1)S(1)} %get-tuple-element.28), channel_id=1, source_target_pairs={{0,8},{8,0},{16,24},{24,16},{1,9},{9,1},{17,25},{25,17},{2,10},{10... | collective-permute-start | bytes 196616 | tf_op jit(solution)/shard_map/ppermute | solution.py:31
  106.8 6.2 %collective-permute-start.6 = (bf16[128,256]{1,0:T(8,128)(2,1)S(1)}, bf16[128,256]{1,0:T(8,128)(2,1)S(1)}, u32[]{:S(2)}, u32[]{:S(2)}) collective-permute-start(bf16[128,256]{1,0:T(8,128)(2,1)S(1)} %get-tuple-element.29), channel_id=1, source_target_pairs={{0,16},{8,24},{16,0},{24,8},{1,17},{9,25},{17,1},{25,9},{2,18},{10... | collective-permute-start | bytes 196616 | tf_op jit(solution)/shard_map/ppermute | solution.py:31

commit v11 on v10

--- a/solution.py
+++ b/solution.py
@@ -13,6 +13,7 @@
 SAMPLES = ("zh", "yk", "yl")
 FEATURES = ("zl", "x", "core")
 NEAR = ("yl", "zl")
+CHIPS = ("yl", "zl", "core")
 F32 = jnp.float32
 BF16 = jnp.bfloat16
 VMEM_LIMIT = 28 * 1024 * 1024
@@ -39,11 +40,11 @@
     return sum(term.astype(F32) for term in terms).astype(BF16)
 
 
-def sample_row(place_ref, t):
+def sample_block(place_ref, t):
     core = t // 8
     x = lax.rem(place_ref[0] + (t // 2) % 4, 4)
     zl = lax.rem(place_ref[1] + t % 2, 2)
-    return pl.multiple_of(((zl * 4 + x) * 2 + core) * BLOCK, BLOCK)
+    return (zl * 4 + x) * 2 + core
 
 
 def fold(values):
@@ -73,20 +74,23 @@
 
 
 def tile_kernel(
-    place_ref, first_hbm, second_ref, moved_ref, out_hbm,
-    first_ref, na_ref, nb_ref, out_ref, load_sem, out_sems,
+    place_ref, first_ref, near_ref, right_ref, far_ref, left_ref, moved_ref, out_hbm,
+    na_ref, nb_ref, out_ref, out_sems,
 ):
     count = BLOCK * BLOCKS
-    width = first_ref.shape[1]
-    load_first = pltpu.make_async_copy(first_hbm, first_ref, load_sem)
-    load_first.start()
-
+    width = first_ref.shape[2]
+    pieces = BLOCK // first_ref.shape[1]
+
+    def first_block(t):
+        return first_ref[pl.ds(t * pieces, pieces)].reshape(BLOCK, width).astype(F32)
+
+    ahead = (near_ref, right_ref, far_ref, left_ref)
     scales = []
     means = []
     for i in range(2):
         y = lax.rem(place_ref[3] + i, 2)
-        load = lambda t: second_ref[
-            t // 8, (t // 2) % 4, y, lax.rem(place_ref[1] + t % 2, 2)
+        load = lambda t: ahead[(t // 2) % 4][
+            y, lax.rem(place_ref[1] + t % 2, 2), t // 8
         ].astype(F32)
         center, scale = column_statistics(load, BLOCKS, count)
         sums = jnp.zeros((8, width), F32)
@@ -99,13 +103,10 @@
     scale_second = jnp.concatenate(scales, axis=1)
     mean_second = jnp.concatenate(means, axis=1)
 
-    load_first.wait()
-    load = lambda t: first_ref[t * BLOCK : (t + 1) * BLOCK, :].astype(F32)
-    center, scale_first = column_statistics(load, BLOCKS, count)
+    center, scale_first = column_statistics(first_block, BLOCKS, count)
     sums = jnp.zeros((8, width), F32)
     for t in range(BLOCKS):
-        values = first_ref[pl.ds(sample_row(place_ref, t), BLOCK), :].astype(F32)
-        norm = ((values - center) * scale_first).astype(BF16)
+        norm = ((first_block(sample_block(place_ref, t)) - center) * scale_first).astype(BF16)
         na_ref[t * BLOCK : (t + 1) * BLOCK, :] = norm
         sums += fold(norm.astype(F32))
     mean_first = sums / count
@@ -159,9 +160,10 @@
         ) * scale_first
         out_ref[some, :] = partial.astype(BF16)
         for t in range(start, start + CHUNK):
+            row = pl.multiple_of(sample_block(place_ref, t) * BLOCK, BLOCK)
             store = pltpu.make_async_copy(
                 out_ref.at[pl.ds(t * BLOCK, BLOCK)],
-                out_hbm.at[pl.ds(sample_row(place_ref, t), BLOCK)],
+                out_hbm.at[pl.ds(row, BLOCK)],
                 out_sems.at[t],
             )
             store.start()
@@ -198,28 +200,25 @@
 
 
 def local_compute(place, first, second):
-    count, width = first.shape
+    count, width = first.shape[0] * first.shape[1], first.shape[2]
     pieces = (BLOCKS, 2, BLOCK, width)
     smem, vmem, hbm = (pl.BlockSpec(memory_space=m) for m in (pltpu.SMEM, pltpu.VMEM, pltpu.HBM))
-    first = pltpu.with_memory_space_constraint(first, pltpu.HBM)
     return pl.pallas_call(
         tile_kernel,
         out_shape=(jax.ShapeDtypeStruct(pieces, BF16), pltpu.HBM((count, width), BF16)),
-        in_specs=[smem, hbm, vmem],
+        in_specs=[smem, vmem] + [vmem] * len(second),
         out_specs=(vmem, hbm),
         scratch_shapes=[
             pltpu.VMEM((count, width), BF16),
-            pltpu.VMEM((count, width), BF16),
             pltpu.VMEM((count, 2 * width), BF16),
             pltpu.VMEM((count, width), BF16),
-            pltpu.SemaphoreType.DMA,
             pltpu.SemaphoreType.DMA((BLOCKS,)),
         ],
         compiler_params=pltpu.CompilerParams(vmem_limit_bytes=VMEM_LIMIT),
         cost_estimate=pl.CostEstimate(
             flops=12 * count * width * width, bytes_accessed=6 << 20, transcendentals=0
         ),
-    )(place, first, second)
+    )(place, first, *second)
 
 
 def shards(first_view_outputs, second_view_outputs):
@@ -227,18 +226,16 @@
     rows_b, width_b = second_view_outputs.shape
     n_dp = lax.axis_size(SAMPLES)
     half = width_a // 2
-    total_count = rows_a * n_dp
-
-    near = exchange(jnp.broadcast_to(second_view_outputs, (4, rows_b, width_b)), NEAR)
+
+    near = exchange(jnp.broadcast_to(second_view_outputs, (8, rows_b, width_b)), CHIPS)
     spread = spread_halves(first_view_outputs, n_dp)
     near, spread = lax.optimization_barrier((near, spread))
 
-    first = exchange(spread, SAMPLES).reshape(total_count, half)
-
-    ahead = jnp.stack([near] + [shift(near, -k) for k in (1, 2, 3)])
-    ahead = jnp.broadcast_to(ahead, (2,) + ahead.shape)
-    first, ahead = lax.optimization_barrier((first, ahead))
-    second = exchange(ahead, "core").reshape(2, 4, 2, 2, rows_b, width_b)
+    first = exchange(spread, SAMPLES)
+
+    left, right = shift(near, 1), shift(near, -1)
+    far = jnp.concatenate([shift(left[:4], 1), shift(right[4:], -1)])
+    second = [v.reshape(2, 2, 2, rows_b, width_b) for v in (near, right, far, left)]
 
     feat = lax.axis_index(FEATURES)
     pair = lax.axis_index(("zh", "yk"))

time: 115 us -> 117 us (1.017)
  starting transfers between devices: 53.7 us -> 59.8 us
  blocking collectives: 10.8 us -> 5.42 us
    ppermute x6 -> x7, waiting for transfers between devices: 19.5 us -> 27.4 us  [shift(): lax.ppermute(values, 'x', [(i, (i + distance) % 4) for i in range(4)])]
    all_to_all x3, waiting for transfers between devices: 15.5 us -> 8.9 us  [exchange(): return lax.all_to_all(values, axes, 0, 0, tiled=True)]
    all_to_all x2 -> x1, blocking collectives: 10.8 us -> 5.42 us  [exchange(): return lax.all_to_all(values, axes, 0, 0, tiled=True)]
    all_to_all x3, starting transfers between devices: 26.7 us -> 31.1 us  [exchange(): return lax.all_to_all(values, axes, 0, 0, tiled=True)]
    ppermute x6 -> x7, starting transfers between devices: 17.8 us -> 19.4 us  [shift(): lax.ppermute(values, 'x', [(i, (i + distance) % 4) for i in range(4)])]
  transfers between devices with their start and end apart: 12 -> 13, of which waited for: 9 -> 9; matrix products, arithmetic and copies ran while one was open for 1% -> 2% of each run, Pallas kernels for 2% -> 2%
where the time goes in v11:
time: 117 us; the launch traced here: 116 us
  starting transfers between devices  59.8 us (51%)
  waiting for transfers between devices  37.4 us (32%)
  Pallas kernels  7.69 us (7%)
  blocking collectives  5.42 us (5%)
  other arithmetic  2.98 us (3%)
  local copies, waits for them, and re-layouts  1.81 us (2%)
    all_to_all x3, starting transfers between devices, exchange(): return lax.all_to_all(values, axes, 0, 0, tiled=True)  31.1 us
    ppermute x7, waiting for transfers between devices, shift(): lax.ppermute(values, 'x', [(i, (i + distance) % 4) for i in range(4)])  27.4 us
    ppermute x7, starting transfers between devices, shift(): lax.ppermute(values, 'x', [(i, (i + distance) % 4) for i in range(4)])  19.4 us
    ppermute x3, starting transfers between devices, near_swap(): return lax.ppermute(values, NEAR, [(i, i ^ flip) for i in range(4)])  9.21 us
    all_to_all x3, waiting for transfers between devices, exchange(): return lax.all_to_all(values, axes, 0, 0, tiled=True)  8.9 us
    pallas_call x1, Pallas kernels, local_compute(): pl.pallas_call(tile_kernel, out_shape=(jax.ShapeDtypeStruct(pieces, BF16)...  5.71 us
    all_to_all x1, blocking collectives, exchange(): return lax.all_to_all(values, axes, 0, 0, tiled=True)  5.42 us
  transfers between devices with their start and end apart: 13, of which 9 were waited for; matrix products, arithmetic and copies ran while one was open for 2% of the time, Pallas kernels for 2%

profile of v11, /device:TPU:6, one launch (start us, length us, event | category | flops | bytes accessed | tf_op | source)
XLA Modules:
  0.0 115.9 jit_solution(18122588647393749635)
XLA Ops:
  0.6 1.7 %broadcast_in_dim.3 = bf16[8,128,256]{2,1,0:T(8,128)(2,1)} broadcast(bf16[128,256]{1,0:T(8,128)(2,1)} %param.3), dimensions={1,2} | broadcast | bytes 589824 | tf_op jit(solution)/shard_map/broadcast_in_dim | solution.py:230
  2.3 4.7 %all-to-all-start = ((bf16[8,128,256]{2,1,0:T(8,128)(2,1)}), bf16[8,128,256]{2,1,0:T(8,128)(2,1)S(1)}, u32[]{:S(2)}, u32[]{:S(2)}) async-start(bf16[8,128,256]{2,1,0:T(8,128)(2,1)} %broadcast_in_dim.3), calls=%async_computation | async-start | bytes 1048576 | tf_op jit(solution)/shard_map/all_to_all | solution.py:27
  7.0 2.0 %shard_map.41 = bf16[32,64,256]{2,1,0:T(8,128)(2,1)} custom-call(bf16[64,512]{1,0:T(8,128)(2,1)} %values_ref.1), custom_call_target="tpu_custom_call" | custom-call | bytes 2097152 | tf_op jit(solution)/shard_map/pallas_call | solution.py:192
  9.0 6.9 %all-to-all-done = bf16[8,128,256]{2,1,0:T(8,128)(2,1)S(1)} async-done(((bf16[8,128,256]{2,1,0:T(8,128)(2,1)}), bf16[8,128,256]{2,1,0:T(8,128)(2,1)S(1)}, u32[]{:S(2)}, u32[]{:S(2)}) %all-to-all-start) | async-done | bytes 524320 | tf_op jit(solution)/shard_map/all_to_all | solution.py:27
  15.8 14.7 %all-to-all-start.1 = ((bf16[32,64,256]{2,1,0:T(8,128)(2,1)}), bf16[32,64,256]{2,1,0:T(8,128)(2,1)S(1)}, u32[]{:S(2)}, u32[]{:S(2)}) async-start(bf16[32,64,256]{2,1,0:T(8,128)(2,1)} %shard_map.41), calls=%async_computation.1 | async-start | bytes 2097152 | tf_op jit(solution)/shard_map/all_to_all | solution.py:27
  30.6 2.4 %collective-permute-start.1 = (bf16[8,128,256]{2,1,0:T(8,128)(2,1)S(1)}, bf16[8,128,256]{2,1,0:T(8,128)(2,1)S(1)}, u32[]{:S(2)}, u32[]{:S(2)}) collective-permute-start(bf16[8,128,256]{2,1,0:T(8,128)(2,1)S(1)} %all-to-all-done), channel_id=1, source_target_pairs={{0,2},{2,4},{4,6},{6,0},{1,3},{3,5},{5,7},{7,1},{8,10},{10,12},{12... | collective-permute-start | bytes 1572872 | tf_op jit(solution)/shard_map/ppermute | solution.py:36
  33.0 3.5 %collective-permute-start = (bf16[8,128,256]{2,1,0:T(8,128)(2,1)S(1)}, bf16[8,128,256]{2,1,0:T(8,128)(2,1)S(1)}, u32[]{:S(2)}, u32[]{:S(2)}) collective-permute-start(bf16[8,128,256]{2,1,0:T(8,128)(2,1)S(1)} %all-to-all-done), channel_id=1, source_target_pairs={{0,6},{2,0},{4,2},{6,4},{1,7},{3,1},{5,3},{7,5},{8,14},{10,8},{12,... | collective-permute-start | bytes 1572872 | tf_op jit(solution)/shard_map/ppermute | solution.py:36
  36.4 9.2 %collective-permute-done.1 = bf16[8,128,256]{2,1,0:T(8,128)(2,1)S(1)} collective-permute-done((bf16[8,128,256]{2,1,0:T(8,128)(2,1)S(1)}, bf16[8,128,256]{2,1,0:T(8,128)(2,1)S(1)}, u32[]{:S(2)}, u32[]{:S(2)}) %collective-permute-start.1) | collective-permute-done | bytes 524320 | tf_op jit(solution)/shard_map/ppermute | solution.py:36
  45.7 3.6 %collective-permute-start.2 = (bf16[4,128,256]{2,1,0:T(8,128)(2,1)S(1)}, bf16[4,128,256]{2,1,0:T(8,128)(2,1)S(1)}, u32[]{:S(2)}, u32[]{:S(2)}) collective-permute-start(bf16[4,128,256]{2,1,0:T(8,128)(2,1)S(1)} %slice.60), channel_id=1, source_target_pairs={{0,2},{2,4},{4,6},{6,0},{1,3},{3,5},{5,7},{7,1},{8,10},{10,12},{12... | collective-permute-start | bytes 786440 | tf_op jit(solution)/shard_map/ppermute | solution.py:36
  49.3 0.0 collective-permute-done
  49.3 2.2 %collective-permute-start.3 = (bf16[4,128,256]{2,1,0:T(8,128)(2,1)S(1)}, bf16[4,128,256]{2,1,0:T(8,128)(2,1)}, u32[]{:S(2)}, u32[]{:S(2)}) collective-permute-start(bf16[4,128,256]{2,1,0:T(8,128)(2,1)S(1)} %slice.61), channel_id=1, source_target_pairs={{0,6},{2,0},{4,2},{6,4},{1,7},{3,1},{5,3},{7,5},{8,14},{10,8},{12,... | collective-permute-start | bytes 786440 | tf_op jit(solution)/shard_map/ppermute | solution.py:36
  51.6 0.1 pad_add_fusion.place_ref
  51.6 2.5 %collective-permute-done.2 = bf16[4,128,256]{2,1,0:T(8,128)(2,1)S(1)} collective-permute-done((bf16[4,128,256]{2,1,0:T(8,128)(2,1)S(1)}, bf16[4,128,256]{2,1,0:T(8,128)(2,1)S(1)}, u32[]{:S(2)}, u32[]{:S(2)}) %collective-permute-start.2) | collective-permute-done | bytes 262176 | tf_op jit(solution)/shard_map/ppermute | solution.py:36
  54.2 4.7 %collective-permute-done.3 = bf16[4,128,256]{2,1,0:T(8,128)(2,1)} collective-permute-done((bf16[4,128,256]{2,1,0:T(8,128)(2,1)S(1)}, bf16[4,128,256]{2,1,0:T(8,128)(2,1)}, u32[]{:S(2)}, u32[]{:S(2)}) %collective-permute-start.3) | collective-permute-done | bytes 262176 | tf_op jit(solution)/shard_map/ppermute | solution.py:36
  58.9 1.0 pad_maximum_fusion
  59.9 0.2 all-to-all-done.1.first_ref
  60.1 5.7 %shard_map.42 = (bf16[16,2,128,256]{3,2,1,0:T(8,128)(2,1)S(1)}, bf16[2048,256]{1,0:T(8,128)(2,1)}) custom-call(s32[4]{0:T(128)S(1)} %pad_add_fusion.place_ref, bf16[32,64,256]{2,1,0:T(8,128)(2,1)S(1)} %all-to-all-done.1.first_ref, bf16[2,2,2,128,256]{4,3,2,1,0:T(8,128)(2,1)S(1)} %bitcast.35, bf16[2,2,2,128,256]{4,3,2,1,0:T(8,128)(2,1)S(1)} %bitcast.38, ...), custom_call_target="tpu_custom_call" | custom-call | flops 1610612736 | bytes 6291456 | tf_op jit(solution)/shard_map/pallas_call | solution.py:206
  65.8 5.4 %all_to_all.20 = bf16[2,4,4,128,256]{4,3,2,1,0:T(8,128)(2,1)S(1)} all-to-all(bf16[2,4,4,128,256]{4,3,2,1,0:T(8,128)(2,1)S(1)} %bitcast.34), channel_id=1, replica_groups=mesh['zh'=4,'yk'=4,'yl'=2,'zl'=2,'x'=4,'core'=2] {'core'}, dimensions={0} | all-to-all | bytes 4194304 | tf_op jit(solution)/shard_map/all_to_all | solution.py:27
  71.2 11.7 %all-to-all-start.2 = ((bf16[32,64,256]{2,1,0:T(8,128)(2,1)}), bf16[32,64,256]{2,1,0:T(8,128)(2,1)S(1)}, u32[]{:S(2)}, u32[]{:S(2)}) async-start(bf16[32,64,256]{2,1,0:T(8,128)(2,1)} %bitcast.40), calls=%async_computation.2 | async-start | bytes 2097152 | tf_op jit(solution)/shard_map/all_to_all | solution.py:27
  83.0 0.3 add_convert_fusion
  83.3 0.1 slice_bitcast_fusion.2
  83.3 1.9 %collective-permute-start.4 = (bf16[4,128,256]{2,1,0:T(8,128)(2,1)S(1)}, bf16[4,128,256]{2,1,0:T(8,128)(2,1)S(1)}, u32[]{:S(2)}, u32[]{:S(2)}) collective-permute-start(bf16[4,128,256]{2,1,0:T(8,128)(2,1)S(1)} %get-tuple-element.20), channel_id=1, source_target_pairs={{0,2},{2,4},{4,6},{6,0},{1,3},{3,5},{5,7},{7,1},{8,10},{10,12},{12... | collective-permute-start | bytes 786440 | tf_op jit(solution)/shard_map/ppermute | solution.py:36
  85.3 3.9 %collective-permute-start.6 = (bf16[4,128,256]{2,1,0:T(8,128)(2,1)S(1)}, bf16[4,128,256]{2,1,0:T(8,128)(2,1)S(1)}, u32[]{:S(2)}, u32[]{:S(2)}) collective-permute-start(bf16[4,128,256]{2,1,0:T(8,128)(2,1)S(1)} %get-tuple-element.21), channel_id=1, source_target_pairs={{0,6},{2,0},{4,2},{6,4},{1,7},{3,1},{5,3},{7,5},{8,14},{10,8},{12,... | collective-permute-start | bytes 786440 | tf_op jit(solution)/shard_map/ppermute | solution.py:36
  89.2 1.9 %collective-permute-start.5 = (bf16[4,128,256]{2,1,0:T(8,128)(2,1)S(1)}, bf16[4,128,256]{2,1,0:T(8,128)(2,1)S(1)}, u32[]{:S(2)}, u32[]{:S(2)}) collective-permute-start(bf16[4,128,256]{2,1,0:T(8,128)(2,1)S(1)} %get-tuple-element.22), channel_id=1, source_target_pairs={{0,4},{2,6},{4,0},{6,2},{1,5},{3,7},{5,1},{7,3},{8,12},{10,14},{12... | collective-permute-start | bytes 786440 | tf_op jit(solution)/shard_map/ppermute | solution.py:36
  91.1 2.2 %collective-permute-done.4 = bf16[4,128,256]{2,1,0:T(8,128)(2,1)S(1)} collective-permute-done((bf16[4,128,256]{2,1,0:T(8,128)(2,1)S(1)}, bf16[4,128,256]{2,1,0:T(8,128)(2,1)S(1)}, u32[]{:S(2)}, u32[]{:S(2)}) %collective-permute-start.4) | collective-permute-done | bytes 262176 | tf_op jit(solution)/shard_map/ppermute | solution.py:36
  93.3 8.8 %collective-permute-done.6 = bf16[4,128,256]{2,1,0:T(8,128)(2,1)S(1)} collective-permute-done((bf16[4,128,256]{2,1,0:T(8,128)(2,1)S(1)}, bf16[4,128,256]{2,1,0:T(8,128)(2,1)S(1)}, u32[]{:S(2)}, u32[]{:S(2)}) %collective-permute-start.6) | collective-permute-done | bytes 262176 | tf_op jit(solution)/shard_map/ppermute | solution.py:36
  102.0 0.0 collective-permute-done.5
  102.1 0.1 fusion.2
  102.2 4.3 %collective-permute-start.9 = (bf16[128,256]{1,0:T(8,128)(2,1)S(1)}, bf16[128,256]{1,0:T(8,128)(2,1)S(1)}, u32[]{:S(2)}, u32[]{:S(2)}) collective-permute-start(bf16[128,256]{1,0:T(8,128)(2,1)S(1)} %get-tuple-element.23), channel_id=1, source_target_pairs={{0,24},{8,16},{16,8},{24,0},{1,25},{9,17},{17,9},{25,1},{2,26},{10... | collective-permute-start | bytes 196616 | tf_op jit(solution)/shard_map/ppermute | solution.py:32
  106.6 2.5 %collective-permute-start.8 = (bf16[128,256]{1,0:T(8,128)(2,1)S(1)}, bf16[128,256]{1,0:T(8,128)(2,1)S(1)}, u32[]{:S(2)}, u32[]{:S(2)}) collective-permute-start(bf16[128,256]{1,0:T(8,128)(2,1)S(1)} %get-tuple-element.24), channel_id=1, source_target_pairs={{0,8},{8,0},{16,24},{24,16},{1,9},{9,1},{17,25},{25,17},{2,10},{10... | collective-permute-start | bytes 196616 | tf_op jit(solution)/shard_map/ppermute | solution.py:32
  109.0 2.4 %collective-permute-start.7 = (bf16[128,256]{1,0:T(8,128)(2,1)S(1)}, bf16[128,256]{1,0:T(8,128)(2,1)S(1)}, u32[]{:S(2)}, u32[]{:S(2)}) collective-permute-start(bf16[128,256]{1,0:T(8,128)(2,1)S(1)} %get-tuple-element.25), channel_id=1, source_target_pairs={{0,16},{8,24},{16,0},{24,8},{1,17},{9,25},{17,1},{25,9},{2,18},{10... | collective-permute-start | bytes 196616 | tf_op jit(solution)/shard_map/ppermute | solution.py:32
  111.5 1.8 %all-to-all-done.2 = bf16[32,64,256]{2,1,0:T(8,128)(2,1)S(1)} async-done(((bf16[32,64,256]{2,1,0:T(8,128)(2,1)}), bf16[32,64,256]{2,1,0:T(8,128)(2,1)S(1)}, u32[]{:S(2)}, u32[]{:S(2)}) %all-to-all-start.2) | async-done | bytes 1048608 | tf_op jit(solution)/shard_map/all_to_all | solution.py:27
  113.3 0.1 reduce_sum.12
  113.5 0.6 pad_maximum_fusion.1
  114.1 0.0 collective-permute-done.9
  114.1 0.0 collective-permute-done.8
  114.1 1.1 collective-permute-done.7
  115.2 0.7 add_convert_fusion.1
  (4 shorter events, 0.1 us)
Async XLA Ops:
  2.3 13.5 %all-to-all-start = ((bf16[8,128,256]{2,1,0:T(8,128)(2,1)}), bf16[8,128,256]{2,1,0:T(8,128)(2,1)S(1)}, u32[]{:S(2)}, u32[]{:S(2)}) async-start(bf16[8,128,256]{2,1,0:T(8,128)(2,1)} %broadcast_in_dim.3), calls=%async_computation | async-start | bytes 1048576 | tf_op jit(solution)/shard_map/all_to_all | solution.py:27
  15.8 44.2 %all-to-all-start.1 = ((bf16[32,64,256]{2,1,0:T(8,128)(2,1)}), bf16[32,64,256]{2,1,0:T(8,128)(2,1)S(1)}, u32[]{:S(2)}, u32[]{:S(2)}) async-start(bf16[32,64,256]{2,1,0:T(8,128)(2,1)} %shard_map.41), calls=%async_computation.1 | async-start | bytes 2097152 | tf_op jit(solution)/shard_map/all_to_all | solution.py:27
  30.6 15.1 %collective-permute-start.1 = (bf16[8,128,256]{2,1,0:T(8,128)(2,1)S(1)}, bf16[8,128,256]{2,1,0:T(8,128)(2,1)S(1)}, u32[]{:S(2)}, u32[]{:S(2)}) collective-permute-start(bf16[8,128,256]{2,1,0:T(8,128)(2,1)S(1)} %all-to-all-done), channel_id=1, source_target_pairs={{0,2},{2,4},{4,6},{6,0},{1,3},{3,5},{5,7},{7,1},{8,10},{10,12},{12... | collective-permute-start | bytes 1572872 | tf_op jit(solution)/shard_map/ppermute | solution.py:36
  33.0 16.3 %collective-permute-start = (bf16[8,128,256]{2,1,0:T(8,128)(2,1)S(1)}, bf16[8,128,256]{2,1,0:T(8,128)(2,1)S(1)}, u32[]{:S(2)}, u32[]{:S(2)}) collective-permute-start(bf16[8,128,256]{2,1,0:T(8,128)(2,1)S(1)} %all-to-all-done), channel_id=1, source_target_pairs={{0,6},{2,0},{4,2},{6,4},{1,7},{3,1},{5,3},{7,5},{8,14},{10,8},{12,... | collective-permute-start | bytes 1572872 | tf_op jit(solution)/shard_map/ppermute | solution.py:36
  45.7 8.5 %collective-permute-start.2 = (bf16[4,128,256]{2,1,0:T(8,128)(2,1)S(1)}, bf16[4,128,256]{2,1,0:T(8,128)(2,1)S(1)}, u32[]{:S(2)}, u32[]{:S(2)}) collective-permute-start(bf16[4,128,256]{2,1,0:T(8,128)(2,1)S(1)} %slice.60), channel_id=1, source_target_pairs={{0,2},{2,4},{4,6},{6,0},{1,3},{3,5},{5,7},{7,1},{8,10},{10,12},{12... | collective-permute-start | bytes 786440 | tf_op jit(solution)/shard_map/ppermute | solution.py:36
  49.3 9.6 %collective-permute-start.3 = (bf16[4,128,256]{2,1,0:T(8,128)(2,1)S(1)}, bf16[4,128,256]{2,1,0:T(8,128)(2,1)}, u32[]{:S(2)}, u32[]{:S(2)}) collective-permute-start(bf16[4,128,256]{2,1,0:T(8,128)(2,1)S(1)} %slice.61), channel_id=1, source_target_pairs={{0,6},{2,0},{4,2},{6,4},{1,7},{3,1},{5,3},{7,5},{8,14},{10,8},{12,... | collective-permute-start | bytes 786440 | tf_op jit(solution)/shard_map/ppermute | solution.py:36
  71.2 42.1 %all-to-all-start.2 = ((bf16[32,64,256]{2,1,0:T(8,128)(2,1)}), bf16[32,64,256]{2,1,0:T(8,128)(2,1)S(1)}, u32[]{:S(2)}, u32[]{:S(2)}) async-start(bf16[32,64,256]{2,1,0:T(8,128)(2,1)} %bitcast.40), calls=%async_computation.2 | async-start | bytes 2097152 | tf_op jit(solution)/shard_map/all_to_all | solution.py:27
  83.3 10.0 %collective-permute-start.4 = (bf16[4,128,256]{2,1,0:T(8,128)(2,1)S(1)}, bf16[4,128,256]{2,1,0:T(8,128)(2,1)S(1)}, u32[]{:S(2)}, u32[]{:S(2)}) collective-permute-start(bf16[4,128,256]{2,1,0:T(8,128)(2,1)S(1)} %get-tuple-element.20), channel_id=1, source_target_pairs={{0,2},{2,4},{4,6},{6,0},{1,3},{3,5},{5,7},{7,1},{8,10},{10,12},{12... | collective-permute-start | bytes 786440 | tf_op jit(solution)/shard_map/ppermute | solution.py:36
  85.3 16.8 %collective-permute-start.6 = (bf16[4,128,256]{2,1,0:T(8,128)(2,1)S(1)}, bf16[4,128,256]{2,1,0:T(8,128)(2,1)S(1)}, u32[]{:S(2)}, u32[]{:S(2)}) collective-permute-start(bf16[4,128,256]{2,1,0:T(8,128)(2,1)S(1)} %get-tuple-element.21), channel_id=1, source_target_pairs={{0,6},{2,0},{4,2},{6,4},{1,7},{3,1},{5,3},{7,5},{8,14},{10,8},{12,... | collective-permute-start | bytes 786440 | tf_op jit(solution)/shard_map/ppermute | solution.py:36
  89.2 12.9 %collective-permute-start.5 = (bf16[4,128,256]{2,1,0:T(8,128)(2,1)S(1)}, bf16[4,128,256]{2,1,0:T(8,128)(2,1)S(1)}, u32[]{:S(2)}, u32[]{:S(2)}) collective-permute-start(bf16[4,128,256]{2,1,0:T(8,128)(2,1)S(1)} %get-tuple-element.22), channel_id=1, source_target_pairs={{0,4},{2,6},{4,0},{6,2},{1,5},{3,7},{5,1},{7,3},{8,12},{10,14},{12... | collective-permute-start | bytes 786440 | tf_op jit(solution)/shard_map/ppermute | solution.py:36
  102.2 11.9 %collective-permute-start.9 = (bf16[128,256]{1,0:T(8,128)(2,1)S(1)}, bf16[128,256]{1,0:T(8,128)(2,1)S(1)}, u32[]{:S(2)}, u32[]{:S(2)}) collective-permute-start(bf16[128,256]{1,0:T(8,128)(2,1)S(1)} %get-tuple-element.23), channel_id=1, source_target_pairs={{0,24},{8,16},{16,8},{24,0},{1,25},{9,17},{17,9},{25,1},{2,26},{10... | collective-permute-start | bytes 196616 | tf_op jit(solution)/shard_map/ppermute | solution.py:32
  106.6 7.5 %collective-permute-start.8 = (bf16[128,256]{1,0:T(8,128)(2,1)S(1)}, bf16[128,256]{1,0:T(8,128)(2,1)S(1)}, u32[]{:S(2)}, u32[]{:S(2)}) collective-permute-start(bf16[128,256]{1,0:T(8,128)(2,1)S(1)} %get-tuple-element.24), channel_id=1, source_target_pairs={{0,8},{8,0},{16,24},{24,16},{1,9},{9,1},{17,25},{25,17},{2,10},{10... | collective-permute-start | bytes 196616 | tf_op jit(solution)/shard_map/ppermute | solution.py:32
  109.0 6.2 %collective-permute-start.7 = (bf16[128,256]{1,0:T(8,128)(2,1)S(1)}, bf16[128,256]{1,0:T(8,128)(2,1)S(1)}, u32[]{:S(2)}, u32[]{:S(2)}) collective-permute-start(bf16[128,256]{1,0:T(8,128)(2,1)S(1)} %get-tuple-element.25), channel_id=1, source_target_pairs={{0,16},{8,24},{16,0},{24,8},{1,17},{9,25},{17,1},{25,9},{2,18},{10... | collective-permute-start | bytes 196616 | tf_op jit(solution)/shard_map/ppermute | solution.py:32

commit v12 on v11

--- a/solution.py
+++ b/solution.py
@@ -13,7 +13,6 @@
 SAMPLES = ("zh", "yk", "yl")
 FEATURES = ("zl", "x", "core")
 NEAR = ("yl", "zl")
-CHIPS = ("yl", "zl", "core")
 F32 = jnp.float32
 BF16 = jnp.bfloat16
 VMEM_LIMIT = 28 * 1024 * 1024
@@ -51,16 +50,20 @@
     return values.reshape(-1, 8, values.shape[-1]).sum(axis=0)
 
 
-def split_rows(sums):
-    row = jnp.sum(sums, axis=0, keepdims=True)
+def split_bf16(row):
     rows = []
     for _ in range(3):
         rows.append(row.astype(BF16))
         row = row - rows[-1].astype(F32)
-    return jnp.concatenate(rows + [jnp.zeros((13, row.shape[1]), BF16)], axis=0)
-
-
-def column_statistics(load, blocks, count):
+    return rows
+
+
+def split_rows(sums):
+    rows = split_bf16(jnp.sum(sums, axis=0, keepdims=True))
+    return jnp.concatenate(rows + [jnp.zeros((13, sums.shape[1]), BF16)], axis=0)
+
+
+def column_moments(load, blocks, count):
     pivot = jnp.mean(load(0), axis=0, keepdims=True)
     sums = jnp.zeros((8, pivot.shape[1]), F32)
     squares = sums
@@ -68,13 +71,42 @@
         shifted = load(t) - pivot
         sums += fold(shifted)
         squares += fold(shifted * shifted)
-    offset = jnp.sum(sums, axis=0, keepdims=True) / count
-    spread = jnp.sum(squares, axis=0, keepdims=True) / count - offset * offset
-    return pivot + offset, lax.rsqrt(jnp.maximum(spread, 0.0) + EPSILON)
+    sums = jnp.sum(sums, axis=0, keepdims=True)
+    offset = sums / count
+    return pivot + offset, jnp.sum(squares, axis=0, keepdims=True) - offset * sums
+
+
+def half_kernel(*refs):
+    block_refs, out_ref = refs[:-1], refs[-1]
+    blocks = len(block_refs) * 2
+    rows = []
+    for y in range(2):
+        load = lambda t: block_refs[t // 2][2 * y + t % 2].astype(F32)
+        mean, squares = column_moments(load, blocks, blocks * BLOCK)
+        rows += split_bf16(mean) + split_bf16(squares)
+    rows.append(jnp.zeros((4, rows[0].shape[1]), BF16))
+    for x, ref in enumerate(block_refs):
+        for i in range(4):
+            row = (x * 4 + i) * BLOCK
+            out_ref[row : row + BLOCK, :] = ref[i]
+    out_ref[len(block_refs) * 4 * BLOCK :, :] = jnp.concatenate(rows, axis=0)
+
+
+def join_halves(first, second, y):
+    first, second = first.astype(F32), second.astype(F32)
+
+    def value(rows, i):
+        return sum(rows[y * 6 + i * 3 + k : y * 6 + i * 3 + k + 1] for k in range(3))
+
+    count = BLOCKS * BLOCK
+    apart = value(first, 0) - value(second, 0)
+    squares = value(first, 1) + value(second, 1) + apart * apart * (count / 4)
+    mean = 0.5 * (value(first, 0) + value(second, 0))
+    return mean, lax.rsqrt(jnp.maximum(squares, 0.0) / count + EPSILON)
 
 
 def tile_kernel(
-    place_ref, first_ref, near_ref, right_ref, far_ref, left_ref, moved_ref, out_hbm,
+    place_ref, first_ref, second_ref, moved_ref, out_hbm,
     na_ref, nb_ref, out_ref, out_sems,
 ):
     count = BLOCK * BLOCKS
@@ -84,15 +116,21 @@
     def first_block(t):
         return first_ref[pl.ds(t * pieces, pieces)].reshape(BLOCK, width).astype(F32)
 
-    ahead = (near_ref, right_ref, far_ref, left_ref)
+    statistics = [
+        join_halves(*(second_ref[c, BLOCKS * BLOCK :, :] for c in range(2)), y)
+        for y in range(2)
+    ]
     scales = []
     means = []
     for i in range(2):
         y = lax.rem(place_ref[3] + i, 2)
-        load = lambda t: ahead[(t // 2) % 4][
-            y, lax.rem(place_ref[1] + t % 2, 2), t // 8
-        ].astype(F32)
-        center, scale = column_statistics(load, BLOCKS, count)
+
+        def load(t):
+            block = (t // 2) % 4 * 4 + y * 2 + lax.rem(place_ref[1] + t % 2, 2)
+            rows = pl.ds(pl.multiple_of(block * BLOCK, BLOCK), BLOCK)
+            return second_ref[t // 8, rows, :].astype(F32)
+
+        center, scale = (jnp.where(y == 0, u, v) for u, v in zip(*statistics))
         sums = jnp.zeros((8, width), F32)
         for t in range(BLOCKS):
             norm = ((load(t) - center) * scale).astype(BF16)
@@ -103,7 +141,8 @@
     scale_second = jnp.concatenate(scales, axis=1)
     mean_second = jnp.concatenate(means, axis=1)
 
-    center, scale_first = column_statistics(first_block, BLOCKS, count)
+    center, squares = column_moments(first_block, BLOCKS, count)
+    scale_first = lax.rsqrt(jnp.maximum(squares, 0.0) / count + EPSILON)
     sums = jnp.zeros((8, width), F32)
     for t in range(BLOCKS):
         norm = ((first_block(sample_block(place_ref, t)) - center) * scale_first).astype(BF16)
@@ -199,6 +238,19 @@
     )(values)
 
 
+def gather_half(parts):
+    rows = len(parts) * 4 * BLOCK + 16
+    spec = pl.BlockSpec(memory_space=pltpu.VMEM)
+    return pl.pallas_call(
+        half_kernel,
+        out_shape=jax.ShapeDtypeStruct((rows, parts[0].shape[2]), BF16),
+        in_specs=[spec] * len(parts),
+        out_specs=spec,
+        compiler_params=pltpu.CompilerParams(vmem_limit_bytes=VMEM_LIMIT),
+        cost_estimate=pl.CostEstimate(flops=4 << 20, bytes_accessed=2 << 20, transcendentals=0),
+    )(*parts)
+
+
 def local_compute(place, first, second):
     count, width = first.shape[0] * first.shape[1], first.shape[2]
     pieces = (BLOCKS, 2, BLOCK, width)
@@ -206,7 +258,7 @@
     return pl.pallas_call(
         tile_kernel,
         out_shape=(jax.ShapeDtypeStruct(pieces, BF16), pltpu.HBM((count, width), BF16)),
-        in_specs=[smem, vmem] + [vmem] * len(second),
+        in_specs=[smem, vmem, vmem],
         out_specs=(vmem, hbm),
         scratch_shapes=[
             pltpu.VMEM((count, width), BF16),
@@ -218,7 +270,7 @@
         cost_estimate=pl.CostEstimate(
             flops=12 * count * width * width, bytes_accessed=6 << 20, transcendentals=0
         ),
-    )(place, first, *second)
+    )(place, first, second)
 
 
 def shards(first_view_outputs, second_view_outputs):
@@ -227,15 +279,16 @@
     n_dp = lax.axis_size(SAMPLES)
     half = width_a // 2
 
-    near = exchange(jnp.broadcast_to(second_view_outputs, (8, rows_b, width_b)), CHIPS)
+    near = exchange(jnp.broadcast_to(second_view_outputs, (4, rows_b, width_b)), NEAR)
     spread = spread_halves(first_view_outputs, n_dp)
     near, spread = lax.optimization_barrier((near, spread))
 
     first = exchange(spread, SAMPLES)
 
-    left, right = shift(near, 1), shift(near, -1)
-    far = jnp.concatenate([shift(left[:4], 1), shift(right[4:], -1)])
-    second = [v.reshape(2, 2, 2, rows_b, width_b) for v in (near, right, far, left)]
+    own = gather_half([near] + [shift(near, -k) for k in (1, 2, 3)])
+    own = jnp.broadcast_to(own, (2,) + own.shape)
+    first, own = lax.optimization_barrier((first, own))
+    second = exchange(own, "core")
 
     feat = lax.axis_index(FEATURES)
     pair = lax.axis_index(("zh", "yk"))

time: 117 us -> 114 us (0.974)
  starting transfers between devices: 59.8 us -> 53.7 us
  blocking collectives: 5.42 us -> 10.8 us
  waiting for transfers between devices: 37.4 us -> 36.1 us
    ppermute x7 -> x6, waiting for transfers between devices: 27.4 us -> 19.5 us  [shift(): lax.ppermute(values, 'x', [(i, (i + distance) % 4) for i in range(4)])]
    all_to_all x3, waiting for transfers between devices: 8.9 us -> 15.2 us  [exchange(): return lax.all_to_all(values, axes, 0, 0, tiled=True)]
    all_to_all x1 -> x2, blocking collectives: 5.42 us -> 10.8 us  [exchange(): return lax.all_to_all(values, axes, 0, 0, tiled=True)]
    all_to_all x3, starting transfers between devices: 31.1 us -> 26.7 us  [exchange(): return lax.all_to_all(values, axes, 0, 0, tiled=True)]
    ppermute x7 -> x6, starting transfers between devices: 19.4 us -> 17.8 us  [shift(): lax.ppermute(values, 'x', [(i, (i + distance) % 4) for i in range(4)])]
  transfers between devices with their start and end apart: 13 -> 12, of which waited for: 9 -> 9; matrix products, arithmetic and copies ran while one was open for 2% -> 1% of each run, Pallas kernels for 2% -> 2%
where the time goes in v12:
time: 114 us; the launch traced here: 113 us
  starting transfers between devices  53.7 us (47%)
  waiting for transfers between devices  36.1 us (32%)
  blocking collectives  10.8 us (9%)
  Pallas kernels  7.33 us (6%)
  other arithmetic  1.98 us (2%)
  local copies, waits for them, and re-layouts  1.8 us (2%)
    all_to_all x3, starting transfers between devices, exchange(): return lax.all_to_all(values, axes, 0, 0, tiled=True)  26.7 us
    ppermute x6, waiting for transfers between devices, shift(): lax.ppermute(values, 'x', [(i, (i + distance) % 4) for i in range(4)])  19.5 us
    ppermute x6, starting transfers between devices, shift(): lax.ppermute(values, 'x', [(i, (i + distance) % 4) for i in range(4)])  17.8 us
    all_to_all x3, waiting for transfers between devices, exchange(): return lax.all_to_all(values, axes, 0, 0, tiled=True)  15.2 us
    all_to_all x2, blocking collectives, exchange(): return lax.all_to_all(values, axes, 0, 0, tiled=True)  10.8 us
    ppermute x3, starting transfers between devices, near_swap(): return lax.ppermute(values, NEAR, [(i, i ^ flip) for i in range(4)])  9.21 us
    pallas_call x1, Pallas kernels, local_compute(): pl.pallas_call(tile_kernel, out_shape=(jax.ShapeDtypeStruct(pieces, BF16)...  4.88 us
  transfers between devices with their start and end apart: 12, of which 9 were waited for; matrix products, arithmetic and copies ran while one was open for 1% of the time, Pallas kernels for 2%

profile of v12, /device:TPU:6, one launch (start us, length us, event | category | flops | bytes accessed | tf_op | source)
XLA Modules:
  0.0 112.5 jit_solution(15746185309966752232)
XLA Ops:
  0.6 1.6 %broadcast_in_dim.6 = bf16[4,128,256]{2,1,0:T(8,128)(2,1)} broadcast(bf16[128,256]{1,0:T(8,128)(2,1)} %param.3), dimensions={1,2} | broadcast | bytes 327680 | tf_op jit(solution)/shard_map/broadcast_in_dim | solution.py:282
  2.2 4.7 %all-to-all-start = ((bf16[4,128,256]{2,1,0:T(8,128)(2,1)}), bf16[4,128,256]{2,1,0:T(8,128)(2,1)S(1)}, u32[]{:S(2)}, u32[]{:S(2)}) async-start(bf16[4,128,256]{2,1,0:T(8,128)(2,1)} %broadcast_in_dim.6), calls=%async_computation | async-start | bytes 524288 | tf_op jit(solution)/shard_map/all_to_all | solution.py:26
  6.9 2.0 %shard_map.41 = bf16[32,64,256]{2,1,0:T(8,128)(2,1)} custom-call(bf16[64,512]{1,0:T(8,128)(2,1)} %values_ref.1), custom_call_target="tpu_custom_call" | custom-call | bytes 2097152 | tf_op jit(solution)/shard_map/pallas_call | solution.py:231
  8.8 3.4 %all-to-all-done.refs_0_ = bf16[4,128,256]{2,1,0:T(8,128)(2,1)S(1)} async-done(((bf16[4,128,256]{2,1,0:T(8,128)(2,1)}), bf16[4,128,256]{2,1,0:T(8,128)(2,1)S(1)}, u32[]{:S(2)}, u32[]{:S(2)}) %all-to-all-start) | async-done | bytes 262176 | tf_op jit(solution)/shard_map/all_to_all | solution.py:26
  12.2 15.0 %all-to-all-start.1 = ((bf16[32,64,256]{2,1,0:T(8,128)(2,1)}), bf16[32,64,256]{2,1,0:T(8,128)(2,1)S(1)}, u32[]{:S(2)}, u32[]{:S(2)}) async-start(bf16[32,64,256]{2,1,0:T(8,128)(2,1)} %shard_map.41), calls=%async_computation.1 | async-start | bytes 2097152 | tf_op jit(solution)/shard_map/all_to_all | solution.py:26
  27.2 2.4 %collective-permute-start.2 = (bf16[4,128,256]{2,1,0:T(8,128)(2,1)S(1)}, bf16[4,128,256]{2,1,0:T(8,128)(2,1)S(1)}, u32[]{:S(2)}, u32[]{:S(2)}) collective-permute-start(bf16[4,128,256]{2,1,0:T(8,128)(2,1)S(1)} %all-to-all-done.refs_0_), channel_id=1, source_target_pairs={{0,2},{2,4},{4,6},{6,0},{1,3},{3,5},{5,7},{7,1},{8,10},{10,12},{12... | collective-permute-start | bytes 786440 | tf_op jit(solution)/shard_map/ppermute | solution.py:35
  29.6 4.3 %collective-permute-start.1 = (bf16[4,128,256]{2,1,0:T(8,128)(2,1)S(1)}, bf16[4,128,256]{2,1,0:T(8,128)(2,1)S(1)}, u32[]{:S(2)}, u32[]{:S(2)}) collective-permute-start(bf16[4,128,256]{2,1,0:T(8,128)(2,1)S(1)} %all-to-all-done.refs_0_), channel_id=1, source_target_pairs={{0,4},{2,6},{4,0},{6,2},{1,5},{3,7},{5,1},{7,3},{8,12},{10,14},{12... | collective-permute-start | bytes 786440 | tf_op jit(solution)/shard_map/ppermute | solution.py:35
  33.9 1.9 %collective-permute-start = (bf16[4,128,256]{2,1,0:T(8,128)(2,1)S(1)}, bf16[4,128,256]{2,1,0:T(8,128)(2,1)S(1)}, u32[]{:S(2)}, u32[]{:S(2)}) collective-permute-start(bf16[4,128,256]{2,1,0:T(8,128)(2,1)S(1)} %all-to-all-done.refs_0_), channel_id=1, source_target_pairs={{0,6},{2,0},{4,2},{6,4},{1,7},{3,1},{5,3},{7,5},{8,14},{10,8},{12,... | collective-permute-start | bytes 786440 | tf_op jit(solution)/shard_map/ppermute | solution.py:35
  35.9 0.1 pad_add_fusion.place_ref
  35.9 2.4 %collective-permute-done.2.refs_3_ = bf16[4,128,256]{2,1,0:T(8,128)(2,1)S(1)} collective-permute-done((bf16[4,128,256]{2,1,0:T(8,128)(2,1)S(1)}, bf16[4,128,256]{2,1,0:T(8,128)(2,1)S(1)}, u32[]{:S(2)}, u32[]{:S(2)}) %collective-permute-start.2) | collective-permute-done | bytes 262176 | tf_op jit(solution)/shard_map/ppermute | solution.py:35
  38.3 3.5 %collective-permute-done.1.refs_2_ = bf16[4,128,256]{2,1,0:T(8,128)(2,1)S(1)} collective-permute-done((bf16[4,128,256]{2,1,0:T(8,128)(2,1)S(1)}, bf16[4,128,256]{2,1,0:T(8,128)(2,1)S(1)}, u32[]{:S(2)}, u32[]{:S(2)}) %collective-permute-start.1) | collective-permute-done | bytes 262176 | tf_op jit(solution)/shard_map/ppermute | solution.py:35
  41.9 3.9 %collective-permute-done.refs_1_ = bf16[4,128,256]{2,1,0:T(8,128)(2,1)S(1)} collective-permute-done((bf16[4,128,256]{2,1,0:T(8,128)(2,1)S(1)}, bf16[4,128,256]{2,1,0:T(8,128)(2,1)S(1)}, u32[]{:S(2)}, u32[]{:S(2)}) %collective-permute-start) | collective-permute-done | bytes 262176 | tf_op jit(solution)/shard_map/ppermute | solution.py:35
  45.7 0.5 shard_map.42
  46.2 10.3 %all-to-all-done.1.first_ref = bf16[32,64,256]{2,1,0:T(8,128)(2,1)S(1)} async-done(((bf16[32,64,256]{2,1,0:T(8,128)(2,1)}), bf16[32,64,256]{2,1,0:T(8,128)(2,1)S(1)}, u32[]{:S(2)}, u32[]{:S(2)}) %all-to-all-start.1) | async-done | bytes 1048608 | tf_op jit(solution)/shard_map/all_to_all | solution.py:26
  56.5 0.1 broadcast_in_dim.7
  56.7 5.4 %all_to_all.25.second_ref = bf16[2,2064,256]{2,1,0:T(8,128)(2,1)S(1)} all-to-all(bf16[2,2064,256]{2,1,0:T(8,128)(2,1)S(1)} %broadcast_in_dim.7), channel_id=1, replica_groups=mesh['zh'=4,'yk'=4,'yl'=2,'zl'=2,'x'=4,'core'=2] {'core'}, dimensions={0} | all-to-all | bytes 4227072 | tf_op jit(solution)/shard_map/all_to_all | solution.py:26
  62.1 4.9 %shard_map.43 = (bf16[16,2,128,256]{3,2,1,0:T(8,128)(2,1)S(1)}, bf16[2048,256]{1,0:T(8,128)(2,1)}) custom-call(s32[4]{0:T(128)S(1)} %pad_add_fusion.place_ref, bf16[32,64,256]{2,1,0:T(8,128)(2,1)S(1)} %all-to-all-done.1.first_ref, bf16[2,2064,256]{2,1,0:T(8,128)(2,1)S(1)} %all_to_all.25.second_ref), custom_call_target="tpu_custom_call" | custom-call | flops 1610612736 | bytes 6291456 | tf_op jit(solution)/shard_map/pallas_call | solution.py:258
  67.0 5.4 %all_to_all.26 = bf16[2,4,4,128,256]{4,3,2,1,0:T(8,128)(2,1)S(1)} all-to-all(bf16[2,4,4,128,256]{4,3,2,1,0:T(8,128)(2,1)S(1)} %bitcast.30), channel_id=1, replica_groups=mesh['zh'=4,'yk'=4,'yl'=2,'zl'=2,'x'=4,'core'=2] {'core'}, dimensions={0} | all-to-all | bytes 4194304 | tf_op jit(solution)/shard_map/all_to_all | solution.py:26
  72.4 7.1 %all-to-all-start.3 = ((bf16[32,64,256]{2,1,0:T(8,128)(2,1)}), bf16[32,64,256]{2,1,0:T(8,128)(2,1)S(1)}, u32[]{:S(2)}, u32[]{:S(2)}) async-start(bf16[32,64,256]{2,1,0:T(8,128)(2,1)} %bitcast.32), calls=%async_computation.3 | async-start | bytes 2097152 | tf_op jit(solution)/shard_map/all_to_all | solution.py:26
  79.4 0.3 add_convert_fusion
  79.8 0.1 slice_bitcast_fusion.2
  79.8 2.4 %collective-permute-start.3 = (bf16[4,128,256]{2,1,0:T(8,128)(2,1)S(1)}, bf16[4,128,256]{2,1,0:T(8,128)(2,1)S(1)}, u32[]{:S(2)}, u32[]{:S(2)}) collective-permute-start(bf16[4,128,256]{2,1,0:T(8,128)(2,1)S(1)} %get-tuple-element.24), channel_id=1, source_target_pairs={{0,2},{2,4},{4,6},{6,0},{1,3},{3,5},{5,7},{7,1},{8,10},{10,12},{12... | collective-permute-start | bytes 786440 | tf_op jit(solution)/shard_map/ppermute | solution.py:35
  82.2 3.5 %collective-permute-start.5 = (bf16[4,128,256]{2,1,0:T(8,128)(2,1)S(1)}, bf16[4,128,256]{2,1,0:T(8,128)(2,1)S(1)}, u32[]{:S(2)}, u32[]{:S(2)}) collective-permute-start(bf16[4,128,256]{2,1,0:T(8,128)(2,1)S(1)} %get-tuple-element.25), channel_id=1, source_target_pairs={{0,6},{2,0},{4,2},{6,4},{1,7},{3,1},{5,3},{7,5},{8,14},{10,8},{12,... | collective-permute-start | bytes 786440 | tf_op jit(solution)/shard_map/ppermute | solution.py:35
  85.7 3.3 %collective-permute-start.4 = (bf16[4,128,256]{2,1,0:T(8,128)(2,1)S(1)}, bf16[4,128,256]{2,1,0:T(8,128)(2,1)S(1)}, u32[]{:S(2)}, u32[]{:S(2)}) collective-permute-start(bf16[4,128,256]{2,1,0:T(8,128)(2,1)S(1)} %get-tuple-element.26), channel_id=1, source_target_pairs={{0,4},{2,6},{4,0},{6,2},{1,5},{3,7},{5,1},{7,3},{8,12},{10,14},{12... | collective-permute-start | bytes 786440 | tf_op jit(solution)/shard_map/ppermute | solution.py:35
  89.0 0.8 collective-permute-done.3
  89.8 8.9 %collective-permute-done.5 = bf16[4,128,256]{2,1,0:T(8,128)(2,1)S(1)} collective-permute-done((bf16[4,128,256]{2,1,0:T(8,128)(2,1)S(1)}, bf16[4,128,256]{2,1,0:T(8,128)(2,1)S(1)}, u32[]{:S(2)}, u32[]{:S(2)}) %collective-permute-start.5) | collective-permute-done | bytes 262176 | tf_op jit(solution)/shard_map/ppermute | solution.py:35
  98.7 0.0 collective-permute-done.4
  98.7 0.1 fusion.2
  98.9 3.9 %collective-permute-start.8 = (bf16[128,256]{1,0:T(8,128)(2,1)S(1)}, bf16[128,256]{1,0:T(8,128)(2,1)S(1)}, u32[]{:S(2)}, u32[]{:S(2)}) collective-permute-start(bf16[128,256]{1,0:T(8,128)(2,1)S(1)} %get-tuple-element.27), channel_id=1, source_target_pairs={{0,24},{8,16},{16,8},{24,0},{1,25},{9,17},{17,9},{25,1},{2,26},{10... | collective-permute-start | bytes 196616 | tf_op jit(solution)/shard_map/ppermute | solution.py:31
  102.8 2.9 %collective-permute-start.7 = (bf16[128,256]{1,0:T(8,128)(2,1)S(1)}, bf16[128,256]{1,0:T(8,128)(2,1)S(1)}, u32[]{:S(2)}, u32[]{:S(2)}) collective-permute-start(bf16[128,256]{1,0:T(8,128)(2,1)S(1)} %get-tuple-element.28), channel_id=1, source_target_pairs={{0,8},{8,0},{16,24},{24,16},{1,9},{9,1},{17,25},{25,17},{2,10},{10... | collective-permute-start | bytes 196616 | tf_op jit(solution)/shard_map/ppermute | solution.py:31
  105.7 2.4 %collective-permute-start.6 = (bf16[128,256]{1,0:T(8,128)(2,1)S(1)}, bf16[128,256]{1,0:T(8,128)(2,1)S(1)}, u32[]{:S(2)}, u32[]{:S(2)}) collective-permute-start(bf16[128,256]{1,0:T(8,128)(2,1)S(1)} %get-tuple-element.29), channel_id=1, source_target_pairs={{0,16},{8,24},{16,0},{24,8},{1,17},{9,25},{17,1},{25,9},{2,18},{10... | collective-permute-start | bytes 196616 | tf_op jit(solution)/shard_map/ppermute | solution.py:31
  108.1 1.5 %all-to-all-done.3 = bf16[32,64,256]{2,1,0:T(8,128)(2,1)S(1)} async-done(((bf16[32,64,256]{2,1,0:T(8,128)(2,1)}), bf16[32,64,256]{2,1,0:T(8,128)(2,1)S(1)}, u32[]{:S(2)}, u32[]{:S(2)}) %all-to-all-start.3) | async-done | bytes 1048608 | tf_op jit(solution)/shard_map/all_to_all | solution.py:26
  109.6 0.1 reduce_sum.12
  109.7 0.6 pad_maximum_fusion
  110.4 0.0 collective-permute-done.8
  110.4 0.0 collective-permute-done.7
  110.4 1.5 %collective-permute-done.6 = bf16[128,256]{1,0:T(8,128)(2,1)S(1)} collective-permute-done((bf16[128,256]{1,0:T(8,128)(2,1)S(1)}, bf16[128,256]{1,0:T(8,128)(2,1)S(1)}, u32[]{:S(2)}, u32[]{:S(2)}) %collective-permute-start.6) | collective-permute-done | bytes 65568 | tf_op jit(solution)/shard_map/ppermute | solution.py:31
  111.9 0.7 add_convert_fusion.1
  (2 shorter events, 0.0 us)
Async XLA Ops:
  2.2 10.0 %all-to-all-start = ((bf16[4,128,256]{2,1,0:T(8,128)(2,1)}), bf16[4,128,256]{2,1,0:T(8,128)(2,1)S(1)}, u32[]{:S(2)}, u32[]{:S(2)}) async-start(bf16[4,128,256]{2,1,0:T(8,128)(2,1)} %broadcast_in_dim.6), calls=%async_computation | async-start | bytes 524288 | tf_op jit(solution)/shard_map/all_to_all | solution.py:26
  12.2 44.3 %all-to-all-start.1 = ((bf16[32,64,256]{2,1,0:T(8,128)(2,1)}), bf16[32,64,256]{2,1,0:T(8,128)(2,1)S(1)}, u32[]{:S(2)}, u32[]{:S(2)}) async-start(bf16[32,64,256]{2,1,0:T(8,128)(2,1)} %shard_map.41), calls=%async_computation.1 | async-start | bytes 2097152 | tf_op jit(solution)/shard_map/all_to_all | solution.py:26
  27.2 11.1 %collective-permute-start.2 = (bf16[4,128,256]{2,1,0:T(8,128)(2,1)S(1)}, bf16[4,128,256]{2,1,0:T(8,128)(2,1)S(1)}, u32[]{:S(2)}, u32[]{:S(2)}) collective-permute-start(bf16[4,128,256]{2,1,0:T(8,128)(2,1)S(1)} %all-to-all-done.refs_0_), channel_id=1, source_target_pairs={{0,2},{2,4},{4,6},{6,0},{1,3},{3,5},{5,7},{7,1},{8,10},{10,12},{12... | collective-permute-start | bytes 786440 | tf_op jit(solution)/shard_map/ppermute | solution.py:35
  29.6 12.3 %collective-permute-start.1 = (bf16[4,128,256]{2,1,0:T(8,128)(2,1)S(1)}, bf16[4,128,256]{2,1,0:T(8,128)(2,1)S(1)}, u32[]{:S(2)}, u32[]{:S(2)}) collective-permute-start(bf16[4,128,256]{2,1,0:T(8,128)(2,1)S(1)} %all-to-all-done.refs_0_), channel_id=1, source_target_pairs={{0,4},{2,6},{4,0},{6,2},{1,5},{3,7},{5,1},{7,3},{8,12},{10,14},{12... | collective-permute-start | bytes 786440 | tf_op jit(solution)/shard_map/ppermute | solution.py:35
  33.9 11.8 %collective-permute-start = (bf16[4,128,256]{2,1,0:T(8,128)(2,1)S(1)}, bf16[4,128,256]{2,1,0:T(8,128)(2,1)S(1)}, u32[]{:S(2)}, u32[]{:S(2)}) collective-permute-start(bf16[4,128,256]{2,1,0:T(8,128)(2,1)S(1)} %all-to-all-done.refs_0_), channel_id=1, source_target_pairs={{0,6},{2,0},{4,2},{6,4},{1,7},{3,1},{5,3},{7,5},{8,14},{10,8},{12,... | collective-permute-start | bytes 786440 | tf_op jit(solution)/shard_map/ppermute | solution.py:35
  72.4 37.2 %all-to-all-start.3 = ((bf16[32,64,256]{2,1,0:T(8,128)(2,1)}), bf16[32,64,256]{2,1,0:T(8,128)(2,1)S(1)}, u32[]{:S(2)}, u32[]{:S(2)}) async-start(bf16[32,64,256]{2,1,0:T(8,128)(2,1)} %bitcast.32), calls=%async_computation.3 | async-start | bytes 2097152 | tf_op jit(solution)/shard_map/all_to_all | solution.py:26
  79.8 10.0 %collective-permute-start.3 = (bf16[4,128,256]{2,1,0:T(8,128)(2,1)S(1)}, bf16[4,128,256]{2,1,0:T(8,128)(2,1)S(1)}, u32[]{:S(2)}, u32[]{:S(2)}) collective-permute-start(bf16[4,128,256]{2,1,0:T(8,128)(2,1)S(1)} %get-tuple-element.24), channel_id=1, source_target_pairs={{0,2},{2,4},{4,6},{6,0},{1,3},{3,5},{5,7},{7,1},{8,10},{10,12},{12... | collective-permute-start | bytes 786440 | tf_op jit(solution)/shard_map/ppermute | solution.py:35
  82.2 16.5 %collective-permute-start.5 = (bf16[4,128,256]{2,1,0:T(8,128)(2,1)S(1)}, bf16[4,128,256]{2,1,0:T(8,128)(2,1)S(1)}, u32[]{:S(2)}, u32[]{:S(2)}) collective-permute-start(bf16[4,128,256]{2,1,0:T(8,128)(2,1)S(1)} %get-tuple-element.25), channel_id=1, source_target_pairs={{0,6},{2,0},{4,2},{6,4},{1,7},{3,1},{5,3},{7,5},{8,14},{10,8},{12,... | collective-permute-start | bytes 786440 | tf_op jit(solution)/shard_map/ppermute | solution.py:35
  85.7 13.0 %collective-permute-start.4 = (bf16[4,128,256]{2,1,0:T(8,128)(2,1)S(1)}, bf16[4,128,256]{2,1,0:T(8,128)(2,1)S(1)}, u32[]{:S(2)}, u32[]{:S(2)}) collective-permute-start(bf16[4,128,256]{2,1,0:T(8,128)(2,1)S(1)} %get-tuple-element.26), channel_id=1, source_target_pairs={{0,4},{2,6},{4,0},{6,2},{1,5},{3,7},{5,1},{7,3},{8,12},{10,14},{12... | collective-permute-start | bytes 786440 | tf_op jit(solution)/shard_map/ppermute | solution.py:35
  98.9 11.5 %collective-permute-start.8 = (bf16[128,256]{1,0:T(8,128)(2,1)S(1)}, bf16[128,256]{1,0:T(8,128)(2,1)S(1)}, u32[]{:S(2)}, u32[]{:S(2)}) collective-permute-start(bf16[128,256]{1,0:T(8,128)(2,1)S(1)} %get-tuple-element.27), channel_id=1, source_target_pairs={{0,24},{8,16},{16,8},{24,0},{1,25},{9,17},{17,9},{25,1},{2,26},{10... | collective-permute-start | bytes 196616 | tf_op jit(solution)/shard_map/ppermute | solution.py:31
  102.8 7.6 %collective-permute-start.7 = (bf16[128,256]{1,0:T(8,128)(2,1)S(1)}, bf16[128,256]{1,0:T(8,128)(2,1)S(1)}, u32[]{:S(2)}, u32[]{:S(2)}) collective-permute-start(bf16[128,256]{1,0:T(8,128)(2,1)S(1)} %get-tuple-element.28), channel_id=1, source_target_pairs={{0,8},{8,0},{16,24},{24,16},{1,9},{9,1},{17,25},{25,17},{2,10},{10... | collective-permute-start | bytes 196616 | tf_op jit(solution)/shard_map/ppermute | solution.py:31
  105.7 6.2 %collective-permute-start.6 = (bf16[128,256]{1,0:T(8,128)(2,1)S(1)}, bf16[128,256]{1,0:T(8,128)(2,1)S(1)}, u32[]{:S(2)}, u32[]{:S(2)}) collective-permute-start(bf16[128,256]{1,0:T(8,128)(2,1)S(1)} %get-tuple-element.29), channel_id=1, source_target_pairs={{0,16},{8,24},{16,0},{24,8},{1,17},{9,25},{17,1},{25,9},{2,18},{10... | collective-permute-start | bytes 196616 | tf_op jit(solution)/shard_map/ppermute | solution.py:31

commit v13 on v12

--- a/solution.py
+++ b/solution.py
@@ -304,7 +304,7 @@
 
     pieces = exchange(moved.reshape(2, 4, 4, rows_b, width_b), "core")
     pieces = narrow_sum(pieces[0], pieces[1])
-    pieces = narrow_sum(pieces[0], *[shift(pieces[k], k) for k in (1, 2, 3)])
+    pieces = narrow_sum(pieces[0], *[shift(pieces[k], k) for k in (2, 1, 3)])
     pieces = [pieces[0]] + [near_swap(pieces[k], k) for k in (1, 2, 3)]
 
     parts = exchange(partial_first.reshape(n_dp, rows_a, half), SAMPLES)

time: 114 us -> 113 us (level)
  the two profiles are of different devices: /device:TPU:6 before, /device:TPU:14 now
where the time goes in v13:
time: 113 us
  starting transfers between devices  54.3 us (48%)
  waiting for transfers between devices  35.5 us (31%)
  blocking collectives  10.8 us (10%)
  Pallas kernels  7.33 us (6%)
  other arithmetic  1.98 us (2%)
  local copies, waits for them, and re-layouts  1.8 us (2%)
    all_to_all x3, starting transfers between devices, exchange(): return lax.all_to_all(values, axes, 0, 0, tiled=True)  26.1 us
    all_to_all x3, waiting for transfers between devices, exchange(): return lax.all_to_all(values, axes, 0, 0, tiled=True)  19.5 us
    ppermute x6, starting transfers between devices, shift(): lax.ppermute(values, 'x', [(i, (i + distance) % 4) for i in range(4)])  19 us
    ppermute x6, waiting for transfers between devices, shift(): lax.ppermute(values, 'x', [(i, (i + distance) % 4) for i in range(4)])  15.9 us
    all_to_all x2, blocking collectives, exchange(): return lax.all_to_all(values, axes, 0, 0, tiled=True)  10.8 us
    ppermute x3, starting transfers between devices, near_swap(): return lax.ppermute(values, NEAR, [(i, i ^ flip) for i in range(4)])  9.21 us
    pallas_call x1, Pallas kernels, local_compute(): pl.pallas_call(tile_kernel, out_shape=(jax.ShapeDtypeStruct(pieces, BF16)...  4.89 us
  transfers between devices with their start and end apart: 12, of which 8 were waited for; matrix products, arithmetic and copies ran while one was open for 1% of the time, Pallas kernels for 2%

profile of v13, /device:TPU:14, one launch (start us, length us, event | category | flops | bytes accessed | tf_op | source)
XLA Modules:
  0.0 112.5 jit_solution(12025797735338796357)
XLA Ops:
  0.6 1.6 %broadcast_in_dim.6 = bf16[4,128,256]{2,1,0:T(8,128)(2,1)} broadcast(bf16[128,256]{1,0:T(8,128)(2,1)} %param.3), dimensions={1,2} | broadcast | bytes 327680 | tf_op jit(solution)/shard_map/broadcast_in_dim | solution.py:282
  2.2 5.1 %all-to-all-start = ((bf16[4,128,256]{2,1,0:T(8,128)(2,1)}), bf16[4,128,256]{2,1,0:T(8,128)(2,1)S(1)}, u32[]{:S(2)}, u32[]{:S(2)}) async-start(bf16[4,128,256]{2,1,0:T(8,128)(2,1)} %broadcast_in_dim.6), calls=%async_computation | async-start | bytes 524288 | tf_op jit(solution)/shard_map/all_to_all | solution.py:26
  7.3 2.0 %shard_map.41 = bf16[32,64,256]{2,1,0:T(8,128)(2,1)} custom-call(bf16[64,512]{1,0:T(8,128)(2,1)} %values_ref.1), custom_call_target="tpu_custom_call" | custom-call | bytes 2097152 | tf_op jit(solution)/shard_map/pallas_call | solution.py:231
  9.3 2.6 %all-to-all-done.refs_0_ = bf16[4,128,256]{2,1,0:T(8,128)(2,1)S(1)} async-done(((bf16[4,128,256]{2,1,0:T(8,128)(2,1)}), bf16[4,128,256]{2,1,0:T(8,128)(2,1)S(1)}, u32[]{:S(2)}, u32[]{:S(2)}) %all-to-all-start) | async-done | bytes 262176 | tf_op jit(solution)/shard_map/all_to_all | solution.py:26
  11.9 15.5 %all-to-all-start.1 = ((bf16[32,64,256]{2,1,0:T(8,128)(2,1)}), bf16[32,64,256]{2,1,0:T(8,128)(2,1)S(1)}, u32[]{:S(2)}, u32[]{:S(2)}) async-start(bf16[32,64,256]{2,1,0:T(8,128)(2,1)} %shard_map.41), calls=%async_computation.1 | async-start | bytes 2097152 | tf_op jit(solution)/shard_map/all_to_all | solution.py:26
  27.4 2.4 %collective-permute-start.2 = (bf16[4,128,256]{2,1,0:T(8,128)(2,1)S(1)}, bf16[4,128,256]{2,1,0:T(8,128)(2,1)S(1)}, u32[]{:S(2)}, u32[]{:S(2)}) collective-permute-start(bf16[4,128,256]{2,1,0:T(8,128)(2,1)S(1)} %all-to-all-done.refs_0_), channel_id=1, source_target_pairs={{0,2},{2,4},{4,6},{6,0},{1,3},{3,5},{5,7},{7,1},{8,10},{10,12},{12... | collective-permute-start | bytes 786440 | tf_op jit(solution)/shard_map/ppermute | solution.py:35
  29.8 4.3 %collective-permute-start.1 = (bf16[4,128,256]{2,1,0:T(8,128)(2,1)S(1)}, bf16[4,128,256]{2,1,0:T(8,128)(2,1)S(1)}, u32[]{:S(2)}, u32[]{:S(2)}) collective-permute-start(bf16[4,128,256]{2,1,0:T(8,128)(2,1)S(1)} %all-to-all-done.refs_0_), channel_id=1, source_target_pairs={{0,4},{2,6},{4,0},{6,2},{1,5},{3,7},{5,1},{7,3},{8,12},{10,14},{12... | collective-permute-start | bytes 786440 | tf_op jit(solution)/shard_map/ppermute | solution.py:35
  34.1 1.9 %collective-permute-start = (bf16[4,128,256]{2,1,0:T(8,128)(2,1)S(1)}, bf16[4,128,256]{2,1,0:T(8,128)(2,1)S(1)}, u32[]{:S(2)}, u32[]{:S(2)}) collective-permute-start(bf16[4,128,256]{2,1,0:T(8,128)(2,1)S(1)} %all-to-all-done.refs_0_), channel_id=1, source_target_pairs={{0,6},{2,0},{4,2},{6,4},{1,7},{3,1},{5,3},{7,5},{8,14},{10,8},{12,... | collective-permute-start | bytes 786440 | tf_op jit(solution)/shard_map/ppermute | solution.py:35
  36.1 0.1 pad_add_fusion.place_ref
  36.2 2.4 %collective-permute-done.2.refs_3_ = bf16[4,128,256]{2,1,0:T(8,128)(2,1)S(1)} collective-permute-done((bf16[4,128,256]{2,1,0:T(8,128)(2,1)S(1)}, bf16[4,128,256]{2,1,0:T(8,128)(2,1)S(1)}, u32[]{:S(2)}, u32[]{:S(2)}) %collective-permute-start.2) | collective-permute-done | bytes 262176 | tf_op jit(solution)/shard_map/ppermute | solution.py:35
  38.5 3.2 %collective-permute-done.1.refs_2_ = bf16[4,128,256]{2,1,0:T(8,128)(2,1)S(1)} collective-permute-done((bf16[4,128,256]{2,1,0:T(8,128)(2,1)S(1)}, bf16[4,128,256]{2,1,0:T(8,128)(2,1)S(1)}, u32[]{:S(2)}, u32[]{:S(2)}) %collective-permute-start.1) | collective-permute-done | bytes 262176 | tf_op jit(solution)/shard_map/ppermute | solution.py:35
  41.8 3.9 %collective-permute-done.refs_1_ = bf16[4,128,256]{2,1,0:T(8,128)(2,1)S(1)} collective-permute-done((bf16[4,128,256]{2,1,0:T(8,128)(2,1)S(1)}, bf16[4,128,256]{2,1,0:T(8,128)(2,1)S(1)}, u32[]{:S(2)}, u32[]{:S(2)}) %collective-permute-start) | collective-permute-done | bytes 262176 | tf_op jit(solution)/shard_map/ppermute | solution.py:35
  45.7 0.5 shard_map.42
  46.1 12.1 %all-to-all-done.1.first_ref = bf16[32,64,256]{2,1,0:T(8,128)(2,1)S(1)} async-done(((bf16[32,64,256]{2,1,0:T(8,128)(2,1)}), bf16[32,64,256]{2,1,0:T(8,128)(2,1)S(1)}, u32[]{:S(2)}, u32[]{:S(2)}) %all-to-all-start.1) | async-done | bytes 1048608 | tf_op jit(solution)/shard_map/all_to_all | solution.py:26
  58.2 0.1 broadcast_in_dim.7
  58.4 5.4 %all_to_all.25.second_ref = bf16[2,2064,256]{2,1,0:T(8,128)(2,1)S(1)} all-to-all(bf16[2,2064,256]{2,1,0:T(8,128)(2,1)S(1)} %broadcast_in_dim.7), channel_id=1, replica_groups=mesh['zh'=4,'yk'=4,'yl'=2,'zl'=2,'x'=4,'core'=2] {'core'}, dimensions={0} | all-to-all | bytes 4227072 | tf_op jit(solution)/shard_map/all_to_all | solution.py:26
  63.8 4.9 %shard_map.43 = (bf16[16,2,128,256]{3,2,1,0:T(8,128)(2,1)S(1)}, bf16[2048,256]{1,0:T(8,128)(2,1)}) custom-call(s32[4]{0:T(128)S(1)} %pad_add_fusion.place_ref, bf16[32,64,256]{2,1,0:T(8,128)(2,1)S(1)} %all-to-all-done.1.first_ref, bf16[2,2064,256]{2,1,0:T(8,128)(2,1)S(1)} %all_to_all.25.second_ref), custom_call_target="tpu_custom_call" | custom-call | flops 1610612736 | bytes 6291456 | tf_op jit(solution)/shard_map/pallas_call | solution.py:258
  68.7 5.4 %all_to_all.26 = bf16[2,4,4,128,256]{4,3,2,1,0:T(8,128)(2,1)S(1)} all-to-all(bf16[2,4,4,128,256]{4,3,2,1,0:T(8,128)(2,1)S(1)} %bitcast.30), channel_id=1, replica_groups=mesh['zh'=4,'yk'=4,'yl'=2,'zl'=2,'x'=4,'core'=2] {'core'}, dimensions={0} | all-to-all | bytes 4194304 | tf_op jit(solution)/shard_map/all_to_all | solution.py:26
  74.1 5.6 %all-to-all-start.3 = ((bf16[32,64,256]{2,1,0:T(8,128)(2,1)}), bf16[32,64,256]{2,1,0:T(8,128)(2,1)S(1)}, u32[]{:S(2)}, u32[]{:S(2)}) async-start(bf16[32,64,256]{2,1,0:T(8,128)(2,1)} %bitcast.32), calls=%async_computation.3 | async-start | bytes 2097152 | tf_op jit(solution)/shard_map/all_to_all | solution.py:26
  79.6 0.3 add_convert_fusion
  80.0 0.1 slice_bitcast_fusion.2
  80.0 3.3 %collective-permute-start.3 = (bf16[4,128,256]{2,1,0:T(8,128)(2,1)S(1)}, bf16[4,128,256]{2,1,0:T(8,128)(2,1)S(1)}, u32[]{:S(2)}, u32[]{:S(2)}) collective-permute-start(bf16[4,128,256]{2,1,0:T(8,128)(2,1)S(1)} %get-tuple-element.24), channel_id=1, source_target_pairs={{0,4},{2,6},{4,0},{6,2},{1,5},{3,7},{5,1},{7,3},{8,12},{10,14},{12... | collective-permute-start | bytes 786440 | tf_op jit(solution)/shard_map/ppermute | solution.py:35
  83.3 1.9 %collective-permute-start.5 = (bf16[4,128,256]{2,1,0:T(8,128)(2,1)S(1)}, bf16[4,128,256]{2,1,0:T(8,128)(2,1)S(1)}, u32[]{:S(2)}, u32[]{:S(2)}) collective-permute-start(bf16[4,128,256]{2,1,0:T(8,128)(2,1)S(1)} %get-tuple-element.25), channel_id=1, source_target_pairs={{0,6},{2,0},{4,2},{6,4},{1,7},{3,1},{5,3},{7,5},{8,14},{10,8},{12,... | collective-permute-start | bytes 786440 | tf_op jit(solution)/shard_map/ppermute | solution.py:35
  85.3 5.1 %collective-permute-start.4 = (bf16[4,128,256]{2,1,0:T(8,128)(2,1)S(1)}, bf16[4,128,256]{2,1,0:T(8,128)(2,1)S(1)}, u32[]{:S(2)}, u32[]{:S(2)}) collective-permute-start(bf16[4,128,256]{2,1,0:T(8,128)(2,1)S(1)} %get-tuple-element.26), channel_id=1, source_target_pairs={{0,2},{2,4},{4,6},{6,0},{1,3},{3,5},{5,7},{7,1},{8,10},{10,12},{12... | collective-permute-start | bytes 786440 | tf_op jit(solution)/shard_map/ppermute | solution.py:35
  90.4 2.2 %collective-permute-done.3 = bf16[4,128,256]{2,1,0:T(8,128)(2,1)S(1)} collective-permute-done((bf16[4,128,256]{2,1,0:T(8,128)(2,1)S(1)}, bf16[4,128,256]{2,1,0:T(8,128)(2,1)S(1)}, u32[]{:S(2)}, u32[]{:S(2)}) %collective-permute-start.3) | collective-permute-done | bytes 262176 | tf_op jit(solution)/shard_map/ppermute | solution.py:35
  92.7 4.2 %collective-permute-done.5 = bf16[4,128,256]{2,1,0:T(8,128)(2,1)S(1)} collective-permute-done((bf16[4,128,256]{2,1,0:T(8,128)(2,1)S(1)}, bf16[4,128,256]{2,1,0:T(8,128)(2,1)S(1)}, u32[]{:S(2)}, u32[]{:S(2)}) %collective-permute-start.5) | collective-permute-done | bytes 262176 | tf_op jit(solution)/shard_map/ppermute | solution.py:35
  96.8 0.0 collective-permute-done.4
  96.8 0.1 fusion.2
  97.0 2.9 %collective-permute-start.8 = (bf16[128,256]{1,0:T(8,128)(2,1)S(1)}, bf16[128,256]{1,0:T(8,128)(2,1)S(1)}, u32[]{:S(2)}, u32[]{:S(2)}) collective-permute-start(bf16[128,256]{1,0:T(8,128)(2,1)S(1)} %get-tuple-element.27), channel_id=1, source_target_pairs={{0,24},{8,16},{16,8},{24,0},{1,25},{9,17},{17,9},{25,1},{2,26},{10... | collective-permute-start | bytes 196616 | tf_op jit(solution)/shard_map/ppermute | solution.py:31
  100.0 2.9 %collective-permute-start.7 = (bf16[128,256]{1,0:T(8,128)(2,1)S(1)}, bf16[128,256]{1,0:T(8,128)(2,1)S(1)}, u32[]{:S(2)}, u32[]{:S(2)}) collective-permute-start(bf16[128,256]{1,0:T(8,128)(2,1)S(1)} %get-tuple-element.28), channel_id=1, source_target_pairs={{0,8},{8,0},{16,24},{24,16},{1,9},{9,1},{17,25},{25,17},{2,10},{10... | collective-permute-start | bytes 196616 | tf_op jit(solution)/shard_map/ppermute | solution.py:31
  102.8 3.4 %collective-permute-start.6 = (bf16[128,256]{1,0:T(8,128)(2,1)S(1)}, bf16[128,256]{1,0:T(8,128)(2,1)S(1)}, u32[]{:S(2)}, u32[]{:S(2)}) collective-permute-start(bf16[128,256]{1,0:T(8,128)(2,1)S(1)} %get-tuple-element.29), channel_id=1, source_target_pairs={{0,16},{8,24},{16,0},{24,8},{1,17},{9,25},{17,1},{25,9},{2,18},{10... | collective-permute-start | bytes 196616 | tf_op jit(solution)/shard_map/ppermute | solution.py:31
  106.2 4.8 %all-to-all-done.3 = bf16[32,64,256]{2,1,0:T(8,128)(2,1)S(1)} async-done(((bf16[32,64,256]{2,1,0:T(8,128)(2,1)}), bf16[32,64,256]{2,1,0:T(8,128)(2,1)S(1)}, u32[]{:S(2)}, u32[]{:S(2)}) %all-to-all-start.3) | async-done | bytes 1048608 | tf_op jit(solution)/shard_map/all_to_all | solution.py:26
  111.1 0.1 reduce_sum.12
  111.2 0.6 pad_maximum_fusion
  111.9 0.0 collective-permute-done.8
  111.9 0.0 collective-permute-done.7
  111.9 0.0 collective-permute-done.6
  111.9 0.7 add_convert_fusion.1
  (2 shorter events, 0.0 us)
Async XLA Ops:
  2.2 9.7 %all-to-all-start = ((bf16[4,128,256]{2,1,0:T(8,128)(2,1)}), bf16[4,128,256]{2,1,0:T(8,128)(2,1)S(1)}, u32[]{:S(2)}, u32[]{:S(2)}) async-start(bf16[4,128,256]{2,1,0:T(8,128)(2,1)} %broadcast_in_dim.6), calls=%async_computation | async-start | bytes 524288 | tf_op jit(solution)/shard_map/all_to_all | solution.py:26
  11.9 46.3 %all-to-all-start.1 = ((bf16[32,64,256]{2,1,0:T(8,128)(2,1)}), bf16[32,64,256]{2,1,0:T(8,128)(2,1)S(1)}, u32[]{:S(2)}, u32[]{:S(2)}) async-start(bf16[32,64,256]{2,1,0:T(8,128)(2,1)} %shard_map.41), calls=%async_computation.1 | async-start | bytes 2097152 | tf_op jit(solution)/shard_map/all_to_all | solution.py:26
  27.4 11.1 %collective-permute-start.2 = (bf16[4,128,256]{2,1,0:T(8,128)(2,1)S(1)}, bf16[4,128,256]{2,1,0:T(8,128)(2,1)S(1)}, u32[]{:S(2)}, u32[]{:S(2)}) collective-permute-start(bf16[4,128,256]{2,1,0:T(8,128)(2,1)S(1)} %all-to-all-done.refs_0_), channel_id=1, source_target_pairs={{0,2},{2,4},{4,6},{6,0},{1,3},{3,5},{5,7},{7,1},{8,10},{10,12},{12... | collective-permute-start | bytes 786440 | tf_op jit(solution)/shard_map/ppermute | solution.py:35
  29.8 12.0 %collective-permute-start.1 = (bf16[4,128,256]{2,1,0:T(8,128)(2,1)S(1)}, bf16[4,128,256]{2,1,0:T(8,128)(2,1)S(1)}, u32[]{:S(2)}, u32[]{:S(2)}) collective-permute-start(bf16[4,128,256]{2,1,0:T(8,128)(2,1)S(1)} %all-to-all-done.refs_0_), channel_id=1, source_target_pairs={{0,4},{2,6},{4,0},{6,2},{1,5},{3,7},{5,1},{7,3},{8,12},{10,14},{12... | collective-permute-start | bytes 786440 | tf_op jit(solution)/shard_map/ppermute | solution.py:35
  34.1 11.5 %collective-permute-start = (bf16[4,128,256]{2,1,0:T(8,128)(2,1)S(1)}, bf16[4,128,256]{2,1,0:T(8,128)(2,1)S(1)}, u32[]{:S(2)}, u32[]{:S(2)}) collective-permute-start(bf16[4,128,256]{2,1,0:T(8,128)(2,1)S(1)} %all-to-all-done.refs_0_), channel_id=1, source_target_pairs={{0,6},{2,0},{4,2},{6,4},{1,7},{3,1},{5,3},{7,5},{8,14},{10,8},{12,... | collective-permute-start | bytes 786440 | tf_op jit(solution)/shard_map/ppermute | solution.py:35
  74.1 37.0 %all-to-all-start.3 = ((bf16[32,64,256]{2,1,0:T(8,128)(2,1)}), bf16[32,64,256]{2,1,0:T(8,128)(2,1)S(1)}, u32[]{:S(2)}, u32[]{:S(2)}) async-start(bf16[32,64,256]{2,1,0:T(8,128)(2,1)} %bitcast.32), calls=%async_computation.3 | async-start | bytes 2097152 | tf_op jit(solution)/shard_map/all_to_all | solution.py:26
  80.0 12.6 %collective-permute-start.3 = (bf16[4,128,256]{2,1,0:T(8,128)(2,1)S(1)}, bf16[4,128,256]{2,1,0:T(8,128)(2,1)S(1)}, u32[]{:S(2)}, u32[]{:S(2)}) collective-permute-start(bf16[4,128,256]{2,1,0:T(8,128)(2,1)S(1)} %get-tuple-element.24), channel_id=1, source_target_pairs={{0,4},{2,6},{4,0},{6,2},{1,5},{3,7},{5,1},{7,3},{8,12},{10,14},{12... | collective-permute-start | bytes 786440 | tf_op jit(solution)/shard_map/ppermute | solution.py:35
  83.3 13.5 %collective-permute-start.5 = (bf16[4,128,256]{2,1,0:T(8,128)(2,1)S(1)}, bf16[4,128,256]{2,1,0:T(8,128)(2,1)S(1)}, u32[]{:S(2)}, u32[]{:S(2)}) collective-permute-start(bf16[4,128,256]{2,1,0:T(8,128)(2,1)S(1)} %get-tuple-element.25), channel_id=1, source_target_pairs={{0,6},{2,0},{4,2},{6,4},{1,7},{3,1},{5,3},{7,5},{8,14},{10,8},{12,... | collective-permute-start | bytes 786440 | tf_op jit(solution)/shard_map/ppermute | solution.py:35
  85.3 11.6 %collective-permute-start.4 = (bf16[4,128,256]{2,1,0:T(8,128)(2,1)S(1)}, bf16[4,128,256]{2,1,0:T(8,128)(2,1)S(1)}, u32[]{:S(2)}, u32[]{:S(2)}) collective-permute-start(bf16[4,128,256]{2,1,0:T(8,128)(2,1)S(1)} %get-tuple-element.26), channel_id=1, source_target_pairs={{0,2},{2,4},{4,6},{6,0},{1,3},{3,5},{5,7},{7,1},{8,10},{10,12},{12... | collective-permute-start | bytes 786440 | tf_op jit(solution)/shard_map/ppermute | solution.py:35
  97.0 14.9 %collective-permute-start.8 = (bf16[128,256]{1,0:T(8,128)(2,1)S(1)}, bf16[128,256]{1,0:T(8,128)(2,1)S(1)}, u32[]{:S(2)}, u32[]{:S(2)}) collective-permute-start(bf16[128,256]{1,0:T(8,128)(2,1)S(1)} %get-tuple-element.27), channel_id=1, source_target_pairs={{0,24},{8,16},{16,8},{24,0},{1,25},{9,17},{17,9},{25,1},{2,26},{10... | collective-permute-start | bytes 196616 | tf_op jit(solution)/shard_map/ppermute | solution.py:31
  100.0 11.9 %collective-permute-start.7 = (bf16[128,256]{1,0:T(8,128)(2,1)S(1)}, bf16[128,256]{1,0:T(8,128)(2,1)S(1)}, u32[]{:S(2)}, u32[]{:S(2)}) collective-permute-start(bf16[128,256]{1,0:T(8,128)(2,1)S(1)} %get-tuple-element.28), channel_id=1, source_target_pairs={{0,8},{8,0},{16,24},{24,16},{1,9},{9,1},{17,25},{25,17},{2,10},{10... | collective-permute-start | bytes 196616 | tf_op jit(solution)/shard_map/ppermute | solution.py:31
  102.8 9.1 %collective-permute-start.6 = (bf16[128,256]{1,0:T(8,128)(2,1)S(1)}, bf16[128,256]{1,0:T(8,128)(2,1)S(1)}, u32[]{:S(2)}, u32[]{:S(2)}) collective-permute-start(bf16[128,256]{1,0:T(8,128)(2,1)S(1)} %get-tuple-element.29), channel_id=1, source_target_pairs={{0,16},{8,24},{16,0},{24,8},{1,17},{9,25},{17,1},{25,9},{2,18},{10... | collective-permute-start | bytes 196616 | tf_op jit(solution)/shard_map/ppermute | solution.py:31

commit v14 on v13

--- a/solution.py
+++ b/solution.py
@@ -279,8 +279,9 @@
     n_dp = lax.axis_size(SAMPLES)
     half = width_a // 2
 
-    near = exchange(jnp.broadcast_to(second_view_outputs, (4, rows_b, width_b)), NEAR)
     spread = spread_halves(first_view_outputs, n_dp)
+    spread, local = lax.optimization_barrier((spread, second_view_outputs))
+    near = exchange(jnp.broadcast_to(local, (4, rows_b, width_b)), NEAR)
     near, spread = lax.optimization_barrier((near, spread))
 
     first = exchange(spread, SAMPLES)

time: 113 us -> 113 us (level)
  the two profiles are of different devices: /device:TPU:14 before, /device:TPU:6 now
where the time goes in v14:
time: 113 us; the launch traced here: 111 us
  starting transfers between devices  49.4 us (44%)
  waiting for transfers between devices  29.4 us (26%)
  blocking collectives  21 us (19%)
  Pallas kernels  7.35 us (7%)
  other arithmetic  1.98 us (2%)
    all_to_all x2, starting transfers between devices, exchange(): return lax.all_to_all(values, axes, 0, 0, tiled=True)  21.2 us
    all_to_all x3, blocking collectives, exchange(): return lax.all_to_all(values, axes, 0, 0, tiled=True)  21 us
    ppermute x6, starting transfers between devices, shift(): lax.ppermute(values, 'x', [(i, (i + distance) % 4) for i in range(4)])  19 us
    ppermute x6, waiting for transfers between devices, shift(): lax.ppermute(values, 'x', [(i, (i + distance) % 4) for i in range(4)])  15.7 us
    all_to_all x2, waiting for transfers between devices, exchange(): return lax.all_to_all(values, axes, 0, 0, tiled=True)  13.7 us
    ppermute x3, starting transfers between devices, near_swap(): return lax.ppermute(values, NEAR, [(i, i ^ flip) for i in range(4)])  9.21 us
    pallas_call x1, Pallas kernels, local_compute(): pl.pallas_call(tile_kernel, out_shape=(jax.ShapeDtypeStruct(pieces, BF16)...  4.9 us
  transfers between devices with their start and end apart: 11, of which 7 were waited for; matrix products, arithmetic and copies ran while one was open for 1% of the time, Pallas kernels for 0%

profile of v14, /device:TPU:6, one launch (start us, length us, event | category | flops | bytes accessed | tf_op | source)
XLA Modules:
  0.0 111.1 jit_solution(10251831915999970749)
XLA Ops:
  0.6 2.0 %shard_map.41 = bf16[32,64,256]{2,1,0:T(8,128)(2,1)} custom-call(bf16[64,512]{1,0:T(8,128)(2,1)} %values_ref.1), custom_call_target="tpu_custom_call" | custom-call | bytes 2097152 | tf_op jit(solution)/shard_map/pallas_call | solution.py:231
  2.6 0.9 broadcast_in_dim.6
  3.5 10.2 %all_to_all.25.refs_0_ = bf16[4,128,256]{2,1,0:T(8,128)(2,1)S(1)} all-to-all(bf16[4,128,256]{2,1,0:T(8,128)(2,1)S(1)} %broadcast_in_dim.6), channel_id=1, replica_groups=mesh['zh'=4,'yk'=4,'yl'=2,'zl'=2,'x'=4,'core'=2] {'yl','zl'}, dimensions={0} | all-to-all | bytes 524288 | tf_op jit(solution)/shard_map/all_to_all | solution.py:26
  13.6 14.2 %all-to-all-start.1 = ((bf16[32,64,256]{2,1,0:T(8,128)(2,1)}), bf16[32,64,256]{2,1,0:T(8,128)(2,1)S(1)}, u32[]{:S(2)}, u32[]{:S(2)}) async-start(bf16[32,64,256]{2,1,0:T(8,128)(2,1)} %shard_map.41), calls=%async_computation.1 | async-start | bytes 2097152 | tf_op jit(solution)/shard_map/all_to_all | solution.py:26
  27.8 2.4 %collective-permute-start.2 = (bf16[4,128,256]{2,1,0:T(8,128)(2,1)S(1)}, bf16[4,128,256]{2,1,0:T(8,128)(2,1)S(1)}, u32[]{:S(2)}, u32[]{:S(2)}) collective-permute-start(bf16[4,128,256]{2,1,0:T(8,128)(2,1)S(1)} %all_to_all.25.refs_0_), channel_id=1, source_target_pairs={{0,2},{2,4},{4,6},{6,0},{1,3},{3,5},{5,7},{7,1},{8,10},{10,12},{12... | collective-permute-start | bytes 786440 | tf_op jit(solution)/shard_map/ppermute | solution.py:35
  30.2 4.3 %collective-permute-start.1 = (bf16[4,128,256]{2,1,0:T(8,128)(2,1)S(1)}, bf16[4,128,256]{2,1,0:T(8,128)(2,1)S(1)}, u32[]{:S(2)}, u32[]{:S(2)}) collective-permute-start(bf16[4,128,256]{2,1,0:T(8,128)(2,1)S(1)} %all_to_all.25.refs_0_), channel_id=1, source_target_pairs={{0,4},{2,6},{4,0},{6,2},{1,5},{3,7},{5,1},{7,3},{8,12},{10,14},{12... | collective-permute-start | bytes 786440 | tf_op jit(solution)/shard_map/ppermute | solution.py:35
  34.5 1.9 %collective-permute-start = (bf16[4,128,256]{2,1,0:T(8,128)(2,1)S(1)}, bf16[4,128,256]{2,1,0:T(8,128)(2,1)S(1)}, u32[]{:S(2)}, u32[]{:S(2)}) collective-permute-start(bf16[4,128,256]{2,1,0:T(8,128)(2,1)S(1)} %all_to_all.25.refs_0_), channel_id=1, source_target_pairs={{0,6},{2,0},{4,2},{6,4},{1,7},{3,1},{5,3},{7,5},{8,14},{10,8},{12,... | collective-permute-start | bytes 786440 | tf_op jit(solution)/shard_map/ppermute | solution.py:35
  36.5 0.1 pad_add_fusion.place_ref
  36.6 2.4 %collective-permute-done.2.refs_3_ = bf16[4,128,256]{2,1,0:T(8,128)(2,1)S(1)} collective-permute-done((bf16[4,128,256]{2,1,0:T(8,128)(2,1)S(1)}, bf16[4,128,256]{2,1,0:T(8,128)(2,1)S(1)}, u32[]{:S(2)}, u32[]{:S(2)}) %collective-permute-start.2) | collective-permute-done | bytes 262176 | tf_op jit(solution)/shard_map/ppermute | solution.py:35
  38.9 3.1 %collective-permute-done.1.refs_2_ = bf16[4,128,256]{2,1,0:T(8,128)(2,1)S(1)} collective-permute-done((bf16[4,128,256]{2,1,0:T(8,128)(2,1)S(1)}, bf16[4,128,256]{2,1,0:T(8,128)(2,1)S(1)}, u32[]{:S(2)}, u32[]{:S(2)}) %collective-permute-start.1) | collective-permute-done | bytes 262176 | tf_op jit(solution)/shard_map/ppermute | solution.py:35
  42.0 3.6 %collective-permute-done.refs_1_ = bf16[4,128,256]{2,1,0:T(8,128)(2,1)S(1)} collective-permute-done((bf16[4,128,256]{2,1,0:T(8,128)(2,1)S(1)}, bf16[4,128,256]{2,1,0:T(8,128)(2,1)S(1)}, u32[]{:S(2)}, u32[]{:S(2)}) %collective-permute-start) | collective-permute-done | bytes 262176 | tf_op jit(solution)/shard_map/ppermute | solution.py:35
  45.6 0.5 shard_map.42
  46.1 10.4 %all-to-all-done.1.first_ref = bf16[32,64,256]{2,1,0:T(8,128)(2,1)S(1)} async-done(((bf16[32,64,256]{2,1,0:T(8,128)(2,1)}), bf16[32,64,256]{2,1,0:T(8,128)(2,1)S(1)}, u32[]{:S(2)}, u32[]{:S(2)}) %all-to-all-start.1) | async-done | bytes 1048608 | tf_op jit(solution)/shard_map/all_to_all | solution.py:26
  56.5 0.1 broadcast_in_dim.7
  56.6 5.4 %all_to_all.26.second_ref = bf16[2,2064,256]{2,1,0:T(8,128)(2,1)S(1)} all-to-all(bf16[2,2064,256]{2,1,0:T(8,128)(2,1)S(1)} %broadcast_in_dim.7), channel_id=1, replica_groups=mesh['zh'=4,'yk'=4,'yl'=2,'zl'=2,'x'=4,'core'=2] {'core'}, dimensions={0} | all-to-all | bytes 4227072 | tf_op jit(solution)/shard_map/all_to_all | solution.py:26
  62.0 4.9 %shard_map.43 = (bf16[16,2,128,256]{3,2,1,0:T(8,128)(2,1)S(1)}, bf16[2048,256]{1,0:T(8,128)(2,1)}) custom-call(s32[4]{0:T(128)S(1)} %pad_add_fusion.place_ref, bf16[32,64,256]{2,1,0:T(8,128)(2,1)S(1)} %all-to-all-done.1.first_ref, bf16[2,2064,256]{2,1,0:T(8,128)(2,1)S(1)} %all_to_all.26.second_ref), custom_call_target="tpu_custom_call" | custom-call | flops 1610612736 | bytes 6291456 | tf_op jit(solution)/shard_map/pallas_call | solution.py:258
  67.0 5.4 %all_to_all.27 = bf16[2,4,4,128,256]{4,3,2,1,0:T(8,128)(2,1)S(1)} all-to-all(bf16[2,4,4,128,256]{4,3,2,1,0:T(8,128)(2,1)S(1)} %bitcast.30), channel_id=1, replica_groups=mesh['zh'=4,'yk'=4,'yl'=2,'zl'=2,'x'=4,'core'=2] {'core'}, dimensions={0} | all-to-all | bytes 4194304 | tf_op jit(solution)/shard_map/all_to_all | solution.py:26
  72.4 7.1 %all-to-all-start.3 = ((bf16[32,64,256]{2,1,0:T(8,128)(2,1)}), bf16[32,64,256]{2,1,0:T(8,128)(2,1)S(1)}, u32[]{:S(2)}, u32[]{:S(2)}) async-start(bf16[32,64,256]{2,1,0:T(8,128)(2,1)} %bitcast.32), calls=%async_computation.3 | async-start | bytes 2097152 | tf_op jit(solution)/shard_map/all_to_all | solution.py:26
  79.4 0.3 add_convert_fusion
  79.8 0.1 slice_bitcast_fusion.2
  79.8 3.3 %collective-permute-start.3 = (bf16[4,128,256]{2,1,0:T(8,128)(2,1)S(1)}, bf16[4,128,256]{2,1,0:T(8,128)(2,1)S(1)}, u32[]{:S(2)}, u32[]{:S(2)}) collective-permute-start(bf16[4,128,256]{2,1,0:T(8,128)(2,1)S(1)} %get-tuple-element.28), channel_id=1, source_target_pairs={{0,4},{2,6},{4,0},{6,2},{1,5},{3,7},{5,1},{7,3},{8,12},{10,14},{12... | collective-permute-start | bytes 786440 | tf_op jit(solution)/shard_map/ppermute | solution.py:35
  83.1 1.9 %collective-permute-start.5 = (bf16[4,128,256]{2,1,0:T(8,128)(2,1)S(1)}, bf16[4,128,256]{2,1,0:T(8,128)(2,1)S(1)}, u32[]{:S(2)}, u32[]{:S(2)}) collective-permute-start(bf16[4,128,256]{2,1,0:T(8,128)(2,1)S(1)} %get-tuple-element.29), channel_id=1, source_target_pairs={{0,6},{2,0},{4,2},{6,4},{1,7},{3,1},{5,3},{7,5},{8,14},{10,8},{12,... | collective-permute-start | bytes 786440 | tf_op jit(solution)/shard_map/ppermute | solution.py:35
  85.1 5.1 %collective-permute-start.4 = (bf16[4,128,256]{2,1,0:T(8,128)(2,1)S(1)}, bf16[4,128,256]{2,1,0:T(8,128)(2,1)S(1)}, u32[]{:S(2)}, u32[]{:S(2)}) collective-permute-start(bf16[4,128,256]{2,1,0:T(8,128)(2,1)S(1)} %get-tuple-element.30), channel_id=1, source_target_pairs={{0,2},{2,4},{4,6},{6,0},{1,3},{3,5},{5,7},{7,1},{8,10},{10,12},{12... | collective-permute-start | bytes 786440 | tf_op jit(solution)/shard_map/ppermute | solution.py:35
  90.2 2.2 %collective-permute-done.3 = bf16[4,128,256]{2,1,0:T(8,128)(2,1)S(1)} collective-permute-done((bf16[4,128,256]{2,1,0:T(8,128)(2,1)S(1)}, bf16[4,128,256]{2,1,0:T(8,128)(2,1)S(1)}, u32[]{:S(2)}, u32[]{:S(2)}) %collective-permute-start.3) | collective-permute-done | bytes 262176 | tf_op jit(solution)/shard_map/ppermute | solution.py:35
  92.4 4.5 %collective-permute-done.5 = bf16[4,128,256]{2,1,0:T(8,128)(2,1)S(1)} collective-permute-done((bf16[4,128,256]{2,1,0:T(8,128)(2,1)S(1)}, bf16[4,128,256]{2,1,0:T(8,128)(2,1)S(1)}, u32[]{:S(2)}, u32[]{:S(2)}) %collective-permute-start.5) | collective-permute-done | bytes 262176 | tf_op jit(solution)/shard_map/ppermute | solution.py:35
  96.9 0.0 collective-permute-done.4
  96.9 0.1 fusion.2
  97.1 3.8 %collective-permute-start.8 = (bf16[128,256]{1,0:T(8,128)(2,1)S(1)}, bf16[128,256]{1,0:T(8,128)(2,1)S(1)}, u32[]{:S(2)}, u32[]{:S(2)}) collective-permute-start(bf16[128,256]{1,0:T(8,128)(2,1)S(1)} %get-tuple-element.31), channel_id=1, source_target_pairs={{0,24},{8,16},{16,8},{24,0},{1,25},{9,17},{17,9},{25,1},{2,26},{10... | collective-permute-start | bytes 196616 | tf_op jit(solution)/shard_map/ppermute | solution.py:31
  100.9 3.0 %collective-permute-start.7 = (bf16[128,256]{1,0:T(8,128)(2,1)S(1)}, bf16[128,256]{1,0:T(8,128)(2,1)S(1)}, u32[]{:S(2)}, u32[]{:S(2)}) collective-permute-start(bf16[128,256]{1,0:T(8,128)(2,1)S(1)} %get-tuple-element.32), channel_id=1, source_target_pairs={{0,8},{8,0},{16,24},{24,16},{1,9},{9,1},{17,25},{25,17},{2,10},{10... | collective-permute-start | bytes 196616 | tf_op jit(solution)/shard_map/ppermute | solution.py:31
  103.9 2.4 %collective-permute-start.6 = (bf16[128,256]{1,0:T(8,128)(2,1)S(1)}, bf16[128,256]{1,0:T(8,128)(2,1)S(1)}, u32[]{:S(2)}, u32[]{:S(2)}) collective-permute-start(bf16[128,256]{1,0:T(8,128)(2,1)S(1)} %get-tuple-element.33), channel_id=1, source_target_pairs={{0,16},{8,24},{16,0},{24,8},{1,17},{9,25},{17,1},{25,9},{2,18},{10... | collective-permute-start | bytes 196616 | tf_op jit(solution)/shard_map/ppermute | solution.py:31
  106.3 3.3 %all-to-all-done.3 = bf16[32,64,256]{2,1,0:T(8,128)(2,1)S(1)} async-done(((bf16[32,64,256]{2,1,0:T(8,128)(2,1)}), bf16[32,64,256]{2,1,0:T(8,128)(2,1)S(1)}, u32[]{:S(2)}, u32[]{:S(2)}) %all-to-all-start.3) | async-done | bytes 1048608 | tf_op jit(solution)/shard_map/all_to_all | solution.py:26
  109.6 0.1 reduce_sum.12
  109.8 0.6 pad_maximum_fusion
  110.4 0.0 collective-permute-done.8
  110.4 0.0 collective-permute-done.7
  110.4 0.0 collective-permute-done.6
  110.4 0.7 add_convert_fusion.1
  (2 shorter events, 0.0 us)
Async XLA Ops:
  13.6 42.9 %all-to-all-start.1 = ((bf16[32,64,256]{2,1,0:T(8,128)(2,1)}), bf16[32,64,256]{2,1,0:T(8,128)(2,1)S(1)}, u32[]{:S(2)}, u32[]{:S(2)}) async-start(bf16[32,64,256]{2,1,0:T(8,128)(2,1)} %shard_map.41), calls=%async_computation.1 | async-start | bytes 2097152 | tf_op jit(solution)/shard_map/all_to_all | solution.py:26
  27.8 11.1 %collective-permute-start.2 = (bf16[4,128,256]{2,1,0:T(8,128)(2,1)S(1)}, bf16[4,128,256]{2,1,0:T(8,128)(2,1)S(1)}, u32[]{:S(2)}, u32[]{:S(2)}) collective-permute-start(bf16[4,128,256]{2,1,0:T(8,128)(2,1)S(1)} %all_to_all.25.refs_0_), channel_id=1, source_target_pairs={{0,2},{2,4},{4,6},{6,0},{1,3},{3,5},{5,7},{7,1},{8,10},{10,12},{12... | collective-permute-start | bytes 786440 | tf_op jit(solution)/shard_map/ppermute | solution.py:35
  30.2 11.8 %collective-permute-start.1 = (bf16[4,128,256]{2,1,0:T(8,128)(2,1)S(1)}, bf16[4,128,256]{2,1,0:T(8,128)(2,1)S(1)}, u32[]{:S(2)}, u32[]{:S(2)}) collective-permute-start(bf16[4,128,256]{2,1,0:T(8,128)(2,1)S(1)} %all_to_all.25.refs_0_), channel_id=1, source_target_pairs={{0,4},{2,6},{4,0},{6,2},{1,5},{3,7},{5,1},{7,3},{8,12},{10,14},{12... | collective-permute-start | bytes 786440 | tf_op jit(solution)/shard_map/ppermute | solution.py:35
  34.5 11.1 %collective-permute-start = (bf16[4,128,256]{2,1,0:T(8,128)(2,1)S(1)}, bf16[4,128,256]{2,1,0:T(8,128)(2,1)S(1)}, u32[]{:S(2)}, u32[]{:S(2)}) collective-permute-start(bf16[4,128,256]{2,1,0:T(8,128)(2,1)S(1)} %all_to_all.25.refs_0_), channel_id=1, source_target_pairs={{0,6},{2,0},{4,2},{6,4},{1,7},{3,1},{5,3},{7,5},{8,14},{10,8},{12,... | collective-permute-start | bytes 786440 | tf_op jit(solution)/shard_map/ppermute | solution.py:35
  72.4 37.2 %all-to-all-start.3 = ((bf16[32,64,256]{2,1,0:T(8,128)(2,1)}), bf16[32,64,256]{2,1,0:T(8,128)(2,1)S(1)}, u32[]{:S(2)}, u32[]{:S(2)}) async-start(bf16[32,64,256]{2,1,0:T(8,128)(2,1)} %bitcast.32), calls=%async_computation.3 | async-start | bytes 2097152 | tf_op jit(solution)/shard_map/all_to_all | solution.py:26
  79.8 12.6 %collective-permute-start.3 = (bf16[4,128,256]{2,1,0:T(8,128)(2,1)S(1)}, bf16[4,128,256]{2,1,0:T(8,128)(2,1)S(1)}, u32[]{:S(2)}, u32[]{:S(2)}) collective-permute-start(bf16[4,128,256]{2,1,0:T(8,128)(2,1)S(1)} %get-tuple-element.28), channel_id=1, source_target_pairs={{0,4},{2,6},{4,0},{6,2},{1,5},{3,7},{5,1},{7,3},{8,12},{10,14},{12... | collective-permute-start | bytes 786440 | tf_op jit(solution)/shard_map/ppermute | solution.py:35
  83.1 13.8 %collective-permute-start.5 = (bf16[4,128,256]{2,1,0:T(8,128)(2,1)S(1)}, bf16[4,128,256]{2,1,0:T(8,128)(2,1)S(1)}, u32[]{:S(2)}, u32[]{:S(2)}) collective-permute-start(bf16[4,128,256]{2,1,0:T(8,128)(2,1)S(1)} %get-tuple-element.29), channel_id=1, source_target_pairs={{0,6},{2,0},{4,2},{6,4},{1,7},{3,1},{5,3},{7,5},{8,14},{10,8},{12,... | collective-permute-start | bytes 786440 | tf_op jit(solution)/shard_map/ppermute | solution.py:35
  85.1 11.8 %collective-permute-start.4 = (bf16[4,128,256]{2,1,0:T(8,128)(2,1)S(1)}, bf16[4,128,256]{2,1,0:T(8,128)(2,1)S(1)}, u32[]{:S(2)}, u32[]{:S(2)}) collective-permute-start(bf16[4,128,256]{2,1,0:T(8,128)(2,1)S(1)} %get-tuple-element.30), channel_id=1, source_target_pairs={{0,2},{2,4},{4,6},{6,0},{1,3},{3,5},{5,7},{7,1},{8,10},{10,12},{12... | collective-permute-start | bytes 786440 | tf_op jit(solution)/shard_map/ppermute | solution.py:35
  97.1 13.3 %collective-permute-start.8 = (bf16[128,256]{1,0:T(8,128)(2,1)S(1)}, bf16[128,256]{1,0:T(8,128)(2,1)S(1)}, u32[]{:S(2)}, u32[]{:S(2)}) collective-permute-start(bf16[128,256]{1,0:T(8,128)(2,1)S(1)} %get-tuple-element.31), channel_id=1, source_target_pairs={{0,24},{8,16},{16,8},{24,0},{1,25},{9,17},{17,9},{25,1},{2,26},{10... | collective-permute-start | bytes 196616 | tf_op jit(solution)/shard_map/ppermute | solution.py:31
  100.9 9.5 %collective-permute-start.7 = (bf16[128,256]{1,0:T(8,128)(2,1)S(1)}, bf16[128,256]{1,0:T(8,128)(2,1)S(1)}, u32[]{:S(2)}, u32[]{:S(2)}) collective-permute-start(bf16[128,256]{1,0:T(8,128)(2,1)S(1)} %get-tuple-element.32), channel_id=1, source_target_pairs={{0,8},{8,0},{16,24},{24,16},{1,9},{9,1},{17,25},{25,17},{2,10},{10... | collective-permute-start | bytes 196616 | tf_op jit(solution)/shard_map/ppermute | solution.py:31
  103.9 6.5 %collective-permute-start.6 = (bf16[128,256]{1,0:T(8,128)(2,1)S(1)}, bf16[128,256]{1,0:T(8,128)(2,1)S(1)}, u32[]{:S(2)}, u32[]{:S(2)}) collective-permute-start(bf16[128,256]{1,0:T(8,128)(2,1)S(1)} %get-tuple-element.33), channel_id=1, source_target_pairs={{0,16},{8,24},{16,0},{24,8},{1,17},{9,25},{17,1},{25,9},{2,18},{10... | collective-permute-start | bytes 196616 | tf_op jit(solution)/shard_map/ppermute | solution.py:31

commit v15 on v13

--- a/solution.py
+++ b/solution.py
@@ -19,7 +19,7 @@
 
 BLOCK = 128
 BLOCKS = 16
-CHUNK = 4
+CHUNK = 2
 
 
 def exchange(values, axes):
@@ -169,12 +169,14 @@
     centering_second = jnp.sum(
         jnp.dot(split_rows(mean_first), grad, preferred_element_type=F32), axis=0, keepdims=True
     )
+    grad_second = (grad_wide * scale_second).astype(BF16)
+    centering_second *= scale_second
+    projection_second *= scale_second
     for start in range(0, BLOCKS, CHUNK):
         some = slice(start * BLOCK, (start + CHUNK) * BLOCK)
-        partial = jnp.dot(na_ref[some, :], grad, preferred_element_type=F32)
+        partial = jnp.dot(na_ref[some, :], grad_second, preferred_element_type=F32)
         partial = (
-            (partial - centering_second - nb_ref[some, :].astype(F32) * projection_second)
-            * scale_second
+            partial - centering_second - nb_ref[some, :].astype(F32) * projection_second
         ).astype(BF16)
         for i in range(2):
             moved_ref[start : start + CHUNK, i] = partial[:, i * width : (i + 1) * width].reshape(
@@ -190,13 +192,15 @@
         axis=0,
         keepdims=True,
     )
+    scale_rows = jnp.broadcast_to(scale_first, (lanes, width)).T[:, :1]
+    grad_first = (grad_wide * scale_rows).astype(BF16)
+    centering_first *= scale_first
+    projection_first *= scale_first
     stores = []
     for start in range(0, BLOCKS, CHUNK):
         some = slice(start * BLOCK, (start + CHUNK) * BLOCK)
-        partial = lax.dot_general(nb_ref[some, :], grad, across, preferred_element_type=F32)
-        partial = (
-            partial - centering_first - na_ref[some, :].astype(F32) * projection_first
-        ) * scale_first
+        partial = lax.dot_general(nb_ref[some, :], grad_first, across, preferred_element_type=F32)
+        partial = partial - centering_first - na_ref[some, :].astype(F32) * projection_first
         out_ref[some, :] = partial.astype(BF16)
         for t in range(start, start + CHUNK):
             row = pl.multiple_of(sample_block(place_ref, t) * BLOCK, BLOCK)

time: 113 us -> 113 us (level)
  no operation moved by 1% of the time
where the time goes in v15:
time: 113 us; the launch traced here: 112 us
  starting transfers between devices  54.3 us (48%)
  waiting for transfers between devices  35.5 us (31%)
  blocking collectives  10.8 us (10%)
  Pallas kernels  7.16 us (6%)
  other arithmetic  1.98 us (2%)
  local copies, waits for them, and re-layouts  1.8 us (2%)
    all_to_all x3, starting transfers between devices, exchange(): return lax.all_to_all(values, axes, 0, 0, tiled=True)  26.1 us
    all_to_all x3, waiting for transfers between devices, exchange(): return lax.all_to_all(values, axes, 0, 0, tiled=True)  19.5 us
    ppermute x6, starting transfers between devices, shift(): lax.ppermute(values, 'x', [(i, (i + distance) % 4) for i in range(4)])  18.9 us
    ppermute x6, waiting for transfers between devices, shift(): lax.ppermute(values, 'x', [(i, (i + distance) % 4) for i in range(4)])  16 us
    all_to_all x2, blocking collectives, exchange(): return lax.all_to_all(values, axes, 0, 0, tiled=True)  10.8 us
    ppermute x3, starting transfers between devices, near_swap(): return lax.ppermute(values, NEAR, [(i, i ^ flip) for i in range(4)])  9.21 us
    pallas_call x1, Pallas kernels, local_compute(): pl.pallas_call(tile_kernel, out_shape=(jax.ShapeDtypeStruct(pieces, BF16)...  4.72 us
  transfers between devices with their start and end apart: 12, of which 8 were waited for; matrix products, arithmetic and copies ran while one was open for 1% of the time, Pallas kernels for 2%

profile of v15, /device:TPU:14, one launch (start us, length us, event | category | flops | bytes accessed | tf_op | source)
XLA Modules:
  0.0 112.4 jit_solution(15705363094278677709)
XLA Ops:
  0.6 1.6 %broadcast_in_dim.6 = bf16[4,128,256]{2,1,0:T(8,128)(2,1)} broadcast(bf16[128,256]{1,0:T(8,128)(2,1)} %param.3), dimensions={1,2} | broadcast | bytes 327680 | tf_op jit(solution)/shard_map/broadcast_in_dim | solution.py:286
  2.2 5.1 %all-to-all-start = ((bf16[4,128,256]{2,1,0:T(8,128)(2,1)}), bf16[4,128,256]{2,1,0:T(8,128)(2,1)S(1)}, u32[]{:S(2)}, u32[]{:S(2)}) async-start(bf16[4,128,256]{2,1,0:T(8,128)(2,1)} %broadcast_in_dim.6), calls=%async_computation | async-start | bytes 524288 | tf_op jit(solution)/shard_map/all_to_all | solution.py:26
  7.3 2.0 %shard_map.41 = bf16[32,64,256]{2,1,0:T(8,128)(2,1)} custom-call(bf16[64,512]{1,0:T(8,128)(2,1)} %values_ref.1), custom_call_target="tpu_custom_call" | custom-call | bytes 2097152 | tf_op jit(solution)/shard_map/pallas_call | solution.py:235
  9.3 2.6 %all-to-all-done.refs_0_ = bf16[4,128,256]{2,1,0:T(8,128)(2,1)S(1)} async-done(((bf16[4,128,256]{2,1,0:T(8,128)(2,1)}), bf16[4,128,256]{2,1,0:T(8,128)(2,1)S(1)}, u32[]{:S(2)}, u32[]{:S(2)}) %all-to-all-start) | async-done | bytes 262176 | tf_op jit(solution)/shard_map/all_to_all | solution.py:26
  11.9 15.5 %all-to-all-start.1 = ((bf16[32,64,256]{2,1,0:T(8,128)(2,1)}), bf16[32,64,256]{2,1,0:T(8,128)(2,1)S(1)}, u32[]{:S(2)}, u32[]{:S(2)}) async-start(bf16[32,64,256]{2,1,0:T(8,128)(2,1)} %shard_map.41), calls=%async_computation.1 | async-start | bytes 2097152 | tf_op jit(solution)/shard_map/all_to_all | solution.py:26
  27.4 2.4 %collective-permute-start.2 = (bf16[4,128,256]{2,1,0:T(8,128)(2,1)S(1)}, bf16[4,128,256]{2,1,0:T(8,128)(2,1)S(1)}, u32[]{:S(2)}, u32[]{:S(2)}) collective-permute-start(bf16[4,128,256]{2,1,0:T(8,128)(2,1)S(1)} %all-to-all-done.refs_0_), channel_id=1, source_target_pairs={{0,2},{2,4},{4,6},{6,0},{1,3},{3,5},{5,7},{7,1},{8,10},{10,12},{12... | collective-permute-start | bytes 786440 | tf_op jit(solution)/shard_map/ppermute | solution.py:35
  29.8 4.3 %collective-permute-start.1 = (bf16[4,128,256]{2,1,0:T(8,128)(2,1)S(1)}, bf16[4,128,256]{2,1,0:T(8,128)(2,1)S(1)}, u32[]{:S(2)}, u32[]{:S(2)}) collective-permute-start(bf16[4,128,256]{2,1,0:T(8,128)(2,1)S(1)} %all-to-all-done.refs_0_), channel_id=1, source_target_pairs={{0,4},{2,6},{4,0},{6,2},{1,5},{3,7},{5,1},{7,3},{8,12},{10,14},{12... | collective-permute-start | bytes 786440 | tf_op jit(solution)/shard_map/ppermute | solution.py:35
  34.1 1.9 %collective-permute-start = (bf16[4,128,256]{2,1,0:T(8,128)(2,1)S(1)}, bf16[4,128,256]{2,1,0:T(8,128)(2,1)S(1)}, u32[]{:S(2)}, u32[]{:S(2)}) collective-permute-start(bf16[4,128,256]{2,1,0:T(8,128)(2,1)S(1)} %all-to-all-done.refs_0_), channel_id=1, source_target_pairs={{0,6},{2,0},{4,2},{6,4},{1,7},{3,1},{5,3},{7,5},{8,14},{10,8},{12,... | collective-permute-start | bytes 786440 | tf_op jit(solution)/shard_map/ppermute | solution.py:35
  36.1 0.1 pad_add_fusion.place_ref
  36.2 2.4 %collective-permute-done.2.refs_3_ = bf16[4,128,256]{2,1,0:T(8,128)(2,1)S(1)} collective-permute-done((bf16[4,128,256]{2,1,0:T(8,128)(2,1)S(1)}, bf16[4,128,256]{2,1,0:T(8,128)(2,1)S(1)}, u32[]{:S(2)}, u32[]{:S(2)}) %collective-permute-start.2) | collective-permute-done | bytes 262176 | tf_op jit(solution)/shard_map/ppermute | solution.py:35
  38.5 3.2 %collective-permute-done.1.refs_2_ = bf16[4,128,256]{2,1,0:T(8,128)(2,1)S(1)} collective-permute-done((bf16[4,128,256]{2,1,0:T(8,128)(2,1)S(1)}, bf16[4,128,256]{2,1,0:T(8,128)(2,1)S(1)}, u32[]{:S(2)}, u32[]{:S(2)}) %collective-permute-start.1) | collective-permute-done | bytes 262176 | tf_op jit(solution)/shard_map/ppermute | solution.py:35
  41.8 3.9 %collective-permute-done.refs_1_ = bf16[4,128,256]{2,1,0:T(8,128)(2,1)S(1)} collective-permute-done((bf16[4,128,256]{2,1,0:T(8,128)(2,1)S(1)}, bf16[4,128,256]{2,1,0:T(8,128)(2,1)S(1)}, u32[]{:S(2)}, u32[]{:S(2)}) %collective-permute-start) | collective-permute-done | bytes 262176 | tf_op jit(solution)/shard_map/ppermute | solution.py:35
  45.7 0.5 shard_map.42
  46.1 12.1 %all-to-all-done.1.first_ref = bf16[32,64,256]{2,1,0:T(8,128)(2,1)S(1)} async-done(((bf16[32,64,256]{2,1,0:T(8,128)(2,1)}), bf16[32,64,256]{2,1,0:T(8,128)(2,1)S(1)}, u32[]{:S(2)}, u32[]{:S(2)}) %all-to-all-start.1) | async-done | bytes 1048608 | tf_op jit(solution)/shard_map/all_to_all | solution.py:26
  58.2 0.1 broadcast_in_dim.7
  58.4 5.4 %all_to_all.25.second_ref = bf16[2,2064,256]{2,1,0:T(8,128)(2,1)S(1)} all-to-all(bf16[2,2064,256]{2,1,0:T(8,128)(2,1)S(1)} %broadcast_in_dim.7), channel_id=1, replica_groups=mesh['zh'=4,'yk'=4,'yl'=2,'zl'=2,'x'=4,'core'=2] {'core'}, dimensions={0} | all-to-all | bytes 4227072 | tf_op jit(solution)/shard_map/all_to_all | solution.py:26
  63.8 4.7 %shard_map.43 = (bf16[16,2,128,256]{3,2,1,0:T(8,128)(2,1)S(1)}, bf16[2048,256]{1,0:T(8,128)(2,1)}) custom-call(s32[4]{0:T(128)S(1)} %pad_add_fusion.place_ref, bf16[32,64,256]{2,1,0:T(8,128)(2,1)S(1)} %all-to-all-done.1.first_ref, bf16[2,2064,256]{2,1,0:T(8,128)(2,1)S(1)} %all_to_all.25.second_ref), custom_call_target="tpu_custom_call" | custom-call | flops 1610612736 | bytes 6291456 | tf_op jit(solution)/shard_map/pallas_call | solution.py:262
  68.5 5.4 %all_to_all.26 = bf16[2,4,4,128,256]{4,3,2,1,0:T(8,128)(2,1)S(1)} all-to-all(bf16[2,4,4,128,256]{4,3,2,1,0:T(8,128)(2,1)S(1)} %bitcast.30), channel_id=1, replica_groups=mesh['zh'=4,'yk'=4,'yl'=2,'zl'=2,'x'=4,'core'=2] {'core'}, dimensions={0} | all-to-all | bytes 4194304 | tf_op jit(solution)/shard_map/all_to_all | solution.py:26
  73.9 5.6 %all-to-all-start.3 = ((bf16[32,64,256]{2,1,0:T(8,128)(2,1)}), bf16[32,64,256]{2,1,0:T(8,128)(2,1)S(1)}, u32[]{:S(2)}, u32[]{:S(2)}) async-start(bf16[32,64,256]{2,1,0:T(8,128)(2,1)} %bitcast.32), calls=%async_computation.3 | async-start | bytes 2097152 | tf_op jit(solution)/shard_map/all_to_all | solution.py:26
  79.5 0.3 add_convert_fusion
  79.8 0.1 slice_bitcast_fusion.2
  79.9 3.3 %collective-permute-start.3 = (bf16[4,128,256]{2,1,0:T(8,128)(2,1)S(1)}, bf16[4,128,256]{2,1,0:T(8,128)(2,1)S(1)}, u32[]{:S(2)}, u32[]{:S(2)}) collective-permute-start(bf16[4,128,256]{2,1,0:T(8,128)(2,1)S(1)} %get-tuple-element.24), channel_id=1, source_target_pairs={{0,4},{2,6},{4,0},{6,2},{1,5},{3,7},{5,1},{7,3},{8,12},{10,14},{12... | collective-permute-start | bytes 786440 | tf_op jit(solution)/shard_map/ppermute | solution.py:35
  83.1 1.9 %collective-permute-start.5 = (bf16[4,128,256]{2,1,0:T(8,128)(2,1)S(1)}, bf16[4,128,256]{2,1,0:T(8,128)(2,1)S(1)}, u32[]{:S(2)}, u32[]{:S(2)}) collective-permute-start(bf16[4,128,256]{2,1,0:T(8,128)(2,1)S(1)} %get-tuple-element.25), channel_id=1, source_target_pairs={{0,6},{2,0},{4,2},{6,4},{1,7},{3,1},{5,3},{7,5},{8,14},{10,8},{12,... | collective-permute-start | bytes 786440 | tf_op jit(solution)/shard_map/ppermute | solution.py:35
  85.1 5.1 %collective-permute-start.4 = (bf16[4,128,256]{2,1,0:T(8,128)(2,1)S(1)}, bf16[4,128,256]{2,1,0:T(8,128)(2,1)S(1)}, u32[]{:S(2)}, u32[]{:S(2)}) collective-permute-start(bf16[4,128,256]{2,1,0:T(8,128)(2,1)S(1)} %get-tuple-element.26), channel_id=1, source_target_pairs={{0,2},{2,4},{4,6},{6,0},{1,3},{3,5},{5,7},{7,1},{8,10},{10,12},{12... | collective-permute-start | bytes 786440 | tf_op jit(solution)/shard_map/ppermute | solution.py:35
  90.2 2.3 %collective-permute-done.3 = bf16[4,128,256]{2,1,0:T(8,128)(2,1)S(1)} collective-permute-done((bf16[4,128,256]{2,1,0:T(8,128)(2,1)S(1)}, bf16[4,128,256]{2,1,0:T(8,128)(2,1)S(1)}, u32[]{:S(2)}, u32[]{:S(2)}) %collective-permute-start.3) | collective-permute-done | bytes 262176 | tf_op jit(solution)/shard_map/ppermute | solution.py:35
  92.5 4.2 %collective-permute-done.5 = bf16[4,128,256]{2,1,0:T(8,128)(2,1)S(1)} collective-permute-done((bf16[4,128,256]{2,1,0:T(8,128)(2,1)S(1)}, bf16[4,128,256]{2,1,0:T(8,128)(2,1)S(1)}, u32[]{:S(2)}, u32[]{:S(2)}) %collective-permute-start.5) | collective-permute-done | bytes 262176 | tf_op jit(solution)/shard_map/ppermute | solution.py:35
  96.7 0.0 collective-permute-done.4
  96.7 0.1 fusion.2
  96.8 2.9 %collective-permute-start.8 = (bf16[128,256]{1,0:T(8,128)(2,1)S(1)}, bf16[128,256]{1,0:T(8,128)(2,1)S(1)}, u32[]{:S(2)}, u32[]{:S(2)}) collective-permute-start(bf16[128,256]{1,0:T(8,128)(2,1)S(1)} %get-tuple-element.27), channel_id=1, source_target_pairs={{0,24},{8,16},{16,8},{24,0},{1,25},{9,17},{17,9},{25,1},{2,26},{10... | collective-permute-start | bytes 196616 | tf_op jit(solution)/shard_map/ppermute | solution.py:31
  99.8 2.9 %collective-permute-start.7 = (bf16[128,256]{1,0:T(8,128)(2,1)S(1)}, bf16[128,256]{1,0:T(8,128)(2,1)S(1)}, u32[]{:S(2)}, u32[]{:S(2)}) collective-permute-start(bf16[128,256]{1,0:T(8,128)(2,1)S(1)} %get-tuple-element.28), channel_id=1, source_target_pairs={{0,8},{8,0},{16,24},{24,16},{1,9},{9,1},{17,25},{25,17},{2,10},{10... | collective-permute-start | bytes 196616 | tf_op jit(solution)/shard_map/ppermute | solution.py:31
  102.7 3.4 %collective-permute-start.6 = (bf16[128,256]{1,0:T(8,128)(2,1)S(1)}, bf16[128,256]{1,0:T(8,128)(2,1)S(1)}, u32[]{:S(2)}, u32[]{:S(2)}) collective-permute-start(bf16[128,256]{1,0:T(8,128)(2,1)S(1)} %get-tuple-element.29), channel_id=1, source_target_pairs={{0,16},{8,24},{16,0},{24,8},{1,17},{9,25},{17,1},{25,9},{2,18},{10... | collective-permute-start | bytes 196616 | tf_op jit(solution)/shard_map/ppermute | solution.py:31
  106.1 4.8 %all-to-all-done.3 = bf16[32,64,256]{2,1,0:T(8,128)(2,1)S(1)} async-done(((bf16[32,64,256]{2,1,0:T(8,128)(2,1)}), bf16[32,64,256]{2,1,0:T(8,128)(2,1)S(1)}, u32[]{:S(2)}, u32[]{:S(2)}) %all-to-all-start.3) | async-done | bytes 1048608 | tf_op jit(solution)/shard_map/all_to_all | solution.py:26
  110.9 0.1 reduce_sum.12
  111.1 0.6 pad_maximum_fusion
  111.7 0.0 collective-permute-done.8
  111.7 0.0 collective-permute-done.7
  111.7 0.0 collective-permute-done.6
  111.7 0.7 add_convert_fusion.1
  (2 shorter events, 0.0 us)
Async XLA Ops:
  2.2 9.7 %all-to-all-start = ((bf16[4,128,256]{2,1,0:T(8,128)(2,1)}), bf16[4,128,256]{2,1,0:T(8,128)(2,1)S(1)}, u32[]{:S(2)}, u32[]{:S(2)}) async-start(bf16[4,128,256]{2,1,0:T(8,128)(2,1)} %broadcast_in_dim.6), calls=%async_computation | async-start | bytes 524288 | tf_op jit(solution)/shard_map/all_to_all | solution.py:26
  11.9 46.3 %all-to-all-start.1 = ((bf16[32,64,256]{2,1,0:T(8,128)(2,1)}), bf16[32,64,256]{2,1,0:T(8,128)(2,1)S(1)}, u32[]{:S(2)}, u32[]{:S(2)}) async-start(bf16[32,64,256]{2,1,0:T(8,128)(2,1)} %shard_map.41), calls=%async_computation.1 | async-start | bytes 2097152 | tf_op jit(solution)/shard_map/all_to_all | solution.py:26
  27.4 11.1 %collective-permute-start.2 = (bf16[4,128,256]{2,1,0:T(8,128)(2,1)S(1)}, bf16[4,128,256]{2,1,0:T(8,128)(2,1)S(1)}, u32[]{:S(2)}, u32[]{:S(2)}) collective-permute-start(bf16[4,128,256]{2,1,0:T(8,128)(2,1)S(1)} %all-to-all-done.refs_0_), channel_id=1, source_target_pairs={{0,2},{2,4},{4,6},{6,0},{1,3},{3,5},{5,7},{7,1},{8,10},{10,12},{12... | collective-permute-start | bytes 786440 | tf_op jit(solution)/shard_map/ppermute | solution.py:35
  29.8 12.0 %collective-permute-start.1 = (bf16[4,128,256]{2,1,0:T(8,128)(2,1)S(1)}, bf16[4,128,256]{2,1,0:T(8,128)(2,1)S(1)}, u32[]{:S(2)}, u32[]{:S(2)}) collective-permute-start(bf16[4,128,256]{2,1,0:T(8,128)(2,1)S(1)} %all-to-all-done.refs_0_), channel_id=1, source_target_pairs={{0,4},{2,6},{4,0},{6,2},{1,5},{3,7},{5,1},{7,3},{8,12},{10,14},{12... | collective-permute-start | bytes 786440 | tf_op jit(solution)/shard_map/ppermute | solution.py:35
  34.1 11.5 %collective-permute-start = (bf16[4,128,256]{2,1,0:T(8,128)(2,1)S(1)}, bf16[4,128,256]{2,1,0:T(8,128)(2,1)S(1)}, u32[]{:S(2)}, u32[]{:S(2)}) collective-permute-start(bf16[4,128,256]{2,1,0:T(8,128)(2,1)S(1)} %all-to-all-done.refs_0_), channel_id=1, source_target_pairs={{0,6},{2,0},{4,2},{6,4},{1,7},{3,1},{5,3},{7,5},{8,14},{10,8},{12,... | collective-permute-start | bytes 786440 | tf_op jit(solution)/shard_map/ppermute | solution.py:35
  73.9 37.0 %all-to-all-start.3 = ((bf16[32,64,256]{2,1,0:T(8,128)(2,1)}), bf16[32,64,256]{2,1,0:T(8,128)(2,1)S(1)}, u32[]{:S(2)}, u32[]{:S(2)}) async-start(bf16[32,64,256]{2,1,0:T(8,128)(2,1)} %bitcast.32), calls=%async_computation.3 | async-start | bytes 2097152 | tf_op jit(solution)/shard_map/all_to_all | solution.py:26
  79.9 12.6 %collective-permute-start.3 = (bf16[4,128,256]{2,1,0:T(8,128)(2,1)S(1)}, bf16[4,128,256]{2,1,0:T(8,128)(2,1)S(1)}, u32[]{:S(2)}, u32[]{:S(2)}) collective-permute-start(bf16[4,128,256]{2,1,0:T(8,128)(2,1)S(1)} %get-tuple-element.24), channel_id=1, source_target_pairs={{0,4},{2,6},{4,0},{6,2},{1,5},{3,7},{5,1},{7,3},{8,12},{10,14},{12... | collective-permute-start | bytes 786440 | tf_op jit(solution)/shard_map/ppermute | solution.py:35
  83.1 13.5 %collective-permute-start.5 = (bf16[4,128,256]{2,1,0:T(8,128)(2,1)S(1)}, bf16[4,128,256]{2,1,0:T(8,128)(2,1)S(1)}, u32[]{:S(2)}, u32[]{:S(2)}) collective-permute-start(bf16[4,128,256]{2,1,0:T(8,128)(2,1)S(1)} %get-tuple-element.25), channel_id=1, source_target_pairs={{0,6},{2,0},{4,2},{6,4},{1,7},{3,1},{5,3},{7,5},{8,14},{10,8},{12,... | collective-permute-start | bytes 786440 | tf_op jit(solution)/shard_map/ppermute | solution.py:35
  85.1 11.6 %collective-permute-start.4 = (bf16[4,128,256]{2,1,0:T(8,128)(2,1)S(1)}, bf16[4,128,256]{2,1,0:T(8,128)(2,1)S(1)}, u32[]{:S(2)}, u32[]{:S(2)}) collective-permute-start(bf16[4,128,256]{2,1,0:T(8,128)(2,1)S(1)} %get-tuple-element.26), channel_id=1, source_target_pairs={{0,2},{2,4},{4,6},{6,0},{1,3},{3,5},{5,7},{7,1},{8,10},{10,12},{12... | collective-permute-start | bytes 786440 | tf_op jit(solution)/shard_map/ppermute | solution.py:35
  96.8 14.9 %collective-permute-start.8 = (bf16[128,256]{1,0:T(8,128)(2,1)S(1)}, bf16[128,256]{1,0:T(8,128)(2,1)S(1)}, u32[]{:S(2)}, u32[]{:S(2)}) collective-permute-start(bf16[128,256]{1,0:T(8,128)(2,1)S(1)} %get-tuple-element.27), channel_id=1, source_target_pairs={{0,24},{8,16},{16,8},{24,0},{1,25},{9,17},{17,9},{25,1},{2,26},{10... | collective-permute-start | bytes 196616 | tf_op jit(solution)/shard_map/ppermute | solution.py:31
  99.8 11.9 %collective-permute-start.7 = (bf16[128,256]{1,0:T(8,128)(2,1)S(1)}, bf16[128,256]{1,0:T(8,128)(2,1)S(1)}, u32[]{:S(2)}, u32[]{:S(2)}) collective-permute-start(bf16[128,256]{1,0:T(8,128)(2,1)S(1)} %get-tuple-element.28), channel_id=1, source_target_pairs={{0,8},{8,0},{16,24},{24,16},{1,9},{9,1},{17,25},{25,17},{2,10},{10... | collective-permute-start | bytes 196616 | tf_op jit(solution)/shard_map/ppermute | solution.py:31
  102.7 9.1 %collective-permute-start.6 = (bf16[128,256]{1,0:T(8,128)(2,1)S(1)}, bf16[128,256]{1,0:T(8,128)(2,1)S(1)}, u32[]{:S(2)}, u32[]{:S(2)}) collective-permute-start(bf16[128,256]{1,0:T(8,128)(2,1)S(1)} %get-tuple-element.29), channel_id=1, source_target_pairs={{0,16},{8,24},{16,0},{24,8},{1,17},{9,25},{17,1},{25,9},{2,18},{10... | collective-permute-start | bytes 196616 | tf_op jit(solution)/shard_map/ppermute | solution.py:31

commit v16 on v15

--- a/solution.py
+++ b/solution.py
@@ -242,6 +242,27 @@
     )(values)
 
 
+def repeat_kernel(values_hbm, out_hbm, sems):
+    copies = [
+        pltpu.make_async_copy(values_hbm, out_hbm.at[i], sems.at[i]) for i in range(out_hbm.shape[0])
+    ]
+    for copy in copies:
+        copy.start()
+    for copy in copies:
+        copy.wait()
+
+
+def repeat(values, copies):
+    hbm = pl.BlockSpec(memory_space=pltpu.HBM)
+    return pl.pallas_call(
+        repeat_kernel,
+        out_shape=pltpu.HBM((copies,) + values.shape, BF16),
+        in_specs=[hbm],
+        out_specs=hbm,
+        scratch_shapes=[pltpu.SemaphoreType.DMA((copies,))],
+    )(values)
+
+
 def gather_half(parts):
     rows = len(parts) * 4 * BLOCK + 16
     spec = pl.BlockSpec(memory_space=pltpu.VMEM)
@@ -283,7 +304,7 @@
     n_dp = lax.axis_size(SAMPLES)
     half = width_a // 2
 
-    near = exchange(jnp.broadcast_to(second_view_outputs, (4, rows_b, width_b)), NEAR)
+    near = exchange(repeat(second_view_outputs, 4), NEAR)
     spread = spread_halves(first_view_outputs, n_dp)
     near, spread = lax.optimization_barrier((near, spread))
 

time: 113 us -> 121 us (1.071)
  the two profiles are of different devices: /device:TPU:14 before, /device:TPU:6 now
where the time goes in v16:
time: 121 us; the launch traced here: 118 us
  starting transfers between devices  54.8 us (45%)
  waiting for transfers between devices  33.5 us (28%)
  Pallas kernels  16.2 us (13%)
  blocking collectives  10.8 us (9%)
  other arithmetic  1.98 us (2%)
    all_to_all x3, starting transfers between devices, exchange(): return lax.all_to_all(values, axes, 0, 0, tiled=True)  26.7 us
    ppermute x6, starting transfers between devices, shift(): lax.ppermute(values, 'x', [(i, (i + distance) % 4) for i in range(4)])  18.9 us
    all_to_all x3, waiting for transfers between devices, exchange(): return lax.all_to_all(values, axes, 0, 0, tiled=True)  17 us
    ppermute x6, waiting for transfers between devices, shift(): lax.ppermute(values, 'x', [(i, (i + distance) % 4) for i in range(4)])  16.5 us
    all_to_all x2, blocking collectives, exchange(): return lax.all_to_all(values, axes, 0, 0, tiled=True)  10.8 us
    ppermute x3, starting transfers between devices, near_swap(): return lax.ppermute(values, NEAR, [(i, i ^ flip) for i in range(4)])  9.21 us
    pallas_call x1, Pallas kernels, repeat(): pl.pallas_call(repeat_kernel, out_shape=pltpu.HBM((copies,) + values.shap...  9.08 us
    pallas_call x1, Pallas kernels, local_compute(): pl.pallas_call(tile_kernel, out_shape=(jax.ShapeDtypeStruct(pieces, BF16)...  4.73 us
  transfers between devices with their start and end apart: 12, of which 8 were waited for; matrix products, arithmetic and copies ran while one was open for 1% of the time, Pallas kernels for 2%

profile of v16, /device:TPU:6, one launch (start us, length us, event | category | flops | bytes accessed | tf_op | source)
XLA Modules:
  0.0 118.4 jit_solution(13982654568499405945)
XLA Ops:
  0.6 9.1 %shard_map.41 = bf16[4,128,256]{2,1,0:T(8,128)(2,1)} custom-call(bf16[128,256]{1,0:T(8,128)(2,1)} %values_hbm.1), custom_call_target="tpu_custom_call" | custom-call | tf_op jit(solution)/shard_map/pallas_call | solution.py:257
  9.7 4.7 %all-to-all-start = ((bf16[4,128,256]{2,1,0:T(8,128)(2,1)}), bf16[4,128,256]{2,1,0:T(8,128)(2,1)S(1)}, u32[]{:S(2)}, u32[]{:S(2)}) async-start(bf16[4,128,256]{2,1,0:T(8,128)(2,1)} %shard_map.41), calls=%async_computation | async-start | bytes 524288 | tf_op jit(solution)/shard_map/all_to_all | solution.py:26
  14.4 2.0 %shard_map.42 = bf16[32,64,256]{2,1,0:T(8,128)(2,1)} custom-call(bf16[64,512]{1,0:T(8,128)(2,1)} %values_ref.1), custom_call_target="tpu_custom_call" | custom-call | bytes 2097152 | tf_op jit(solution)/shard_map/pallas_call | solution.py:235
  16.3 3.4 %all-to-all-done.refs_0_ = bf16[4,128,256]{2,1,0:T(8,128)(2,1)S(1)} async-done(((bf16[4,128,256]{2,1,0:T(8,128)(2,1)}), bf16[4,128,256]{2,1,0:T(8,128)(2,1)S(1)}, u32[]{:S(2)}, u32[]{:S(2)}) %all-to-all-start) | async-done | bytes 262176 | tf_op jit(solution)/shard_map/all_to_all | solution.py:26
  19.8 15.0 %all-to-all-start.1 = ((bf16[32,64,256]{2,1,0:T(8,128)(2,1)}), bf16[32,64,256]{2,1,0:T(8,128)(2,1)S(1)}, u32[]{:S(2)}, u32[]{:S(2)}) async-start(bf16[32,64,256]{2,1,0:T(8,128)(2,1)} %shard_map.42), calls=%async_computation.1 | async-start | bytes 2097152 | tf_op jit(solution)/shard_map/all_to_all | solution.py:26
  34.7 2.4 %collective-permute-start.2 = (bf16[4,128,256]{2,1,0:T(8,128)(2,1)S(1)}, bf16[4,128,256]{2,1,0:T(8,128)(2,1)S(1)}, u32[]{:S(2)}, u32[]{:S(2)}) collective-permute-start(bf16[4,128,256]{2,1,0:T(8,128)(2,1)S(1)} %all-to-all-done.refs_0_), channel_id=1, source_target_pairs={{0,2},{2,4},{4,6},{6,0},{1,3},{3,5},{5,7},{7,1},{8,10},{10,12},{12... | collective-permute-start | bytes 786440 | tf_op jit(solution)/shard_map/ppermute | solution.py:35
  37.1 4.3 %collective-permute-start.1 = (bf16[4,128,256]{2,1,0:T(8,128)(2,1)S(1)}, bf16[4,128,256]{2,1,0:T(8,128)(2,1)S(1)}, u32[]{:S(2)}, u32[]{:S(2)}) collective-permute-start(bf16[4,128,256]{2,1,0:T(8,128)(2,1)S(1)} %all-to-all-done.refs_0_), channel_id=1, source_target_pairs={{0,4},{2,6},{4,0},{6,2},{1,5},{3,7},{5,1},{7,3},{8,12},{10,14},{12... | collective-permute-start | bytes 786440 | tf_op jit(solution)/shard_map/ppermute | solution.py:35
  41.4 1.9 %collective-permute-start = (bf16[4,128,256]{2,1,0:T(8,128)(2,1)S(1)}, bf16[4,128,256]{2,1,0:T(8,128)(2,1)S(1)}, u32[]{:S(2)}, u32[]{:S(2)}) collective-permute-start(bf16[4,128,256]{2,1,0:T(8,128)(2,1)S(1)} %all-to-all-done.refs_0_), channel_id=1, source_target_pairs={{0,6},{2,0},{4,2},{6,4},{1,7},{3,1},{5,3},{7,5},{8,14},{10,8},{12,... | collective-permute-start | bytes 786440 | tf_op jit(solution)/shard_map/ppermute | solution.py:35
  43.4 0.1 pad_add_fusion.place_ref
  43.5 2.4 %collective-permute-done.2.refs_3_ = bf16[4,128,256]{2,1,0:T(8,128)(2,1)S(1)} collective-permute-done((bf16[4,128,256]{2,1,0:T(8,128)(2,1)S(1)}, bf16[4,128,256]{2,1,0:T(8,128)(2,1)S(1)}, u32[]{:S(2)}, u32[]{:S(2)}) %collective-permute-start.2) | collective-permute-done | bytes 262176 | tf_op jit(solution)/shard_map/ppermute | solution.py:35
  45.9 3.5 %collective-permute-done.1.refs_2_ = bf16[4,128,256]{2,1,0:T(8,128)(2,1)S(1)} collective-permute-done((bf16[4,128,256]{2,1,0:T(8,128)(2,1)S(1)}, bf16[4,128,256]{2,1,0:T(8,128)(2,1)S(1)}, u32[]{:S(2)}, u32[]{:S(2)}) %collective-permute-start.1) | collective-permute-done | bytes 262176 | tf_op jit(solution)/shard_map/ppermute | solution.py:35
  49.4 3.9 %collective-permute-done.refs_1_ = bf16[4,128,256]{2,1,0:T(8,128)(2,1)S(1)} collective-permute-done((bf16[4,128,256]{2,1,0:T(8,128)(2,1)S(1)}, bf16[4,128,256]{2,1,0:T(8,128)(2,1)S(1)}, u32[]{:S(2)}, u32[]{:S(2)}) %collective-permute-start) | collective-permute-done | bytes 262176 | tf_op jit(solution)/shard_map/ppermute | solution.py:35
  53.2 0.5 shard_map.43
  53.7 10.3 %all-to-all-done.1.first_ref = bf16[32,64,256]{2,1,0:T(8,128)(2,1)S(1)} async-done(((bf16[32,64,256]{2,1,0:T(8,128)(2,1)}), bf16[32,64,256]{2,1,0:T(8,128)(2,1)S(1)}, u32[]{:S(2)}, u32[]{:S(2)}) %all-to-all-start.1) | async-done | bytes 1048608 | tf_op jit(solution)/shard_map/all_to_all | solution.py:26
  64.0 0.1 broadcast_in_dim.3
  64.2 5.4 %all_to_all.25.second_ref = bf16[2,2064,256]{2,1,0:T(8,128)(2,1)S(1)} all-to-all(bf16[2,2064,256]{2,1,0:T(8,128)(2,1)S(1)} %broadcast_in_dim.3), channel_id=1, replica_groups=mesh['zh'=4,'yk'=4,'yl'=2,'zl'=2,'x'=4,'core'=2] {'core'}, dimensions={0} | all-to-all | bytes 4227072 | tf_op jit(solution)/shard_map/all_to_all | solution.py:26
  69.6 4.7 %shard_map.44 = (bf16[16,2,128,256]{3,2,1,0:T(8,128)(2,1)S(1)}, bf16[2048,256]{1,0:T(8,128)(2,1)}) custom-call(s32[4]{0:T(128)S(1)} %pad_add_fusion.place_ref, bf16[32,64,256]{2,1,0:T(8,128)(2,1)S(1)} %all-to-all-done.1.first_ref, bf16[2,2064,256]{2,1,0:T(8,128)(2,1)S(1)} %all_to_all.25.second_ref), custom_call_target="tpu_custom_call" | custom-call | flops 1610612736 | bytes 6291456 | tf_op jit(solution)/shard_map/pallas_call | solution.py:283
  74.3 5.4 %all_to_all.26 = bf16[2,4,4,128,256]{4,3,2,1,0:T(8,128)(2,1)S(1)} all-to-all(bf16[2,4,4,128,256]{4,3,2,1,0:T(8,128)(2,1)S(1)} %bitcast.30), channel_id=1, replica_groups=mesh['zh'=4,'yk'=4,'yl'=2,'zl'=2,'x'=4,'core'=2] {'core'}, dimensions={0} | all-to-all | bytes 4194304 | tf_op jit(solution)/shard_map/all_to_all | solution.py:26
  79.7 7.0 %all-to-all-start.3 = ((bf16[32,64,256]{2,1,0:T(8,128)(2,1)}), bf16[32,64,256]{2,1,0:T(8,128)(2,1)S(1)}, u32[]{:S(2)}, u32[]{:S(2)}) async-start(bf16[32,64,256]{2,1,0:T(8,128)(2,1)} %bitcast.32), calls=%async_computation.3 | async-start | bytes 2097152 | tf_op jit(solution)/shard_map/all_to_all | solution.py:26
  86.8 0.3 add_convert_fusion
  87.1 0.1 slice_bitcast_fusion.2
  87.2 3.3 %collective-permute-start.3 = (bf16[4,128,256]{2,1,0:T(8,128)(2,1)S(1)}, bf16[4,128,256]{2,1,0:T(8,128)(2,1)S(1)}, u32[]{:S(2)}, u32[]{:S(2)}) collective-permute-start(bf16[4,128,256]{2,1,0:T(8,128)(2,1)S(1)} %get-tuple-element.24), channel_id=1, source_target_pairs={{0,4},{2,6},{4,0},{6,2},{1,5},{3,7},{5,1},{7,3},{8,12},{10,14},{12... | collective-permute-start | bytes 786440 | tf_op jit(solution)/shard_map/ppermute | solution.py:35
  90.4 1.9 %collective-permute-start.5 = (bf16[4,128,256]{2,1,0:T(8,128)(2,1)S(1)}, bf16[4,128,256]{2,1,0:T(8,128)(2,1)S(1)}, u32[]{:S(2)}, u32[]{:S(2)}) collective-permute-start(bf16[4,128,256]{2,1,0:T(8,128)(2,1)S(1)} %get-tuple-element.25), channel_id=1, source_target_pairs={{0,6},{2,0},{4,2},{6,4},{1,7},{3,1},{5,3},{7,5},{8,14},{10,8},{12,... | collective-permute-start | bytes 786440 | tf_op jit(solution)/shard_map/ppermute | solution.py:35
  92.4 5.1 %collective-permute-start.4 = (bf16[4,128,256]{2,1,0:T(8,128)(2,1)S(1)}, bf16[4,128,256]{2,1,0:T(8,128)(2,1)S(1)}, u32[]{:S(2)}, u32[]{:S(2)}) collective-permute-start(bf16[4,128,256]{2,1,0:T(8,128)(2,1)S(1)} %get-tuple-element.26), channel_id=1, source_target_pairs={{0,2},{2,4},{4,6},{6,0},{1,3},{3,5},{5,7},{7,1},{8,10},{10,12},{12... | collective-permute-start | bytes 786440 | tf_op jit(solution)/shard_map/ppermute | solution.py:35
  97.5 2.3 %collective-permute-done.3 = bf16[4,128,256]{2,1,0:T(8,128)(2,1)S(1)} collective-permute-done((bf16[4,128,256]{2,1,0:T(8,128)(2,1)S(1)}, bf16[4,128,256]{2,1,0:T(8,128)(2,1)S(1)}, u32[]{:S(2)}, u32[]{:S(2)}) %collective-permute-start.3) | collective-permute-done | bytes 262176 | tf_op jit(solution)/shard_map/ppermute | solution.py:35
  99.8 4.5 %collective-permute-done.5 = bf16[4,128,256]{2,1,0:T(8,128)(2,1)S(1)} collective-permute-done((bf16[4,128,256]{2,1,0:T(8,128)(2,1)S(1)}, bf16[4,128,256]{2,1,0:T(8,128)(2,1)S(1)}, u32[]{:S(2)}, u32[]{:S(2)}) %collective-permute-start.5) | collective-permute-done | bytes 262176 | tf_op jit(solution)/shard_map/ppermute | solution.py:35
  104.2 0.0 collective-permute-done.4
  104.2 0.1 fusion.2
  104.4 3.9 %collective-permute-start.8 = (bf16[128,256]{1,0:T(8,128)(2,1)S(1)}, bf16[128,256]{1,0:T(8,128)(2,1)S(1)}, u32[]{:S(2)}, u32[]{:S(2)}) collective-permute-start(bf16[128,256]{1,0:T(8,128)(2,1)S(1)} %get-tuple-element.27), channel_id=1, source_target_pairs={{0,24},{8,16},{16,8},{24,0},{1,25},{9,17},{17,9},{25,1},{2,26},{10... | collective-permute-start | bytes 196616 | tf_op jit(solution)/shard_map/ppermute | solution.py:31
  108.3 2.9 %collective-permute-start.7 = (bf16[128,256]{1,0:T(8,128)(2,1)S(1)}, bf16[128,256]{1,0:T(8,128)(2,1)S(1)}, u32[]{:S(2)}, u32[]{:S(2)}) collective-permute-start(bf16[128,256]{1,0:T(8,128)(2,1)S(1)} %get-tuple-element.28), channel_id=1, source_target_pairs={{0,8},{8,0},{16,24},{24,16},{1,9},{9,1},{17,25},{25,17},{2,10},{10... | collective-permute-start | bytes 196616 | tf_op jit(solution)/shard_map/ppermute | solution.py:31
  111.2 2.4 %collective-permute-start.6 = (bf16[128,256]{1,0:T(8,128)(2,1)S(1)}, bf16[128,256]{1,0:T(8,128)(2,1)S(1)}, u32[]{:S(2)}, u32[]{:S(2)}) collective-permute-start(bf16[128,256]{1,0:T(8,128)(2,1)S(1)} %get-tuple-element.29), channel_id=1, source_target_pairs={{0,16},{8,24},{16,0},{24,8},{1,17},{9,25},{17,1},{25,9},{2,18},{10... | collective-permute-start | bytes 196616 | tf_op jit(solution)/shard_map/ppermute | solution.py:31
  113.7 3.3 %all-to-all-done.3 = bf16[32,64,256]{2,1,0:T(8,128)(2,1)S(1)} async-done(((bf16[32,64,256]{2,1,0:T(8,128)(2,1)}), bf16[32,64,256]{2,1,0:T(8,128)(2,1)S(1)}, u32[]{:S(2)}, u32[]{:S(2)}) %all-to-all-start.3) | async-done | bytes 1048608 | tf_op jit(solution)/shard_map/all_to_all | solution.py:26
  116.9 0.1 reduce_sum.12
  117.1 0.6 pad_maximum_fusion
  117.7 0.0 collective-permute-done.8
  117.7 0.0 collective-permute-done.7
  117.7 0.0 collective-permute-done.6
  117.8 0.7 add_convert_fusion.1
  (2 shorter events, 0.0 us)
Async XLA Ops:
  9.7 10.0 %all-to-all-start = ((bf16[4,128,256]{2,1,0:T(8,128)(2,1)}), bf16[4,128,256]{2,1,0:T(8,128)(2,1)S(1)}, u32[]{:S(2)}, u32[]{:S(2)}) async-start(bf16[4,128,256]{2,1,0:T(8,128)(2,1)} %shard_map.41), calls=%async_computation | async-start | bytes 524288 | tf_op jit(solution)/shard_map/all_to_all | solution.py:26
  19.8 44.3 %all-to-all-start.1 = ((bf16[32,64,256]{2,1,0:T(8,128)(2,1)}), bf16[32,64,256]{2,1,0:T(8,128)(2,1)S(1)}, u32[]{:S(2)}, u32[]{:S(2)}) async-start(bf16[32,64,256]{2,1,0:T(8,128)(2,1)} %shard_map.42), calls=%async_computation.1 | async-start | bytes 2097152 | tf_op jit(solution)/shard_map/all_to_all | solution.py:26
  34.7 11.1 %collective-permute-start.2 = (bf16[4,128,256]{2,1,0:T(8,128)(2,1)S(1)}, bf16[4,128,256]{2,1,0:T(8,128)(2,1)S(1)}, u32[]{:S(2)}, u32[]{:S(2)}) collective-permute-start(bf16[4,128,256]{2,1,0:T(8,128)(2,1)S(1)} %all-to-all-done.refs_0_), channel_id=1, source_target_pairs={{0,2},{2,4},{4,6},{6,0},{1,3},{3,5},{5,7},{7,1},{8,10},{10,12},{12... | collective-permute-start | bytes 786440 | tf_op jit(solution)/shard_map/ppermute | solution.py:35
  37.1 12.3 %collective-permute-start.1 = (bf16[4,128,256]{2,1,0:T(8,128)(2,1)S(1)}, bf16[4,128,256]{2,1,0:T(8,128)(2,1)S(1)}, u32[]{:S(2)}, u32[]{:S(2)}) collective-permute-start(bf16[4,128,256]{2,1,0:T(8,128)(2,1)S(1)} %all-to-all-done.refs_0_), channel_id=1, source_target_pairs={{0,4},{2,6},{4,0},{6,2},{1,5},{3,7},{5,1},{7,3},{8,12},{10,14},{12... | collective-permute-start | bytes 786440 | tf_op jit(solution)/shard_map/ppermute | solution.py:35
  41.4 11.8 %collective-permute-start = (bf16[4,128,256]{2,1,0:T(8,128)(2,1)S(1)}, bf16[4,128,256]{2,1,0:T(8,128)(2,1)S(1)}, u32[]{:S(2)}, u32[]{:S(2)}) collective-permute-start(bf16[4,128,256]{2,1,0:T(8,128)(2,1)S(1)} %all-to-all-done.refs_0_), channel_id=1, source_target_pairs={{0,6},{2,0},{4,2},{6,4},{1,7},{3,1},{5,3},{7,5},{8,14},{10,8},{12,... | collective-permute-start | bytes 786440 | tf_op jit(solution)/shard_map/ppermute | solution.py:35
  79.7 37.2 %all-to-all-start.3 = ((bf16[32,64,256]{2,1,0:T(8,128)(2,1)}), bf16[32,64,256]{2,1,0:T(8,128)(2,1)S(1)}, u32[]{:S(2)}, u32[]{:S(2)}) async-start(bf16[32,64,256]{2,1,0:T(8,128)(2,1)} %bitcast.32), calls=%async_computation.3 | async-start | bytes 2097152 | tf_op jit(solution)/shard_map/all_to_all | solution.py:26
  87.2 12.6 %collective-permute-start.3 = (bf16[4,128,256]{2,1,0:T(8,128)(2,1)S(1)}, bf16[4,128,256]{2,1,0:T(8,128)(2,1)S(1)}, u32[]{:S(2)}, u32[]{:S(2)}) collective-permute-start(bf16[4,128,256]{2,1,0:T(8,128)(2,1)S(1)} %get-tuple-element.24), channel_id=1, source_target_pairs={{0,4},{2,6},{4,0},{6,2},{1,5},{3,7},{5,1},{7,3},{8,12},{10,14},{12... | collective-permute-start | bytes 786440 | tf_op jit(solution)/shard_map/ppermute | solution.py:35
  90.4 13.8 %collective-permute-start.5 = (bf16[4,128,256]{2,1,0:T(8,128)(2,1)S(1)}, bf16[4,128,256]{2,1,0:T(8,128)(2,1)S(1)}, u32[]{:S(2)}, u32[]{:S(2)}) collective-permute-start(bf16[4,128,256]{2,1,0:T(8,128)(2,1)S(1)} %get-tuple-element.25), channel_id=1, source_target_pairs={{0,6},{2,0},{4,2},{6,4},{1,7},{3,1},{5,3},{7,5},{8,14},{10,8},{12,... | collective-permute-start | bytes 786440 | tf_op jit(solution)/shard_map/ppermute | solution.py:35
  92.4 11.9 %collective-permute-start.4 = (bf16[4,128,256]{2,1,0:T(8,128)(2,1)S(1)}, bf16[4,128,256]{2,1,0:T(8,128)(2,1)S(1)}, u32[]{:S(2)}, u32[]{:S(2)}) collective-permute-start(bf16[4,128,256]{2,1,0:T(8,128)(2,1)S(1)} %get-tuple-element.26), channel_id=1, source_target_pairs={{0,2},{2,4},{4,6},{6,0},{1,3},{3,5},{5,7},{7,1},{8,10},{10,12},{12... | collective-permute-start | bytes 786440 | tf_op jit(solution)/shard_map/ppermute | solution.py:35
  104.4 13.3 %collective-permute-start.8 = (bf16[128,256]{1,0:T(8,128)(2,1)S(1)}, bf16[128,256]{1,0:T(8,128)(2,1)S(1)}, u32[]{:S(2)}, u32[]{:S(2)}) collective-permute-start(bf16[128,256]{1,0:T(8,128)(2,1)S(1)} %get-tuple-element.27), channel_id=1, source_target_pairs={{0,24},{8,16},{16,8},{24,0},{1,25},{9,17},{17,9},{25,1},{2,26},{10... | collective-permute-start | bytes 196616 | tf_op jit(solution)/shard_map/ppermute | solution.py:31
  108.3 9.4 %collective-permute-start.7 = (bf16[128,256]{1,0:T(8,128)(2,1)S(1)}, bf16[128,256]{1,0:T(8,128)(2,1)S(1)}, u32[]{:S(2)}, u32[]{:S(2)}) collective-permute-start(bf16[128,256]{1,0:T(8,128)(2,1)S(1)} %get-tuple-element.28), channel_id=1, source_target_pairs={{0,8},{8,0},{16,24},{24,16},{1,9},{9,1},{17,25},{25,17},{2,10},{10... | collective-permute-start | bytes 196616 | tf_op jit(solution)/shard_map/ppermute | solution.py:31
  111.2 6.5 %collective-permute-start.6 = (bf16[128,256]{1,0:T(8,128)(2,1)S(1)}, bf16[128,256]{1,0:T(8,128)(2,1)S(1)}, u32[]{:S(2)}, u32[]{:S(2)}) collective-permute-start(bf16[128,256]{1,0:T(8,128)(2,1)S(1)} %get-tuple-element.29), channel_id=1, source_target_pairs={{0,16},{8,24},{16,0},{24,8},{1,17},{9,25},{17,1},{25,9},{2,18},{10... | collective-permute-start | bytes 196616 | tf_op jit(solution)/shard_map/ppermute | solution.py:31
